TPU v7x, 32 devices: a whole 2x2x4 slice. The times are simulated.
32 devices in a mesh: groups: 2 (over y), particle: 16 (over z, x, core).
Axes of the slice: x: 2, y: 2, z: 4, core: 2. Of those that a mesh axis runs over, the one named last changes fastest.
Arguments:
- images: bfloat16 [1024, 32768], P(('groups', 'particle')), parts along dimension 0, may hold values from -6 to 6
- noise_precision: float32 [1024], P(('groups', 'particle')), parts along dimension 0, may hold values from 0.3 to 4.05
- assigned_class: int32 [1024], P(('groups', 'particle')), parts along dimension 0, may hold values from 0 to 7
- class_refs: bfloat16 [4, 8, 2, 32768], P('groups'), parts along dimension 0, may hold values from -6 to 6
- interp_index: int32 [16, 16384], P('particle'), may hold values from 0 to 32766
- interp_frac: float32 [16, 16384], P('particle'), may hold values from 0 to 1
- shift_grid: int32 [8, 2], replicated, may hold values from -6 to 6
Outputs:
- back_slices: float32 [32, 32768], P(('groups', 'particle')), parts along dimension 0
- class_weight: float32 [16], P('groups'), parts along dimension 0
There are 2 independent parts, one for each index of `groups`. A program takes and returns all parts, laid end to end along the dimension named above; an argument that names none is the same for every part. Nothing has to cross between parts.
All inputs are finite; a program needn't handle non-finite values.
Results may differ from a plain program's by a relative error of at most 0.0089.
Values may be sent and summed in bfloat16 or wider, within the bound.
No kernel may reach another device: no remote copies, remote signals or barrier semaphores. Data moves between devices by JAX's collectives and lax.ppermute only.
A program may use at most 128 MiB of HBM per device.

v0:
```python
import math

import jax
import jax.numpy as jnp
from jax import lax
from jax.sharding import PartitionSpec as P

KY = 128
BOX = 256
CLASSES = 8
LOWK = 16


PRIOR_REWARD = 1.0


def swapped(value, axis, bit):
    mask = 2**bit
    pairs = [(source, source ^ mask) for source in range(lax.axis_size(axis))]
    return lax.ppermute(value, axis, pairs)


def phase_tables(shift_grid, pixel_count):
    pixel_ids = jnp.arange(pixel_count, dtype=jnp.int32)
    freq_x = pixel_ids // KY
    freq_y = pixel_ids % KY - KY // 2
    phase_turns = jnp.mod(
        freq_x[None, :] * shift_grid[:, 0:1] + freq_y[None, :] * shift_grid[:, 1:2], BOX
    )
    angles = phase_turns.astype(jnp.float32) * (2.0 * math.pi / BOX)
    return (jnp.cos(angles), jnp.sin(angles))


def shift_images(images, cos_table, sin_table, pixel_count):
    real_part = images[:, :pixel_count].astype(jnp.float32)[None]
    imag_part = images[:, pixel_count:].astype(jnp.float32)[None]
    cos_b = cos_table[:, None, :]
    sin_b = sin_table[:, None, :]
    return jnp.concatenate(
        [real_part * cos_b + imag_part * sin_b, imag_part * cos_b - real_part * sin_b], axis=2
    ).astype(jnp.bfloat16)


def project_rows(ref_table, interp_index, interp_frac):
    row_count, pixel_count = interp_index.shape
    wide_index = jnp.broadcast_to(interp_index[:, None, :], (row_count, 2, pixel_count))
    low_value = jnp.take_along_axis(ref_table, wide_index, axis=2).astype(jnp.float32)
    high_value = jnp.take_along_axis(ref_table, wide_index + 1, axis=2).astype(jnp.float32)
    frac_wide = interp_frac[:, None, :]
    blended = (1.0 - frac_wide) * low_value + frac_wide * high_value
    return blended.reshape(row_count, 2 * pixel_count).astype(jnp.bfloat16)


def correlate(flat_stack, proj_rows):
    return lax.dot_general(
        flat_stack, proj_rows, (((1,), (1,)), ((), ())), preferred_element_type=jnp.float32
    )


def local(
    images, noise_precision, assigned_class, class_refs, interp_index, interp_frac, shift_grid
):
    dev_count = lax.axis_size("particle")
    dev_index = lax.axis_index("particle")
    orient_count = dev_count // 2
    half_set = dev_index // 2 % 2
    orient_row = 2 * (dev_index // 4) + dev_index % 2
    class_id = orient_row // (orient_count // CLASSES)
    pixel_count = images.shape[1] // 2
    part_count = images.shape[0]
    half_refs = lax.dynamic_index_in_dim(class_refs, half_set, 0, False)
    ref_table = lax.dynamic_index_in_dim(half_refs, class_id, 0, False)
    own_proj = project_rows(ref_table[None], interp_index, interp_frac)
    cos_table, sin_table = phase_tables(shift_grid, pixel_count)
    stacked = shift_images(images, cos_table, sin_table, pixel_count)
    shift_count = stacked.shape[0]
    flat_stack = stacked.reshape(shift_count * part_count, 2 * pixel_count)
    all_proj = lax.all_gather(own_proj, "particle", axis=0, tiled=True)
    grouped_proj = all_proj.reshape(dev_count // 4, 2, 2, 2 * pixel_count)
    half_proj = lax.dynamic_index_in_dim(grouped_proj, half_set, 1, False).reshape(
        orient_count, 2 * pixel_count
    )
    cross_correlation = correlate(flat_stack, half_proj).reshape(
        shift_count, part_count, orient_count
    )
    projection_power = jnp.sum(jnp.square(half_proj.astype(jnp.float32)), axis=1)
    class_of_row = jnp.arange(orient_count, dtype=jnp.int32) // (orient_count // CLASSES)
    likelihood_scale = 1.0 / math.sqrt(2 * pixel_count)
    match_scores = (class_of_row[None, None, :] == assigned_class[None, :, None]).astype(
        jnp.float32
    )
    log_likelihoods = (
        noise_precision[None, :, None]
        * (cross_correlation - 0.5 * projection_power[None, None, :])
        * likelihood_scale
        + PRIOR_REWARD * match_scores
    )
    peak_score = jnp.max(log_likelihoods, axis=(0, 2), keepdims=True)
    exp_terms = jnp.exp(log_likelihoods - peak_score)
    posterior = exp_terms / jnp.sum(exp_terms, axis=(0, 2), keepdims=True)
    weights = posterior.astype(jnp.bfloat16)
    class_share = (
        jnp.sum(posterior, axis=0).reshape(part_count, CLASSES, orient_count // CLASSES).sum(axis=2)
    )
    local_mass = jnp.sum(noise_precision[:, None] * class_share, axis=0)
    total_mass = lax.psum(local_mass, "particle")
    class_weight = total_mass * (CLASSES / (part_count * dev_count))
    back_term = jnp.einsum(
        "snr,snq->rq", weights, stacked, preferred_element_type=jnp.float32
    ) / math.sqrt(part_count)
    low_width = LOWK * KY
    global_rows = jnp.arange(1 * lax.axis_size("particle"), dtype=jnp.int32)
    is_valid = (global_rows // 2 % 2 == half_set).astype(jnp.float32)
    local_rows = 2 * (global_rows // 4) + global_rows % 2
    picked = jnp.take(back_term, local_rows, axis=0)
    own_row = lax.psum_scatter(
        picked * is_valid[:, None], "particle", scatter_dimension=0, tiled=True
    )
    low_slab = jnp.concatenate(
        [own_row[:, :low_width], own_row[:, pixel_count : pixel_count + low_width]], axis=1
    )
    partner = swapped(low_slab, "particle", 1)
    averaged = (low_slab + partner) * 0.5
    back_slices = jnp.concatenate(
        [
            averaged[:, :low_width],
            own_row[:, low_width:pixel_count],
            averaged[:, low_width:],
            own_row[:, pixel_count + low_width :],
        ],
        axis=1,
    )
    return (back_slices, class_weight)


def solution(mesh):
    in_specs = (
        P(("groups", "particle"), None),
        P(("groups", "particle")),
        P(("groups", "particle")),
        P("groups", None, None, None),
        P("particle", None),
        P("particle", None),
        P(),
    )
    out_specs = (P(("groups", "particle"), None), P("groups"))
    return jax.shard_map(local, mesh=mesh, in_specs=in_specs, out_specs=out_specs, check_vma=False)
```

profile of v0, /device:TPU:0, one launch (start us, length us, event | category | flops | bytes accessed | tf_op | source)
XLA Modules:
  0.0 725.7 jit_solution(49252836152048039)
XLA Ops:
  7.3 1.0 broadcast_compare_fusion
  8.3 0.9 broadcast_add_fusion.2
  9.2 1.2 fusion.14
  10.5 260.3 %gather_fusion.1 = bf16[32768]{0:T(1024)(128)(2,1)S(1)} fusion(bf16[2,32768]{1,0:T(2,128)(2,1)S(1)} %dynamic-slice_bitcast_fusion, s32[32768]{0:T(1024)S(1)} %bitcast.39), kind=kCustom, calls=%fused_computation.clone | custom fusion | bytes 393216 | tf_op jit(solution)/shard_map/jit(take_along_axis)/gather | solution.py:47
  270.9 260.3 %gather_fusion.2 = bf16[32768]{0:T(1024)(128)(2,1)S(1)} fusion(bf16[2,32768]{1,0:T(2,128)(2,1)S(1)} %dynamic-slice_bitcast_fusion, s32[32768]{0:T(1024)S(1)} %bitcast.40), kind=kCustom, calls=%fused_computation.1.clone | custom fusion | bytes 393216 | tf_op jit(solution)/shard_map/jit(take_along_axis)/gather | solution.py:48
  531.7 0.7 reshape.392
  532.7 1.8 slice_convert_fusion.1
  534.5 2.1 fusion.10
  536.7 7.3 %add_convert_fusion = (bf16[8,32,16384]{2,1,0:T(8,128)(2,1)}, bf16[8,32,16384]{2,1,0:T(8,128)(2,1)}) fusion(f32[8,16384]{1,0:T(8,128)S(1)} %get-tuple-element.14, f32[32,16384]{1,0:T(8,128)S(1)} %get-tuple-element.12, f32[8,16384]{1,0:T(8,128)S(1)} %get-tuple-element.13, f32[32,16384]{1,0:T(8,128)S(1)} %get-tuple-element.11), kind=kLoop, calls=%fused_computation.7 | loop fusion | flops 33554432 | bytes 22020096 | tf_op jit(solution)/shard_map/convert
  544.1 32.6 %all-gather.3.cloned.1.call-done = bf16[16,1,32768]{2,1,0:T(2,128)(2,1)} async-done(((bf16[1,1,32768]{2,1,0:T(2,128)(2,1)}), bf16[16,1,32768]{2,1,0:T(2,128)(2,1)}) %all-gather.3.cloned.1.call-update) | async-done | bytes 1048592 | tf_op jit(solution)/shard_map/all_gather | solution.py:78
  576.6 7.7 %reduce.2 = bf16[16,32768]{1,0:T(8,128)(2,1)S(1)} reduce(bf16[16,1,32768]{2,1,0:T(2,128)(2,1)} %all-gather.3.cloned.1.call-done, bf16[]{:T(256)} %constant.261), dimensions={1}, to_apply=%all-gather.reduce_sub_computation | reduce | bytes 2097154 | tf_op jit(solution)/shard_map/all_gather | solution.py:78
  584.4 1.5 reshape.353
  585.9 1.9 multiply_reduce_fusion
  588.1 14.8 %fusion.43 = (f32[32]{0:T(128)S(1)}, f32[8,32,8]{1,2,0:T(8,128)S(1)}) fusion(f32[32,8]{0,1:T(8,128)S(1)} %fusion.32, f32[8]{0:T(128)S(1)} %mul.210, bf16[8,32768,1]{1,0,2:T(8,128)(2,1)S(1)} %reshape.408, bf16[8,32,16384]{2,1,0:T(8,128)(2,1)} %get-tuple-element.6, bf16[8,32,16384]{2,1,0:T(8,128)(2,1)} %get-tuple-element.5, f32[32]{0:T(128)S(1)} %copy-done.5), kind=kOutput, calls=%fused_computation.106 | convolution fusion | flops 167782368 | bytes 17311008 | tf_op jit(solution)/shard_map/dot_general | solution.py:55
  602.9 7.4 %fusion = f32[8,32768]{1,0:T(8,128)S(1)} fusion(bf16[8,32,16384]{2,1,0:T(8,128)(2,1)} %get-tuple-element.6, bf16[8,32,16384]{2,1,0:T(8,128)(2,1)} %get-tuple-element.5, f32[8,32,8]{1,2,0:T(8,128)S(1)} %get-tuple-element.25, f32[32]{0:T(128)S(1)} %fusion.28, f32[32]{0:T(128)S(1)} %get-tuple-element.24), kind=kOutput, calls=%fused_computation.4 | convolution fusion | flops 168040448 | bytes 17834240 | tf_op jit(solution)/shard_map/snr,snq->rq/dot_general | solution.py:108
  610.4 2.4 gather_fusion
  612.8 3.1 select_multiply_fusion
  616.1 0.6 dynamic-slice.2
  616.7 32.4 %psum.7 = f32[8]{0:T(128)S(1)} all-reduce(f32[8]{0:T(128)S(1)} %multiply_reduce_fusion.1), channel_id=1, replica_groups=mesh['groups'=2,'particle'=16] {'particle'}, use_global_device_ids=true, to_apply=%region_6.8 | all-reduce | flops 8 | bytes 64 | tf_op jit(solution)/shard_map/psum | solution.py:106
  649.5 63.1 %all-reduce.3.cloned.1.call-done = f32[16,32768]{1,0:T(8,128)} async-done(((f32[16,32768]{1,0:T(8,128)}), f32[16,32768]{1,0:T(8,128)}) %all-reduce.3.cloned.1.call-update) | async-done | bytes 2097168
  712.6 1.7 constant_dynamic-slice_fusion.1
  714.3 1.5 collective-permute-start
  715.8 2.1 fusion.41
  718.1 0.8 pad_maximum_fusion.11
  (42 shorter events, 2.2 us)
Async XLA Ops:
  7.2 3.2 copy-start
  7.2 569.5 %all-gather.3.cloned.1.call-start = ((), (), s32[]{:S(2)}) async-start(), calls=%async_computation | async-start | bytes 2228224 | tf_op jit(solution)/shard_map/all_gather | solution.py:78
  270.8 260.4 %copy-start.2 = (f32[1,16384]{1,0:T(1,128)S(1)}, f32[1,16384]{1,0:T(1,128)}, u32[]{:S(2)}) copy-start(f32[1,16384]{1,0:T(1,128)} %param.14) | copy-start | bytes 196612
  270.8 260.4 %copy-start.1 = (s32[1,16384]{1,0:T(1,128)S(1)}, s32[1,16384]{1,0:T(1,128)}, u32[]{:S(2)}) copy-start(s32[1,16384]{1,0:T(1,128)} %param.13) | copy-start | bytes 196612
  270.9 261.8 %copy-start.3 = (s32[8,2]{0,1:T(2,128)S(1)}, s32[8,2]{0,1:T(2,128)}, u32[]{:S(2)}) copy-start(s32[8,2]{0,1:T(2,128)} %param.15) | copy-start | bytes 196
  532.4 180.2 %all-reduce.3.cloned.1.call-start = ((), (), s32[]{:S(2)}) async-start(), calls=%async_computation.1 | async-start | bytes 4194304
  536.6 7.4 %copy-start.4 = (s32[32]{0:T(128)S(1)}, s32[32]{0:T(128)}, u32[]{:S(2)}) copy-start(s32[32]{0:T(128)} %param.11) | copy-start | bytes 388
  536.6 51.5 %copy-start.5 = (f32[32]{0:T(128)S(1)}, f32[32]{0:T(128)}, u32[]{:S(2)}) copy-start(f32[32]{0:T(128)} %param.10) | copy-start | bytes 388
  610.4 5.7 copy-start.6
  714.3 3.8 collective-permute-start
Sparse Core Ops, SparseCore 0:
  532.5 44.0 all-gather.2
  616.0 96.5 all-reduce.2
where the time goes:
time: 726 us
  local copies, waits for them, and re-layouts  530 us (73%)
  waiting for transfers between devices  95.9 us (13%)
  blocking collectives  32.4 us (4%)
  other arithmetic  29 us (4%)
  matrix products  22.2 us (3%)
  between operations  14.4 us (2%)
    gather x2, local copies, waits for them, and re-layouts, project_rows(): jnp.take_along_axis(ref_table, wide_index, axis=2).astype(jnp.float32)  260 us
    gather x2, local copies, waits for them, and re-layouts, project_rows(): jnp.take_along_axis(ref_table, wide_index + 1, axis=2).astype(jnp.float32)  260 us
    unnamed x3, waiting for transfers between devices  63.1 us
    all_gather x1, waiting for transfers between devices, local(): all_proj = lax.all_gather(own_proj, 'particle', axis=0, tiled=True)  32.6 us
    psum x1, blocking collectives, local(): total_mass = lax.psum(local_mass, 'particle')  32.4 us
    dot_general x1, matrix products, correlate(): lax.dot_general(flat_stack, proj_rows, (((1,), (1,)), ((), ())), preferre...  14.8 us
  transfers between devices with their start and end apart: 3, of which 3 were waited for; matrix products, arithmetic and copies ran while one was open for 2% of the time, Pallas kernels for 0%

commit v1 on v0

v1 whole, which is shorter than its diff:
```python
import functools
import math

import jax
import jax.numpy as jnp
from jax import lax
from jax.experimental import pallas as pl
from jax.experimental.pallas import tpu as pltpu
from jax.sharding import PartitionSpec as P

KY = 128
BOX = 256
CLASSES = 8
LOWK = 16
LANES = 128
PRIOR_REWARD = 1.0
MASS_ROWS = 16
MIB = 1 << 20


def exchange(value, mask):
    pairs = [(source, source ^ mask) for source in range(lax.axis_size("particle"))]
    return lax.ppermute(value, "particle", pairs)


def whole_vmem(count):
    return [pl.BlockSpec(memory_space=pltpu.VMEM)] * count


def project_kernel(pick_ref, table_ref, index_ref, frac_ref, out_ref, flat, table, blended, *, chunk):
    highs = flat.shape[1]
    pixels = index_ref.shape[1]
    stride = table.shape[0] // 2

    def unfold(step, carry):
        piece = table_ref[0, 0, :, pl.ds(step * 8 * LANES, 8 * LANES)].astype(jnp.float32)
        for k in range(8):
            for comp in range(2):
                flat[comp, pl.ds(step * 8 + k, 1), :] = piece[comp : comp + 1, k * LANES : (k + 1) * LANES]
        return carry

    lax.fori_loop(0, highs // 8, unfold, 0)
    for comp in range(2):
        turned = flat[comp].T
        following = jnp.broadcast_to(pltpu.roll(turned[0:8], highs - 1, 1)[0:1], (16, highs))
        table[comp * stride : comp * stride + LANES, :] = turned.astype(jnp.bfloat16)
        table[comp * stride + LANES : (comp + 1) * stride, :] = following.astype(jnp.bfloat16)

    def body(step, carry):
        where = pl.ds(step * chunk, chunk)
        index = index_ref[:, where]
        frac = frac_ref[:, where]
        high = index // LANES
        low = index % LANES
        high_ids = lax.broadcasted_iota(jnp.int32, (highs, chunk), 0)
        one_hot = jnp.where(high_ids == high, 1.0, 0.0).astype(jnp.bfloat16)
        rows = jnp.dot(table[...], one_hot, preferred_element_type=jnp.float32)
        low_ids = lax.broadcasted_iota(jnp.int32, (LANES + 8, chunk), 0)
        weight = jnp.where(low_ids == low, 1.0 - frac, jnp.where(low_ids == low + 1, frac, 0.0))
        for comp in range(2):
            value = jnp.sum(
                rows[comp * stride : comp * stride + LANES + 8] * weight, axis=0, keepdims=True
            )
            for k in range(chunk // LANES):
                row = comp * (pixels // LANES) + step * (chunk // LANES) + k
                blended[pl.ds(row, 1), :] = value[:, k * LANES : (k + 1) * LANES]
        return carry

    lax.fori_loop(0, pixels // chunk, body, 0)
    out_ref[...] = blended[...].astype(jnp.bfloat16)


def project_row(class_refs, pick, interp_index, interp_frac):
    vox = class_refs.shape[3]
    pixels = interp_index.shape[1]
    highs = vox // LANES
    out_rows = 2 * pixels // LANES
    grid_spec = pltpu.PrefetchScalarGridSpec(
        num_scalar_prefetch=1,
        grid=(1,),
        in_specs=[
            pl.BlockSpec((1, 1, 2, vox), lambda i, pick: (pick[0], pick[1], 0, 0)),
            pl.BlockSpec((1, pixels), lambda i, pick: (0, 0)),
            pl.BlockSpec((1, pixels), lambda i, pick: (0, 0)),
        ],
        out_specs=pl.BlockSpec((out_rows, LANES), lambda i, pick: (0, 0)),
        scratch_shapes=[
            pltpu.VMEM((2, highs, LANES), jnp.float32),
            pltpu.VMEM((2 * (LANES + 16), highs), jnp.bfloat16),
            pltpu.VMEM((out_rows, LANES), jnp.float32),
        ],
    )
    return pl.pallas_call(
        functools.partial(project_kernel, chunk=1024),
        grid_spec=grid_spec,
        out_shape=jax.ShapeDtypeStruct((out_rows, LANES), jnp.bfloat16),
        compiler_params=pltpu.CompilerParams(vmem_limit_bytes=16 * MIB),
        name="project_row",
    )(pick, class_refs, interp_index, interp_frac)


def slot_rows(device, slots):
    ids = lax.broadcasted_iota(jnp.int32, (slots, 1), 0)
    flips, core_flip = ids % (slots // 2), ids // (slots // 2)
    return 2 * ((device // 4) ^ flips) + ((device % 2) ^ core_flip)


def split_mass(mass_row):
    ids = lax.broadcasted_iota(jnp.int32, (MASS_ROWS, LANES), 0)
    upper = mass_row.astype(jnp.bfloat16).astype(jnp.float32)
    lower = mass_row - upper
    return jnp.where(ids == 0, upper, jnp.where(ids == 1, lower, 0.0)).astype(jnp.bfloat16)


def joined_mass(block):
    return jnp.sum(block.astype(jnp.float32), axis=0, keepdims=True)


def expect_kernel(*refs, slots, chunk):
    device_ref, images, precision_ref, assigned_ref, shift_ref = refs[:5]
    row_refs = refs[5 : 5 + slots]
    keep, to_core, to_half, to_both, own_mass = refs[5 + slots : 10 + slots]
    proj, sums, cos_ref, sin_ref = refs[10 + slots :]
    device = device_ref[0]
    shifts = shift_ref.shape[0]
    parts = images.shape[0]
    pixels = images.shape[1] // 2
    tiles = pixels // LANES
    per_row = 2 * tiles
    half = slots // 2

    grid_x = shift_ref[:, 0:1]
    grid_y = shift_ref[:, 1:2]
    lane = lax.broadcasted_iota(jnp.int32, (shifts, KY), 1)
    turn_x = (lane * grid_x) & (BOX - 1)
    turn_y = ((lane - KY // 2) * grid_y) & (BOX - 1)
    angle_x = turn_x.astype(jnp.float32) * (2.0 * math.pi / BOX)
    angle_y = turn_y.astype(jnp.float32) * (2.0 * math.pi / BOX)
    cos_x, sin_x = jnp.cos(angle_x), jnp.sin(angle_x)
    cos_y, sin_y = jnp.cos(angle_y), jnp.sin(angle_y)
    for j in range(tiles):
        where = slice(j * LANES, (j + 1) * LANES)
        cos_j, sin_j = cos_x[:, j : j + 1], sin_x[:, j : j + 1]
        cos_ref[:, where] = cos_j * cos_y - sin_j * sin_y
        sin_ref[:, where] = sin_j * cos_y + cos_j * sin_y
    for slot in range(slots):
        proj[slot * per_row : (slot + 1) * per_row, :] = row_refs[slot][...].astype(jnp.float32)

    chunk_tiles = chunk // LANES
    contract_lanes = (((1,), (1,)), ((), ()))

    def correlate(step, carry):
        total, power = carry
        first = step * chunk_tiles
        real = jnp.concatenate(
            [proj[pl.ds(first + k, slots, stride=per_row), :] for k in range(chunk_tiles)], axis=1
        )
        imag = jnp.concatenate(
            [proj[pl.ds(tiles + first + k, slots, stride=per_row), :] for k in range(chunk_tiles)],
            axis=1,
        )
        where = pl.ds(pl.multiple_of(step * chunk, chunk), chunk)
        reals, imags = [], []
        for s in range(shifts):
            cos_s, sin_s = cos_ref[s : s + 1, where], sin_ref[s : s + 1, where]
            reals.append(real * cos_s - imag * sin_s)
            imags.append(real * sin_s + imag * cos_s)
        turned_real = jnp.concatenate(reals, axis=0).astype(jnp.bfloat16)
        turned_imag = jnp.concatenate(imags, axis=0).astype(jnp.bfloat16)
        image_real = images[:, where]
        image_imag = images[:, pl.ds(pl.multiple_of(pixels + step * chunk, chunk), chunk)]
        total = total + lax.dot_general(
            turned_real, image_real, contract_lanes, preferred_element_type=jnp.float32
        )
        total = total + lax.dot_general(
            turned_imag, image_imag, contract_lanes, preferred_element_type=jnp.float32
        )
        squares = real * real + imag * imag
        for k in range(chunk_tiles):
            power = power + squares[:, k * LANES : (k + 1) * LANES]
        return total, power

    total, power = lax.fori_loop(
        0,
        pixels // chunk,
        correlate,
        (
            jnp.zeros((shifts * slots, parts), jnp.float32),
            jnp.zeros((slots, LANES), jnp.float32),
        ),
    )
    power = jnp.sum(power, axis=1, keepdims=True)
    slot_class = slot_rows(device, slots) // (slots // CLASSES)
    match = (slot_class == assigned_ref[...]).astype(jnp.float32) * PRIOR_REWARD
    precision = precision_ref[...]
    likelihood_scale = 1.0 / math.sqrt(2 * pixels)
    logits = [
        precision * (total[s * slots : (s + 1) * slots] - 0.5 * power) * likelihood_scale + match
        for s in range(shifts)
    ]
    peak = functools.reduce(jnp.maximum, logits)
    peak = jnp.max(peak, axis=0, keepdims=True)
    terms = [jnp.exp(value - peak) for value in logits]
    mass = functools.reduce(jnp.add, terms)
    norm = jnp.sum(mass, axis=0, keepdims=True)
    weights = jnp.concatenate([term / norm for term in terms], axis=0).astype(jnp.bfloat16)
    slot_mass = jnp.sum(mass / norm * precision, axis=1, keepdims=True)
    class_lane = lax.broadcasted_iota(jnp.int32, (slots, LANES), 1)
    mass_row = jnp.sum(
        jnp.where(class_lane == slot_class, slot_mass, 0.0), axis=0, keepdims=True
    )

    def backproject(step, carry):
        where = pl.ds(pl.multiple_of(step * chunk, chunk), chunk)
        image_real = images[:, where]
        image_imag = images[:, pl.ds(pl.multiple_of(pixels + step * chunk, chunk), chunk)]
        from_real = jnp.dot(weights, image_real, preferred_element_type=jnp.float32)
        from_imag = jnp.dot(weights, image_imag, preferred_element_type=jnp.float32)
        real = jnp.zeros((slots, chunk), jnp.float32)
        imag = jnp.zeros((slots, chunk), jnp.float32)
        for s in range(shifts):
            cos_s, sin_s = cos_ref[s : s + 1, where], sin_ref[s : s + 1, where]
            part_real = from_real[s * slots : (s + 1) * slots]
            part_imag = from_imag[s * slots : (s + 1) * slots]
            real = real + (part_real * cos_s + part_imag * sin_s)
            imag = imag + (part_imag * cos_s - part_real * sin_s)
        first = step * chunk_tiles
        for k in range(chunk_tiles):
            piece = slice(k * LANES, (k + 1) * LANES)
            sums[pl.ds(first + k, slots, stride=per_row), :] = real[:, piece]
            sums[pl.ds(tiles + first + k, slots, stride=per_row), :] = imag[:, piece]
        return carry

    lax.fori_loop(0, pixels // chunk, backproject, 0)

    body = half * per_row
    low_rows = LOWK * KY // LANES
    mass_block = split_mass(mass_row)
    keep[...] = sums[0:body, :]
    to_core[0:body, :] = sums[body : 2 * body, :].astype(jnp.bfloat16)
    to_core[body:, :] = mass_block
    for target, start in ((to_half, 0), (to_both, half)):
        for m in range(half):
            for comp in range(2):
                source = (start + m) * per_row + comp * tiles
                dest = (2 * m + comp) * low_rows
                target[dest : dest + low_rows, :] = sums[source : source + low_rows, :].astype(
                    jnp.bfloat16
                )
        target[2 * half * low_rows :, :] = mass_block
    own_mass[...] = jnp.broadcast_to(mass_row, own_mass.shape)


def expect(device, images, precision, assigned, shift_grid, rows):
    slots = len(rows)
    half = slots // 2
    pixels = images.shape[1] // 2
    per_row = 2 * pixels // LANES
    shifts = shift_grid.shape[0]
    low = 2 * half * (LOWK * KY // LANES) + MASS_ROWS
    limit = (12 + 2 * slots) * MIB
    return pl.pallas_call(
        functools.partial(expect_kernel, slots=slots, chunk=512),
        in_specs=[pl.BlockSpec(memory_space=pltpu.SMEM)] + whole_vmem(4 + slots),
        out_specs=whole_vmem(5),
        out_shape=[
            jax.ShapeDtypeStruct((half * per_row, LANES), jnp.float32),
            jax.ShapeDtypeStruct((half * per_row + MASS_ROWS, LANES), jnp.bfloat16),
            jax.ShapeDtypeStruct((low, LANES), jnp.bfloat16),
            jax.ShapeDtypeStruct((low, LANES), jnp.bfloat16),
            jax.ShapeDtypeStruct((8, LANES), jnp.float32),
        ],
        scratch_shapes=[
            pltpu.VMEM((slots * per_row, LANES), jnp.float32),
            pltpu.VMEM((slots * per_row, LANES), jnp.float32),
            pltpu.VMEM((shifts, pixels), jnp.float32),
            pltpu.VMEM((shifts, pixels), jnp.float32),
        ],
        compiler_params=pltpu.CompilerParams(vmem_limit_bytes=limit),
        name="expect",
    )(device, images, precision, assigned, shift_grid, *rows)


def merge_kernel(keep, from_core, from_half, from_both, mass, *outs, half):
    own, own_mass, sends = outs[0], outs[1], outs[2:]
    per_row = own.shape[0]
    tiles = per_row // 2
    low_rows = LOWK * KY // LANES
    body = half * per_row
    low_body = 2 * half * low_rows
    total_mass = (
        mass[0:1, :]
        + joined_mass(from_core[body:, :])
        + joined_mass(from_half[low_body:, :])
        + joined_mass(from_both[low_body:, :])
    )
    mass_block = split_mass(total_mass)
    own_mass[...] = jnp.broadcast_to(total_mass, own_mass.shape)
    for m in range(half):
        target = own if m == 0 else sends[m - 1]
        for comp in range(2):
            start = comp * tiles
            source = m * per_row + start
            low = (2 * m + comp) * low_rows
            own_low = keep[source : source + low_rows, :] + from_core[
                source : source + low_rows, :
            ].astype(jnp.float32)
            other_low = from_half[low : low + low_rows, :].astype(jnp.float32) + from_both[
                low : low + low_rows, :
            ].astype(jnp.float32)
            target[start : start + low_rows, :] = ((own_low + other_low) * 0.5).astype(target.dtype)
            rest = slice(source + low_rows, source + tiles)
            target[start + low_rows : start + tiles, :] = (
                keep[rest, :] + from_core[rest, :].astype(jnp.float32)
            ).astype(target.dtype)
        if m > 0:
            target[per_row:, :] = mass_block


def merge(keep, from_core, from_half, from_both, mass, half):
    per_row = keep.shape[0] // half
    return pl.pallas_call(
        functools.partial(merge_kernel, half=half),
        in_specs=whole_vmem(5),
        out_specs=whole_vmem(1 + half),
        out_shape=[
            jax.ShapeDtypeStruct((per_row, LANES), jnp.float32),
            jax.ShapeDtypeStruct((8, LANES), jnp.float32),
        ]
        + [jax.ShapeDtypeStruct((per_row + MASS_ROWS, LANES), jnp.bfloat16)] * (half - 1),
        compiler_params=pltpu.CompilerParams(vmem_limit_bytes=(12 + 2 * half) * MIB),
        name="merge",
    )(keep, from_core, from_half, from_both, mass)


def finish_kernel(*refs, scale, mass_scale):
    own, mass = refs[0], refs[1]
    received, (out, mass_out) = refs[2:-2], refs[-2:]
    per_row = own.shape[0]
    total = own[...]
    total_mass = mass[0:1, :]
    for ref in received:
        total = total + ref[0:per_row, :].astype(jnp.float32)
        total_mass = total_mass + joined_mass(ref[per_row:, :])
    out[...] = total * scale
    mass_out[...] = jnp.broadcast_to(total_mass * mass_scale, mass_out.shape)


def finish(own, mass, received, scale, mass_scale):
    return pl.pallas_call(
        functools.partial(finish_kernel, scale=scale, mass_scale=mass_scale),
        in_specs=whole_vmem(2 + len(received)),
        out_specs=whole_vmem(2),
        out_shape=[
            jax.ShapeDtypeStruct(own.shape, jnp.float32),
            jax.ShapeDtypeStruct(mass.shape, jnp.float32),
        ],
        compiler_params=pltpu.CompilerParams(vmem_limit_bytes=16 * MIB),
        name="finish",
    )(own, mass, *received)


def local(
    images, noise_precision, assigned_class, class_refs, interp_index, interp_frac, shift_grid
):
    dev_count = lax.axis_size("particle")
    device = lax.axis_index("particle").astype(jnp.int32)
    orient_count = dev_count // 2
    half = dev_count // 4
    part_count = images.shape[0]
    half_set = device // 2 % 2
    class_id = (2 * (device // 4) + device % 2) // (orient_count // CLASSES)
    own_row = project_row(
        class_refs, jnp.stack([half_set, class_id]), interp_index, interp_frac
    )
    same_core = [own_row] + [exchange(own_row, 4 * m) for m in range(1, half)]
    rows = same_core + [exchange(row, 1) for row in same_core]
    keep, to_core, to_half, to_both, mass = expect(
        device.reshape(1),
        images,
        noise_precision.reshape(1, part_count),
        assigned_class.reshape(1, part_count),
        shift_grid,
        rows,
    )
    merged = merge(
        keep, exchange(to_core, 1), exchange(to_half, 2), exchange(to_both, 3), mass, half
    )
    own, mass, sends = merged[0], merged[1], merged[2:]
    received = [exchange(send, 4 * (m + 1)) for m, send in enumerate(sends)]
    back, class_mass = finish(
        own,
        mass,
        received,
        1.0 / math.sqrt(part_count),
        CLASSES / (part_count * dev_count),
    )
    return back.reshape(1, images.shape[1]), class_mass[0, :CLASSES]


def solution(mesh):
    in_specs = (
        P(("groups", "particle"), None),
        P(("groups", "particle")),
        P(("groups", "particle")),
        P("groups", None, None, None),
        P("particle", None),
        P("particle", None),
        P(),
    )
    out_specs = (P(("groups", "particle"), None), P("groups"))
    return jax.shard_map(local, mesh=mesh, in_specs=in_specs, out_specs=out_specs, check_vma=False)
```

time: 726 us -> 53.2 us (0.07)
  local copies, waits for them, and re-layouts: 530 us -> 3.88 us
  waiting for transfers between devices: 95.9 us -> 14.6 us
  blocking collectives: 32.4 us -> 0 us
  other arithmetic: 29 us -> 0.08 us
  matrix products: 22.2 us -> 0 us
  Pallas kernels: 0 us -> 21 us
  between operations: 14.4 us -> 0.74 us
  starting transfers between devices: 1.72 us -> 12.7 us
    gather x5 -> x0, local copies, waits for them, and re-layouts: 523 us -> none  [the longest x2 260 us: project_rows(): jnp.take_along_axis(ref_table, wide_index, axis=2).astype(jnp.float32)]
    unnamed x3 -> x0, waiting for transfers between devices: 63.1 us -> none
    all_gather x1 -> x0, waiting for transfers between devices: 32.6 us -> none  [local(): all_proj = lax.all_gather(own_proj, 'particle', axis=0, tiled=True)]
    psum x1 -> x0, blocking collectives: 32.4 us -> none  [local(): total_mass = lax.psum(local_mass, 'particle')]
    dot_general x2 -> x0, matrix products: 22.2 us -> none  [the longest x1 14.8 us: correlate(): lax.dot_general(flat_stack, proj_rows, (((1,), (1,)), ((), ())), preferre...]
    pallas_call x0 -> x4, Pallas kernels: none -> 21 us  [the longest x1 13.2 us: expect(): pl.pallas_call(functools.partial(expect_kernel, slots=slots, chunk=512),...]
    ppermute x1 -> x13, waiting for transfers between devices: 0.23 us -> 14.6 us  [exchange(): return lax.ppermute(value, 'particle', pairs)]
    ppermute x1 -> x13, starting transfers between devices: 1.46 us -> 12.7 us  [exchange(): return lax.ppermute(value, 'particle', pairs)]
  transfers between devices with their start and end apart: 3 -> 13, of which waited for: 3 -> 9; matrix products, arithmetic and copies ran while one was open for 2% -> 0% of each run, Pallas kernels for 0% -> 0%
where the time goes in v1:
time: 53.2 us; the launch traced here: 52.9 us
  Pallas kernels  21 us (39%)
  waiting for transfers between devices  14.6 us (27%)
  starting transfers between devices  12.7 us (24%)
  local copies, waits for them, and re-layouts  3.88 us (7%)
  between operations  0.74 us (1%)
    ppermute x13, waiting for transfers between devices, exchange(): return lax.ppermute(value, 'particle', pairs)  14.6 us
    pallas_call x1, Pallas kernels, expect(): pl.pallas_call(functools.partial(expect_kernel, slots=slots, chunk=512),...  13.2 us
    ppermute x13, starting transfers between devices, exchange(): return lax.ppermute(value, 'particle', pairs)  12.7 us
    pallas_call x1, Pallas kernels, project_row(): pl.pallas_call(functools.partial(project_kernel, chunk=1024), grid_spec=g...  7.02 us
    unnamed x15, local copies, waits for them, and re-layouts  3.37 us
  transfers between devices with their start and end apart: 13, of which 9 were waited for; matrix products, arithmetic and copies ran while one was open for 0% of the time, Pallas kernels for 0%

profile of v1, /device:TPU:0, one launch (start us, length us, event | category | flops | bytes accessed | tf_op | source)
XLA Modules:
  0.0 52.9 jit_solution(4837169531812904202)
XLA Ops:
  0.8 1.6 %copy-done = bf16[2,8,2,32768]{3,2,1,0:T(2,128)(2,1)S(1)} copy-done((bf16[2,8,2,32768]{3,2,1,0:T(2,128)(2,1)S(1)}, bf16[2,8,2,32768]{3,2,1,0:T(2,128)(2,1)}, u32[]{:S(2)}) %copy-start) | copy-done | bytes 2097176
  2.4 0.8 %copy-done.2 = s32[1,16384]{1,0:T(1,128)S(1)} copy-done((s32[1,16384]{1,0:T(1,128)S(1)}, s32[1,16384]{1,0:T(1,128)}, u32[]{:S(2)}) %copy-start.2) | copy-done | bytes 65560
  3.2 0.8 %copy-done.3 = f32[1,16384]{1,0:T(1,128)S(1)} copy-done((f32[1,16384]{1,0:T(1,128)S(1)}, f32[1,16384]{1,0:T(1,128)}, u32[]{:S(2)}) %copy-start.3) | copy-done | bytes 65560
  4.1 7.0 %project_row.1.refs_5_ = bf16[256,128]{1,0:T(8,128)(2,1)S(1)} custom-call(s32[2]{0:T(128)S(1)} %pad_add_fusion.pick_ref, bf16[2,8,2,32768]{3,2,1,0:T(2,128)(2,1)S(1)} %copy-done, s32[1,16384]{1,0:T(1,128)S(1)} %copy-done.2, f32[1,16384]{1,0:T(1,128)S(1)} %copy-done.3), custom_call_target="tpu_custom_call" | custom-call | tf_op jit(solution)/shard_map/project_row/pallas_call | solution.py:93
  11.1 5.1 %collective-permute-start.2 = (bf16[256,128]{1,0:T(8,128)(2,1)S(1)}, bf16[256,128]{1,0:T(8,128)(2,1)S(1)}, u32[]{:S(2)}, u32[]{:S(2)}) collective-permute-start(bf16[256,128]{1,0:T(8,128)(2,1)S(1)} %project_row.1.refs_5_), channel_id=1, source_target_pairs={{0,12},{1,13},{2,14},{3,15},{4,8},{5,9},{6,10},{7,11},{8,4},{9,5},... | collective-permute-start | bytes 196616 | tf_op jit(solution)/shard_map/ppermute | solution.py:23
  16.2 0.6 %collective-permute-start = (bf16[256,128]{1,0:T(8,128)(2,1)S(1)}, bf16[256,128]{1,0:T(8,128)(2,1)S(1)}, u32[]{:S(2)}, u32[]{:S(2)}) collective-permute-start(bf16[256,128]{1,0:T(8,128)(2,1)S(1)} %project_row.1.refs_5_), channel_id=1, source_target_pairs={{0,4},{1,5},{2,6},{3,7},{4,0},{5,1},{6,2},{7,3},{8,12},{9,13},{10,... | collective-permute-start | bytes 196616 | tf_op jit(solution)/shard_map/ppermute | solution.py:23
  16.8 1.9 %collective-permute-done.2.refs_8_ = bf16[256,128]{1,0:T(8,128)(2,1)S(1)} collective-permute-done((bf16[256,128]{1,0:T(8,128)(2,1)S(1)}, bf16[256,128]{1,0:T(8,128)(2,1)S(1)}, u32[]{:S(2)}, u32[]{:S(2)}) %collective-permute-start.2) | collective-permute-done | bytes 65568 | tf_op jit(solution)/shard_map/ppermute | solution.py:23
  18.8 3.0 %collective-permute-done.1.refs_7_ = bf16[256,128]{1,0:T(8,128)(2,1)S(1)} collective-permute-done((bf16[256,128]{1,0:T(8,128)(2,1)S(1)}, bf16[256,128]{1,0:T(8,128)(2,1)S(1)}, u32[]{:S(2)}, u32[]{:S(2)}) %collective-permute-start.1) | collective-permute-done | bytes 65568 | tf_op jit(solution)/shard_map/ppermute | solution.py:23
  21.8 0.5 collective-permute-start.4
  22.4 0.7 %collective-permute-done.5.refs_11_ = bf16[256,128]{1,0:T(8,128)(2,1)S(1)} collective-permute-done((bf16[256,128]{1,0:T(8,128)(2,1)S(1)}, bf16[256,128]{1,0:T(8,128)(2,1)S(1)}, u32[]{:S(2)}, u32[]{:S(2)}) %collective-permute-start.5) | collective-permute-done | bytes 65568 | tf_op jit(solution)/shard_map/ppermute | solution.py:23
  23.1 0.2 collective-permute-done.4.refs_10_
  23.2 13.2 %expect.1 = (f32[1024,128]{1,0:T(8,128)S(1)}, bf16[1040,128]{1,0:T(8,128)(2,1)S(1)}, bf16[144,128]{1,0:T(8,128)(2,1)S(1)}, bf16[144,128]{1,0:T(8,128)(2,1)S(1)}, f32[8,128]{1,0:T(8,128)S(1)}) custom-call(s32[1]{0:T(128)} %bitcast.refs_0_, bf16[32,32768]{1,0:T(8,128)(2,1)S(1)} %copy-done.1, f32[1,32]{1,0:T(1,128)S(1)} %bitcast.8, s32[1,32]{1,0:T(1,128)S(1)} %bitcast.9, ...), custom_call_target="tpu_custom_call" | custom-call | tf_op jit(solution)/shard_map/expect/pallas_call | solution.py:262
  36.4 0.4 collective-permute-start.7
  36.9 1.5 %collective-permute-start.8 = (bf16[144,128]{1,0:T(8,128)(2,1)S(1)}, bf16[144,128]{1,0:T(8,128)(2,1)S(1)}, u32[]{:S(2)}, u32[]{:S(2)}) collective-permute-start(bf16[144,128]{1,0:T(8,128)(2,1)S(1)} %get-tuple-element.16), channel_id=1, source_target_pairs={{0,2},{1,3},{2,0},{3,1},{4,6},{5,7},{6,4},{7,5},{8,10},{9,11},{10,... | collective-permute-start | bytes 110600 | tf_op jit(solution)/shard_map/ppermute | solution.py:23
  38.4 2.4 %collective-permute-done.8.from_half = bf16[144,128]{1,0:T(8,128)(2,1)S(1)} collective-permute-done((bf16[144,128]{1,0:T(8,128)(2,1)S(1)}, bf16[144,128]{1,0:T(8,128)(2,1)S(1)}, u32[]{:S(2)}, u32[]{:S(2)}) %collective-permute-start.8) | collective-permute-done | bytes 36896 | tf_op jit(solution)/shard_map/ppermute | solution.py:23
  40.8 1.3 %collective-permute-done.9.from_both = bf16[144,128]{1,0:T(8,128)(2,1)S(1)} collective-permute-done((bf16[144,128]{1,0:T(8,128)(2,1)S(1)}, bf16[144,128]{1,0:T(8,128)(2,1)S(1)}, u32[]{:S(2)}, u32[]{:S(2)}) %collective-permute-start.9) | collective-permute-done | bytes 36896 | tf_op jit(solution)/shard_map/ppermute | solution.py:23
  42.1 0.6 %collective-permute-start.10 = (bf16[272,128]{1,0:T(8,128)(2,1)S(1)}, bf16[272,128]{1,0:T(8,128)(2,1)S(1)}, u32[]{:S(2)}, u32[]{:S(2)}) collective-permute-start(bf16[272,128]{1,0:T(8,128)(2,1)S(1)} %get-tuple-element.21), channel_id=1, source_target_pairs={{0,4},{1,5},{2,6},{3,7},{4,0},{5,1},{6,2},{7,3},{8,12},{9,13},{10,... | collective-permute-start | bytes 208904 | tf_op jit(solution)/shard_map/ppermute | solution.py:23
  42.7 2.7 %collective-permute-start.11 = (bf16[272,128]{1,0:T(8,128)(2,1)S(1)}, bf16[272,128]{1,0:T(8,128)(2,1)S(1)}, u32[]{:S(2)}, u32[]{:S(2)}) collective-permute-start(bf16[272,128]{1,0:T(8,128)(2,1)S(1)} %get-tuple-element.22), channel_id=1, source_target_pairs={{0,8},{1,9},{2,10},{3,11},{4,12},{5,13},{6,14},{7,15},{8,0},{9,1},... | collective-permute-start | bytes 208904 | tf_op jit(solution)/shard_map/ppermute | solution.py:23
  45.5 1.1 %collective-permute-start.12 = (bf16[272,128]{1,0:T(8,128)(2,1)S(1)}, bf16[272,128]{1,0:T(8,128)(2,1)S(1)}, u32[]{:S(2)}, u32[]{:S(2)}) collective-permute-start(bf16[272,128]{1,0:T(8,128)(2,1)S(1)} %get-tuple-element.23), channel_id=1, source_target_pairs={{0,12},{1,13},{2,14},{3,15},{4,8},{5,9},{6,10},{7,11},{8,4},{9,5},... | collective-permute-start | bytes 208904 | tf_op jit(solution)/shard_map/ppermute | solution.py:23
  46.6 0.7 %collective-permute-done.10.refs_2_ = bf16[272,128]{1,0:T(8,128)(2,1)S(1)} collective-permute-done((bf16[272,128]{1,0:T(8,128)(2,1)S(1)}, bf16[272,128]{1,0:T(8,128)(2,1)S(1)}, u32[]{:S(2)}, u32[]{:S(2)}) %collective-permute-start.10) | collective-permute-done | bytes 69664 | tf_op jit(solution)/shard_map/ppermute | solution.py:23
  47.3 3.4 %collective-permute-done.11.refs_3_ = bf16[272,128]{1,0:T(8,128)(2,1)S(1)} collective-permute-done((bf16[272,128]{1,0:T(8,128)(2,1)S(1)}, bf16[272,128]{1,0:T(8,128)(2,1)S(1)}, u32[]{:S(2)}, u32[]{:S(2)}) %collective-permute-start.11) | collective-permute-done | bytes 69664 | tf_op jit(solution)/shard_map/ppermute | solution.py:23
  50.7 1.0 %collective-permute-done.12.refs_4_ = bf16[272,128]{1,0:T(8,128)(2,1)S(1)} collective-permute-done((bf16[272,128]{1,0:T(8,128)(2,1)S(1)}, bf16[272,128]{1,0:T(8,128)(2,1)S(1)}, u32[]{:S(2)}, u32[]{:S(2)}) %collective-permute-start.12) | collective-permute-done | bytes 69664 | tf_op jit(solution)/shard_map/ppermute | solution.py:23
  51.7 0.7 %finish.1 = (f32[256,128]{1,0:T(8,128)}, f32[8,128]{1,0:T(8,128)S(1)}) custom-call(f32[256,128]{1,0:T(8,128)S(1)} %get-tuple-element.19.refs_0_, f32[8,128]{1,0:T(8,128)S(1)} %get-tuple-element.20.refs_1_, bf16[272,128]{1,0:T(8,128)(2,1)S(1)} %collective-permute-done.10.refs_2_, bf16[272,128]{1,0:T(8,128)(2,1)S(1)} %collective-permute-done.11.refs_3_, ...), custom_call_target="tpu_custom_call" | custom-call | tf_op jit(solution)/shard_map/finish/pallas_call | solution.py:350
  52.4 0.5 slice_bitcast_fusion
  (23 shorter events, 0.3 us)
Async XLA Ops:
  0.6 21.7 %copy-start.6 = (s32[8,2]{0,1:T(2,128)S(1)}, s32[8,2]{0,1:T(2,128)}, u32[]{:S(2)}) copy-start(s32[8,2]{0,1:T(2,128)} %param.13) | copy-start | bytes 196
  0.6 22.6 %copy-start.5 = (s32[32]{0:T(128)S(1)}, s32[32]{0:T(128)}, u32[]{:S(2)}) copy-start(s32[32]{0:T(128)} %param.9) | copy-start | bytes 388
  0.7 22.6 %copy-start.4 = (f32[32]{0:T(128)S(1)}, f32[32]{0:T(128)}, u32[]{:S(2)}) copy-start(f32[32]{0:T(128)} %param.8) | copy-start | bytes 388
  0.8 1.6 %copy-start = (bf16[2,8,2,32768]{3,2,1,0:T(2,128)(2,1)S(1)}, bf16[2,8,2,32768]{3,2,1,0:T(2,128)(2,1)}, u32[]{:S(2)}) copy-start(bf16[2,8,2,32768]{3,2,1,0:T(2,128)(2,1)} %table_ref.1) | copy-start | bytes 6291460
  2.4 0.8 %copy-start.2 = (s32[1,16384]{1,0:T(1,128)S(1)}, s32[1,16384]{1,0:T(1,128)}, u32[]{:S(2)}) copy-start(s32[1,16384]{1,0:T(1,128)} %index_ref.1) | copy-start | bytes 196612
  3.2 0.8 %copy-start.3 = (f32[1,16384]{1,0:T(1,128)S(1)}, f32[1,16384]{1,0:T(1,128)}, u32[]{:S(2)}) copy-start(f32[1,16384]{1,0:T(1,128)} %frac_ref.1) | copy-start | bytes 196612
  4.1 19.2 %copy-start.1 = (bf16[32,32768]{1,0:T(8,128)(2,1)S(1)}, bf16[32,32768]{1,0:T(8,128)(2,1)}, u32[]{:S(2)}) copy-start(bf16[32,32768]{1,0:T(8,128)(2,1)} %refs_1_.1) | copy-start | bytes 6291460
  11.1 7.7 %collective-permute-start.2 = (bf16[256,128]{1,0:T(8,128)(2,1)S(1)}, bf16[256,128]{1,0:T(8,128)(2,1)S(1)}, u32[]{:S(2)}, u32[]{:S(2)}) collective-permute-start(bf16[256,128]{1,0:T(8,128)(2,1)S(1)} %project_row.1.refs_5_), channel_id=1, source_target_pairs={{0,12},{1,13},{2,14},{3,15},{4,8},{5,9},{6,10},{7,11},{8,4},{9,5},... | collective-permute-start | bytes 196616 | tf_op jit(solution)/shard_map/ppermute | solution.py:23
  16.2 5.6 %collective-permute-start.1 = (bf16[256,128]{1,0:T(8,128)(2,1)S(1)}, bf16[256,128]{1,0:T(8,128)(2,1)S(1)}, u32[]{:S(2)}, u32[]{:S(2)}) collective-permute-start(bf16[256,128]{1,0:T(8,128)(2,1)S(1)} %project_row.1.refs_5_), channel_id=1, source_target_pairs={{0,8},{1,9},{2,10},{3,11},{4,12},{5,13},{6,14},{7,15},{8,0},{9,1},... | collective-permute-start | bytes 196616 | tf_op jit(solution)/shard_map/ppermute | solution.py:23
  16.2 5.6 %collective-permute-start = (bf16[256,128]{1,0:T(8,128)(2,1)S(1)}, bf16[256,128]{1,0:T(8,128)(2,1)S(1)}, u32[]{:S(2)}, u32[]{:S(2)}) collective-permute-start(bf16[256,128]{1,0:T(8,128)(2,1)S(1)} %project_row.1.refs_5_), channel_id=1, source_target_pairs={{0,4},{1,5},{2,6},{3,7},{4,0},{5,1},{6,2},{7,3},{8,12},{9,13},{10,... | collective-permute-start | bytes 196616 | tf_op jit(solution)/shard_map/ppermute | solution.py:23
  16.8 5.6 %collective-permute-start.3 = (bf16[256,128]{1,0:T(8,128)(2,1)S(1)}, bf16[256,128]{1,0:T(8,128)(2,1)S(1)}, u32[]{:S(2)}, u32[]{:S(2)}) collective-permute-start(bf16[256,128]{1,0:T(8,128)(2,1)S(1)} %project_row.1.refs_5_), channel_id=1, source_target_pairs={{0,1},{1,0},{2,3},{3,2},{4,5},{5,4},{6,7},{7,6},{8,9},{9,8},{10,11... | collective-permute-start | bytes 196616 | tf_op jit(solution)/shard_map/ppermute | solution.py:23
  18.8 3.6 %collective-permute-start.6 = (bf16[256,128]{1,0:T(8,128)(2,1)S(1)}, bf16[256,128]{1,0:T(8,128)(2,1)S(1)}, u32[]{:S(2)}, u32[]{:S(2)}) collective-permute-start(bf16[256,128]{1,0:T(8,128)(2,1)S(1)} %collective-permute-done.2.refs_8_), channel_id=1, source_target_pairs={{0,1},{1,0},{2,3},{3,2},{4,5},{5,4},{6,7},{7,6},{8,9},{9,8},{10,11... | collective-permute-start | bytes 196616 | tf_op jit(solution)/shard_map/ppermute | solution.py:23
  21.8 1.3 %collective-permute-start.5 = (bf16[256,128]{1,0:T(8,128)(2,1)S(1)}, bf16[256,128]{1,0:T(8,128)(2,1)S(1)}, u32[]{:S(2)}, u32[]{:S(2)}) collective-permute-start(bf16[256,128]{1,0:T(8,128)(2,1)S(1)} %collective-permute-done.1.refs_7_), channel_id=1, source_target_pairs={{0,1},{1,0},{2,3},{3,2},{4,5},{5,4},{6,7},{7,6},{8,9},{9,8},{10,11... | collective-permute-start | bytes 196616 | tf_op jit(solution)/shard_map/ppermute | solution.py:23
  21.8 1.4 %collective-permute-start.4 = (bf16[256,128]{1,0:T(8,128)(2,1)S(1)}, bf16[256,128]{1,0:T(8,128)(2,1)S(1)}, u32[]{:S(2)}, u32[]{:S(2)}) collective-permute-start(bf16[256,128]{1,0:T(8,128)(2,1)S(1)} %collective-permute-done.refs_6_), channel_id=1, source_target_pairs={{0,1},{1,0},{2,3},{3,2},{4,5},{5,4},{6,7},{7,6},{8,9},{9,8},{10,11... | collective-permute-start | bytes 196616 | tf_op jit(solution)/shard_map/ppermute | solution.py:23
  36.4 5.6 %collective-permute-start.7 = (bf16[1040,128]{1,0:T(8,128)(2,1)S(1)}, bf16[1040,128]{1,0:T(8,128)(2,1)S(1)}, u32[]{:S(2)}, u32[]{:S(2)}) collective-permute-start(bf16[1040,128]{1,0:T(8,128)(2,1)S(1)} %get-tuple-element.15), channel_id=1, source_target_pairs={{0,1},{1,0},{2,3},{3,2},{4,5},{5,4},{6,7},{7,6},{8,9},{9,8},{10,11... | collective-permute-start | bytes 798728 | tf_op jit(solution)/shard_map/ppermute | solution.py:23
  36.9 4.0 %collective-permute-start.8 = (bf16[144,128]{1,0:T(8,128)(2,1)S(1)}, bf16[144,128]{1,0:T(8,128)(2,1)S(1)}, u32[]{:S(2)}, u32[]{:S(2)}) collective-permute-start(bf16[144,128]{1,0:T(8,128)(2,1)S(1)} %get-tuple-element.16), channel_id=1, source_target_pairs={{0,2},{1,3},{2,0},{3,1},{4,6},{5,7},{6,4},{7,5},{8,10},{9,11},{10,... | collective-permute-start | bytes 110600 | tf_op jit(solution)/shard_map/ppermute | solution.py:23
  38.3 3.7 %collective-permute-start.9 = (bf16[144,128]{1,0:T(8,128)(2,1)S(1)}, bf16[144,128]{1,0:T(8,128)(2,1)S(1)}, u32[]{:S(2)}, u32[]{:S(2)}) collective-permute-start(bf16[144,128]{1,0:T(8,128)(2,1)S(1)} %get-tuple-element.17), channel_id=1, source_target_pairs={{0,3},{1,2},{2,1},{3,0},{4,7},{5,6},{6,5},{7,4},{8,11},{9,10},{10,... | collective-permute-start | bytes 110600 | tf_op jit(solution)/shard_map/ppermute | solution.py:23
  42.1 5.2 %collective-permute-start.10 = (bf16[272,128]{1,0:T(8,128)(2,1)S(1)}, bf16[272,128]{1,0:T(8,128)(2,1)S(1)}, u32[]{:S(2)}, u32[]{:S(2)}) collective-permute-start(bf16[272,128]{1,0:T(8,128)(2,1)S(1)} %get-tuple-element.21), channel_id=1, source_target_pairs={{0,4},{1,5},{2,6},{3,7},{4,0},{5,1},{6,2},{7,3},{8,12},{9,13},{10,... | collective-permute-start | bytes 208904 | tf_op jit(solution)/shard_map/ppermute | solution.py:23
  42.7 7.9 %collective-permute-start.11 = (bf16[272,128]{1,0:T(8,128)(2,1)S(1)}, bf16[272,128]{1,0:T(8,128)(2,1)S(1)}, u32[]{:S(2)}, u32[]{:S(2)}) collective-permute-start(bf16[272,128]{1,0:T(8,128)(2,1)S(1)} %get-tuple-element.22), channel_id=1, source_target_pairs={{0,8},{1,9},{2,10},{3,11},{4,12},{5,13},{6,14},{7,15},{8,0},{9,1},... | collective-permute-start | bytes 208904 | tf_op jit(solution)/shard_map/ppermute | solution.py:23
  45.5 6.2 %collective-permute-start.12 = (bf16[272,128]{1,0:T(8,128)(2,1)S(1)}, bf16[272,128]{1,0:T(8,128)(2,1)S(1)}, u32[]{:S(2)}, u32[]{:S(2)}) collective-permute-start(bf16[272,128]{1,0:T(8,128)(2,1)S(1)} %get-tuple-element.23), channel_id=1, source_target_pairs={{0,12},{1,13},{2,14},{3,15},{4,8},{5,9},{6,10},{7,11},{8,4},{9,5},... | collective-permute-start | bytes 208904 | tf_op jit(solution)/shard_map/ppermute | solution.py:23

commit v2 on v1

v2 whole, which is shorter than its diff:
```python
import functools
import math

import jax
import jax.numpy as jnp
from jax import lax
from jax.experimental import pallas as pl
from jax.experimental.pallas import tpu as pltpu
from jax.sharding import PartitionSpec as P

KY = 128
BOX = 256
CLASSES = 8
LOWK = 16
LANES = 128
PRIOR_REWARD = 1.0
MASS_ROWS = 16
MIB = 1 << 20


def exchange(value, mask):
    pairs = [(source, source ^ mask) for source in range(lax.axis_size("particle"))]
    return lax.ppermute(value, "particle", pairs)


def across_z(value):
    count = lax.axis_size("particle")
    groups = [list(range(first, count, 4)) for first in range(4)]
    return lax.all_to_all(
        value, "particle", split_axis=0, concat_axis=0, axis_index_groups=groups, tiled=True
    )


def whole_vmem(count):
    return [pl.BlockSpec(memory_space=pltpu.VMEM)] * count


def project_kernel(pick_ref, table_ref, index_ref, frac_ref, out_ref, flat, table, blended, *, chunk):
    highs = flat.shape[1]
    pixels = index_ref.shape[1]
    stride = table.shape[0] // 2

    def unfold(step, carry):
        piece = table_ref[0, 0, :, pl.ds(step * 8 * LANES, 8 * LANES)].astype(jnp.float32)
        for k in range(8):
            for comp in range(2):
                flat[comp, pl.ds(step * 8 + k, 1), :] = piece[comp : comp + 1, k * LANES : (k + 1) * LANES]
        return carry

    lax.fori_loop(0, highs // 8, unfold, 0)
    for comp in range(2):
        turned = flat[comp].T
        following = jnp.broadcast_to(pltpu.roll(turned[0:8], highs - 1, 1)[0:1], (16, highs))
        table[comp * stride : comp * stride + LANES, :] = turned.astype(jnp.bfloat16)
        table[comp * stride + LANES : (comp + 1) * stride, :] = following.astype(jnp.bfloat16)

    def body(step, carry):
        where = pl.ds(step * chunk, chunk)
        index = index_ref[:, where]
        frac = frac_ref[:, where]
        high = index // LANES
        low = index % LANES
        high_ids = lax.broadcasted_iota(jnp.int32, (highs, chunk), 0)
        one_hot = jnp.where(high_ids == high, 1.0, 0.0).astype(jnp.bfloat16)
        rows = jnp.dot(table[...], one_hot, preferred_element_type=jnp.float32)
        low_ids = lax.broadcasted_iota(jnp.int32, (LANES + 8, chunk), 0)
        weight = jnp.where(low_ids == low, 1.0 - frac, jnp.where(low_ids == low + 1, frac, 0.0))
        for comp in range(2):
            value = jnp.sum(
                rows[comp * stride : comp * stride + LANES + 8] * weight, axis=0, keepdims=True
            )
            for k in range(chunk // LANES):
                row = comp * (pixels // LANES) + step * (chunk // LANES) + k
                blended[pl.ds(row, 1), :] = value[:, k * LANES : (k + 1) * LANES]
        return carry

    lax.fori_loop(0, pixels // chunk, body, 0)
    row = blended[...].astype(jnp.bfloat16)
    for m in range(out_ref.shape[0]):
        out_ref[m] = row


def project_row(class_refs, pick, interp_index, interp_frac, copies):
    vox = class_refs.shape[3]
    pixels = interp_index.shape[1]
    highs = vox // LANES
    out_rows = 2 * pixels // LANES
    grid_spec = pltpu.PrefetchScalarGridSpec(
        num_scalar_prefetch=1,
        grid=(1,),
        in_specs=[
            pl.BlockSpec((1, 1, 2, vox), lambda i, pick: (pick[0], pick[1], 0, 0)),
            pl.BlockSpec((1, pixels), lambda i, pick: (0, 0)),
            pl.BlockSpec((1, pixels), lambda i, pick: (0, 0)),
        ],
        out_specs=pl.BlockSpec((copies, out_rows, LANES), lambda i, pick: (0, 0, 0)),
        scratch_shapes=[
            pltpu.VMEM((2, highs, LANES), jnp.float32),
            pltpu.VMEM((2 * (LANES + 16), highs), jnp.bfloat16),
            pltpu.VMEM((out_rows, LANES), jnp.float32),
        ],
    )
    return pl.pallas_call(
        functools.partial(project_kernel, chunk=1024),
        grid_spec=grid_spec,
        out_shape=jax.ShapeDtypeStruct((copies, out_rows, LANES), jnp.bfloat16),
        compiler_params=pltpu.CompilerParams(vmem_limit_bytes=56 * MIB),
        name="project_row",
    )(pick, class_refs, interp_index, interp_frac)


def slot_rows(device, slots):
    ids = lax.broadcasted_iota(jnp.int32, (slots, 1), 0)
    place, core_flip = ids % (slots // 2), ids // (slots // 2)
    return 2 * place + ((device % 2) ^ core_flip)


def split_mass(mass_row):
    ids = lax.broadcasted_iota(jnp.int32, (MASS_ROWS, LANES), 0)
    upper = mass_row.astype(jnp.bfloat16).astype(jnp.float32)
    lower = mass_row - upper
    return jnp.where(ids == 0, upper, jnp.where(ids == 1, lower, 0.0)).astype(jnp.bfloat16)


def joined_mass(block):
    return jnp.sum(block.astype(jnp.float32), axis=0, keepdims=True)


def table_kernel(shift_ref, cos_ref, sin_ref):
    shifts, pixels = cos_ref.shape
    grid_x = shift_ref[:, 0:1]
    grid_y = shift_ref[:, 1:2]
    lane = lax.broadcasted_iota(jnp.int32, (shifts, KY), 1)
    turn_x = (lane * grid_x) & (BOX - 1)
    turn_y = ((lane - KY // 2) * grid_y) & (BOX - 1)
    angle_x = turn_x.astype(jnp.float32) * (2.0 * math.pi / BOX)
    angle_y = turn_y.astype(jnp.float32) * (2.0 * math.pi / BOX)
    cos_x, sin_x = jnp.cos(angle_x), jnp.sin(angle_x)
    cos_y, sin_y = jnp.cos(angle_y), jnp.sin(angle_y)
    for j in range(pixels // LANES):
        where = slice(j * LANES, (j + 1) * LANES)
        cos_j, sin_j = cos_x[:, j : j + 1], sin_x[:, j : j + 1]
        cos_ref[:, where] = cos_j * cos_y - sin_j * sin_y
        sin_ref[:, where] = sin_j * cos_y + cos_j * sin_y


def phase_tables(shift_grid, pixels):
    shape = jax.ShapeDtypeStruct((shift_grid.shape[0], pixels), jnp.float32)
    return pl.pallas_call(
        table_kernel,
        in_specs=whole_vmem(1),
        out_specs=whole_vmem(2),
        out_shape=[shape, shape],
        compiler_params=pltpu.CompilerParams(vmem_limit_bytes=16 * MIB),
        cost_estimate=pl.CostEstimate(flops=2000000, bytes_accessed=2000000, transcendentals=0),
        name="phase_tables",
    )(shift_grid)


def rotate_back(weights, images, cos_ref, sin_ref, where, imag_where, slots):
    from_real = jnp.dot(weights, images[:, where], preferred_element_type=jnp.float32)
    from_imag = jnp.dot(weights, images[:, imag_where], preferred_element_type=jnp.float32)
    real = imag = None
    for s in range(cos_ref.shape[0]):
        cos_s, sin_s = cos_ref[s : s + 1, where], sin_ref[s : s + 1, where]
        part_real = from_real[s * slots : (s + 1) * slots]
        part_imag = from_imag[s * slots : (s + 1) * slots]
        real_s = part_real * cos_s + part_imag * sin_s
        imag_s = part_imag * cos_s - part_real * sin_s
        real = real_s if real is None else real + real_s
        imag = imag_s if imag is None else imag + imag_s
    return real, imag


def expect_kernel(
    device_ref, images, precision_ref, assigned_ref, cos_ref, sin_ref, row_ref, other_ref,
    weight_ref, low_ref, low_send, own_mass, proj, *, slots, chunk
):
    device = device_ref[0]
    shifts = cos_ref.shape[0]
    parts = images.shape[0]
    pixels = images.shape[1] // 2
    tiles = pixels // LANES
    per_row = 2 * tiles
    half = slots // 2
    for m in range(half):
        proj[m * per_row : (m + 1) * per_row, :] = row_ref[m].astype(jnp.float32)
        proj[(half + m) * per_row : (half + m + 1) * per_row, :] = other_ref[m].astype(jnp.float32)

    chunk_tiles = chunk // LANES
    contract_lanes = (((1,), (1,)), ((), ()))

    def correlate(step, carry):
        total, power = carry
        first = step * chunk_tiles
        real = jnp.concatenate(
            [proj[pl.ds(first + k, slots, stride=per_row), :] for k in range(chunk_tiles)], axis=1
        )
        imag = jnp.concatenate(
            [proj[pl.ds(tiles + first + k, slots, stride=per_row), :] for k in range(chunk_tiles)],
            axis=1,
        )
        where = pl.ds(pl.multiple_of(step * chunk, chunk), chunk)
        reals, imags = [], []
        for s in range(shifts):
            cos_s, sin_s = cos_ref[s : s + 1, where], sin_ref[s : s + 1, where]
            reals.append(real * cos_s - imag * sin_s)
            imags.append(real * sin_s + imag * cos_s)
        turned_real = jnp.concatenate(reals, axis=0).astype(jnp.bfloat16)
        turned_imag = jnp.concatenate(imags, axis=0).astype(jnp.bfloat16)
        image_real = images[:, where]
        image_imag = images[:, pl.ds(pl.multiple_of(pixels + step * chunk, chunk), chunk)]
        total = total + lax.dot_general(
            turned_real, image_real, contract_lanes, preferred_element_type=jnp.float32
        )
        total = total + lax.dot_general(
            turned_imag, image_imag, contract_lanes, preferred_element_type=jnp.float32
        )
        squares = real * real + imag * imag
        for k in range(chunk_tiles):
            power = power + squares[:, k * LANES : (k + 1) * LANES]
        return total, power

    total, power = lax.fori_loop(
        0,
        pixels // chunk,
        correlate,
        (
            jnp.zeros((shifts * slots, parts), jnp.float32),
            jnp.zeros((slots, LANES), jnp.float32),
        ),
    )
    power = jnp.sum(power, axis=1, keepdims=True)
    slot_class = slot_rows(device, slots) // (slots // CLASSES)
    match = (slot_class == assigned_ref[...]).astype(jnp.float32) * PRIOR_REWARD
    precision = precision_ref[...]
    likelihood_scale = 1.0 / math.sqrt(2 * pixels)
    logits = [
        precision * (total[s * slots : (s + 1) * slots] - 0.5 * power) * likelihood_scale + match
        for s in range(shifts)
    ]
    peak = functools.reduce(jnp.maximum, logits)
    peak = jnp.max(peak, axis=0, keepdims=True)
    terms = [jnp.exp(value - peak) for value in logits]
    mass = functools.reduce(jnp.add, terms)
    norm = jnp.sum(mass, axis=0, keepdims=True)
    weights = jnp.concatenate([term / norm for term in terms], axis=0).astype(jnp.bfloat16)
    weight_ref[...] = weights
    slot_mass = jnp.sum(mass / norm * precision, axis=1, keepdims=True)
    class_lane = lax.broadcasted_iota(jnp.int32, (slots, LANES), 1)
    mass_row = jnp.sum(
        jnp.where(class_lane == slot_class, slot_mass, 0.0), axis=0, keepdims=True
    )
    own_mass[...] = jnp.broadcast_to(mass_row, own_mass.shape)

    low_rows = LOWK * KY // LANES
    low_width = LOWK * KY
    real, imag = rotate_back(
        weights, images, cos_ref, sin_ref, slice(0, low_width), slice(pixels, pixels + low_width), slots
    )
    for k in range(low_rows):
        piece = slice(k * LANES, (k + 1) * LANES)
        low_ref[pl.ds(k, slots, stride=2 * low_rows), :] = real[:, piece]
        low_ref[pl.ds(low_rows + k, slots, stride=2 * low_rows), :] = imag[:, piece]
    low_body = low_ref.shape[0]
    low_send[0:low_body, :] = low_ref[...].astype(jnp.bfloat16)
    low_send[low_body:, :] = split_mass(mass_row)


def expect(device, images, precision, assigned, cos_table, sin_table, rows, others):
    slots = 2 * rows.shape[0]
    pixels = images.shape[1] // 2
    per_row = 2 * pixels // LANES
    shifts = cos_table.shape[0]
    low = slots * 2 * (LOWK * KY // LANES)
    return pl.pallas_call(
        functools.partial(expect_kernel, slots=slots, chunk=2048),
        in_specs=[pl.BlockSpec(memory_space=pltpu.SMEM)] + whole_vmem(7),
        out_specs=whole_vmem(4),
        out_shape=[
            jax.ShapeDtypeStruct((shifts * slots, images.shape[0]), jnp.bfloat16),
            jax.ShapeDtypeStruct((low, LANES), jnp.float32),
            jax.ShapeDtypeStruct((low + MASS_ROWS, LANES), jnp.bfloat16),
            jax.ShapeDtypeStruct((8, LANES), jnp.float32),
        ],
        scratch_shapes=[pltpu.VMEM((slots * per_row, LANES), jnp.float32)],
        compiler_params=pltpu.CompilerParams(vmem_limit_bytes=(14 + slots // 2) * MIB),
        name="expect",
    )(device, images, precision, assigned, cos_table, sin_table, rows, others)


def backproject_kernel(weight_ref, images, cos_ref, sin_ref, sums, *, slots, chunk):
    pixels = images.shape[1] // 2
    tiles = pixels // LANES
    per_row = 2 * tiles
    chunk_tiles = chunk // LANES
    weights = weight_ref[...]

    def body(step, carry):
        where = pl.ds(pl.multiple_of(step * chunk, chunk), chunk)
        imag_where = pl.ds(pl.multiple_of(pixels + step * chunk, chunk), chunk)
        real, imag = rotate_back(weights, images, cos_ref, sin_ref, where, imag_where, slots)
        first = step * chunk_tiles
        for k in range(chunk_tiles):
            piece = slice(k * LANES, (k + 1) * LANES)
            sums[pl.ds(first + k, slots, stride=per_row), :] = real[:, piece]
            sums[pl.ds(tiles + first + k, slots, stride=per_row), :] = imag[:, piece]
        return carry

    lax.fori_loop(LOWK * KY // chunk, pixels // chunk, body, 0)


def backproject(weights, images, cos_table, sin_table, slots):
    per_row = images.shape[1] // LANES
    return pl.pallas_call(
        functools.partial(backproject_kernel, slots=slots, chunk=2048),
        in_specs=whole_vmem(4),
        out_specs=pl.BlockSpec(memory_space=pltpu.VMEM),
        out_shape=jax.ShapeDtypeStruct((slots * per_row, LANES), jnp.float32),
        compiler_params=pltpu.CompilerParams(vmem_limit_bytes=(14 + slots // 2) * MIB),
        cost_estimate=pl.CostEstimate(flops=20000000, bytes_accessed=20000000, transcendentals=0),
        name="backproject",
    )(weights, images, cos_table, sin_table)


def fold_kernel(sums_in, low_ref, low_received, mass, keep, to_core, total_mass, *, slots):
    per_row = sums_in.shape[0] // slots
    tiles = per_row // 2
    low_rows = LOWK * KY // LANES
    half = slots // 2
    low_body = low_ref.shape[0]
    folded = mass[0:1, :] + joined_mass(low_received[low_body:, :])
    total_mass[...] = jnp.broadcast_to(folded, total_mass.shape)
    for slot in range(slots):
        target = keep if slot < half else to_core
        for comp in range(2):
            low = slice((2 * slot + comp) * low_rows, (2 * slot + comp + 1) * low_rows)
            start = slot * per_row + comp * tiles
            dest = (slot % half) * per_row + comp * tiles
            value = (low_ref[low, :] + low_received[low, :].astype(jnp.float32)) * 0.5
            target[dest : dest + low_rows, :] = value.astype(target.dtype)
            target[dest + low_rows : dest + tiles, :] = sums_in[
                start + low_rows : start + tiles, :
            ].astype(target.dtype)
    to_core[half * per_row :, :] = split_mass(folded)


def fold(sums, low, low_received, mass, slots):
    half_rows = sums.shape[0] // 2
    return pl.pallas_call(
        functools.partial(fold_kernel, slots=slots),
        in_specs=whole_vmem(4),
        out_specs=whole_vmem(3),
        out_shape=[
            jax.ShapeDtypeStruct((half_rows, LANES), jnp.float32),
            jax.ShapeDtypeStruct((half_rows + MASS_ROWS, LANES), jnp.bfloat16),
            jax.ShapeDtypeStruct((8, LANES), jnp.float32),
        ],
        compiler_params=pltpu.CompilerParams(vmem_limit_bytes=(10 + slots // 2) * MIB),
        name="fold",
    )(sums, low, low_received, mass)


def merge_kernel(keep, from_core, mass, out, *, half):
    per_row = keep.shape[0] // half
    total_mass = mass[0:1, :] + joined_mass(from_core[half * per_row :, :])
    block = split_mass(total_mass)
    for m in range(half):
        rows = slice(m * per_row, (m + 1) * per_row)
        out[m, 0:per_row, :] = (keep[rows, :] + from_core[rows, :].astype(jnp.float32)).astype(
            jnp.bfloat16
        )
        out[m, per_row:, :] = block


def merge(keep, from_core, mass, half):
    per_row = keep.shape[0] // half
    return pl.pallas_call(
        functools.partial(merge_kernel, half=half),
        in_specs=whole_vmem(3),
        out_specs=pl.BlockSpec(memory_space=pltpu.VMEM),
        out_shape=jax.ShapeDtypeStruct((half, per_row + MASS_ROWS, LANES), jnp.bfloat16),
        compiler_params=pltpu.CompilerParams(vmem_limit_bytes=(12 + half) * MIB),
        name="merge",
    )(keep, from_core, mass)


def finish_kernel(received, out, mass_out, *, scale, mass_scale):
    per_row = out.shape[0]
    total, total_mass = None, None
    for m in range(received.shape[0]):
        value = received[m, 0:per_row, :].astype(jnp.float32)
        mass = joined_mass(received[m, per_row:, :])
        total = value if total is None else total + value
        total_mass = mass if total_mass is None else total_mass + mass
    out[...] = total * scale
    mass_out[...] = total_mass[0, :CLASSES] * mass_scale


def finish(received, scale, mass_scale):
    return pl.pallas_call(
        functools.partial(finish_kernel, scale=scale, mass_scale=mass_scale),
        in_specs=whole_vmem(1),
        out_specs=whole_vmem(2),
        out_shape=[
            jax.ShapeDtypeStruct((received.shape[1] - MASS_ROWS, LANES), jnp.float32),
            jax.ShapeDtypeStruct((CLASSES,), jnp.float32),
        ],
        compiler_params=pltpu.CompilerParams(vmem_limit_bytes=16 * MIB),
        name="finish",
    )(received)


def local(
    images, noise_precision, assigned_class, class_refs, interp_index, interp_frac, shift_grid
):
    dev_count = lax.axis_size("particle")
    device = lax.axis_index("particle").astype(jnp.int32)
    slots = dev_count // 2
    part_count = images.shape[0]
    half_set = device // 2 % 2
    class_id = (2 * (device // 4) + device % 2) // (slots // CLASSES)
    copies = project_row(
        class_refs, jnp.stack([half_set, class_id]), interp_index, interp_frac, slots // 2
    )
    rows = across_z(copies)
    cos_table, sin_table = phase_tables(shift_grid, images.shape[1] // 2)
    weights, low, low_send, mass = expect(
        device.reshape(1),
        images,
        noise_precision.reshape(1, part_count),
        assigned_class.reshape(1, part_count),
        cos_table,
        sin_table,
        rows,
        exchange(rows, 1),
    )
    low_received = exchange(low_send, 2)
    sums = backproject(weights, images, cos_table, sin_table, slots)
    keep, to_core, mass = fold(sums, low, low_received, mass, slots)
    received = across_z(merge(keep, exchange(to_core, 1), mass, slots // 2))
    back, class_mass = finish(
        received, 1.0 / math.sqrt(part_count), CLASSES / (part_count * dev_count)
    )
    return back.reshape(1, images.shape[1]), class_mass


def solution(mesh):
    in_specs = (
        P(("groups", "particle"), None),
        P(("groups", "particle")),
        P(("groups", "particle")),
        P("groups", None, None, None),
        P("particle", None),
        P("particle", None),
        P(),
    )
    out_specs = (P(("groups", "particle"), None), P("groups"))
    return jax.shard_map(local, mesh=mesh, in_specs=in_specs, out_specs=out_specs, check_vma=False)
```

time: 53.2 us -> 50.8 us (0.955)
  blocking collectives: 0 us -> 27.4 us
  waiting for transfers between devices: 14.6 us -> 2.37 us
  starting transfers between devices: 12.7 us -> 1.63 us
  local copies, waits for them, and re-layouts: 3.88 us -> 0.1 us
  Pallas kernels: 21 us -> 17.7 us
    all_to_all x0 -> x2, blocking collectives: none -> 27.4 us  [across_z(): lax.all_to_all(value, 'particle', split_axis=0, concat_axis=0, axis_index...]
    ppermute x13 -> x3, waiting for transfers between devices: 14.6 us -> 2.37 us  [exchange(): return lax.ppermute(value, 'particle', pairs)]
    ppermute x13 -> x3, starting transfers between devices: 12.7 us -> 1.63 us  [exchange(): return lax.ppermute(value, 'particle', pairs)]
    pallas_call x1 -> x4, Pallas kernels: 13.2 us -> 8.02 us  [the longest x1 3.91 us: expect(): pl.pallas_call(functools.partial(expect_kernel, slots=slots, chunk=2048),...]
    unnamed x15 -> x9, local copies, waits for them, and re-layouts: 3.37 us -> 0.1 us
    pallas_call x1, Pallas kernels: 7.02 us -> 8.96 us  [project_row(): pl.pallas_call(functools.partial(project_kernel, chunk=1024), grid_spec=g...]
  transfers between devices with their start and end apart: 13 -> 3, of which waited for: 9 -> 2; matrix products, arithmetic and copies ran while one was open for 0% -> 0% of each run, Pallas kernels for 0% -> 8%
where the time goes in v2:
time: 50.8 us; the launch traced here: 50.5 us
  blocking collectives  27.4 us (54%)
  Pallas kernels  17.7 us (35%)
  waiting for transfers between devices  2.37 us (5%)
  starting transfers between devices  1.63 us (3%)
  between operations  0.75 us (1%)
  other arithmetic  0.59 us (1%)
    all_to_all x2, blocking collectives, across_z(): lax.all_to_all(value, 'particle', split_axis=0, concat_axis=0, axis_index...  27.4 us
    pallas_call x1, Pallas kernels, project_row(): pl.pallas_call(functools.partial(project_kernel, chunk=1024), grid_spec=g...  8.96 us
    pallas_call x1, Pallas kernels, expect(): pl.pallas_call(functools.partial(expect_kernel, slots=slots, chunk=2048),...  3.91 us
    pallas_call x1, Pallas kernels, backproject(): pl.pallas_call(functools.partial(backproject_kernel, slots=slots, chunk=2...  3.42 us
    ppermute x3, waiting for transfers between devices, exchange(): return lax.ppermute(value, 'particle', pairs)  2.37 us
    ppermute x3, starting transfers between devices, exchange(): return lax.ppermute(value, 'particle', pairs)  1.63 us
  transfers between devices with their start and end apart: 3, of which 2 were waited for; matrix products, arithmetic and copies ran while one was open for 0% of the time, Pallas kernels for 8%

profile of v2, /device:TPU:0, one launch (start us, length us, event | category | flops | bytes accessed | tf_op | source)
XLA Modules:
  0.0 50.5 jit_solution(13222432160920683007)
XLA Ops:
  0.6 0.0 copy-start.3
  0.6 0.0 copy-start
  0.7 0.0 copy-start.2
  0.7 0.0 copy-start.1
  0.7 0.6 %pad_add_fusion.pick_ref = s32[2]{0:T(128)} fusion(s32[1]{0:T(128)} %bitcast.4, s32[1]{0:T(128)} %bitcast.3), kind=kLoop, calls=%fused_computation | loop fusion | flops 2 | bytes 16 | tf_op jit(solution)/shard_map/stack | solution.py:424
  1.3 9.0 %project_row.1 = bf16[4,256,128]{2,1,0:T(8,128)(2,1)} custom-call(s32[2]{0:T(128)} %pad_add_fusion.pick_ref, bf16[2,8,2,32768]{3,2,1,0:T(2,128)(2,1)} %table_ref.1, s32[1,16384]{1,0:T(1,128)} %index_ref.1, f32[1,16384]{1,0:T(1,128)} %frac_ref.1), custom_call_target="tpu_custom_call" | custom-call | tf_op jit(solution)/shard_map/project_row/pallas_call | solution.py:103
  10.3 15.2 %all_to_all.10.row_ref = bf16[4,256,128]{2,1,0:T(8,128)(2,1)S(1)} all-to-all(bf16[4,256,128]{2,1,0:T(8,128)(2,1)} %project_row.1), channel_id=1, replica_groups={{0,4,8,12},{1,5,9,13},{2,6,10,14},{3,7,11,15},{16,20,24,28},{17,21,25,2..., dimensions={0} | all-to-all | bytes 524288 | tf_op jit(solution)/shard_map/all_to_all | solution.py:29
  25.5 0.0 collective-permute-start
  25.5 0.0 copy-done.3
  25.5 0.1 copy.9.shift_ref
  25.5 0.6 %phase_tables.1 = (f32[8,16384]{1,0:T(8,128)S(1)}, f32[8,16384]{1,0:T(8,128)S(1)}) custom-call(s32[8,2]{1,0:T(8,128)S(1)} %copy.9.shift_ref), custom_call_target="tpu_custom_call" | custom-call | flops 2000000 | bytes 2000000 | tf_op jit(solution)/shard_map/phase_tables/pallas_call | solution.py:149
  26.2 0.8 %collective-permute-done.other_ref = bf16[4,256,128]{2,1,0:T(8,128)(2,1)S(1)} collective-permute-done((bf16[4,256,128]{2,1,0:T(8,128)(2,1)S(1)}, bf16[4,256,128]{2,1,0:T(8,128)(2,1)S(1)}, u32[]{:S(2)}, u32[]{:S(2)}) %collective-permute-start) | collective-permute-done | bytes 262176 | tf_op jit(solution)/shard_map/ppermute | solution.py:23
  27.0 0.0 copy-done
  27.0 0.0 copy-done.2
  27.0 3.9 %expect.1 = (bf16[64,32]{1,0:T(8,128)(2,1)S(1)}, f32[256,128]{1,0:T(8,128)S(1)}, bf16[272,128]{1,0:T(8,128)(2,1)S(1)}, f32[8,128]{1,0:T(8,128)S(1)}) custom-call(s32[1]{0:T(128)} %bitcast.device_ref, bf16[32,32768]{1,0:T(8,128)(2,1)S(1)} %copy-done, f32[1,32]{1,0:T(1,128)S(1)} %bitcast.6, s32[1,32]{1,0:T(1,128)S(1)} %bitcast.7, ...), custom_call_target="tpu_custom_call" | custom-call | tf_op jit(solution)/shard_map/expect/pallas_call | solution.py:276
  30.9 1.6 %collective-permute-start.1 = (bf16[272,128]{1,0:T(8,128)(2,1)S(1)}, bf16[272,128]{1,0:T(8,128)(2,1)S(1)}, u32[]{:S(2)}, u32[]{:S(2)}) collective-permute-start(bf16[272,128]{1,0:T(8,128)(2,1)S(1)} %get-tuple-element.17), channel_id=1, source_target_pairs={{0,2},{1,3},{2,0},{3,1},{4,6},{5,7},{6,4},{7,5},{8,10},{9,11},{10,... | collective-permute-start | bytes 208904 | tf_op jit(solution)/shard_map/ppermute | solution.py:23
  32.5 3.4 %backproject.1.sums_in = f32[2048,128]{1,0:T(8,128)S(1)} custom-call(bf16[64,32]{1,0:T(8,128)(2,1)S(1)} %get-tuple-element.15.weight_ref, bf16[32,32768]{1,0:T(8,128)(2,1)S(1)} %copy-done, f32[8,16384]{1,0:T(8,128)S(1)} %get-tuple-element.13.cos_ref, f32[8,16384]{1,0:T(8,128)S(1)} %get-tuple-element.14.sin_ref), custom_call_target="tpu_custom_call" | custom-call | flops 20000000 | bytes 20000000 | tf_op jit(solution)/shard_map/backproject/pallas_call | solution.py:315
  35.9 0.0 collective-permute-done.1.low_received
  35.9 0.1 fold.1
  36.0 0.1 collective-permute-start.2
  36.1 1.5 %collective-permute-done.2.from_core = bf16[1040,128]{1,0:T(8,128)(2,1)S(1)} collective-permute-done((bf16[1040,128]{1,0:T(8,128)(2,1)S(1)}, bf16[1040,128]{1,0:T(8,128)(2,1)S(1)}, u32[]{:S(2)}, u32[]{:S(2)}) %collective-permute-start.2) | collective-permute-done | bytes 266272 | tf_op jit(solution)/shard_map/ppermute | solution.py:23
  37.6 0.1 merge.1
  37.7 12.2 %all_to_all.11.received = bf16[4,272,128]{2,1,0:T(8,128)(2,1)S(1)} all-to-all(bf16[4,272,128]{2,1,0:T(8,128)(2,1)S(1)} %merge.1), channel_id=1, replica_groups={{0,4,8,12},{1,5,9,13},{2,6,10,14},{3,7,11,15},{16,20,24,28},{17,21,25,2..., dimensions={0} | all-to-all | bytes 557056 | tf_op jit(solution)/shard_map/all_to_all | solution.py:29
  49.8 0.7 %finish.1 = (f32[256,128]{1,0:T(8,128)}, f32[8]{0:T(128)}) custom-call(bf16[4,272,128]{2,1,0:T(8,128)(2,1)S(1)} %all_to_all.11.received), custom_call_target="tpu_custom_call" | custom-call | tf_op jit(solution)/shard_map/finish/pallas_call | solution.py:401
  (1 shorter events, 0.0 us)
Async XLA Ops:
  0.6 24.8 %copy-start.3 = (s32[8,2]{0,1:T(2,128)S(1)}, s32[8,2]{0,1:T(2,128)}, u32[]{:S(2)}) copy-start(s32[8,2]{0,1:T(2,128)} %param.13) | copy-start | bytes 196
  0.6 26.4 %copy-start = (bf16[32,32768]{1,0:T(8,128)(2,1)S(1)}, bf16[32,32768]{1,0:T(8,128)(2,1)}, u32[]{:S(2)}) copy-start(bf16[32,32768]{1,0:T(8,128)(2,1)} %images.3) | copy-start | bytes 6291460
  0.7 26.3 %copy-start.2 = (s32[32]{0:T(128)S(1)}, s32[32]{0:T(128)}, u32[]{:S(2)}) copy-start(s32[32]{0:T(128)} %param.9) | copy-start | bytes 388
  0.7 26.3 %copy-start.1 = (f32[32]{0:T(128)S(1)}, f32[32]{0:T(128)}, u32[]{:S(2)}) copy-start(f32[32]{0:T(128)} %param.8) | copy-start | bytes 388
  25.5 1.5 %collective-permute-start = (bf16[4,256,128]{2,1,0:T(8,128)(2,1)S(1)}, bf16[4,256,128]{2,1,0:T(8,128)(2,1)S(1)}, u32[]{:S(2)}, u32[]{:S(2)}) collective-permute-start(bf16[4,256,128]{2,1,0:T(8,128)(2,1)S(1)} %all_to_all.10.row_ref), channel_id=1, source_target_pairs={{0,1},{1,0},{2,3},{3,2},{4,5},{5,4},{6,7},{7,6},{8,9},{9,8},{10,11... | collective-permute-start | bytes 786440 | tf_op jit(solution)/shard_map/ppermute | solution.py:23
  30.9 5.0 %collective-permute-start.1 = (bf16[272,128]{1,0:T(8,128)(2,1)S(1)}, bf16[272,128]{1,0:T(8,128)(2,1)S(1)}, u32[]{:S(2)}, u32[]{:S(2)}) collective-permute-start(bf16[272,128]{1,0:T(8,128)(2,1)S(1)} %get-tuple-element.17), channel_id=1, source_target_pairs={{0,2},{1,3},{2,0},{3,1},{4,6},{5,7},{6,4},{7,5},{8,10},{9,11},{10,... | collective-permute-start | bytes 208904 | tf_op jit(solution)/shard_map/ppermute | solution.py:23
  36.0 1.6 %collective-permute-start.2 = (bf16[1040,128]{1,0:T(8,128)(2,1)S(1)}, bf16[1040,128]{1,0:T(8,128)(2,1)S(1)}, u32[]{:S(2)}, u32[]{:S(2)}) collective-permute-start(bf16[1040,128]{1,0:T(8,128)(2,1)S(1)} %get-tuple-element.20), channel_id=1, source_target_pairs={{0,1},{1,0},{2,3},{3,2},{4,5},{5,4},{6,7},{7,6},{8,9},{9,8},{10,11... | collective-permute-start | bytes 798728 | tf_op jit(solution)/shard_map/ppermute | solution.py:23

commit v3 on v2

--- a/solution.py
+++ b/solution.py
@@ -23,96 +23,125 @@
     return lax.ppermute(value, "particle", pairs)
 
 
-def across_z(value):
-    count = lax.axis_size("particle")
-    groups = [list(range(first, count, 4)) for first in range(4)]
-    return lax.all_to_all(
-        value, "particle", split_axis=0, concat_axis=0, axis_index_groups=groups, tiled=True
-    )
+def in_hbm(value):
+    return pltpu.with_memory_space_constraint(value, pltpu.HBM)
 
 
 def whole_vmem(count):
     return [pl.BlockSpec(memory_space=pltpu.VMEM)] * count
 
 
-def project_kernel(pick_ref, table_ref, index_ref, frac_ref, out_ref, flat, table, blended, *, chunk):
+def tree_select(values, masks):
+    for mask in masks:
+        values = [
+            jnp.where(mask, values[i + 1], values[i]) if i + 1 < len(values) else values[i]
+            for i in range(0, len(values), 2)
+        ]
+    return values[0]
+
+
+def project_kernel(
+    table_hbm, index_hbm, frac_hbm, out_ref,
+    table_in, index_ref, frac_ref, flat, wide, table, blended, sems, *, chunk
+):
+    device = lax.axis_index("particle")
+    row_count = lax.axis_size("particle") // 2
+    half_set = device // 2 % 2
+    class_id = (2 * (device // 4) + device % 2) // (row_count // CLASSES)
+    copies = [
+        pltpu.make_async_copy(
+            table_hbm.at[pl.ds(half_set, 1), pl.ds(class_id, 1)], table_in, sems.at[0]
+        ),
+        pltpu.make_async_copy(index_hbm, index_ref, sems.at[1]),
+        pltpu.make_async_copy(frac_hbm, frac_ref, sems.at[2]),
+    ]
+    for copy in copies:
+        copy.start()
+    copies[0].wait()
     highs = flat.shape[1]
     pixels = index_ref.shape[1]
-    stride = table.shape[0] // 2
+    groups = table.shape[0] // 16
+    stride = 8 * groups
 
     def unfold(step, carry):
-        piece = table_ref[0, 0, :, pl.ds(step * 8 * LANES, 8 * LANES)].astype(jnp.float32)
+        piece = table_in[0, 0, :, pl.ds(step * 8 * LANES, 8 * LANES)].astype(jnp.float32)
         for k in range(8):
             for comp in range(2):
                 flat[comp, pl.ds(step * 8 + k, 1), :] = piece[comp : comp + 1, k * LANES : (k + 1) * LANES]
         return carry
 
-    lax.fori_loop(0, highs // 8, unfold, 0)
+    lax.fori_loop(0, highs // 8, unfold, 0, unroll=4)
+    picked = []
     for comp in range(2):
         turned = flat[comp].T
-        following = jnp.broadcast_to(pltpu.roll(turned[0:8], highs - 1, 1)[0:1], (16, highs))
-        table[comp * stride : comp * stride + LANES, :] = turned.astype(jnp.bfloat16)
-        table[comp * stride + LANES : (comp + 1) * stride, :] = following.astype(jnp.bfloat16)
+        wide[0:LANES, :] = turned
+        wide[LANES : LANES + 8, :] = pltpu.roll(turned[0:8], highs - 1, 1)
+        picked += [wide[7 * g : 7 * g + 8, :] for g in range(groups)]
+    for pair in range(groups):
+        table[16 * pair : 16 * (pair + 1), :] = jnp.concatenate(
+            picked[2 * pair : 2 * pair + 2], axis=0
+        ).astype(jnp.bfloat16)
+    copies[1].wait()
+    copies[2].wait()
 
     def body(step, carry):
-        where = pl.ds(step * chunk, chunk)
+        where = pl.ds(pl.multiple_of(step * chunk, chunk), chunk)
         index = index_ref[:, where]
         frac = frac_ref[:, where]
-        high = index // LANES
-        low = index % LANES
+        high = index >> 7
+        low = index & (LANES - 1)
+        group = (low * 147) >> 10
+        first = low - 7 * group
         high_ids = lax.broadcasted_iota(jnp.int32, (highs, chunk), 0)
         one_hot = jnp.where(high_ids == high, 1.0, 0.0).astype(jnp.bfloat16)
         rows = jnp.dot(table[...], one_hot, preferred_element_type=jnp.float32)
-        low_ids = lax.broadcasted_iota(jnp.int32, (LANES + 8, chunk), 0)
-        weight = jnp.where(low_ids == low, 1.0 - frac, jnp.where(low_ids == low + 1, frac, 0.0))
+        group = jnp.broadcast_to(group, (8, chunk))
+        masks = [(group & (1 << bit)) != 0 for bit in range((groups - 1).bit_length())]
+        ids = lax.broadcasted_iota(jnp.int32, (8, chunk), 0)
+        weight = jnp.where(ids == first, 1.0 - frac, jnp.where(ids == first + 1, frac, 0.0))
         for comp in range(2):
-            value = jnp.sum(
-                rows[comp * stride : comp * stride + LANES + 8] * weight, axis=0, keepdims=True
-            )
+            start = comp * stride
+            picked = tree_select([rows[start + 8 * g : start + 8 * g + 8] for g in range(groups)], masks)
+            value = jnp.sum(picked * weight, axis=0, keepdims=True)
             for k in range(chunk // LANES):
                 row = comp * (pixels // LANES) + step * (chunk // LANES) + k
                 blended[pl.ds(row, 1), :] = value[:, k * LANES : (k + 1) * LANES]
         return carry
 
-    lax.fori_loop(0, pixels // chunk, body, 0)
-    row = blended[...].astype(jnp.bfloat16)
-    for m in range(out_ref.shape[0]):
-        out_ref[m] = row
-
-
-def project_row(class_refs, pick, interp_index, interp_frac, copies):
+    lax.fori_loop(0, pixels // chunk, body, 0, unroll=2)
+    out_ref[...] = blended[...].astype(jnp.bfloat16)
+
+
+def project_row(class_refs, interp_index, interp_frac):
     vox = class_refs.shape[3]
     pixels = interp_index.shape[1]
     highs = vox // LANES
     out_rows = 2 * pixels // LANES
-    grid_spec = pltpu.PrefetchScalarGridSpec(
-        num_scalar_prefetch=1,
-        grid=(1,),
-        in_specs=[
-            pl.BlockSpec((1, 1, 2, vox), lambda i, pick: (pick[0], pick[1], 0, 0)),
-            pl.BlockSpec((1, pixels), lambda i, pick: (0, 0)),
-            pl.BlockSpec((1, pixels), lambda i, pick: (0, 0)),
+    groups = -(-LANES // 7)
+    return pl.pallas_call(
+        functools.partial(project_kernel, chunk=1024),
+        in_specs=[pl.BlockSpec(memory_space=pltpu.HBM)] * 3,
+        out_specs=pl.BlockSpec(memory_space=pltpu.VMEM),
+        out_shape=jax.ShapeDtypeStruct((out_rows, LANES), jnp.bfloat16),
+        scratch_shapes=[
+            pltpu.VMEM((1, 1, 2, vox), jnp.bfloat16),
+            pltpu.VMEM((1, pixels), jnp.int32),
+            pltpu.VMEM((1, pixels), jnp.float32),
+            pltpu.VMEM((2, highs, LANES), jnp.float32),
+            pltpu.VMEM((LANES + 8, highs), jnp.float32),
+            pltpu.VMEM((16 * groups, highs), jnp.bfloat16),
+            pltpu.VMEM((out_rows, LANES), jnp.float32),
+            pltpu.SemaphoreType.DMA((3,)),
         ],
-        out_specs=pl.BlockSpec((copies, out_rows, LANES), lambda i, pick: (0, 0, 0)),
-        scratch_shapes=[
-            pltpu.VMEM((2, highs, LANES), jnp.float32),
-            pltpu.VMEM((2 * (LANES + 16), highs), jnp.bfloat16),
-            pltpu.VMEM((out_rows, LANES), jnp.float32),
-        ],
-    )
-    return pl.pallas_call(
-        functools.partial(project_kernel, chunk=1024),
-        grid_spec=grid_spec,
-        out_shape=jax.ShapeDtypeStruct((copies, out_rows, LANES), jnp.bfloat16),
-        compiler_params=pltpu.CompilerParams(vmem_limit_bytes=56 * MIB),
+        compiler_params=pltpu.CompilerParams(vmem_limit_bytes=16 * MIB),
         name="project_row",
-    )(pick, class_refs, interp_index, interp_frac)
+    )(*(in_hbm(value) for value in (class_refs, interp_index, interp_frac)))
 
 
 def slot_rows(device, slots):
     ids = lax.broadcasted_iota(jnp.int32, (slots, 1), 0)
-    place, core_flip = ids % (slots // 2), ids // (slots // 2)
-    return 2 * place + ((device % 2) ^ core_flip)
+    flips, core_flip = ids % (slots // 2), ids // (slots // 2)
+    return 2 * ((device // 4) ^ flips) + ((device % 2) ^ core_flip)
 
 
 def split_mass(mass_row):
@@ -172,20 +201,16 @@
     return real, imag
 
 
-def expect_kernel(
-    device_ref, images, precision_ref, assigned_ref, cos_ref, sin_ref, row_ref, other_ref,
-    weight_ref, low_ref, low_send, own_mass, proj, *, slots, chunk
-):
-    device = device_ref[0]
+def expect_kernel(images, precision_ref, assigned_ref, cos_ref, sin_ref, *refs, slots, chunk):
+    row_refs, (weight_ref, low_ref, low_send, own_mass, proj) = refs[:slots], refs[slots:]
+    device = lax.axis_index("particle")
     shifts = cos_ref.shape[0]
     parts = images.shape[0]
     pixels = images.shape[1] // 2
     tiles = pixels // LANES
     per_row = 2 * tiles
-    half = slots // 2
-    for m in range(half):
-        proj[m * per_row : (m + 1) * per_row, :] = row_ref[m].astype(jnp.float32)
-        proj[(half + m) * per_row : (half + m + 1) * per_row, :] = other_ref[m].astype(jnp.float32)
+    for slot in range(slots):
+        proj[slot * per_row : (slot + 1) * per_row, :] = row_refs[slot][...].astype(jnp.float32)
 
     chunk_tiles = chunk // LANES
     contract_lanes = (((1,), (1,)), ((), ()))
@@ -267,15 +292,15 @@
     low_send[low_body:, :] = split_mass(mass_row)
 
 
-def expect(device, images, precision, assigned, cos_table, sin_table, rows, others):
-    slots = 2 * rows.shape[0]
+def expect(images, precision, assigned, cos_table, sin_table, rows):
+    slots = len(rows)
     pixels = images.shape[1] // 2
     per_row = 2 * pixels // LANES
     shifts = cos_table.shape[0]
     low = slots * 2 * (LOWK * KY // LANES)
     return pl.pallas_call(
         functools.partial(expect_kernel, slots=slots, chunk=2048),
-        in_specs=[pl.BlockSpec(memory_space=pltpu.SMEM)] + whole_vmem(7),
+        in_specs=whole_vmem(5 + slots),
         out_specs=whole_vmem(4),
         out_shape=[
             jax.ShapeDtypeStruct((shifts * slots, images.shape[0]), jnp.bfloat16),
@@ -286,7 +311,7 @@
         scratch_shapes=[pltpu.VMEM((slots * per_row, LANES), jnp.float32)],
         compiler_params=pltpu.CompilerParams(vmem_limit_bytes=(14 + slots // 2) * MIB),
         name="expect",
-    )(device, images, precision, assigned, cos_table, sin_table, rows, others)
+    )(images, precision, assigned, cos_table, sin_table, *rows)
 
 
 def backproject_kernel(weight_ref, images, cos_ref, sin_ref, sums, *, slots, chunk):
@@ -361,16 +386,19 @@
     )(sums, low, low_received, mass)
 
 
-def merge_kernel(keep, from_core, mass, out, *, half):
+def merge_kernel(keep, from_core, mass, own, own_mass, *sends, half):
     per_row = keep.shape[0] // half
     total_mass = mass[0:1, :] + joined_mass(from_core[half * per_row :, :])
     block = split_mass(total_mass)
+    own_mass[...] = jnp.broadcast_to(total_mass, own_mass.shape)
     for m in range(half):
         rows = slice(m * per_row, (m + 1) * per_row)
-        out[m, 0:per_row, :] = (keep[rows, :] + from_core[rows, :].astype(jnp.float32)).astype(
-            jnp.bfloat16
-        )
-        out[m, per_row:, :] = block
+        value = keep[rows, :] + from_core[rows, :].astype(jnp.float32)
+        if m == 0:
+            own[...] = value
+        else:
+            sends[m - 1][0:per_row, :] = value.astype(jnp.bfloat16)
+            sends[m - 1][per_row:, :] = block
 
 
 def merge(keep, from_core, mass, half):
@@ -378,69 +406,70 @@
     return pl.pallas_call(
         functools.partial(merge_kernel, half=half),
         in_specs=whole_vmem(3),
-        out_specs=pl.BlockSpec(memory_space=pltpu.VMEM),
-        out_shape=jax.ShapeDtypeStruct((half, per_row + MASS_ROWS, LANES), jnp.bfloat16),
+        out_specs=whole_vmem(1 + half),
+        out_shape=[
+            jax.ShapeDtypeStruct((per_row, LANES), jnp.float32),
+            jax.ShapeDtypeStruct((8, LANES), jnp.float32),
+        ]
+        + [jax.ShapeDtypeStruct((per_row + MASS_ROWS, LANES), jnp.bfloat16)] * (half - 1),
         compiler_params=pltpu.CompilerParams(vmem_limit_bytes=(12 + half) * MIB),
         name="merge",
     )(keep, from_core, mass)
 
 
-def finish_kernel(received, out, mass_out, *, scale, mass_scale):
-    per_row = out.shape[0]
-    total, total_mass = None, None
-    for m in range(received.shape[0]):
-        value = received[m, 0:per_row, :].astype(jnp.float32)
-        mass = joined_mass(received[m, per_row:, :])
-        total = value if total is None else total + value
-        total_mass = mass if total_mass is None else total_mass + mass
+def finish_kernel(own, mass, *refs, scale, mass_scale):
+    received, (out, mass_out) = refs[:-2], refs[-2:]
+    per_row = own.shape[0]
+    total = own[...]
+    total_mass = mass[0:1, :]
+    for ref in received:
+        total = total + ref[0:per_row, :].astype(jnp.float32)
+        total_mass = total_mass + joined_mass(ref[per_row:, :])
     out[...] = total * scale
     mass_out[...] = total_mass[0, :CLASSES] * mass_scale
 
 
-def finish(received, scale, mass_scale):
+def finish(own, mass, received, scale, mass_scale):
     return pl.pallas_call(
         functools.partial(finish_kernel, scale=scale, mass_scale=mass_scale),
-        in_specs=whole_vmem(1),
+        in_specs=whole_vmem(2 + len(received)),
         out_specs=whole_vmem(2),
         out_shape=[
-            jax.ShapeDtypeStruct((received.shape[1] - MASS_ROWS, LANES), jnp.float32),
+            jax.ShapeDtypeStruct(own.shape, jnp.float32),
             jax.ShapeDtypeStruct((CLASSES,), jnp.float32),
         ],
         compiler_params=pltpu.CompilerParams(vmem_limit_bytes=16 * MIB),
         name="finish",
-    )(received)
+    )(own, mass, *received)
 
 
 def local(
     images, noise_precision, assigned_class, class_refs, interp_index, interp_frac, shift_grid
 ):
     dev_count = lax.axis_size("particle")
-    device = lax.axis_index("particle").astype(jnp.int32)
     slots = dev_count // 2
+    half = slots // 2
     part_count = images.shape[0]
-    half_set = device // 2 % 2
-    class_id = (2 * (device // 4) + device % 2) // (slots // CLASSES)
-    copies = project_row(
-        class_refs, jnp.stack([half_set, class_id]), interp_index, interp_frac, slots // 2
-    )
-    rows = across_z(copies)
+    own_row = project_row(class_refs, interp_index, interp_frac)
+    same_core = [own_row] + [exchange(own_row, 4 * m) for m in range(1, half)]
+    rows = same_core + [exchange(row, 1) for row in same_core]
     cos_table, sin_table = phase_tables(shift_grid, images.shape[1] // 2)
     weights, low, low_send, mass = expect(
-        device.reshape(1),
         images,
         noise_precision.reshape(1, part_count),
         assigned_class.reshape(1, part_count),
         cos_table,
         sin_table,
         rows,
-        exchange(rows, 1),
     )
     low_received = exchange(low_send, 2)
     sums = backproject(weights, images, cos_table, sin_table, slots)
     keep, to_core, mass = fold(sums, low, low_received, mass, slots)
-    received = across_z(merge(keep, exchange(to_core, 1), mass, slots // 2))
+    merged = merge(keep, exchange(to_core, 1), mass, half)
+    own, mass, sends = merged[0], merged[1], merged[2:]
+    received = [exchange(sends[m - 1], 4 * m) for m in range(half - 1, 0, -1)]
     back, class_mass = finish(
-        received, 1.0 / math.sqrt(part_count), CLASSES / (part_count * dev_count)
+        own, mass, received, 1.0 / math.sqrt(part_count), CLASSES / (part_count * dev_count)
     )
     return back.reshape(1, images.shape[1]), class_mass
 

time: 50.8 us -> 39.4 us (0.78)
  blocking collectives: 27.4 us -> 0 us
  starting transfers between devices: 1.63 us -> 12.4 us
  waiting for transfers between devices: 2.37 us -> 11.4 us
  Pallas kernels: 17.7 us -> 14.6 us
  other arithmetic: 0.59 us -> 0 us
    all_to_all x2 -> x0, blocking collectives: 27.4 us -> none  [across_z(): lax.all_to_all(value, 'particle', split_axis=0, concat_axis=0, axis_index...]
    ppermute x3 -> x12, starting transfers between devices: 1.63 us -> 12.4 us  [exchange(): return lax.ppermute(value, 'particle', pairs)]
    ppermute x3 -> x12, waiting for transfers between devices: 2.37 us -> 11.4 us  [exchange(): return lax.ppermute(value, 'particle', pairs)]
    pallas_call x1, Pallas kernels: 8.96 us -> 5.87 us  [project_row(): pl.pallas_call(functools.partial(project_kernel, chunk=1024), in_specs=[p...]
    another operation x1 -> x0, other arithmetic: 0.59 us -> none  [local(): jnp.stack([half_set, class_id])]
  transfers between devices with their start and end apart: 3 -> 12, of which waited for: 2 -> 6; matrix products, arithmetic and copies ran while one was open for 0% -> 0% of each run, Pallas kernels for 8% -> 10%
where the time goes in v3:
time: 39.4 us; the launch traced here: 39.2 us
  Pallas kernels  14.6 us (37%)
  starting transfers between devices  12.4 us (31%)
  waiting for transfers between devices  11.4 us (29%)
  between operations  0.73 us (2%)
    ppermute x12, starting transfers between devices, exchange(): return lax.ppermute(value, 'particle', pairs)  12.4 us
    ppermute x12, waiting for transfers between devices, exchange(): return lax.ppermute(value, 'particle', pairs)  11.4 us
    pallas_call x1, Pallas kernels, project_row(): pl.pallas_call(functools.partial(project_kernel, chunk=1024), in_specs=[p...  5.87 us
    pallas_call x1, Pallas kernels, expect(): pl.pallas_call(functools.partial(expect_kernel, slots=slots, chunk=2048),...  3.92 us
    pallas_call x1, Pallas kernels, backproject(): pl.pallas_call(functools.partial(backproject_kernel, slots=slots, chunk=2...  3.4 us
  transfers between devices with their start and end apart: 12, of which 6 were waited for; matrix products, arithmetic and copies ran while one was open for 0% of the time, Pallas kernels for 10%

profile of v3, /device:TPU:0, one launch (start us, length us, event | category | flops | bytes accessed | tf_op | source)
XLA Modules:
  0.0 39.2 jit_solution(17718459727302572706)
XLA Ops:
  0.7 5.9 %project_row.1.refs_0_ = bf16[256,128]{1,0:T(8,128)(2,1)S(1)} custom-call(bf16[2,8,2,32768]{3,2,1,0:T(2,128)(2,1)} %table_hbm.1, s32[1,16384]{1,0:T(1,128)} %index_hbm.1, f32[1,16384]{1,0:T(1,128)} %frac_hbm.1), custom_call_target="tpu_custom_call" | custom-call | tf_op jit(solution)/shard_map/project_row/pallas_call | solution.py:121
  6.6 5.1 %collective-permute-start.2 = (bf16[256,128]{1,0:T(8,128)(2,1)S(1)}, bf16[256,128]{1,0:T(8,128)(2,1)S(1)}, u32[]{:S(2)}, u32[]{:S(2)}) collective-permute-start(bf16[256,128]{1,0:T(8,128)(2,1)S(1)} %project_row.1.refs_0_), channel_id=1, source_target_pairs={{0,12},{1,13},{2,14},{3,15},{4,8},{5,9},{6,10},{7,11},{8,4},{9,5},... | collective-permute-start | bytes 196616 | tf_op jit(solution)/shard_map/ppermute | solution.py:23
  11.7 0.0 collective-permute-start.1
  11.7 0.6 %collective-permute-start = (bf16[256,128]{1,0:T(8,128)(2,1)S(1)}, bf16[256,128]{1,0:T(8,128)(2,1)S(1)}, u32[]{:S(2)}, u32[]{:S(2)}) collective-permute-start(bf16[256,128]{1,0:T(8,128)(2,1)S(1)} %project_row.1.refs_0_), channel_id=1, source_target_pairs={{0,4},{1,5},{2,6},{3,7},{4,0},{5,1},{6,2},{7,3},{8,12},{9,13},{10,... | collective-permute-start | bytes 196616 | tf_op jit(solution)/shard_map/ppermute | solution.py:23
  12.3 0.0 collective-permute-start.3
  12.3 1.9 %collective-permute-done.2.refs_3_ = bf16[256,128]{1,0:T(8,128)(2,1)S(1)} collective-permute-done((bf16[256,128]{1,0:T(8,128)(2,1)S(1)}, bf16[256,128]{1,0:T(8,128)(2,1)S(1)}, u32[]{:S(2)}, u32[]{:S(2)}) %collective-permute-start.2) | collective-permute-done | bytes 65568 | tf_op jit(solution)/shard_map/ppermute | solution.py:23
  14.3 3.0 %collective-permute-done.1.refs_2_ = bf16[256,128]{1,0:T(8,128)(2,1)S(1)} collective-permute-done((bf16[256,128]{1,0:T(8,128)(2,1)S(1)}, bf16[256,128]{1,0:T(8,128)(2,1)S(1)}, u32[]{:S(2)}, u32[]{:S(2)}) %collective-permute-start.1) | collective-permute-done | bytes 65568 | tf_op jit(solution)/shard_map/ppermute | solution.py:23
  17.3 0.5 %collective-permute-start.4 = (bf16[256,128]{1,0:T(8,128)(2,1)S(1)}, bf16[256,128]{1,0:T(8,128)(2,1)S(1)}, u32[]{:S(2)}, u32[]{:S(2)}) collective-permute-start(bf16[256,128]{1,0:T(8,128)(2,1)S(1)} %collective-permute-done.refs_1_), channel_id=1, source_target_pairs={{0,1},{1,0},{2,3},{3,2},{4,5},{5,4},{6,7},{7,6},{8,9},{9,8},{10,11... | collective-permute-start | bytes 196616 | tf_op jit(solution)/shard_map/ppermute | solution.py:23
  17.8 0.1 copy.9.shift_ref
  17.9 0.6 %phase_tables.1 = (f32[8,16384]{1,0:T(8,128)S(1)}, f32[8,16384]{1,0:T(8,128)S(1)}) custom-call(s32[8,2]{1,0:T(8,128)S(1)} %copy.9.shift_ref), custom_call_target="tpu_custom_call" | custom-call | flops 2000000 | bytes 2000000 | tf_op jit(solution)/shard_map/phase_tables/pallas_call | solution.py:178
  18.5 0.0 collective-permute-done.5.refs_6_
  18.5 0.2 collective-permute-done.4.refs_5_
  18.7 3.9 %expect.1 = (bf16[64,32]{1,0:T(8,128)(2,1)S(1)}, f32[256,128]{1,0:T(8,128)S(1)}, bf16[272,128]{1,0:T(8,128)(2,1)S(1)}, f32[8,128]{1,0:T(8,128)S(1)}) custom-call(bf16[32,32768]{1,0:T(8,128)(2,1)S(1)} %copy-done, f32[1,32]{1,0:T(1,128)S(1)} %bitcast.3, s32[1,32]{1,0:T(1,128)S(1)} %bitcast.4, f32[8,16384]{1,0:T(8,128)S(1)} %get-tuple-element.18.cos_ref, ...), custom_call_target="tpu_custom_call" | custom-call | tf_op jit(solution)/shard_map/expect/pallas_call | solution.py:301
  22.6 1.6 %collective-permute-start.7 = (bf16[272,128]{1,0:T(8,128)(2,1)S(1)}, bf16[272,128]{1,0:T(8,128)(2,1)S(1)}, u32[]{:S(2)}, u32[]{:S(2)}) collective-permute-start(bf16[272,128]{1,0:T(8,128)(2,1)S(1)} %get-tuple-element.22), channel_id=1, source_target_pairs={{0,2},{1,3},{2,0},{3,1},{4,6},{5,7},{6,4},{7,5},{8,10},{9,11},{10,... | collective-permute-start | bytes 208904 | tf_op jit(solution)/shard_map/ppermute | solution.py:23
  24.2 3.4 %backproject.1.sums_in = f32[2048,128]{1,0:T(8,128)S(1)} custom-call(bf16[64,32]{1,0:T(8,128)(2,1)S(1)} %get-tuple-element.20.weight_ref, bf16[32,32768]{1,0:T(8,128)(2,1)S(1)} %copy-done, f32[8,16384]{1,0:T(8,128)S(1)} %get-tuple-element.18.cos_ref, f32[8,16384]{1,0:T(8,128)S(1)} %get-tuple-element.19.sin_ref), custom_call_target="tpu_custom_call" | custom-call | flops 20000000 | bytes 20000000 | tf_op jit(solution)/shard_map/backproject/pallas_call | solution.py:340
  27.6 0.1 fold.1
  27.7 0.1 collective-permute-start.8
  27.8 1.5 %collective-permute-done.8.from_core = bf16[1040,128]{1,0:T(8,128)(2,1)S(1)} collective-permute-done((bf16[1040,128]{1,0:T(8,128)(2,1)S(1)}, bf16[1040,128]{1,0:T(8,128)(2,1)S(1)}, u32[]{:S(2)}, u32[]{:S(2)}) %collective-permute-start.8) | collective-permute-done | bytes 266272 | tf_op jit(solution)/shard_map/ppermute | solution.py:23
  29.3 0.1 merge.1
  29.4 2.8 %collective-permute-start.9 = (bf16[272,128]{1,0:T(8,128)(2,1)S(1)}, bf16[272,128]{1,0:T(8,128)(2,1)S(1)}, u32[]{:S(2)}, u32[]{:S(2)}) collective-permute-start(bf16[272,128]{1,0:T(8,128)(2,1)S(1)} %get-tuple-element.29), channel_id=1, source_target_pairs={{0,12},{1,13},{2,14},{3,15},{4,8},{5,9},{6,10},{7,11},{8,4},{9,5},... | collective-permute-start | bytes 208904 | tf_op jit(solution)/shard_map/ppermute | solution.py:23
  32.1 1.7 %collective-permute-start.11 = (bf16[272,128]{1,0:T(8,128)(2,1)S(1)}, bf16[272,128]{1,0:T(8,128)(2,1)S(1)}, u32[]{:S(2)}, u32[]{:S(2)}) collective-permute-start(bf16[272,128]{1,0:T(8,128)(2,1)S(1)} %get-tuple-element.31), channel_id=1, source_target_pairs={{0,4},{1,5},{2,6},{3,7},{4,0},{5,1},{6,2},{7,3},{8,12},{9,13},{10,... | collective-permute-start | bytes 208904 | tf_op jit(solution)/shard_map/ppermute | solution.py:23
  33.8 2.5 %collective-permute-done.9.refs_0_ = bf16[272,128]{1,0:T(8,128)(2,1)S(1)} collective-permute-done((bf16[272,128]{1,0:T(8,128)(2,1)S(1)}, bf16[272,128]{1,0:T(8,128)(2,1)S(1)}, u32[]{:S(2)}, u32[]{:S(2)}) %collective-permute-start.9) | collective-permute-done | bytes 69664 | tf_op jit(solution)/shard_map/ppermute | solution.py:23
  36.3 2.2 %collective-permute-done.10.refs_1_ = bf16[272,128]{1,0:T(8,128)(2,1)S(1)} collective-permute-done((bf16[272,128]{1,0:T(8,128)(2,1)S(1)}, bf16[272,128]{1,0:T(8,128)(2,1)S(1)}, u32[]{:S(2)}, u32[]{:S(2)}) %collective-permute-start.10) | collective-permute-done | bytes 69664 | tf_op jit(solution)/shard_map/ppermute | solution.py:23
  38.5 0.7 %finish.1 = (f32[256,128]{1,0:T(8,128)}, f32[8]{0:T(128)}) custom-call(f32[256,128]{1,0:T(8,128)S(1)} %get-tuple-element.27.own, f32[8,128]{1,0:T(8,128)S(1)} %get-tuple-element.28.mass, bf16[272,128]{1,0:T(8,128)(2,1)S(1)} %collective-permute-done.9.refs_0_, bf16[272,128]{1,0:T(8,128)(2,1)S(1)} %collective-permute-done.10.refs_1_, ...), custom_call_target="tpu_custom_call" | custom-call | tf_op jit(solution)/shard_map/finish/pallas_call | solution.py:433
  (16 shorter events, 0.0 us)
Async XLA Ops:
  0.6 17.2 %copy-start.3 = (s32[8,2]{0,1:T(2,128)S(1)}, s32[8,2]{0,1:T(2,128)}, u32[]{:S(2)}) copy-start(s32[8,2]{0,1:T(2,128)} %param.13) | copy-start | bytes 196
  0.6 18.1 %copy-start = (bf16[32,32768]{1,0:T(8,128)(2,1)S(1)}, bf16[32,32768]{1,0:T(8,128)(2,1)}, u32[]{:S(2)}) copy-start(bf16[32,32768]{1,0:T(8,128)(2,1)} %images.3) | copy-start | bytes 6291460
  0.7 18.0 %copy-start.2 = (s32[32]{0:T(128)S(1)}, s32[32]{0:T(128)}, u32[]{:S(2)}) copy-start(s32[32]{0:T(128)} %param.9) | copy-start | bytes 388
  0.7 18.0 %copy-start.1 = (f32[32]{0:T(128)S(1)}, f32[32]{0:T(128)}, u32[]{:S(2)}) copy-start(f32[32]{0:T(128)} %param.8) | copy-start | bytes 388
  6.6 7.7 %collective-permute-start.2 = (bf16[256,128]{1,0:T(8,128)(2,1)S(1)}, bf16[256,128]{1,0:T(8,128)(2,1)S(1)}, u32[]{:S(2)}, u32[]{:S(2)}) collective-permute-start(bf16[256,128]{1,0:T(8,128)(2,1)S(1)} %project_row.1.refs_0_), channel_id=1, source_target_pairs={{0,12},{1,13},{2,14},{3,15},{4,8},{5,9},{6,10},{7,11},{8,4},{9,5},... | collective-permute-start | bytes 196616 | tf_op jit(solution)/shard_map/ppermute | solution.py:23
  11.7 5.6 %collective-permute-start.1 = (bf16[256,128]{1,0:T(8,128)(2,1)S(1)}, bf16[256,128]{1,0:T(8,128)(2,1)S(1)}, u32[]{:S(2)}, u32[]{:S(2)}) collective-permute-start(bf16[256,128]{1,0:T(8,128)(2,1)S(1)} %project_row.1.refs_0_), channel_id=1, source_target_pairs={{0,8},{1,9},{2,10},{3,11},{4,12},{5,13},{6,14},{7,15},{8,0},{9,1},... | collective-permute-start | bytes 196616 | tf_op jit(solution)/shard_map/ppermute | solution.py:23
  11.7 5.6 %collective-permute-start = (bf16[256,128]{1,0:T(8,128)(2,1)S(1)}, bf16[256,128]{1,0:T(8,128)(2,1)S(1)}, u32[]{:S(2)}, u32[]{:S(2)}) collective-permute-start(bf16[256,128]{1,0:T(8,128)(2,1)S(1)} %project_row.1.refs_0_), channel_id=1, source_target_pairs={{0,4},{1,5},{2,6},{3,7},{4,0},{5,1},{6,2},{7,3},{8,12},{9,13},{10,... | collective-permute-start | bytes 196616 | tf_op jit(solution)/shard_map/ppermute | solution.py:23
  12.3 6.2 %collective-permute-start.3 = (bf16[256,128]{1,0:T(8,128)(2,1)S(1)}, bf16[256,128]{1,0:T(8,128)(2,1)S(1)}, u32[]{:S(2)}, u32[]{:S(2)}) collective-permute-start(bf16[256,128]{1,0:T(8,128)(2,1)S(1)} %project_row.1.refs_0_), channel_id=1, source_target_pairs={{0,1},{1,0},{2,3},{3,2},{4,5},{5,4},{6,7},{7,6},{8,9},{9,8},{10,11... | collective-permute-start | bytes 196616 | tf_op jit(solution)/shard_map/ppermute | solution.py:23
  14.3 4.2 %collective-permute-start.6 = (bf16[256,128]{1,0:T(8,128)(2,1)S(1)}, bf16[256,128]{1,0:T(8,128)(2,1)S(1)}, u32[]{:S(2)}, u32[]{:S(2)}) collective-permute-start(bf16[256,128]{1,0:T(8,128)(2,1)S(1)} %collective-permute-done.2.refs_3_), channel_id=1, source_target_pairs={{0,1},{1,0},{2,3},{3,2},{4,5},{5,4},{6,7},{7,6},{8,9},{9,8},{10,11... | collective-permute-start | bytes 196616 | tf_op jit(solution)/shard_map/ppermute | solution.py:23
  17.3 1.3 %collective-permute-start.5 = (bf16[256,128]{1,0:T(8,128)(2,1)S(1)}, bf16[256,128]{1,0:T(8,128)(2,1)S(1)}, u32[]{:S(2)}, u32[]{:S(2)}) collective-permute-start(bf16[256,128]{1,0:T(8,128)(2,1)S(1)} %collective-permute-done.1.refs_2_), channel_id=1, source_target_pairs={{0,1},{1,0},{2,3},{3,2},{4,5},{5,4},{6,7},{7,6},{8,9},{9,8},{10,11... | collective-permute-start | bytes 196616 | tf_op jit(solution)/shard_map/ppermute | solution.py:23
  17.3 1.4 %collective-permute-start.4 = (bf16[256,128]{1,0:T(8,128)(2,1)S(1)}, bf16[256,128]{1,0:T(8,128)(2,1)S(1)}, u32[]{:S(2)}, u32[]{:S(2)}) collective-permute-start(bf16[256,128]{1,0:T(8,128)(2,1)S(1)} %collective-permute-done.refs_1_), channel_id=1, source_target_pairs={{0,1},{1,0},{2,3},{3,2},{4,5},{5,4},{6,7},{7,6},{8,9},{9,8},{10,11... | collective-permute-start | bytes 196616 | tf_op jit(solution)/shard_map/ppermute | solution.py:23
  22.6 5.0 %collective-permute-start.7 = (bf16[272,128]{1,0:T(8,128)(2,1)S(1)}, bf16[272,128]{1,0:T(8,128)(2,1)S(1)}, u32[]{:S(2)}, u32[]{:S(2)}) collective-permute-start(bf16[272,128]{1,0:T(8,128)(2,1)S(1)} %get-tuple-element.22), channel_id=1, source_target_pairs={{0,2},{1,3},{2,0},{3,1},{4,6},{5,7},{6,4},{7,5},{8,10},{9,11},{10,... | collective-permute-start | bytes 208904 | tf_op jit(solution)/shard_map/ppermute | solution.py:23
  27.7 1.6 %collective-permute-start.8 = (bf16[1040,128]{1,0:T(8,128)(2,1)S(1)}, bf16[1040,128]{1,0:T(8,128)(2,1)S(1)}, u32[]{:S(2)}, u32[]{:S(2)}) collective-permute-start(bf16[1040,128]{1,0:T(8,128)(2,1)S(1)} %get-tuple-element.25), channel_id=1, source_target_pairs={{0,1},{1,0},{2,3},{3,2},{4,5},{5,4},{6,7},{7,6},{8,9},{9,8},{10,11... | collective-permute-start | bytes 798728 | tf_op jit(solution)/shard_map/ppermute | solution.py:23
  29.4 6.9 %collective-permute-start.9 = (bf16[272,128]{1,0:T(8,128)(2,1)S(1)}, bf16[272,128]{1,0:T(8,128)(2,1)S(1)}, u32[]{:S(2)}, u32[]{:S(2)}) collective-permute-start(bf16[272,128]{1,0:T(8,128)(2,1)S(1)} %get-tuple-element.29), channel_id=1, source_target_pairs={{0,12},{1,13},{2,14},{3,15},{4,8},{5,9},{6,10},{7,11},{8,4},{9,5},... | collective-permute-start | bytes 208904 | tf_op jit(solution)/shard_map/ppermute | solution.py:23
  32.1 6.4 %collective-permute-start.10 = (bf16[272,128]{1,0:T(8,128)(2,1)S(1)}, bf16[272,128]{1,0:T(8,128)(2,1)S(1)}, u32[]{:S(2)}, u32[]{:S(2)}) collective-permute-start(bf16[272,128]{1,0:T(8,128)(2,1)S(1)} %get-tuple-element.30), channel_id=1, source_target_pairs={{0,8},{1,9},{2,10},{3,11},{4,12},{5,13},{6,14},{7,15},{8,0},{9,1},... | collective-permute-start | bytes 208904 | tf_op jit(solution)/shard_map/ppermute | solution.py:23
  32.1 6.4 %collective-permute-start.11 = (bf16[272,128]{1,0:T(8,128)(2,1)S(1)}, bf16[272,128]{1,0:T(8,128)(2,1)S(1)}, u32[]{:S(2)}, u32[]{:S(2)}) collective-permute-start(bf16[272,128]{1,0:T(8,128)(2,1)S(1)} %get-tuple-element.31), channel_id=1, source_target_pairs={{0,4},{1,5},{2,6},{3,7},{4,0},{5,1},{6,2},{7,3},{8,12},{9,13},{10,... | collective-permute-start | bytes 208904 | tf_op jit(solution)/shard_map/ppermute | solution.py:23

commit v4 on v3

v4 whole, which is shorter than its diff:
```python
import functools
import math

import jax
import jax.numpy as jnp
from jax import lax
from jax.experimental import pallas as pl
from jax.experimental.pallas import tpu as pltpu
from jax.sharding import PartitionSpec as P

KY = 128
BOX = 256
CLASSES = 8
LOWK = 16
LANES = 128
PRIOR_REWARD = 1.0
MASS_ROWS = 16
BLOCK = 8
LOW_TILES = LOWK * KY // LANES // 2
MIB = 1 << 20


def exchange(value, mask):
    pairs = [(source, source ^ mask) for source in range(lax.axis_size("particle"))]
    return lax.ppermute(value, "particle", pairs)


def in_hbm(value):
    return pltpu.with_memory_space_constraint(value, pltpu.HBM)


def whole_vmem(count):
    return [pl.BlockSpec(memory_space=pltpu.VMEM)] * count


def own_half():
    return lax.axis_index("particle") % 2


def tree_select(values, masks):
    for mask in masks:
        values = [
            jnp.where(mask, values[i + 1], values[i]) if i + 1 < len(values) else values[i]
            for i in range(0, len(values), 2)
        ]
    return values[0]


def project_half(table, index_ref, frac_ref, half, blended):
    pixels = index_ref.shape[1]
    highs = table.shape[1]
    groups = table.shape[0] // 16
    stride = 8 * groups
    chunk = BLOCK * LANES
    blocks = pixels // (2 * chunk)

    def body(step, carry):
        where = pl.ds(pl.multiple_of((2 * step + half) * chunk, chunk), chunk)
        index = index_ref[:, where]
        frac = frac_ref[:, where]
        high = index >> 7
        low = index & (LANES - 1)
        group = (low * 147) >> 10
        first = low - 7 * group
        high_ids = lax.broadcasted_iota(jnp.int32, (highs, chunk), 0)
        one_hot = jnp.where(high_ids == high, 1.0, 0.0).astype(jnp.bfloat16)
        rows = jnp.dot(table[...], one_hot, preferred_element_type=jnp.float32)
        group = jnp.broadcast_to(group, (8, chunk))
        masks = [(group & (1 << bit)) != 0 for bit in range((groups - 1).bit_length())]
        ids = lax.broadcasted_iota(jnp.int32, (8, chunk), 0)
        weight = jnp.where(ids == first, 1.0 - frac, jnp.where(ids == first + 1, frac, 0.0))
        for comp in range(2):
            start = comp * stride
            picked = tree_select([rows[start + 8 * g : start + 8 * g + 8] for g in range(groups)], masks)
            value = jnp.sum(picked * weight, axis=0, keepdims=True)
            for k in range(BLOCK):
                row = (comp * blocks + step) * BLOCK + k
                blended[pl.ds(row, 1), :] = value[:, k * LANES : (k + 1) * LANES]
        return carry

    lax.fori_loop(0, blocks, body, 0, unroll=2)


def project_other_kernel(
    table_hbm, index_hbm, frac_hbm, out_ref, table, index_ref, frac_ref,
    table_in, flat, wide, blended, sems
):
    device = lax.axis_index("particle")
    row_count = lax.axis_size("particle") // 2
    half_set = device // 2 % 2
    class_id = (2 * (device // 4) + device % 2) // (row_count // CLASSES)
    copies = [
        pltpu.make_async_copy(
            table_hbm.at[pl.ds(half_set, 1), pl.ds(class_id, 1)], table_in, sems.at[0]
        ),
        pltpu.make_async_copy(index_hbm, index_ref, sems.at[1]),
        pltpu.make_async_copy(frac_hbm, frac_ref, sems.at[2]),
    ]
    for copy in copies:
        copy.start()
    copies[0].wait()
    highs = flat.shape[1]
    groups = table.shape[0] // 16

    def unfold(step, carry):
        piece = table_in[0, 0, :, pl.ds(step * 8 * LANES, 8 * LANES)].astype(jnp.float32)
        for k in range(8):
            for comp in range(2):
                flat[comp, pl.ds(step * 8 + k, 1), :] = piece[comp : comp + 1, k * LANES : (k + 1) * LANES]
        return carry

    lax.fori_loop(0, highs // 8, unfold, 0, unroll=4)
    picked = []
    for comp in range(2):
        turned = flat[comp].T
        wide[0:LANES, :] = turned
        wide[LANES : LANES + 8, :] = pltpu.roll(turned[0:8], highs - 1, 1)
        picked += [wide[7 * g : 7 * g + 8, :] for g in range(groups)]
    for pair in range(groups):
        table[16 * pair : 16 * (pair + 1), :] = jnp.concatenate(
            picked[2 * pair : 2 * pair + 2], axis=0
        ).astype(jnp.bfloat16)
    copies[1].wait()
    copies[2].wait()
    project_half(table, index_ref, frac_ref, 1 - own_half(), blended)
    out_ref[...] = blended[...].astype(jnp.bfloat16)


def project_other(class_refs, interp_index, interp_frac):
    vox = class_refs.shape[3]
    pixels = interp_index.shape[1]
    highs = vox // LANES
    half_rows = pixels // LANES
    groups = -(-LANES // 7)
    return pl.pallas_call(
        project_other_kernel,
        in_specs=[pl.BlockSpec(memory_space=pltpu.HBM)] * 3,
        out_specs=whole_vmem(4),
        out_shape=[
            jax.ShapeDtypeStruct((half_rows, LANES), jnp.bfloat16),
            jax.ShapeDtypeStruct((16 * groups, highs), jnp.bfloat16),
            jax.ShapeDtypeStruct((1, pixels), jnp.int32),
            jax.ShapeDtypeStruct((1, pixels), jnp.float32),
        ],
        scratch_shapes=[
            pltpu.VMEM((1, 1, 2, vox), jnp.bfloat16),
            pltpu.VMEM((2, highs, LANES), jnp.float32),
            pltpu.VMEM((LANES + 8, highs), jnp.float32),
            pltpu.VMEM((half_rows, LANES), jnp.float32),
            pltpu.SemaphoreType.DMA((3,)),
        ],
        compiler_params=pltpu.CompilerParams(vmem_limit_bytes=16 * MIB),
        name="project_other",
    )(*(in_hbm(value) for value in (class_refs, interp_index, interp_frac)))


def project_own_kernel(
    table, index_ref, frac_ref, images_hbm, out_ref, own_images, other_images, blended, sems
):
    pixels = index_ref.shape[1]
    chunk = BLOCK * LANES
    blocks = pixels // (2 * chunk)
    copies = []
    for target, half in ((other_images, 1 - own_half()), (own_images, own_half())):
        for comp in range(2):
            for step in range(blocks):
                source = pl.multiple_of(comp * pixels + (2 * step + half) * chunk, chunk)
                dest = (comp * blocks + step) * chunk
                copies.append(
                    pltpu.make_async_copy(
                        images_hbm.at[:, pl.ds(source, chunk)],
                        target.at[:, pl.ds(dest, chunk)],
                        sems.at[len(copies)],
                    )
                )
    for copy in copies:
        copy.start()
    project_half(table, index_ref, frac_ref, own_half(), blended)
    out_ref[...] = blended[...].astype(jnp.bfloat16)
    for copy in copies:
        copy.wait()


def project_own(table, index, frac, images):
    parts, width = images.shape
    half_rows = index.shape[1] // LANES
    half_images = jax.ShapeDtypeStruct((parts, width // 2), jnp.bfloat16)
    return pl.pallas_call(
        project_own_kernel,
        in_specs=whole_vmem(3) + [pl.BlockSpec(memory_space=pltpu.HBM)],
        out_specs=whole_vmem(3),
        out_shape=[
            jax.ShapeDtypeStruct((half_rows, LANES), jnp.bfloat16),
            half_images,
            half_images,
        ],
        scratch_shapes=[
            pltpu.VMEM((half_rows, LANES), jnp.float32),
            pltpu.SemaphoreType.DMA((2 * width // (2 * BLOCK * LANES),)),
        ],
        compiler_params=pltpu.CompilerParams(vmem_limit_bytes=16 * MIB),
        cost_estimate=pl.CostEstimate(flops=2000000000, bytes_accessed=8000000, transcendentals=0),
        name="project_own",
    )(table, index, frac, in_hbm(images))


def pair_kernel(own, other, out_ref):
    count = own.shape[0]
    core = own_half()
    out_ref[pl.ds(pl.multiple_of(core * count, count), count), :] = own[...]
    out_ref[pl.ds(pl.multiple_of((1 - core) * count, count), count), :] = other[...]


def pair_rows(own, other):
    return pl.pallas_call(
        pair_kernel,
        in_specs=whole_vmem(2),
        out_specs=pl.BlockSpec(memory_space=pltpu.VMEM),
        out_shape=jax.ShapeDtypeStruct((2 * own.shape[0], LANES), own.dtype),
        compiler_params=pltpu.CompilerParams(vmem_limit_bytes=16 * MIB),
        name="pair_rows",
    )(own, other)


def slot_rows(device, slots):
    ids = lax.broadcasted_iota(jnp.int32, (slots, 1), 0)
    return 2 * ((device // 4) ^ (ids // 2)) + ids % 2


def split_mass(mass_row):
    ids = lax.broadcasted_iota(jnp.int32, (MASS_ROWS, LANES), 0)
    upper = mass_row.astype(jnp.bfloat16).astype(jnp.float32)
    lower = mass_row - upper
    return jnp.where(ids == 0, upper, jnp.where(ids == 1, lower, 0.0)).astype(jnp.bfloat16)


def joined_mass(block):
    return jnp.sum(block.astype(jnp.float32), axis=0, keepdims=True)


def table_kernel(shift_ref, cos_ref, sin_ref):
    shifts, width = cos_ref.shape
    grid_x = shift_ref[:, 0:1]
    grid_y = shift_ref[:, 1:2]
    lane = lax.broadcasted_iota(jnp.int32, (shifts, LANES), 1)
    freq_x = (lane // BLOCK) * (2 * BLOCK) + own_half() * BLOCK + lane % BLOCK
    turn_x = (freq_x * grid_x) & (BOX - 1)
    turn_y = ((lane - KY // 2) * grid_y) & (BOX - 1)
    angle_x = turn_x.astype(jnp.float32) * (2.0 * math.pi / BOX)
    angle_y = turn_y.astype(jnp.float32) * (2.0 * math.pi / BOX)
    cos_x, sin_x = jnp.cos(angle_x), jnp.sin(angle_x)
    cos_y, sin_y = jnp.cos(angle_y), jnp.sin(angle_y)
    for j in range(width // LANES):
        where = slice(j * LANES, (j + 1) * LANES)
        cos_j, sin_j = cos_x[:, j : j + 1], sin_x[:, j : j + 1]
        cos_ref[:, where] = cos_j * cos_y - sin_j * sin_y
        sin_ref[:, where] = sin_j * cos_y + cos_j * sin_y


def phase_tables(shift_grid, width):
    shape = jax.ShapeDtypeStruct((shift_grid.shape[0], width), jnp.float32)
    return pl.pallas_call(
        table_kernel,
        in_specs=whole_vmem(1),
        out_specs=whole_vmem(2),
        out_shape=[shape, shape],
        compiler_params=pltpu.CompilerParams(vmem_limit_bytes=16 * MIB),
        cost_estimate=pl.CostEstimate(flops=2000000, bytes_accessed=2000000, transcendentals=0),
        name="phase_tables",
    )(shift_grid)


def correlate_kernel(own_images, other_images, precision_ref, assigned_ref, cos_ref, sin_ref, *refs, chunk):
    pair_refs, (out_ref, proj) = refs[:-2], refs[-2:]
    shifts = cos_ref.shape[0]
    parts = own_images.shape[0]
    slots = 2 * len(pair_refs)
    width = own_images.shape[1] // 2
    tiles = width // LANES
    per_row = 2 * tiles
    for m, ref in enumerate(pair_refs):
        proj[2 * m * per_row : 2 * (m + 1) * per_row, :] = ref[...].astype(jnp.float32)

    chunk_tiles = chunk // LANES
    contract_lanes = (((1,), (1,)), ((), ()))

    def body(step, carry):
        total, power = carry
        first = step * chunk_tiles
        real = jnp.concatenate(
            [proj[pl.ds(first + k, slots, stride=per_row), :] for k in range(chunk_tiles)], axis=1
        )
        imag = jnp.concatenate(
            [proj[pl.ds(tiles + first + k, slots, stride=per_row), :] for k in range(chunk_tiles)],
            axis=1,
        )
        where = pl.ds(pl.multiple_of(step * chunk, chunk), chunk)
        imag_where = pl.ds(pl.multiple_of(width + step * chunk, chunk), chunk)
        reals, imags = [], []
        for s in range(shifts):
            cos_s, sin_s = cos_ref[s : s + 1, where], sin_ref[s : s + 1, where]
            reals.append(real * cos_s - imag * sin_s)
            imags.append(real * sin_s + imag * cos_s)
        turned_real = jnp.concatenate(reals, axis=0).astype(jnp.bfloat16)
        turned_imag = jnp.concatenate(imags, axis=0).astype(jnp.bfloat16)
        image_real = jnp.concatenate([own_images[:, where], other_images[:, where]], axis=0)
        image_imag = jnp.concatenate([own_images[:, imag_where], other_images[:, imag_where]], axis=0)
        total = total + lax.dot_general(
            turned_real, image_real, contract_lanes, preferred_element_type=jnp.float32
        )
        total = total + lax.dot_general(
            turned_imag, image_imag, contract_lanes, preferred_element_type=jnp.float32
        )
        squares = real * real + imag * imag
        for k in range(chunk_tiles):
            power = power + squares[:, k * LANES : (k + 1) * LANES]
        return total, power

    total, power = lax.fori_loop(
        0,
        width // chunk,
        body,
        (
            jnp.zeros((shifts * slots, 2 * parts), jnp.float32),
            jnp.zeros((slots, LANES), jnp.float32),
        ),
    )
    combos = shifts * slots
    out_ref[...] = jnp.zeros_like(out_ref)
    out_ref[0:combos, 0 : 2 * parts] = total
    out_ref[combos : combos + slots, :] = jnp.broadcast_to(
        jnp.sum(power, axis=1, keepdims=True), (slots, LANES)
    )
    out_ref[combos + slots : combos + slots + 1, 0:parts] = precision_ref[...]
    out_ref[combos + slots + 1 : combos + slots + 2, 0:parts] = assigned_ref[...].astype(jnp.float32)


def correlate(own_images, other_images, precision, assigned, cos_table, sin_table, pairs):
    slots = 2 * len(pairs)
    shifts, width = cos_table.shape
    return pl.pallas_call(
        functools.partial(correlate_kernel, chunk=2048),
        in_specs=whole_vmem(6 + len(pairs)),
        out_specs=pl.BlockSpec(memory_space=pltpu.VMEM),
        out_shape=jax.ShapeDtypeStruct((shifts * slots + slots + 8, LANES), jnp.float32),
        scratch_shapes=[pltpu.VMEM((slots * 2 * width // LANES, LANES), jnp.float32)],
        compiler_params=pltpu.CompilerParams(vmem_limit_bytes=(14 + slots // 2) * MIB),
        name="correlate",
    )(own_images, other_images, precision, assigned, cos_table, sin_table, *pairs)


def rotate_back(weights, own_images, other_images, cos_ref, sin_ref, where, imag_where, slots):
    image_real = jnp.concatenate([own_images[:, where], other_images[:, where]], axis=0)
    image_imag = jnp.concatenate([own_images[:, imag_where], other_images[:, imag_where]], axis=0)
    from_real = jnp.dot(weights, image_real, preferred_element_type=jnp.float32)
    from_imag = jnp.dot(weights, image_imag, preferred_element_type=jnp.float32)
    real = imag = None
    for s in range(cos_ref.shape[0]):
        cos_s, sin_s = cos_ref[s : s + 1, where], sin_ref[s : s + 1, where]
        part_real = from_real[s * slots : (s + 1) * slots]
        part_imag = from_imag[s * slots : (s + 1) * slots]
        real_s = part_real * cos_s + part_imag * sin_s
        imag_s = part_imag * cos_s - part_real * sin_s
        real = real_s if real is None else real + real_s
        imag = imag_s if imag is None else imag + imag_s
    return real, imag


def posterior_kernel(
    mine, received, own_images, other_images, cos_ref, sin_ref,
    weight_ref, low_ref, low_send, own_mass, *, slots
):
    device = lax.axis_index("particle")
    shifts, width = cos_ref.shape
    parts = own_images.shape[0]
    combos = shifts * slots
    theirs = received[...]
    lane = lax.broadcasted_iota(jnp.int32, theirs.shape, 1)
    swapped = jnp.where(
        lane < parts, pltpu.roll(theirs, LANES - parts, 1), pltpu.roll(theirs, parts, 1)
    )
    joint = mine[...] + swapped
    power = mine[combos : combos + slots, :] + received[combos : combos + slots, :]
    precision = joint[combos + slots : combos + slots + 1]
    assigned = joint[combos + slots + 1 : combos + slots + 2].astype(jnp.int32)
    slot_class = slot_rows(device, slots) // (slots // CLASSES)
    match = (slot_class == assigned).astype(jnp.float32) * PRIOR_REWARD
    likelihood_scale = 1.0 / math.sqrt(4 * width)
    logits = [
        precision * (joint[s * slots : (s + 1) * slots] - 0.5 * power) * likelihood_scale + match
        for s in range(shifts)
    ]
    peak = functools.reduce(jnp.maximum, logits)
    peak = jnp.max(peak, axis=0, keepdims=True)
    terms = [jnp.exp(value - peak) for value in logits]
    mass = functools.reduce(jnp.add, terms)
    norm = jnp.sum(mass, axis=0, keepdims=True)
    weights = jnp.concatenate([term / norm for term in terms], axis=0)
    weights = weights[:, 0 : 2 * parts].astype(jnp.bfloat16)
    weight_ref[...] = weights
    counted = lax.broadcasted_iota(jnp.int32, (1, LANES), 1) < 2 * parts
    share = jnp.where(counted, mass / norm * precision, 0.0)
    slot_mass = jnp.sum(share, axis=1, keepdims=True)
    class_lane = lax.broadcasted_iota(jnp.int32, (slots, LANES), 1)
    mass_row = jnp.sum(
        jnp.where(class_lane == slot_class, slot_mass, 0.0), axis=0, keepdims=True
    )
    own_mass[...] = jnp.broadcast_to(mass_row, own_mass.shape)

    low = LOW_TILES * LANES
    real, imag = rotate_back(
        weights, own_images, other_images, cos_ref, sin_ref, slice(0, low), slice(width, width + low), slots
    )
    for k in range(LOW_TILES):
        piece = slice(k * LANES, (k + 1) * LANES)
        low_ref[pl.ds(k, slots, stride=2 * LOW_TILES), :] = real[:, piece]
        low_ref[pl.ds(LOW_TILES + k, slots, stride=2 * LOW_TILES), :] = imag[:, piece]
    low_body = low_ref.shape[0]
    low_send[0:low_body, :] = low_ref[...].astype(jnp.bfloat16)
    low_send[low_body:, :] = split_mass(mass_row)


def posterior(mine, received, own_images, other_images, cos_table, sin_table, slots):
    shifts = cos_table.shape[0]
    low = slots * 2 * LOW_TILES
    return pl.pallas_call(
        functools.partial(posterior_kernel, slots=slots),
        in_specs=whole_vmem(6),
        out_specs=whole_vmem(4),
        out_shape=[
            jax.ShapeDtypeStruct((shifts * slots, 2 * own_images.shape[0]), jnp.bfloat16),
            jax.ShapeDtypeStruct((low, LANES), jnp.float32),
            jax.ShapeDtypeStruct((low + MASS_ROWS, LANES), jnp.bfloat16),
            jax.ShapeDtypeStruct((8, LANES), jnp.float32),
        ],
        compiler_params=pltpu.CompilerParams(vmem_limit_bytes=(14 + slots // 2) * MIB),
        name="posterior",
    )(mine, received, own_images, other_images, cos_table, sin_table)


def backproject_kernel(weight_ref, own_images, other_images, cos_ref, sin_ref, sums, *, slots, chunk):
    width = cos_ref.shape[1]
    tiles = width // LANES
    per_row = 2 * tiles
    chunk_tiles = chunk // LANES
    weights = weight_ref[...]

    def body(step, carry):
        first = LOW_TILES + step * chunk_tiles
        start = pl.multiple_of(first * LANES, LOW_TILES * LANES)
        where = pl.ds(start, chunk)
        imag_where = pl.ds(pl.multiple_of(width + start, LOW_TILES * LANES), chunk)
        real, imag = rotate_back(
            weights, own_images, other_images, cos_ref, sin_ref, where, imag_where, slots
        )
        for k in range(chunk_tiles):
            piece = slice(k * LANES, (k + 1) * LANES)
            sums[pl.ds(first + k, slots, stride=per_row), :] = real[:, piece]
            sums[pl.ds(tiles + first + k, slots, stride=per_row), :] = imag[:, piece]
        return carry

    lax.fori_loop(0, (tiles - LOW_TILES) // chunk_tiles, body, 0)


def backproject(weights, own_images, other_images, cos_table, sin_table, slots):
    width = cos_table.shape[1]
    rows = slots * 2 * width // LANES
    return pl.pallas_call(
        functools.partial(backproject_kernel, slots=slots, chunk=LOW_TILES * LANES),
        in_specs=whole_vmem(5),
        out_specs=pl.BlockSpec(memory_space=pltpu.VMEM),
        out_shape=jax.ShapeDtypeStruct((rows, LANES), jnp.float32),
        compiler_params=pltpu.CompilerParams(vmem_limit_bytes=(14 + slots // 2) * MIB),
        cost_estimate=pl.CostEstimate(flops=20000000, bytes_accessed=20000000, transcendentals=0),
        name="backproject",
    )(weights, own_images, other_images, cos_table, sin_table)


def fold_kernel(sums, low_ref, low_received, mass, own, own_mass, *sends, slots):
    per_row = sums.shape[0] // slots
    tiles = per_row // 2
    low_body = low_ref.shape[0]
    total_mass = mass[0:1, :] + joined_mass(low_received[low_body:, :])
    block = split_mass(total_mass)
    own_mass[...] = jnp.broadcast_to(total_mass, own_mass.shape)
    for slot in range(slots):
        target = own if slot < 2 else sends[slot // 2 - 1]
        for comp in range(2):
            low = slice((2 * slot + comp) * LOW_TILES, (2 * slot + comp + 1) * LOW_TILES)
            start = slot * per_row + comp * tiles
            dest = (slot % 2) * per_row + comp * tiles
            value = (low_ref[low, :] + low_received[low, :].astype(jnp.float32)) * 0.5
            value = jnp.concatenate([value, sums[start + LOW_TILES : start + tiles, :]], axis=0)
            target[dest : dest + tiles, :] = value.astype(target.dtype)
    for send in sends:
        send[2 * per_row :, :] = block


def fold(sums, low, low_received, mass, slots):
    rows = 2 * sums.shape[0] // slots
    chips = slots // 2
    return pl.pallas_call(
        functools.partial(fold_kernel, slots=slots),
        in_specs=whole_vmem(4),
        out_specs=whole_vmem(1 + chips),
        out_shape=[
            jax.ShapeDtypeStruct((rows, LANES), jnp.float32),
            jax.ShapeDtypeStruct((8, LANES), jnp.float32),
        ]
        + [jax.ShapeDtypeStruct((rows + MASS_ROWS, LANES), jnp.bfloat16)] * (chips - 1),
        compiler_params=pltpu.CompilerParams(vmem_limit_bytes=(10 + slots // 2) * MIB),
        name="fold",
    )(sums, low, low_received, mass)


def merge_kernel(own, mass, *refs, mass_scale):
    received, (keep, send, mass_out) = refs[:-3], refs[-3:]
    rows = own.shape[0]
    half = rows // 2
    core = own_half()
    total_mass = mass[0:1, :]
    for ref in received:
        total_mass = total_mass + joined_mass(ref[rows:, :])
    for target, place in ((send, 1 - core), (keep, core)):
        where = pl.ds(pl.multiple_of(place * half, half), half)
        total = own[where, :]
        for ref in received:
            total = total + ref[where, :].astype(jnp.float32)
        target[...] = total.astype(target.dtype)
    mass_out[...] = total_mass[0, :CLASSES] * mass_scale


def merge(own, mass, received, mass_scale):
    rows = own.shape[0] // 2
    return pl.pallas_call(
        functools.partial(merge_kernel, mass_scale=mass_scale),
        in_specs=whole_vmem(2 + len(received)),
        out_specs=whole_vmem(3),
        out_shape=[
            jax.ShapeDtypeStruct((rows, LANES), jnp.float32),
            jax.ShapeDtypeStruct((rows, LANES), jnp.bfloat16),
            jax.ShapeDtypeStruct((CLASSES,), jnp.float32),
        ],
        compiler_params=pltpu.CompilerParams(vmem_limit_bytes=16 * MIB),
        name="merge",
    )(own, mass, *received)


def finish_kernel(own, received, out, *, scale):
    half = own_half()
    for step in range(own.shape[0] // BLOCK):
        rows = slice(step * BLOCK, (step + 1) * BLOCK)
        own_rows = pl.ds(pl.multiple_of((2 * step + half) * BLOCK, BLOCK), BLOCK)
        other_rows = pl.ds(pl.multiple_of((2 * step + 1 - half) * BLOCK, BLOCK), BLOCK)
        out[own_rows, :] = own[rows, :] * scale
        out[other_rows, :] = received[rows, :].astype(jnp.float32) * scale


def finish(own, received, scale):
    return pl.pallas_call(
        functools.partial(finish_kernel, scale=scale),
        in_specs=whole_vmem(2),
        out_specs=pl.BlockSpec(memory_space=pltpu.VMEM),
        out_shape=jax.ShapeDtypeStruct((2 * own.shape[0], LANES), jnp.float32),
        compiler_params=pltpu.CompilerParams(vmem_limit_bytes=16 * MIB),
        name="finish",
    )(own, received)


def local(
    images, noise_precision, assigned_class, class_refs, interp_index, interp_frac, shift_grid
):
    dev_count = lax.axis_size("particle")
    slots = dev_count // 2
    chips = slots // 2
    parts, width = images.shape
    other_half, table, index, frac = project_other(class_refs, interp_index, interp_frac)
    from_core = exchange(other_half, 1)
    own, own_images, other_images = project_own(table, index, frac, images)
    pair = pair_rows(own, from_core)
    pairs = [pair] + [exchange(pair, 4 * m) for m in range(1, chips)]
    images_received = exchange(other_images, 1)
    cos_table, sin_table = phase_tables(shift_grid, width // 4)
    mine = correlate(
        own_images,
        images_received,
        noise_precision.reshape(1, parts),
        assigned_class.reshape(1, parts),
        cos_table,
        sin_table,
        pairs,
    )
    weights, low, low_send, mass = posterior(
        mine, exchange(mine, 1), own_images, images_received, cos_table, sin_table, slots
    )
    low_received = exchange(low_send, 2)
    sums = backproject(weights, own_images, images_received, cos_table, sin_table, slots)
    folded = fold(sums, low, low_received, mass, slots)
    sends = folded[2:]
    received = [exchange(sends[m - 1], 4 * m) for m in range(chips - 1, 0, -1)]
    keep, send, class_mass = merge(
        folded[0], folded[1], received, CLASSES / (parts * dev_count)
    )
    back = finish(keep, exchange(send, 1), 1.0 / math.sqrt(parts))
    return back.reshape(1, width), class_mass


def solution(mesh):
    in_specs = (
        P(("groups", "particle"), None),
        P(("groups", "particle")),
        P(("groups", "particle")),
        P("groups", None, None, None),
        P("particle", None),
        P("particle", None),
        P(),
    )
    out_specs = (P(("groups", "particle"), None), P("groups"))
    return jax.shard_map(local, mesh=mesh, in_specs=in_specs, out_specs=out_specs, check_vma=False)
```

time: 39.4 us -> 40.7 us (1.033)
  waiting for transfers between devices: 11.4 us -> 15.5 us
  Pallas kernels: 14.6 us -> 11.9 us
    ppermute x12 -> x11, waiting for transfers between devices: 11.4 us -> 15.5 us  [exchange(): return lax.ppermute(value, 'particle', pairs)]
    pallas_call x5 -> x8, Pallas kernels: 14 us -> 11.5 us  [the longest x1 3.56 us: project_other(): pl.pallas_call(project_other_kernel, in_specs=[pl.BlockSpec(memory_space=...]
    ppermute x12 -> x11, starting transfers between devices: 12.4 us -> 12.3 us  [exchange(): return lax.ppermute(value, 'particle', pairs)]
  transfers between devices with their start and end apart: 12 -> 11, of which waited for: 6 -> 8; matrix products, arithmetic and copies ran while one was open for 0% -> 0% of each run, Pallas kernels for 10% -> 6%
where the time goes in v4:
time: 40.7 us; the launch traced here: 40.5 us
  waiting for transfers between devices  15.5 us (38%)
  starting transfers between devices  12.3 us (30%)
  Pallas kernels  11.9 us (29%)
  between operations  0.73 us (2%)
    ppermute x11, waiting for transfers between devices, exchange(): return lax.ppermute(value, 'particle', pairs)  15.5 us
    ppermute x11, starting transfers between devices, exchange(): return lax.ppermute(value, 'particle', pairs)  12.3 us
    pallas_call x1, Pallas kernels, project_other(): pl.pallas_call(project_other_kernel, in_specs=[pl.BlockSpec(memory_space=...  3.56 us
    pallas_call x1, Pallas kernels, project_own(): pl.pallas_call(project_own_kernel, in_specs=whole_vmem(3) + [pl.BlockSpec...  2.61 us
    pallas_call x1, Pallas kernels, backproject(): pl.pallas_call(functools.partial(backproject_kernel, slots=slots, chunk=L...  2.02 us
    pallas_call x1, Pallas kernels, correlate(): pl.pallas_call(functools.partial(correlate_kernel, chunk=2048), in_specs=...  1.72 us
  transfers between devices with their start and end apart: 11, of which 8 were waited for; matrix products, arithmetic and copies ran while one was open for 0% of the time, Pallas kernels for 6%

profile of v4, /device:TPU:0, one launch (start us, length us, event | category | flops | bytes accessed | tf_op | source)
XLA Modules:
  0.0 40.5 jit_solution(2578168661423268941)
XLA Ops:
  0.6 3.6 %project_other.1 = (bf16[128,128]{1,0:T(8,128)(2,1)S(1)}, bf16[304,256]{1,0:T(8,128)(2,1)S(1)}, s32[1,16384]{1,0:T(1,128)S(1)}, f32[1,16384]{1,0:T(1,128)S(1)}) custom-call(bf16[2,8,2,32768]{3,2,1,0:T(2,128)(2,1)} %table_hbm.1, s32[1,16384]{1,0:T(1,128)} %index_hbm.1, f32[1,16384]{1,0:T(1,128)} %frac_hbm.1), custom_call_target="tpu_custom_call" | custom-call | tf_op jit(solution)/shard_map/project_other/pallas_call | solution.py:135
  4.2 2.6 %project_own.1 = (bf16[128,128]{1,0:T(8,128)(2,1)S(1)}, bf16[32,16384]{1,0:T(8,128)(2,1)S(1)}, bf16[32,16384]{1,0:T(8,128)(2,1)S(1)}) custom-call(bf16[304,256]{1,0:T(8,128)(2,1)S(1)} %get-tuple-element.23.table, s32[1,16384]{1,0:T(1,128)S(1)} %get-tuple-element.24.index_ref, f32[1,16384]{1,0:T(1,128)S(1)} %get-tuple-element.25.frac_ref, ...), custom_call_target="tpu_custom_call" | custom-call | flops 2000000000 | bytes 8000000 | tf_op jit(solution)/shard_map/project_own/pallas_call | solution.py:188
  6.9 0.5 %collective-permute-start = (bf16[32,16384]{1,0:T(8,128)(2,1)S(1)}, bf16[32,16384]{1,0:T(8,128)(2,1)S(1)}, u32[]{:S(2)}, u32[]{:S(2)}) collective-permute-start(bf16[32,16384]{1,0:T(8,128)(2,1)S(1)} %get-tuple-element.27), channel_id=1, source_target_pairs={{0,1},{1,0},{2,3},{3,2},{4,5},{5,4},{6,7},{7,6},{8,9},{9,8},{10,11... | collective-permute-start | bytes 3145736 | tf_op jit(solution)/shard_map/ppermute | solution.py:25
  7.4 2.3 %collective-permute-done.1.other = bf16[128,128]{1,0:T(8,128)(2,1)S(1)} collective-permute-done((bf16[128,128]{1,0:T(8,128)(2,1)S(1)}, bf16[128,128]{1,0:T(8,128)(2,1)S(1)}, u32[]{:S(2)}, u32[]{:S(2)}) %collective-permute-start.1) | collective-permute-done | bytes 32800 | tf_op jit(solution)/shard_map/ppermute | solution.py:25
  9.7 3.0 %collective-permute-start.2 = (bf16[256,128]{1,0:T(8,128)(2,1)S(1)}, bf16[256,128]{1,0:T(8,128)(2,1)S(1)}, u32[]{:S(2)}, u32[]{:S(2)}) collective-permute-start(bf16[256,128]{1,0:T(8,128)(2,1)S(1)} %pair_rows.1.refs_0_), channel_id=1, source_target_pairs={{0,4},{1,5},{2,6},{3,7},{4,0},{5,1},{6,2},{7,3},{8,12},{9,13},{10,... | collective-permute-start | bytes 196616 | tf_op jit(solution)/shard_map/ppermute | solution.py:25
  12.7 2.6 %collective-permute-start.3 = (bf16[256,128]{1,0:T(8,128)(2,1)S(1)}, bf16[256,128]{1,0:T(8,128)(2,1)S(1)}, u32[]{:S(2)}, u32[]{:S(2)}) collective-permute-start(bf16[256,128]{1,0:T(8,128)(2,1)S(1)} %pair_rows.1.refs_0_), channel_id=1, source_target_pairs={{0,8},{1,9},{2,10},{3,11},{4,12},{5,13},{6,14},{7,15},{8,0},{9,1},... | collective-permute-start | bytes 196616 | tf_op jit(solution)/shard_map/ppermute | solution.py:25
  15.3 0.1 copy.9.shift_ref
  15.4 0.4 phase_tables.1
  15.8 4.4 %collective-permute-done.3.refs_2_ = bf16[256,128]{1,0:T(8,128)(2,1)S(1)} collective-permute-done((bf16[256,128]{1,0:T(8,128)(2,1)S(1)}, bf16[256,128]{1,0:T(8,128)(2,1)S(1)}, u32[]{:S(2)}, u32[]{:S(2)}) %collective-permute-start.3) | collective-permute-done | bytes 65568 | tf_op jit(solution)/shard_map/ppermute | solution.py:25
  20.3 1.2 %collective-permute-done.4.refs_3_ = bf16[256,128]{1,0:T(8,128)(2,1)S(1)} collective-permute-done((bf16[256,128]{1,0:T(8,128)(2,1)S(1)}, bf16[256,128]{1,0:T(8,128)(2,1)S(1)}, u32[]{:S(2)}, u32[]{:S(2)}) %collective-permute-start.4) | collective-permute-done | bytes 65568 | tf_op jit(solution)/shard_map/ppermute | solution.py:25
  21.5 1.7 %correlate.1.mine = f32[80,128]{1,0:T(8,128)S(1)} custom-call(bf16[32,16384]{1,0:T(8,128)(2,1)S(1)} %get-tuple-element.26.own_images, bf16[32,16384]{1,0:T(8,128)(2,1)S(1)} %collective-permute-done.other_images, f32[1,32]{1,0:T(1,128)S(1)} %bitcast.3, s32[1,32]{1,0:T(1,128)S(1)} %bitcast.4, f32[8,8192]{1,0:T(8,128)S(1)} %get-tuple-element.28.cos_ref, ...), custom_call_target="tpu_custom_call" | custom-call | tf_op jit(solution)/shard_map/correlate/pallas_call | solution.py:341
  23.3 1.2 %collective-permute-done.5.received = f32[80,128]{1,0:T(8,128)S(1)} collective-permute-done((f32[80,128]{1,0:T(8,128)S(1)}, f32[80,128]{1,0:T(8,128)S(1)}, u32[]{:S(2)}, u32[]{:S(2)}) %collective-permute-start.5) | collective-permute-done | bytes 40992 | tf_op jit(solution)/shard_map/ppermute | solution.py:25
  24.5 0.4 posterior.1
  24.9 1.6 %collective-permute-start.6 = (bf16[144,128]{1,0:T(8,128)(2,1)S(1)}, bf16[144,128]{1,0:T(8,128)(2,1)S(1)}, u32[]{:S(2)}, u32[]{:S(2)}) collective-permute-start(bf16[144,128]{1,0:T(8,128)(2,1)S(1)} %get-tuple-element.34), channel_id=1, source_target_pairs={{0,2},{1,3},{2,0},{3,1},{4,6},{5,7},{6,4},{7,5},{8,10},{9,11},{10,... | collective-permute-start | bytes 110600 | tf_op jit(solution)/shard_map/ppermute | solution.py:25
  26.5 2.0 %backproject.1.sums = f32[1024,128]{1,0:T(8,128)S(1)} custom-call(bf16[64,64]{1,0:T(8,128)(2,1)S(1)} %get-tuple-element.32.weight_ref, bf16[32,16384]{1,0:T(8,128)(2,1)S(1)} %get-tuple-element.26.own_images, bf16[32,16384]{1,0:T(8,128)(2,1)S(1)} %collective-permute-done.other_images, f32[8,8192]{1,0:T(8,128)S(1)} %get-tuple-element.28.cos_ref, ...), custom_call_target="tpu_custom_call" | custom-call | flops 20000000 | bytes 20000000 | tf_op jit(solution)/shard_map/backproject/pallas_call | solution.py:468
  28.5 0.4 %collective-permute-done.6.low_received = bf16[144,128]{1,0:T(8,128)(2,1)S(1)} collective-permute-done((bf16[144,128]{1,0:T(8,128)(2,1)S(1)}, bf16[144,128]{1,0:T(8,128)(2,1)S(1)}, u32[]{:S(2)}, u32[]{:S(2)}) %collective-permute-start.6) | collective-permute-done | bytes 36896 | tf_op jit(solution)/shard_map/ppermute | solution.py:25
  29.0 2.0 %collective-permute-start.7 = (bf16[272,128]{1,0:T(8,128)(2,1)S(1)}, bf16[272,128]{1,0:T(8,128)(2,1)S(1)}, u32[]{:S(2)}, u32[]{:S(2)}) collective-permute-start(bf16[272,128]{1,0:T(8,128)(2,1)S(1)} %get-tuple-element.38), channel_id=1, source_target_pairs={{0,12},{1,13},{2,14},{3,15},{4,8},{5,9},{6,10},{7,11},{8,4},{9,5},... | collective-permute-start | bytes 208904 | tf_op jit(solution)/shard_map/ppermute | solution.py:25
  31.0 0.3 collective-permute-start.8
  31.3 2.1 %collective-permute-start.9 = (bf16[272,128]{1,0:T(8,128)(2,1)S(1)}, bf16[272,128]{1,0:T(8,128)(2,1)S(1)}, u32[]{:S(2)}, u32[]{:S(2)}) collective-permute-start(bf16[272,128]{1,0:T(8,128)(2,1)S(1)} %get-tuple-element.40), channel_id=1, source_target_pairs={{0,4},{1,5},{2,6},{3,7},{4,0},{5,1},{6,2},{7,3},{8,12},{9,13},{10,... | collective-permute-start | bytes 208904 | tf_op jit(solution)/shard_map/ppermute | solution.py:25
  33.4 2.1 %collective-permute-done.7.refs_0_ = bf16[272,128]{1,0:T(8,128)(2,1)S(1)} collective-permute-done((bf16[272,128]{1,0:T(8,128)(2,1)S(1)}, bf16[272,128]{1,0:T(8,128)(2,1)S(1)}, u32[]{:S(2)}, u32[]{:S(2)}) %collective-permute-start.7) | collective-permute-done | bytes 69664 | tf_op jit(solution)/shard_map/ppermute | solution.py:25
  35.6 2.5 %collective-permute-done.8.refs_1_ = bf16[272,128]{1,0:T(8,128)(2,1)S(1)} collective-permute-done((bf16[272,128]{1,0:T(8,128)(2,1)S(1)}, bf16[272,128]{1,0:T(8,128)(2,1)S(1)}, u32[]{:S(2)}, u32[]{:S(2)}) %collective-permute-start.8) | collective-permute-done | bytes 69664 | tf_op jit(solution)/shard_map/ppermute | solution.py:25
  38.1 0.5 %merge.1 = (f32[128,128]{1,0:T(8,128)S(1)}, bf16[128,128]{1,0:T(8,128)(2,1)S(1)}, f32[8]{0:T(128)}) custom-call(f32[256,128]{1,0:T(8,128)S(1)} %get-tuple-element.36.own, f32[8,128]{1,0:T(8,128)S(1)} %get-tuple-element.37.mass, bf16[272,128]{1,0:T(8,128)(2,1)S(1)} %collective-permute-done.7.refs_0_, bf16[272,128]{1,0:T(8,128)(2,1)S(1)} %collective-permute-done.8.refs_1_, ...), custom_call_target="tpu_custom_call" | custom-call | tf_op jit(solution)/shard_map/merge/pallas_call | solution.py:535
  38.6 1.2 %collective-permute-done.10.received = bf16[128,128]{1,0:T(8,128)(2,1)S(1)} collective-permute-done((bf16[128,128]{1,0:T(8,128)(2,1)S(1)}, bf16[128,128]{1,0:T(8,128)(2,1)S(1)}, u32[]{:S(2)}, u32[]{:S(2)}) %collective-permute-start.10) | collective-permute-done | bytes 32800 | tf_op jit(solution)/shard_map/ppermute | solution.py:25
  39.8 0.7 %finish.1 = f32[256,128]{1,0:T(8,128)} custom-call(f32[128,128]{1,0:T(8,128)S(1)} %get-tuple-element.41.own, bf16[128,128]{1,0:T(8,128)(2,1)S(1)} %collective-permute-done.10.received), custom_call_target="tpu_custom_call" | custom-call | tf_op jit(solution)/shard_map/finish/pallas_call | solution.py:560
  (15 shorter events, 0.2 us)
Async XLA Ops:
  4.2 11.1 %copy-start.2 = (s32[8,2]{0,1:T(2,128)S(1)}, s32[8,2]{0,1:T(2,128)}, u32[]{:S(2)}) copy-start(s32[8,2]{0,1:T(2,128)} %param.13) | copy-start | bytes 196
  4.2 17.3 %copy-start = (f32[32]{0:T(128)S(1)}, f32[32]{0:T(128)}, u32[]{:S(2)}) copy-start(f32[32]{0:T(128)} %param.8) | copy-start | bytes 388
  4.2 17.3 %copy-start.1 = (s32[32]{0:T(128)S(1)}, s32[32]{0:T(128)}, u32[]{:S(2)}) copy-start(s32[32]{0:T(128)} %param.9) | copy-start | bytes 388
  6.9 14.6 %collective-permute-start = (bf16[32,16384]{1,0:T(8,128)(2,1)S(1)}, bf16[32,16384]{1,0:T(8,128)(2,1)S(1)}, u32[]{:S(2)}, u32[]{:S(2)}) collective-permute-start(bf16[32,16384]{1,0:T(8,128)(2,1)S(1)} %get-tuple-element.27), channel_id=1, source_target_pairs={{0,1},{1,0},{2,3},{3,2},{4,5},{5,4},{6,7},{7,6},{8,9},{9,8},{10,11... | collective-permute-start | bytes 3145736 | tf_op jit(solution)/shard_map/ppermute | solution.py:25
  7.4 2.3 %collective-permute-start.1 = (bf16[128,128]{1,0:T(8,128)(2,1)S(1)}, bf16[128,128]{1,0:T(8,128)(2,1)S(1)}, u32[]{:S(2)}, u32[]{:S(2)}) collective-permute-start(bf16[128,128]{1,0:T(8,128)(2,1)S(1)} %get-tuple-element.31), channel_id=1, source_target_pairs={{0,1},{1,0},{2,3},{3,2},{4,5},{5,4},{6,7},{7,6},{8,9},{9,8},{10,11... | collective-permute-start | bytes 98312 | tf_op jit(solution)/shard_map/ppermute | solution.py:25
  9.7 6.1 %collective-permute-start.2 = (bf16[256,128]{1,0:T(8,128)(2,1)S(1)}, bf16[256,128]{1,0:T(8,128)(2,1)S(1)}, u32[]{:S(2)}, u32[]{:S(2)}) collective-permute-start(bf16[256,128]{1,0:T(8,128)(2,1)S(1)} %pair_rows.1.refs_0_), channel_id=1, source_target_pairs={{0,4},{1,5},{2,6},{3,7},{4,0},{5,1},{6,2},{7,3},{8,12},{9,13},{10,... | collective-permute-start | bytes 196616 | tf_op jit(solution)/shard_map/ppermute | solution.py:25
  12.7 7.5 %collective-permute-start.3 = (bf16[256,128]{1,0:T(8,128)(2,1)S(1)}, bf16[256,128]{1,0:T(8,128)(2,1)S(1)}, u32[]{:S(2)}, u32[]{:S(2)}) collective-permute-start(bf16[256,128]{1,0:T(8,128)(2,1)S(1)} %pair_rows.1.refs_0_), channel_id=1, source_target_pairs={{0,8},{1,9},{2,10},{3,11},{4,12},{5,13},{6,14},{7,15},{8,0},{9,1},... | collective-permute-start | bytes 196616 | tf_op jit(solution)/shard_map/ppermute | solution.py:25
  15.3 6.2 %collective-permute-start.4 = (bf16[256,128]{1,0:T(8,128)(2,1)S(1)}, bf16[256,128]{1,0:T(8,128)(2,1)S(1)}, u32[]{:S(2)}, u32[]{:S(2)}) collective-permute-start(bf16[256,128]{1,0:T(8,128)(2,1)S(1)} %pair_rows.1.refs_0_), channel_id=1, source_target_pairs={{0,12},{1,13},{2,14},{3,15},{4,8},{5,9},{6,10},{7,11},{8,4},{9,5},... | collective-permute-start | bytes 196616 | tf_op jit(solution)/shard_map/ppermute | solution.py:25
  23.2 1.3 %collective-permute-start.5 = (f32[80,128]{1,0:T(8,128)S(1)}, f32[80,128]{1,0:T(8,128)S(1)}, u32[]{:S(2)}, u32[]{:S(2)}) collective-permute-start(f32[80,128]{1,0:T(8,128)S(1)} %correlate.1.mine), channel_id=1, source_target_pairs={{0,1},{1,0},{2,3},{3,2},{4,5},{5,4},{6,7},{7,6},{8,9},{9,8},{10,11... | collective-permute-start | bytes 122888 | tf_op jit(solution)/shard_map/ppermute | solution.py:25
  24.9 4.0 %collective-permute-start.6 = (bf16[144,128]{1,0:T(8,128)(2,1)S(1)}, bf16[144,128]{1,0:T(8,128)(2,1)S(1)}, u32[]{:S(2)}, u32[]{:S(2)}) collective-permute-start(bf16[144,128]{1,0:T(8,128)(2,1)S(1)} %get-tuple-element.34), channel_id=1, source_target_pairs={{0,2},{1,3},{2,0},{3,1},{4,6},{5,7},{6,4},{7,5},{8,10},{9,11},{10,... | collective-permute-start | bytes 110600 | tf_op jit(solution)/shard_map/ppermute | solution.py:25
  29.0 6.6 %collective-permute-start.7 = (bf16[272,128]{1,0:T(8,128)(2,1)S(1)}, bf16[272,128]{1,0:T(8,128)(2,1)S(1)}, u32[]{:S(2)}, u32[]{:S(2)}) collective-permute-start(bf16[272,128]{1,0:T(8,128)(2,1)S(1)} %get-tuple-element.38), channel_id=1, source_target_pairs={{0,12},{1,13},{2,14},{3,15},{4,8},{5,9},{6,10},{7,11},{8,4},{9,5},... | collective-permute-start | bytes 208904 | tf_op jit(solution)/shard_map/ppermute | solution.py:25
  31.0 7.1 %collective-permute-start.8 = (bf16[272,128]{1,0:T(8,128)(2,1)S(1)}, bf16[272,128]{1,0:T(8,128)(2,1)S(1)}, u32[]{:S(2)}, u32[]{:S(2)}) collective-permute-start(bf16[272,128]{1,0:T(8,128)(2,1)S(1)} %get-tuple-element.39), channel_id=1, source_target_pairs={{0,8},{1,9},{2,10},{3,11},{4,12},{5,13},{6,14},{7,15},{8,0},{9,1},... | collective-permute-start | bytes 208904 | tf_op jit(solution)/shard_map/ppermute | solution.py:25
  31.3 6.8 %collective-permute-start.9 = (bf16[272,128]{1,0:T(8,128)(2,1)S(1)}, bf16[272,128]{1,0:T(8,128)(2,1)S(1)}, u32[]{:S(2)}, u32[]{:S(2)}) collective-permute-start(bf16[272,128]{1,0:T(8,128)(2,1)S(1)} %get-tuple-element.40), channel_id=1, source_target_pairs={{0,4},{1,5},{2,6},{3,7},{4,0},{5,1},{6,2},{7,3},{8,12},{9,13},{10,... | collective-permute-start | bytes 208904 | tf_op jit(solution)/shard_map/ppermute | solution.py:25
  38.6 1.2 %collective-permute-start.10 = (bf16[128,128]{1,0:T(8,128)(2,1)S(1)}, bf16[128,128]{1,0:T(8,128)(2,1)S(1)}, u32[]{:S(2)}, u32[]{:S(2)}) collective-permute-start(bf16[128,128]{1,0:T(8,128)(2,1)S(1)} %get-tuple-element.42), channel_id=1, source_target_pairs={{0,1},{1,0},{2,3},{3,2},{4,5},{5,4},{6,7},{7,6},{8,9},{9,8},{10,11... | collective-permute-start | bytes 98312 | tf_op jit(solution)/shard_map/ppermute | solution.py:25

commit v5 on v4

--- a/solution.py
+++ b/solution.py
@@ -46,49 +46,21 @@
     return values[0]
 
 
-def project_half(table, index_ref, frac_ref, half, blended):
-    pixels = index_ref.shape[1]
-    highs = table.shape[1]
-    groups = table.shape[0] // 16
-    stride = 8 * groups
-    chunk = BLOCK * LANES
-    blocks = pixels // (2 * chunk)
-
-    def body(step, carry):
-        where = pl.ds(pl.multiple_of((2 * step + half) * chunk, chunk), chunk)
-        index = index_ref[:, where]
-        frac = frac_ref[:, where]
-        high = index >> 7
-        low = index & (LANES - 1)
-        group = (low * 147) >> 10
-        first = low - 7 * group
-        high_ids = lax.broadcasted_iota(jnp.int32, (highs, chunk), 0)
-        one_hot = jnp.where(high_ids == high, 1.0, 0.0).astype(jnp.bfloat16)
-        rows = jnp.dot(table[...], one_hot, preferred_element_type=jnp.float32)
-        group = jnp.broadcast_to(group, (8, chunk))
-        masks = [(group & (1 << bit)) != 0 for bit in range((groups - 1).bit_length())]
-        ids = lax.broadcasted_iota(jnp.int32, (8, chunk), 0)
-        weight = jnp.where(ids == first, 1.0 - frac, jnp.where(ids == first + 1, frac, 0.0))
-        for comp in range(2):
-            start = comp * stride
-            picked = tree_select([rows[start + 8 * g : start + 8 * g + 8] for g in range(groups)], masks)
-            value = jnp.sum(picked * weight, axis=0, keepdims=True)
-            for k in range(BLOCK):
-                row = (comp * blocks + step) * BLOCK + k
-                blended[pl.ds(row, 1), :] = value[:, k * LANES : (k + 1) * LANES]
-        return carry
-
-    lax.fori_loop(0, blocks, body, 0, unroll=2)
-
-
-def project_other_kernel(
-    table_hbm, index_hbm, frac_hbm, out_ref, table, index_ref, frac_ref,
-    table_in, flat, wide, blended, sems
+def project_kernel(
+    table_hbm, index_hbm, frac_hbm, images_hbm, out_ref, own_images, other_images,
+    table_in, index_ref, frac_ref, flat, wide, table, blended, even, odd, sems
 ):
     device = lax.axis_index("particle")
     row_count = lax.axis_size("particle") // 2
     half_set = device // 2 % 2
     class_id = (2 * (device // 4) + device % 2) // (row_count // CLASSES)
+    core = own_half()
+    highs = flat.shape[1]
+    pixels = index_ref.shape[1]
+    groups = table.shape[0] // 16
+    stride = 8 * groups
+    chunk = BLOCK * LANES
+    blocks = pixels // (2 * chunk)
     copies = [
         pltpu.make_async_copy(
             table_hbm.at[pl.ds(half_set, 1), pl.ds(class_id, 1)], table_in, sems.at[0]
@@ -96,11 +68,21 @@
         pltpu.make_async_copy(index_hbm, index_ref, sems.at[1]),
         pltpu.make_async_copy(frac_hbm, frac_ref, sems.at[2]),
     ]
+    for target, half in ((other_images, 1 - core), (own_images, core)):
+        for comp in range(2):
+            for step in range(blocks):
+                source = pl.multiple_of(comp * pixels + (2 * step + half) * chunk, chunk)
+                dest = (comp * blocks + step) * chunk
+                copies.append(
+                    pltpu.make_async_copy(
+                        images_hbm.at[:, pl.ds(source, chunk)],
+                        target.at[:, pl.ds(dest, chunk)],
+                        sems.at[len(copies)],
+                    )
+                )
     for copy in copies:
         copy.start()
     copies[0].wait()
-    highs = flat.shape[1]
-    groups = table.shape[0] // 16
 
     def unfold(step, carry):
         piece = table_in[0, 0, :, pl.ds(step * 8 * LANES, 8 * LANES)].astype(jnp.float32)
@@ -122,104 +104,82 @@
         ).astype(jnp.bfloat16)
     copies[1].wait()
     copies[2].wait()
-    project_half(table, index_ref, frac_ref, 1 - own_half(), blended)
+
+    def place(step):
+        block = 2 * (step % blocks) + jnp.where(step < blocks, core, 1 - core)
+        return pl.ds(pl.multiple_of(block * chunk, chunk), chunk)
+
+    def pick_lanes(step, target):
+        high = index_ref[:, place(step)] >> 7
+        high_ids = lax.broadcasted_iota(jnp.int32, (highs, chunk), 0)
+        one_hot = jnp.where(high_ids == high, 1.0, 0.0).astype(jnp.bfloat16)
+        target[...] = jnp.dot(table[...], one_hot, preferred_element_type=jnp.float32)
+
+    def blend(step, rows):
+        low = index_ref[:, place(step)] & (LANES - 1)
+        frac = frac_ref[:, place(step)]
+        group = (low * 147) >> 10
+        first = low - 7 * group
+        group = jnp.broadcast_to(group, (8, chunk))
+        masks = [(group & (1 << bit)) != 0 for bit in range((groups - 1).bit_length())]
+        ids = lax.broadcasted_iota(jnp.int32, (8, chunk), 0)
+        weight = jnp.where(ids == first, 1.0 - frac, jnp.where(ids == first + 1, frac, 0.0))
+        for comp in range(2):
+            start = comp * stride
+            picked = tree_select(
+                [rows[start + 8 * g : start + 8 * g + 8, :] for g in range(groups)], masks
+            )
+            value = jnp.sum(picked * weight, axis=0, keepdims=True)
+            first_row = (step // blocks * 2 + comp) * blocks * BLOCK + step % blocks * BLOCK
+            for k in range(BLOCK):
+                blended[pl.ds(first_row + k, 1), :] = value[:, k * LANES : (k + 1) * LANES]
+
+    pick_lanes(0, even)
+
+    def body(pair, carry):
+        pick_lanes(2 * pair + 1, odd)
+        blend(2 * pair, even)
+        pick_lanes(2 * pair + 2, even)
+        blend(2 * pair + 1, odd)
+        return carry
+
+    lax.fori_loop(0, blocks - 1, body, 0)
+    pick_lanes(2 * blocks - 1, odd)
+    blend(2 * blocks - 2, even)
+    blend(2 * blocks - 1, odd)
     out_ref[...] = blended[...].astype(jnp.bfloat16)
-
-
-def project_other(class_refs, interp_index, interp_frac):
+    for copy in copies[3:]:
+        copy.wait()
+
+
+def project_row(class_refs, interp_index, interp_frac, images):
     vox = class_refs.shape[3]
     pixels = interp_index.shape[1]
     highs = vox // LANES
-    half_rows = pixels // LANES
+    rows = 2 * pixels // LANES
     groups = -(-LANES // 7)
-    return pl.pallas_call(
-        project_other_kernel,
-        in_specs=[pl.BlockSpec(memory_space=pltpu.HBM)] * 3,
-        out_specs=whole_vmem(4),
-        out_shape=[
-            jax.ShapeDtypeStruct((half_rows, LANES), jnp.bfloat16),
-            jax.ShapeDtypeStruct((16 * groups, highs), jnp.bfloat16),
-            jax.ShapeDtypeStruct((1, pixels), jnp.int32),
-            jax.ShapeDtypeStruct((1, pixels), jnp.float32),
-        ],
+    chunk = BLOCK * LANES
+    half_images = jax.ShapeDtypeStruct((images.shape[0], pixels), jnp.bfloat16)
+    return pl.pallas_call(
+        project_kernel,
+        in_specs=[pl.BlockSpec(memory_space=pltpu.HBM)] * 4,
+        out_specs=whole_vmem(3),
+        out_shape=[jax.ShapeDtypeStruct((rows, LANES), jnp.bfloat16), half_images, half_images],
         scratch_shapes=[
             pltpu.VMEM((1, 1, 2, vox), jnp.bfloat16),
+            pltpu.VMEM((1, pixels), jnp.int32),
+            pltpu.VMEM((1, pixels), jnp.float32),
             pltpu.VMEM((2, highs, LANES), jnp.float32),
             pltpu.VMEM((LANES + 8, highs), jnp.float32),
-            pltpu.VMEM((half_rows, LANES), jnp.float32),
-            pltpu.SemaphoreType.DMA((3,)),
+            pltpu.VMEM((16 * groups, highs), jnp.bfloat16),
+            pltpu.VMEM((rows, LANES), jnp.float32),
+            pltpu.VMEM((16 * groups, chunk), jnp.float32),
+            pltpu.VMEM((16 * groups, chunk), jnp.float32),
+            pltpu.SemaphoreType.DMA((3 + 2 * pixels // chunk,)),
         ],
         compiler_params=pltpu.CompilerParams(vmem_limit_bytes=16 * MIB),
-        name="project_other",
-    )(*(in_hbm(value) for value in (class_refs, interp_index, interp_frac)))
-
-
-def project_own_kernel(
-    table, index_ref, frac_ref, images_hbm, out_ref, own_images, other_images, blended, sems
-):
-    pixels = index_ref.shape[1]
-    chunk = BLOCK * LANES
-    blocks = pixels // (2 * chunk)
-    copies = []
-    for target, half in ((other_images, 1 - own_half()), (own_images, own_half())):
-        for comp in range(2):
-            for step in range(blocks):
-                source = pl.multiple_of(comp * pixels + (2 * step + half) * chunk, chunk)
-                dest = (comp * blocks + step) * chunk
-                copies.append(
-                    pltpu.make_async_copy(
-                        images_hbm.at[:, pl.ds(source, chunk)],
-                        target.at[:, pl.ds(dest, chunk)],
-                        sems.at[len(copies)],
-                    )
-                )
-    for copy in copies:
-        copy.start()
-    project_half(table, index_ref, frac_ref, own_half(), blended)
-    out_ref[...] = blended[...].astype(jnp.bfloat16)
-    for copy in copies:
-        copy.wait()
-
-
-def project_own(table, index, frac, images):
-    parts, width = images.shape
-    half_rows = index.shape[1] // LANES
-    half_images = jax.ShapeDtypeStruct((parts, width // 2), jnp.bfloat16)
-    return pl.pallas_call(
-        project_own_kernel,
-        in_specs=whole_vmem(3) + [pl.BlockSpec(memory_space=pltpu.HBM)],
-        out_specs=whole_vmem(3),
-        out_shape=[
-            jax.ShapeDtypeStruct((half_rows, LANES), jnp.bfloat16),
-            half_images,
-            half_images,
-        ],
-        scratch_shapes=[
-            pltpu.VMEM((half_rows, LANES), jnp.float32),
-            pltpu.SemaphoreType.DMA((2 * width // (2 * BLOCK * LANES),)),
-        ],
-        compiler_params=pltpu.CompilerParams(vmem_limit_bytes=16 * MIB),
-        cost_estimate=pl.CostEstimate(flops=2000000000, bytes_accessed=8000000, transcendentals=0),
-        name="project_own",
-    )(table, index, frac, in_hbm(images))
-
-
-def pair_kernel(own, other, out_ref):
-    count = own.shape[0]
-    core = own_half()
-    out_ref[pl.ds(pl.multiple_of(core * count, count), count), :] = own[...]
-    out_ref[pl.ds(pl.multiple_of((1 - core) * count, count), count), :] = other[...]
-
-
-def pair_rows(own, other):
-    return pl.pallas_call(
-        pair_kernel,
-        in_specs=whole_vmem(2),
-        out_specs=pl.BlockSpec(memory_space=pltpu.VMEM),
-        out_shape=jax.ShapeDtypeStruct((2 * own.shape[0], LANES), own.dtype),
-        compiler_params=pltpu.CompilerParams(vmem_limit_bytes=16 * MIB),
-        name="pair_rows",
-    )(own, other)
+        name="project_row",
+    )(*(in_hbm(value) for value in (class_refs, interp_index, interp_frac, images)))
 
 
 def slot_rows(device, slots):
@@ -271,15 +231,21 @@
 
 
 def correlate_kernel(own_images, other_images, precision_ref, assigned_ref, cos_ref, sin_ref, *refs, chunk):
-    pair_refs, (out_ref, proj) = refs[:-2], refs[-2:]
+    row_refs, (out_ref, proj) = refs[:-2], refs[-2:]
     shifts = cos_ref.shape[0]
     parts = own_images.shape[0]
-    slots = 2 * len(pair_refs)
+    slots = len(row_refs)
     width = own_images.shape[1] // 2
     tiles = width // LANES
     per_row = 2 * tiles
-    for m, ref in enumerate(pair_refs):
-        proj[2 * m * per_row : 2 * (m + 1) * per_row, :] = ref[...].astype(jnp.float32)
+    core = own_half()
+    for m in range(slots // 2):
+        own_place = pl.multiple_of((2 * m + core) * per_row, per_row)
+        other_place = pl.multiple_of((2 * m + 1 - core) * per_row, per_row)
+        proj[pl.ds(own_place, per_row), :] = row_refs[m][0:per_row, :].astype(jnp.float32)
+        proj[pl.ds(other_place, per_row), :] = row_refs[slots // 2 + m][per_row:, :].astype(
+            jnp.float32
+        )
 
     chunk_tiles = chunk // LANES
     contract_lanes = (((1,), (1,)), ((), ()))
@@ -335,18 +301,18 @@
     out_ref[combos + slots + 1 : combos + slots + 2, 0:parts] = assigned_ref[...].astype(jnp.float32)
 
 
-def correlate(own_images, other_images, precision, assigned, cos_table, sin_table, pairs):
-    slots = 2 * len(pairs)
+def correlate(own_images, other_images, precision, assigned, cos_table, sin_table, rows):
+    slots = len(rows)
     shifts, width = cos_table.shape
     return pl.pallas_call(
         functools.partial(correlate_kernel, chunk=2048),
-        in_specs=whole_vmem(6 + len(pairs)),
+        in_specs=whole_vmem(6 + slots),
         out_specs=pl.BlockSpec(memory_space=pltpu.VMEM),
         out_shape=jax.ShapeDtypeStruct((shifts * slots + slots + 8, LANES), jnp.float32),
         scratch_shapes=[pltpu.VMEM((slots * 2 * width // LANES, LANES), jnp.float32)],
         compiler_params=pltpu.CompilerParams(vmem_limit_bytes=(14 + slots // 2) * MIB),
         name="correlate",
-    )(own_images, other_images, precision, assigned, cos_table, sin_table, *pairs)
+    )(own_images, other_images, precision, assigned, cos_table, sin_table, *rows)
 
 
 def rotate_back(weights, own_images, other_images, cos_ref, sin_ref, where, imag_where, slots):
@@ -438,7 +404,9 @@
     )(mine, received, own_images, other_images, cos_table, sin_table)
 
 
-def backproject_kernel(weight_ref, own_images, other_images, cos_ref, sin_ref, sums, *, slots, chunk):
+def backproject_kernel(
+    weight_ref, own_images, other_images, cos_ref, sin_ref, sums, *, slots, chunk, unroll
+):
     width = cos_ref.shape[1]
     tiles = width // LANES
     per_row = 2 * tiles
@@ -459,14 +427,19 @@
             sums[pl.ds(tiles + first + k, slots, stride=per_row), :] = imag[:, piece]
         return carry
 
-    lax.fori_loop(0, (tiles - LOW_TILES) // chunk_tiles, body, 0)
+    lax.fori_loop(0, (tiles - LOW_TILES) // chunk_tiles, body, 0, unroll=unroll)
 
 
 def backproject(weights, own_images, other_images, cos_table, sin_table, slots):
     width = cos_table.shape[1]
     rows = slots * 2 * width // LANES
     return pl.pallas_call(
-        functools.partial(backproject_kernel, slots=slots, chunk=LOW_TILES * LANES),
+        functools.partial(
+            backproject_kernel,
+            slots=slots,
+            chunk=LOW_TILES * LANES,
+            unroll=7 if slots <= 8 else 1,
+        ),
         in_specs=whole_vmem(5),
         out_specs=pl.BlockSpec(memory_space=pltpu.VMEM),
         out_shape=jax.ShapeDtypeStruct((rows, LANES), jnp.float32),
@@ -513,7 +486,47 @@
     )(sums, low, low_received, mass)
 
 
-def merge_kernel(own, mass, *refs, mass_scale):
+def relay_kernel(own, received, out):
+    rows = out.shape[0] - MASS_ROWS
+    total = own[0:rows, :].astype(jnp.float32) + received[0:rows, :].astype(jnp.float32)
+    out[0:rows, :] = total.astype(out.dtype)
+    out[rows:, :] = split_mass(joined_mass(own[rows:, :]) + joined_mass(received[rows:, :]))
+
+
+def relay(own, received):
+    return pl.pallas_call(
+        relay_kernel,
+        in_specs=whole_vmem(2),
+        out_specs=pl.BlockSpec(memory_space=pltpu.VMEM),
+        out_shape=jax.ShapeDtypeStruct(own.shape, own.dtype),
+        compiler_params=pltpu.CompilerParams(vmem_limit_bytes=16 * MIB),
+        name="relay",
+    )(own, received)
+
+
+def gather_chips(row, chips):
+    rows = {0: row}
+    bit = chips // 2
+    while bit:
+        rows.update({m ^ bit: exchange(rows[m], 4 * bit) for m in list(rows)})
+        bit //= 2
+    return [rows[m] for m in range(chips)]
+
+
+def scatter_chips(sends, chips):
+    held = dict(enumerate(sends, start=1))
+    arrived = []
+    bit = 1
+    while bit < chips:
+        away = {m: exchange(held.pop(m), 4 * bit) for m in sorted(held, reverse=True) if m & bit}
+        arrived.append(away.pop(bit))
+        for m, value in away.items():
+            held[m ^ bit] = relay(held[m ^ bit], value)
+        bit *= 2
+    return arrived
+
+
+def merge_kernel(own, mass, *refs):
     received, (keep, send, mass_out) = refs[:-3], refs[-3:]
     rows = own.shape[0]
     half = rows // 2
@@ -521,33 +534,34 @@
     total_mass = mass[0:1, :]
     for ref in received:
         total_mass = total_mass + joined_mass(ref[rows:, :])
+    mass_out[...] = jnp.broadcast_to(total_mass, mass_out.shape)
     for target, place in ((send, 1 - core), (keep, core)):
         where = pl.ds(pl.multiple_of(place * half, half), half)
         total = own[where, :]
         for ref in received:
             total = total + ref[where, :].astype(jnp.float32)
         target[...] = total.astype(target.dtype)
-    mass_out[...] = total_mass[0, :CLASSES] * mass_scale
-
-
-def merge(own, mass, received, mass_scale):
+
+
+def merge(own, mass, received):
     rows = own.shape[0] // 2
     return pl.pallas_call(
-        functools.partial(merge_kernel, mass_scale=mass_scale),
+        merge_kernel,
         in_specs=whole_vmem(2 + len(received)),
         out_specs=whole_vmem(3),
         out_shape=[
             jax.ShapeDtypeStruct((rows, LANES), jnp.float32),
             jax.ShapeDtypeStruct((rows, LANES), jnp.bfloat16),
-            jax.ShapeDtypeStruct((CLASSES,), jnp.float32),
+            jax.ShapeDtypeStruct((8, LANES), jnp.float32),
         ],
         compiler_params=pltpu.CompilerParams(vmem_limit_bytes=16 * MIB),
         name="merge",
     )(own, mass, *received)
 
 
-def finish_kernel(own, received, out, *, scale):
+def finish_kernel(own, received, mass, out, mass_out, *, scale, mass_scale):
     half = own_half()
+    mass_out[...] = mass[0, :CLASSES] * mass_scale
     for step in range(own.shape[0] // BLOCK):
         rows = slice(step * BLOCK, (step + 1) * BLOCK)
         own_rows = pl.ds(pl.multiple_of((2 * step + half) * BLOCK, BLOCK), BLOCK)
@@ -556,15 +570,18 @@
         out[other_rows, :] = received[rows, :].astype(jnp.float32) * scale
 
 
-def finish(own, received, scale):
-    return pl.pallas_call(
-        functools.partial(finish_kernel, scale=scale),
-        in_specs=whole_vmem(2),
-        out_specs=pl.BlockSpec(memory_space=pltpu.VMEM),
-        out_shape=jax.ShapeDtypeStruct((2 * own.shape[0], LANES), jnp.float32),
+def finish(own, received, mass, scale, mass_scale):
+    return pl.pallas_call(
+        functools.partial(finish_kernel, scale=scale, mass_scale=mass_scale),
+        in_specs=whole_vmem(3),
+        out_specs=whole_vmem(2),
+        out_shape=[
+            jax.ShapeDtypeStruct((2 * own.shape[0], LANES), jnp.float32),
+            jax.ShapeDtypeStruct((CLASSES,), jnp.float32),
+        ],
         compiler_params=pltpu.CompilerParams(vmem_limit_bytes=16 * MIB),
         name="finish",
-    )(own, received)
+    )(own, received, mass)
 
 
 def local(
@@ -574,11 +591,9 @@
     slots = dev_count // 2
     chips = slots // 2
     parts, width = images.shape
-    other_half, table, index, frac = project_other(class_refs, interp_index, interp_frac)
-    from_core = exchange(other_half, 1)
-    own, own_images, other_images = project_own(table, index, frac, images)
-    pair = pair_rows(own, from_core)
-    pairs = [pair] + [exchange(pair, 4 * m) for m in range(1, chips)]
+    own_row, own_images, other_images = project_row(class_refs, interp_index, interp_frac, images)
+    rows = gather_chips(own_row, chips)
+    rows = rows + [exchange(row, 1) for row in rows]
     images_received = exchange(other_images, 1)
     cos_table, sin_table = phase_tables(shift_grid, width // 4)
     mine = correlate(
@@ -588,7 +603,7 @@
         assigned_class.reshape(1, parts),
         cos_table,
         sin_table,
-        pairs,
+        rows,
     )
     weights, low, low_send, mass = posterior(
         mine, exchange(mine, 1), own_images, images_received, cos_table, sin_table, slots
@@ -596,12 +611,11 @@
     low_received = exchange(low_send, 2)
     sums = backproject(weights, own_images, images_received, cos_table, sin_table, slots)
     folded = fold(sums, low, low_received, mass, slots)
-    sends = folded[2:]
-    received = [exchange(sends[m - 1], 4 * m) for m in range(chips - 1, 0, -1)]
-    keep, send, class_mass = merge(
-        folded[0], folded[1], received, CLASSES / (parts * dev_count)
-    )
-    back = finish(keep, exchange(send, 1), 1.0 / math.sqrt(parts))
+    received = scatter_chips(folded[2:], chips)
+    keep, send, mass = merge(folded[0], folded[1], received)
+    back, class_mass = finish(
+        keep, exchange(send, 1), mass, 1.0 / math.sqrt(parts), CLASSES / (parts * dev_count)
+    )
     return back.reshape(1, width), class_mass
 
 

time: 40.7 us -> 41.9 us (1.029)
  waiting for transfers between devices: 15.5 us -> 13.7 us
  starting transfers between devices: 12.3 us -> 14.1 us
  Pallas kernels: 11.9 us -> 13.2 us
    ppermute x11 -> x14, starting transfers between devices: 12.3 us -> 14.1 us  [exchange(): return lax.ppermute(value, 'particle', pairs)]
    ppermute x11 -> x14, waiting for transfers between devices: 15.5 us -> 13.7 us  [exchange(): return lax.ppermute(value, 'particle', pairs)]
    pallas_call x5 -> x4, Pallas kernels: 7.38 us -> 9.07 us  [the longest x1 8.32 us: project_row(): pl.pallas_call(project_kernel, in_specs=[pl.BlockSpec(memory_space=pltpu....]
    pallas_call x1, Pallas kernels: 2.02 us -> 1.55 us  [backproject(): pl.pallas_call(functools.partial(backproject_kernel, slots=slots, chunk=L...]
  transfers between devices with their start and end apart: 11 -> 14, of which waited for: 8 -> 8; matrix products, arithmetic and copies ran while one was open for 0% -> 0% of each run, Pallas kernels for 6% -> 5%
where the time goes in v5:
time: 41.9 us; the launch traced here: 41.8 us
  starting transfers between devices  14.1 us (34%)
  waiting for transfers between devices  13.7 us (33%)
  Pallas kernels  13.2 us (32%)
  between operations  0.74 us (2%)
    ppermute x14, starting transfers between devices, exchange(): return lax.ppermute(value, 'particle', pairs)  14.1 us
    ppermute x14, waiting for transfers between devices, exchange(): return lax.ppermute(value, 'particle', pairs)  13.7 us
    pallas_call x1, Pallas kernels, project_row(): pl.pallas_call(project_kernel, in_specs=[pl.BlockSpec(memory_space=pltpu....  8.32 us
    pallas_call x1, Pallas kernels, correlate(): pl.pallas_call(functools.partial(correlate_kernel, chunk=2048), in_specs=...  1.73 us
    pallas_call x1, Pallas kernels, backproject(): pl.pallas_call(functools.partial(backproject_kernel, slots=slots, chunk=L...  1.55 us
  transfers between devices with their start and end apart: 14, of which 8 were waited for; matrix products, arithmetic and copies ran while one was open for 0% of the time, Pallas kernels for 5%

profile of v5, /device:TPU:0, one launch (start us, length us, event | category | flops | bytes accessed | tf_op | source)
XLA Modules:
  0.0 41.8 jit_solution(7287154017270973805)
XLA Ops:
  0.7 8.3 %project_row.1 = (bf16[256,128]{1,0:T(8,128)(2,1)S(1)}, bf16[32,16384]{1,0:T(8,128)(2,1)S(1)}, bf16[32,16384]{1,0:T(8,128)(2,1)}) custom-call(bf16[2,8,2,32768]{3,2,1,0:T(2,128)(2,1)} %table_hbm.1, s32[1,16384]{1,0:T(1,128)} %index_hbm.1, f32[1,16384]{1,0:T(1,128)} %frac_hbm.1, bf16[32,32768]{1,0:T(8,128)(2,1)} %images_hbm.1), custom_call_target="tpu_custom_call" | custom-call | tf_op jit(solution)/shard_map/project_row/pallas_call | solution.py:163
  9.0 0.5 %collective-permute-start = (bf16[32,16384]{1,0:T(8,128)(2,1)}, bf16[32,16384]{1,0:T(8,128)(2,1)S(1)}, u32[]{:S(2)}, u32[]{:S(2)}) collective-permute-start(bf16[32,16384]{1,0:T(8,128)(2,1)} %get-tuple-element.22), channel_id=1, source_target_pairs={{0,1},{1,0},{2,3},{3,2},{4,5},{5,4},{6,7},{7,6},{8,9},{9,8},{10,11... | collective-permute-start | bytes 3145736 | tf_op jit(solution)/shard_map/ppermute | solution.py:25
  9.5 3.7 %collective-permute-start.2 = (bf16[256,128]{1,0:T(8,128)(2,1)S(1)}, bf16[256,128]{1,0:T(8,128)(2,1)S(1)}, u32[]{:S(2)}, u32[]{:S(2)}) collective-permute-start(bf16[256,128]{1,0:T(8,128)(2,1)S(1)} %get-tuple-element.25.refs_0_), channel_id=1, source_target_pairs={{0,8},{1,9},{2,10},{3,11},{4,12},{5,13},{6,14},{7,15},{8,0},{9,1},... | collective-permute-start | bytes 196616 | tf_op jit(solution)/shard_map/ppermute | solution.py:25
  13.2 1.6 %collective-permute-start.1 = (bf16[256,128]{1,0:T(8,128)(2,1)S(1)}, bf16[256,128]{1,0:T(8,128)(2,1)S(1)}, u32[]{:S(2)}, u32[]{:S(2)}) collective-permute-start(bf16[256,128]{1,0:T(8,128)(2,1)S(1)} %get-tuple-element.25.refs_0_), channel_id=1, source_target_pairs={{0,4},{1,5},{2,6},{3,7},{4,0},{5,1},{6,2},{7,3},{8,12},{9,13},{10,... | collective-permute-start | bytes 196616 | tf_op jit(solution)/shard_map/ppermute | solution.py:25
  14.8 2.4 %collective-permute-done.2.refs_2_ = bf16[256,128]{1,0:T(8,128)(2,1)S(1)} collective-permute-done((bf16[256,128]{1,0:T(8,128)(2,1)S(1)}, bf16[256,128]{1,0:T(8,128)(2,1)S(1)}, u32[]{:S(2)}, u32[]{:S(2)}) %collective-permute-start.2) | collective-permute-done | bytes 65568 | tf_op jit(solution)/shard_map/ppermute | solution.py:25
  17.1 0.9 %collective-permute-start.3 = (bf16[256,128]{1,0:T(8,128)(2,1)S(1)}, bf16[256,128]{1,0:T(8,128)(2,1)S(1)}, u32[]{:S(2)}, u32[]{:S(2)}) collective-permute-start(bf16[256,128]{1,0:T(8,128)(2,1)S(1)} %collective-permute-done.2.refs_2_), channel_id=1, source_target_pairs={{0,4},{1,5},{2,6},{3,7},{4,0},{5,1},{6,2},{7,3},{8,12},{9,13},{10,... | collective-permute-start | bytes 196616 | tf_op jit(solution)/shard_map/ppermute | solution.py:25
  18.0 0.5 %collective-permute-start.6 = (bf16[256,128]{1,0:T(8,128)(2,1)S(1)}, bf16[256,128]{1,0:T(8,128)(2,1)S(1)}, u32[]{:S(2)}, u32[]{:S(2)}) collective-permute-start(bf16[256,128]{1,0:T(8,128)(2,1)S(1)} %collective-permute-done.2.refs_2_), channel_id=1, source_target_pairs={{0,1},{1,0},{2,3},{3,2},{4,5},{5,4},{6,7},{7,6},{8,9},{9,8},{10,11... | collective-permute-start | bytes 196616 | tf_op jit(solution)/shard_map/ppermute | solution.py:25
  18.5 2.8 %collective-permute-done.3.refs_3_ = bf16[256,128]{1,0:T(8,128)(2,1)S(1)} collective-permute-done((bf16[256,128]{1,0:T(8,128)(2,1)S(1)}, bf16[256,128]{1,0:T(8,128)(2,1)S(1)}, u32[]{:S(2)}, u32[]{:S(2)}) %collective-permute-start.3) | collective-permute-done | bytes 65568 | tf_op jit(solution)/shard_map/ppermute | solution.py:25
  21.5 0.4 phase_tables.1
  21.9 0.7 %collective-permute-done.7.refs_7_ = bf16[256,128]{1,0:T(8,128)(2,1)S(1)} collective-permute-done((bf16[256,128]{1,0:T(8,128)(2,1)S(1)}, bf16[256,128]{1,0:T(8,128)(2,1)S(1)}, u32[]{:S(2)}, u32[]{:S(2)}) %collective-permute-start.7) | collective-permute-done | bytes 65568 | tf_op jit(solution)/shard_map/ppermute | solution.py:25
  22.6 1.7 %correlate.1.mine = f32[80,128]{1,0:T(8,128)S(1)} custom-call(bf16[32,16384]{1,0:T(8,128)(2,1)S(1)} %get-tuple-element.21.own_images, bf16[32,16384]{1,0:T(8,128)(2,1)S(1)} %collective-permute-done.other_images, f32[1,32]{1,0:T(1,128)S(1)} %bitcast.3, s32[1,32]{1,0:T(1,128)S(1)} %bitcast.4, f32[8,8192]{1,0:T(8,128)S(1)} %get-tuple-element.23.cos_ref, ...), custom_call_target="tpu_custom_call" | custom-call | tf_op jit(solution)/shard_map/correlate/pallas_call | solution.py:307
  24.4 0.2 collective-permute-start.8
  24.6 1.1 %collective-permute-done.8.received = f32[80,128]{1,0:T(8,128)S(1)} collective-permute-done((f32[80,128]{1,0:T(8,128)S(1)}, f32[80,128]{1,0:T(8,128)S(1)}, u32[]{:S(2)}, u32[]{:S(2)}) %collective-permute-start.8) | collective-permute-done | bytes 40992 | tf_op jit(solution)/shard_map/ppermute | solution.py:25
  25.7 0.4 posterior.1
  26.0 1.7 %collective-permute-start.9 = (bf16[144,128]{1,0:T(8,128)(2,1)S(1)}, bf16[144,128]{1,0:T(8,128)(2,1)S(1)}, u32[]{:S(2)}, u32[]{:S(2)}) collective-permute-start(bf16[144,128]{1,0:T(8,128)(2,1)S(1)} %get-tuple-element.28), channel_id=1, source_target_pairs={{0,2},{1,3},{2,0},{3,1},{4,6},{5,7},{6,4},{7,5},{8,10},{9,11},{10,... | collective-permute-start | bytes 110600 | tf_op jit(solution)/shard_map/ppermute | solution.py:25
  27.7 1.6 %backproject.1.sums = f32[1024,128]{1,0:T(8,128)S(1)} custom-call(bf16[64,64]{1,0:T(8,128)(2,1)S(1)} %get-tuple-element.26.weight_ref, bf16[32,16384]{1,0:T(8,128)(2,1)S(1)} %get-tuple-element.21.own_images, bf16[32,16384]{1,0:T(8,128)(2,1)S(1)} %collective-permute-done.other_images, f32[8,8192]{1,0:T(8,128)S(1)} %get-tuple-element.23.cos_ref, ...), custom_call_target="tpu_custom_call" | custom-call | flops 20000000 | bytes 20000000 | tf_op jit(solution)/shard_map/backproject/pallas_call | solution.py:436
  29.3 0.8 %collective-permute-done.9.low_received = bf16[144,128]{1,0:T(8,128)(2,1)S(1)} collective-permute-done((bf16[144,128]{1,0:T(8,128)(2,1)S(1)}, bf16[144,128]{1,0:T(8,128)(2,1)S(1)}, u32[]{:S(2)}, u32[]{:S(2)}) %collective-permute-start.9) | collective-permute-done | bytes 36896 | tf_op jit(solution)/shard_map/ppermute | solution.py:25
  30.1 1.0 %collective-permute-start.11 = (bf16[272,128]{1,0:T(8,128)(2,1)S(1)}, bf16[272,128]{1,0:T(8,128)(2,1)S(1)}, u32[]{:S(2)}, u32[]{:S(2)}) collective-permute-start(bf16[272,128]{1,0:T(8,128)(2,1)S(1)} %get-tuple-element.34), channel_id=1, source_target_pairs={{0,4},{1,5},{2,6},{3,7},{4,0},{5,1},{6,2},{7,3},{8,12},{9,13},{10,... | collective-permute-start | bytes 208904 | tf_op jit(solution)/shard_map/ppermute | solution.py:25
  31.1 1.1 %collective-permute-start.10 = (bf16[272,128]{1,0:T(8,128)(2,1)S(1)}, bf16[272,128]{1,0:T(8,128)(2,1)S(1)}, u32[]{:S(2)}, u32[]{:S(2)}) collective-permute-start(bf16[272,128]{1,0:T(8,128)(2,1)S(1)} %get-tuple-element.32), channel_id=1, source_target_pairs={{0,4},{1,5},{2,6},{3,7},{4,0},{5,1},{6,2},{7,3},{8,12},{9,13},{10,... | collective-permute-start | bytes 208904 | tf_op jit(solution)/shard_map/ppermute | solution.py:25
  32.2 2.3 %collective-permute-done.11.received = bf16[272,128]{1,0:T(8,128)(2,1)S(1)} collective-permute-done((bf16[272,128]{1,0:T(8,128)(2,1)S(1)}, bf16[272,128]{1,0:T(8,128)(2,1)S(1)}, u32[]{:S(2)}, u32[]{:S(2)}) %collective-permute-start.11) | collective-permute-done | bytes 69664 | tf_op jit(solution)/shard_map/ppermute | solution.py:25
  34.5 2.9 %collective-permute-start.12 = (bf16[272,128]{1,0:T(8,128)(2,1)S(1)}, bf16[272,128]{1,0:T(8,128)(2,1)S(1)}, u32[]{:S(2)}, u32[]{:S(2)}) collective-permute-start(bf16[272,128]{1,0:T(8,128)(2,1)S(1)} %relay.1), channel_id=1, source_target_pairs={{0,8},{1,9},{2,10},{3,11},{4,12},{5,13},{6,14},{7,15},{8,0},{9,1},... | collective-permute-start | bytes 208904 | tf_op jit(solution)/shard_map/ppermute | solution.py:25
  37.4 2.4 %collective-permute-done.12.refs_1_ = bf16[272,128]{1,0:T(8,128)(2,1)S(1)} collective-permute-done((bf16[272,128]{1,0:T(8,128)(2,1)S(1)}, bf16[272,128]{1,0:T(8,128)(2,1)S(1)}, u32[]{:S(2)}, u32[]{:S(2)}) %collective-permute-start.12) | collective-permute-done | bytes 69664 | tf_op jit(solution)/shard_map/ppermute | solution.py:25
  39.9 1.2 %collective-permute-done.13.received = bf16[128,128]{1,0:T(8,128)(2,1)S(1)} collective-permute-done((bf16[128,128]{1,0:T(8,128)(2,1)S(1)}, bf16[128,128]{1,0:T(8,128)(2,1)S(1)}, u32[]{:S(2)}, u32[]{:S(2)}) %collective-permute-start.13) | collective-permute-done | bytes 32800 | tf_op jit(solution)/shard_map/ppermute | solution.py:25
  41.1 0.7 %finish.1 = (f32[256,128]{1,0:T(8,128)}, f32[8]{0:T(128)}) custom-call(f32[128,128]{1,0:T(8,128)S(1)} %get-tuple-element.35.own, bf16[128,128]{1,0:T(8,128)(2,1)S(1)} %collective-permute-done.13.received, f32[8,128]{1,0:T(8,128)S(1)} %get-tuple-element.37.mass), custom_call_target="tpu_custom_call" | custom-call | tf_op jit(solution)/shard_map/finish/pallas_call | solution.py:574
  (20 shorter events, 0.3 us)
Async XLA Ops:
  0.6 20.7 %copy-start.2 = (s32[8,2]{0,1:T(2,128)S(1)}, s32[8,2]{0,1:T(2,128)}, u32[]{:S(2)}) copy-start(s32[8,2]{0,1:T(2,128)} %param.13) | copy-start | bytes 196
  0.6 22.0 %copy-start = (f32[32]{0:T(128)S(1)}, f32[32]{0:T(128)}, u32[]{:S(2)}) copy-start(f32[32]{0:T(128)} %param.8) | copy-start | bytes 388
  0.7 22.0 %copy-start.1 = (s32[32]{0:T(128)S(1)}, s32[32]{0:T(128)}, u32[]{:S(2)}) copy-start(s32[32]{0:T(128)} %param.9) | copy-start | bytes 388
  9.0 13.6 %collective-permute-start = (bf16[32,16384]{1,0:T(8,128)(2,1)}, bf16[32,16384]{1,0:T(8,128)(2,1)S(1)}, u32[]{:S(2)}, u32[]{:S(2)}) collective-permute-start(bf16[32,16384]{1,0:T(8,128)(2,1)} %get-tuple-element.22), channel_id=1, source_target_pairs={{0,1},{1,0},{2,3},{3,2},{4,5},{5,4},{6,7},{7,6},{8,9},{9,8},{10,11... | collective-permute-start | bytes 3145736 | tf_op jit(solution)/shard_map/ppermute | solution.py:25
  9.5 7.6 %collective-permute-start.2 = (bf16[256,128]{1,0:T(8,128)(2,1)S(1)}, bf16[256,128]{1,0:T(8,128)(2,1)S(1)}, u32[]{:S(2)}, u32[]{:S(2)}) collective-permute-start(bf16[256,128]{1,0:T(8,128)(2,1)S(1)} %get-tuple-element.25.refs_0_), channel_id=1, source_target_pairs={{0,8},{1,9},{2,10},{3,11},{4,12},{5,13},{6,14},{7,15},{8,0},{9,1},... | collective-permute-start | bytes 196616 | tf_op jit(solution)/shard_map/ppermute | solution.py:25
  13.2 5.4 %collective-permute-start.1 = (bf16[256,128]{1,0:T(8,128)(2,1)S(1)}, bf16[256,128]{1,0:T(8,128)(2,1)S(1)}, u32[]{:S(2)}, u32[]{:S(2)}) collective-permute-start(bf16[256,128]{1,0:T(8,128)(2,1)S(1)} %get-tuple-element.25.refs_0_), channel_id=1, source_target_pairs={{0,4},{1,5},{2,6},{3,7},{4,0},{5,1},{6,2},{7,3},{8,12},{9,13},{10,... | collective-permute-start | bytes 196616 | tf_op jit(solution)/shard_map/ppermute | solution.py:25
  17.1 4.3 %collective-permute-start.3 = (bf16[256,128]{1,0:T(8,128)(2,1)S(1)}, bf16[256,128]{1,0:T(8,128)(2,1)S(1)}, u32[]{:S(2)}, u32[]{:S(2)}) collective-permute-start(bf16[256,128]{1,0:T(8,128)(2,1)S(1)} %collective-permute-done.2.refs_2_), channel_id=1, source_target_pairs={{0,4},{1,5},{2,6},{3,7},{4,0},{5,1},{6,2},{7,3},{8,12},{9,13},{10,... | collective-permute-start | bytes 196616 | tf_op jit(solution)/shard_map/ppermute | solution.py:25
  18.0 3.8 %collective-permute-start.4 = (bf16[256,128]{1,0:T(8,128)(2,1)S(1)}, bf16[256,128]{1,0:T(8,128)(2,1)S(1)}, u32[]{:S(2)}, u32[]{:S(2)}) collective-permute-start(bf16[256,128]{1,0:T(8,128)(2,1)S(1)} %get-tuple-element.25.refs_0_), channel_id=1, source_target_pairs={{0,1},{1,0},{2,3},{3,2},{4,5},{5,4},{6,7},{7,6},{8,9},{9,8},{10,11... | collective-permute-start | bytes 196616 | tf_op jit(solution)/shard_map/ppermute | solution.py:25
  18.0 3.9 %collective-permute-start.6 = (bf16[256,128]{1,0:T(8,128)(2,1)S(1)}, bf16[256,128]{1,0:T(8,128)(2,1)S(1)}, u32[]{:S(2)}, u32[]{:S(2)}) collective-permute-start(bf16[256,128]{1,0:T(8,128)(2,1)S(1)} %collective-permute-done.2.refs_2_), channel_id=1, source_target_pairs={{0,1},{1,0},{2,3},{3,2},{4,5},{5,4},{6,7},{7,6},{8,9},{9,8},{10,11... | collective-permute-start | bytes 196616 | tf_op jit(solution)/shard_map/ppermute | solution.py:25
  18.5 3.3 %collective-permute-start.5 = (bf16[256,128]{1,0:T(8,128)(2,1)S(1)}, bf16[256,128]{1,0:T(8,128)(2,1)S(1)}, u32[]{:S(2)}, u32[]{:S(2)}) collective-permute-start(bf16[256,128]{1,0:T(8,128)(2,1)S(1)} %collective-permute-done.1.refs_1_), channel_id=1, source_target_pairs={{0,1},{1,0},{2,3},{3,2},{4,5},{5,4},{6,7},{7,6},{8,9},{9,8},{10,11... | collective-permute-start | bytes 196616 | tf_op jit(solution)/shard_map/ppermute | solution.py:25
  21.4 1.3 %collective-permute-start.7 = (bf16[256,128]{1,0:T(8,128)(2,1)S(1)}, bf16[256,128]{1,0:T(8,128)(2,1)S(1)}, u32[]{:S(2)}, u32[]{:S(2)}) collective-permute-start(bf16[256,128]{1,0:T(8,128)(2,1)S(1)} %collective-permute-done.3.refs_3_), channel_id=1, source_target_pairs={{0,1},{1,0},{2,3},{3,2},{4,5},{5,4},{6,7},{7,6},{8,9},{9,8},{10,11... | collective-permute-start | bytes 196616 | tf_op jit(solution)/shard_map/ppermute | solution.py:25
  24.4 1.3 %collective-permute-start.8 = (f32[80,128]{1,0:T(8,128)S(1)}, f32[80,128]{1,0:T(8,128)S(1)}, u32[]{:S(2)}, u32[]{:S(2)}) collective-permute-start(f32[80,128]{1,0:T(8,128)S(1)} %correlate.1.mine), channel_id=1, source_target_pairs={{0,1},{1,0},{2,3},{3,2},{4,5},{5,4},{6,7},{7,6},{8,9},{9,8},{10,11... | collective-permute-start | bytes 122888 | tf_op jit(solution)/shard_map/ppermute | solution.py:25
  26.0 4.0 %collective-permute-start.9 = (bf16[144,128]{1,0:T(8,128)(2,1)S(1)}, bf16[144,128]{1,0:T(8,128)(2,1)S(1)}, u32[]{:S(2)}, u32[]{:S(2)}) collective-permute-start(bf16[144,128]{1,0:T(8,128)(2,1)S(1)} %get-tuple-element.28), channel_id=1, source_target_pairs={{0,2},{1,3},{2,0},{3,1},{4,6},{5,7},{6,4},{7,5},{8,10},{9,11},{10,... | collective-permute-start | bytes 110600 | tf_op jit(solution)/shard_map/ppermute | solution.py:25
  30.1 4.4 %collective-permute-start.11 = (bf16[272,128]{1,0:T(8,128)(2,1)S(1)}, bf16[272,128]{1,0:T(8,128)(2,1)S(1)}, u32[]{:S(2)}, u32[]{:S(2)}) collective-permute-start(bf16[272,128]{1,0:T(8,128)(2,1)S(1)} %get-tuple-element.34), channel_id=1, source_target_pairs={{0,4},{1,5},{2,6},{3,7},{4,0},{5,1},{6,2},{7,3},{8,12},{9,13},{10,... | collective-permute-start | bytes 208904 | tf_op jit(solution)/shard_map/ppermute | solution.py:25
  31.1 6.3 %collective-permute-start.10 = (bf16[272,128]{1,0:T(8,128)(2,1)S(1)}, bf16[272,128]{1,0:T(8,128)(2,1)S(1)}, u32[]{:S(2)}, u32[]{:S(2)}) collective-permute-start(bf16[272,128]{1,0:T(8,128)(2,1)S(1)} %get-tuple-element.32), channel_id=1, source_target_pairs={{0,4},{1,5},{2,6},{3,7},{4,0},{5,1},{6,2},{7,3},{8,12},{9,13},{10,... | collective-permute-start | bytes 208904 | tf_op jit(solution)/shard_map/ppermute | solution.py:25
  34.5 5.3 %collective-permute-start.12 = (bf16[272,128]{1,0:T(8,128)(2,1)S(1)}, bf16[272,128]{1,0:T(8,128)(2,1)S(1)}, u32[]{:S(2)}, u32[]{:S(2)}) collective-permute-start(bf16[272,128]{1,0:T(8,128)(2,1)S(1)} %relay.1), channel_id=1, source_target_pairs={{0,8},{1,9},{2,10},{3,11},{4,12},{5,13},{6,14},{7,15},{8,0},{9,1},... | collective-permute-start | bytes 208904 | tf_op jit(solution)/shard_map/ppermute | solution.py:25
  39.8 1.3 %collective-permute-start.13 = (bf16[128,128]{1,0:T(8,128)(2,1)S(1)}, bf16[128,128]{1,0:T(8,128)(2,1)S(1)}, u32[]{:S(2)}, u32[]{:S(2)}) collective-permute-start(bf16[128,128]{1,0:T(8,128)(2,1)S(1)} %get-tuple-element.36), channel_id=1, source_target_pairs={{0,1},{1,0},{2,3},{3,2},{4,5},{5,4},{6,7},{7,6},{8,9},{9,8},{10,11... | collective-permute-start | bytes 98312 | tf_op jit(solution)/shard_map/ppermute | solution.py:25

commit v6 on v5

--- a/solution.py
+++ b/solution.py
@@ -48,7 +48,7 @@
 
 def project_kernel(
     table_hbm, index_hbm, frac_hbm, images_hbm, out_ref, own_images, other_images,
-    table_in, index_ref, frac_ref, flat, wide, table, blended, even, odd, sems
+    table_in, index_ref, frac_ref, flat, wide, table, blended, sems
 ):
     device = lax.axis_index("particle")
     row_count = lax.axis_size("particle") // 2
@@ -109,17 +109,21 @@
         block = 2 * (step % blocks) + jnp.where(step < blocks, core, 1 - core)
         return pl.ds(pl.multiple_of(block * chunk, chunk), chunk)
 
-    def pick_lanes(step, target):
-        high = index_ref[:, place(step)] >> 7
-        high_ids = lax.broadcasted_iota(jnp.int32, (highs, chunk), 0)
-        one_hot = jnp.where(high_ids == high, 1.0, 0.0).astype(jnp.bfloat16)
-        target[...] = jnp.dot(table[...], one_hot, preferred_element_type=jnp.float32)
-
-    def blend(step, rows):
-        low = index_ref[:, place(step)] & (LANES - 1)
+    def body(step, carry):
+        index = index_ref[:, place(step)]
         frac = frac_ref[:, place(step)]
+        high = jnp.broadcast_to((index >> 7).astype(jnp.float32), (16, chunk)).astype(jnp.bfloat16)
+        low = index & (LANES - 1)
         group = (low * 147) >> 10
         first = low - 7 * group
+        one_hot = jnp.concatenate(
+            [
+                jnp.where(high == (ids16 + 16 * k).astype(jnp.bfloat16), ones16, zeros16)
+                for k in range(highs // 16)
+            ],
+            axis=0,
+        )
+        rows = jnp.dot(table[...], one_hot, preferred_element_type=jnp.float32)
         group = jnp.broadcast_to(group, (8, chunk))
         masks = [(group & (1 << bit)) != 0 for bit in range((groups - 1).bit_length())]
         ids = lax.broadcasted_iota(jnp.int32, (8, chunk), 0)
@@ -127,26 +131,18 @@
         for comp in range(2):
             start = comp * stride
             picked = tree_select(
-                [rows[start + 8 * g : start + 8 * g + 8, :] for g in range(groups)], masks
+                [rows[start + 8 * g : start + 8 * g + 8] for g in range(groups)], masks
             )
             value = jnp.sum(picked * weight, axis=0, keepdims=True)
             first_row = (step // blocks * 2 + comp) * blocks * BLOCK + step % blocks * BLOCK
             for k in range(BLOCK):
                 blended[pl.ds(first_row + k, 1), :] = value[:, k * LANES : (k + 1) * LANES]
-
-    pick_lanes(0, even)
-
-    def body(pair, carry):
-        pick_lanes(2 * pair + 1, odd)
-        blend(2 * pair, even)
-        pick_lanes(2 * pair + 2, even)
-        blend(2 * pair + 1, odd)
         return carry
 
-    lax.fori_loop(0, blocks - 1, body, 0)
-    pick_lanes(2 * blocks - 1, odd)
-    blend(2 * blocks - 2, even)
-    blend(2 * blocks - 1, odd)
+    ids16 = lax.broadcasted_iota(jnp.int32, (16, chunk), 0).astype(jnp.float32)
+    ones16 = jnp.ones((16, chunk), jnp.bfloat16)
+    zeros16 = jnp.zeros((16, chunk), jnp.bfloat16)
+    lax.fori_loop(0, 2 * blocks, body, 0, unroll=2)
     out_ref[...] = blended[...].astype(jnp.bfloat16)
     for copy in copies[3:]:
         copy.wait()
@@ -173,8 +169,6 @@
             pltpu.VMEM((LANES + 8, highs), jnp.float32),
             pltpu.VMEM((16 * groups, highs), jnp.bfloat16),
             pltpu.VMEM((rows, LANES), jnp.float32),
-            pltpu.VMEM((16 * groups, chunk), jnp.float32),
-            pltpu.VMEM((16 * groups, chunk), jnp.float32),
             pltpu.SemaphoreType.DMA((3 + 2 * pixels // chunk,)),
         ],
         compiler_params=pltpu.CompilerParams(vmem_limit_bytes=16 * MIB),
@@ -486,46 +480,6 @@
     )(sums, low, low_received, mass)
 
 
-def relay_kernel(own, received, out):
-    rows = out.shape[0] - MASS_ROWS
-    total = own[0:rows, :].astype(jnp.float32) + received[0:rows, :].astype(jnp.float32)
-    out[0:rows, :] = total.astype(out.dtype)
-    out[rows:, :] = split_mass(joined_mass(own[rows:, :]) + joined_mass(received[rows:, :]))
-
-
-def relay(own, received):
-    return pl.pallas_call(
-        relay_kernel,
-        in_specs=whole_vmem(2),
-        out_specs=pl.BlockSpec(memory_space=pltpu.VMEM),
-        out_shape=jax.ShapeDtypeStruct(own.shape, own.dtype),
-        compiler_params=pltpu.CompilerParams(vmem_limit_bytes=16 * MIB),
-        name="relay",
-    )(own, received)
-
-
-def gather_chips(row, chips):
-    rows = {0: row}
-    bit = chips // 2
-    while bit:
-        rows.update({m ^ bit: exchange(rows[m], 4 * bit) for m in list(rows)})
-        bit //= 2
-    return [rows[m] for m in range(chips)]
-
-
-def scatter_chips(sends, chips):
-    held = dict(enumerate(sends, start=1))
-    arrived = []
-    bit = 1
-    while bit < chips:
-        away = {m: exchange(held.pop(m), 4 * bit) for m in sorted(held, reverse=True) if m & bit}
-        arrived.append(away.pop(bit))
-        for m, value in away.items():
-            held[m ^ bit] = relay(held[m ^ bit], value)
-        bit *= 2
-    return arrived
-
-
 def merge_kernel(own, mass, *refs):
     received, (keep, send, mass_out) = refs[:-3], refs[-3:]
     rows = own.shape[0]
@@ -592,7 +546,7 @@
     chips = slots // 2
     parts, width = images.shape
     own_row, own_images, other_images = project_row(class_refs, interp_index, interp_frac, images)
-    rows = gather_chips(own_row, chips)
+    rows = [own_row] + [exchange(own_row, 4 * m) for m in range(1, chips)]
     rows = rows + [exchange(row, 1) for row in rows]
     images_received = exchange(other_images, 1)
     cos_table, sin_table = phase_tables(shift_grid, width // 4)
@@ -611,7 +565,7 @@
     low_received = exchange(low_send, 2)
     sums = backproject(weights, own_images, images_received, cos_table, sin_table, slots)
     folded = fold(sums, low, low_received, mass, slots)
-    received = scatter_chips(folded[2:], chips)
+    received = [exchange(send, 4 * m) for m, send in enumerate(folded[2:], start=1)]
     keep, send, mass = merge(folded[0], folded[1], received)
     back, class_mass = finish(
         keep, exchange(send, 1), mass, 1.0 / math.sqrt(parts), CLASSES / (parts * dev_count)

time: 41.9 us -> 39.6 us (0.945)
  Pallas kernels: 13.2 us -> 11.6 us
  starting transfers between devices: 14.1 us -> 12.5 us
  waiting for transfers between devices: 13.7 us -> 14.5 us
    ppermute x14, starting transfers between devices: 14.1 us -> 12.5 us  [exchange(): return lax.ppermute(value, 'particle', pairs)]
    pallas_call x1, Pallas kernels: 8.32 us -> 6.81 us  [project_row(): pl.pallas_call(project_kernel, in_specs=[pl.BlockSpec(memory_space=pltpu....]
    ppermute x14, waiting for transfers between devices: 13.7 us -> 14.5 us  [exchange(): return lax.ppermute(value, 'particle', pairs)]
  transfers between devices with their start and end apart: 14 -> 14, of which waited for: 8 -> 10; matrix products, arithmetic and copies ran while one was open for 0% -> 0% of each run, Pallas kernels for 5% -> 5%
where the time goes in v6:
time: 39.6 us; the launch traced here: 39.5 us
  waiting for transfers between devices  14.5 us (37%)
  starting transfers between devices  12.5 us (32%)
  Pallas kernels  11.6 us (29%)
  between operations  0.74 us (2%)
    ppermute x14, waiting for transfers between devices, exchange(): return lax.ppermute(value, 'particle', pairs)  14.5 us
    ppermute x14, starting transfers between devices, exchange(): return lax.ppermute(value, 'particle', pairs)  12.5 us
    pallas_call x1, Pallas kernels, project_row(): pl.pallas_call(project_kernel, in_specs=[pl.BlockSpec(memory_space=pltpu....  6.81 us
    pallas_call x1, Pallas kernels, correlate(): pl.pallas_call(functools.partial(correlate_kernel, chunk=2048), in_specs=...  1.73 us
    pallas_call x1, Pallas kernels, backproject(): pl.pallas_call(functools.partial(backproject_kernel, slots=slots, chunk=L...  1.55 us
  transfers between devices with their start and end apart: 14, of which 10 were waited for; matrix products, arithmetic and copies ran while one was open for 0% of the time, Pallas kernels for 5%

profile of v6, /device:TPU:0, one launch (start us, length us, event | category | flops | bytes accessed | tf_op | source)
XLA Modules:
  0.0 39.5 jit_solution(15067045281471233446)
XLA Ops:
  0.7 6.8 %project_row.1 = (bf16[256,128]{1,0:T(8,128)(2,1)S(1)}, bf16[32,16384]{1,0:T(8,128)(2,1)S(1)}, bf16[32,16384]{1,0:T(8,128)(2,1)}) custom-call(bf16[2,8,2,32768]{3,2,1,0:T(2,128)(2,1)} %table_hbm.1, s32[1,16384]{1,0:T(1,128)} %index_hbm.1, f32[1,16384]{1,0:T(1,128)} %frac_hbm.1, bf16[32,32768]{1,0:T(8,128)(2,1)} %images_hbm.1), custom_call_target="tpu_custom_call" | custom-call | tf_op jit(solution)/shard_map/project_row/pallas_call | solution.py:159
  7.5 0.5 %collective-permute-start = (bf16[32,16384]{1,0:T(8,128)(2,1)}, bf16[32,16384]{1,0:T(8,128)(2,1)S(1)}, u32[]{:S(2)}, u32[]{:S(2)}) collective-permute-start(bf16[32,16384]{1,0:T(8,128)(2,1)} %get-tuple-element.22), channel_id=1, source_target_pairs={{0,1},{1,0},{2,3},{3,2},{4,5},{5,4},{6,7},{7,6},{8,9},{9,8},{10,11... | collective-permute-start | bytes 3145736 | tf_op jit(solution)/shard_map/ppermute | solution.py:25
  8.0 2.6 %collective-permute-start.1 = (bf16[256,128]{1,0:T(8,128)(2,1)S(1)}, bf16[256,128]{1,0:T(8,128)(2,1)S(1)}, u32[]{:S(2)}, u32[]{:S(2)}) collective-permute-start(bf16[256,128]{1,0:T(8,128)(2,1)S(1)} %get-tuple-element.25.refs_0_), channel_id=1, source_target_pairs={{0,4},{1,5},{2,6},{3,7},{4,0},{5,1},{6,2},{7,3},{8,12},{9,13},{10,... | collective-permute-start | bytes 196616 | tf_op jit(solution)/shard_map/ppermute | solution.py:25
  10.6 2.6 %collective-permute-start.2 = (bf16[256,128]{1,0:T(8,128)(2,1)S(1)}, bf16[256,128]{1,0:T(8,128)(2,1)S(1)}, u32[]{:S(2)}, u32[]{:S(2)}) collective-permute-start(bf16[256,128]{1,0:T(8,128)(2,1)S(1)} %get-tuple-element.25.refs_0_), channel_id=1, source_target_pairs={{0,8},{1,9},{2,10},{3,11},{4,12},{5,13},{6,14},{7,15},{8,0},{9,1},... | collective-permute-start | bytes 196616 | tf_op jit(solution)/shard_map/ppermute | solution.py:25
  13.3 0.4 %collective-permute-start.5 = (bf16[256,128]{1,0:T(8,128)(2,1)S(1)}, bf16[256,128]{1,0:T(8,128)(2,1)S(1)}, u32[]{:S(2)}, u32[]{:S(2)}) collective-permute-start(bf16[256,128]{1,0:T(8,128)(2,1)S(1)} %collective-permute-done.1.refs_1_), channel_id=1, source_target_pairs={{0,1},{1,0},{2,3},{3,2},{4,5},{5,4},{6,7},{7,6},{8,9},{9,8},{10,11... | collective-permute-start | bytes 196616 | tf_op jit(solution)/shard_map/ppermute | solution.py:25
  13.8 4.6 %collective-permute-done.2.refs_2_ = bf16[256,128]{1,0:T(8,128)(2,1)S(1)} collective-permute-done((bf16[256,128]{1,0:T(8,128)(2,1)S(1)}, bf16[256,128]{1,0:T(8,128)(2,1)S(1)}, u32[]{:S(2)}, u32[]{:S(2)}) %collective-permute-start.2) | collective-permute-done | bytes 65568 | tf_op jit(solution)/shard_map/ppermute | solution.py:25
  18.4 1.0 %collective-permute-done.3.refs_3_ = bf16[256,128]{1,0:T(8,128)(2,1)S(1)} collective-permute-done((bf16[256,128]{1,0:T(8,128)(2,1)S(1)}, bf16[256,128]{1,0:T(8,128)(2,1)S(1)}, u32[]{:S(2)}, u32[]{:S(2)}) %collective-permute-start.3) | collective-permute-done | bytes 65568 | tf_op jit(solution)/shard_map/ppermute | solution.py:25
  19.4 0.4 %phase_tables.1 = (f32[8,8192]{1,0:T(8,128)S(1)}, f32[8,8192]{1,0:T(8,128)S(1)}) custom-call(s32[8,2]{1,0:T(8,128)S(1)} %copy.9.shift_ref), custom_call_target="tpu_custom_call" | custom-call | flops 2000000 | bytes 2000000 | tf_op jit(solution)/shard_map/phase_tables/pallas_call | solution.py:216
  19.9 0.7 %collective-permute-done.7.refs_7_ = bf16[256,128]{1,0:T(8,128)(2,1)S(1)} collective-permute-done((bf16[256,128]{1,0:T(8,128)(2,1)S(1)}, bf16[256,128]{1,0:T(8,128)(2,1)S(1)}, u32[]{:S(2)}, u32[]{:S(2)}) %collective-permute-start.7) | collective-permute-done | bytes 65568 | tf_op jit(solution)/shard_map/ppermute | solution.py:25
  20.6 1.7 %correlate.1.mine = f32[80,128]{1,0:T(8,128)S(1)} custom-call(bf16[32,16384]{1,0:T(8,128)(2,1)S(1)} %get-tuple-element.21.own_images, bf16[32,16384]{1,0:T(8,128)(2,1)S(1)} %collective-permute-done.other_images, f32[1,32]{1,0:T(1,128)S(1)} %bitcast.3, s32[1,32]{1,0:T(1,128)S(1)} %bitcast.4, f32[8,8192]{1,0:T(8,128)S(1)} %get-tuple-element.23.cos_ref, ...), custom_call_target="tpu_custom_call" | custom-call | tf_op jit(solution)/shard_map/correlate/pallas_call | solution.py:301
  22.4 0.2 collective-permute-start.8
  22.6 1.1 %collective-permute-done.8.received = f32[80,128]{1,0:T(8,128)S(1)} collective-permute-done((f32[80,128]{1,0:T(8,128)S(1)}, f32[80,128]{1,0:T(8,128)S(1)}, u32[]{:S(2)}, u32[]{:S(2)}) %collective-permute-start.8) | collective-permute-done | bytes 40992 | tf_op jit(solution)/shard_map/ppermute | solution.py:25
  23.6 0.4 posterior.1
  24.0 1.6 %collective-permute-start.9 = (bf16[144,128]{1,0:T(8,128)(2,1)S(1)}, bf16[144,128]{1,0:T(8,128)(2,1)S(1)}, u32[]{:S(2)}, u32[]{:S(2)}) collective-permute-start(bf16[144,128]{1,0:T(8,128)(2,1)S(1)} %get-tuple-element.28), channel_id=1, source_target_pairs={{0,2},{1,3},{2,0},{3,1},{4,6},{5,7},{6,4},{7,5},{8,10},{9,11},{10,... | collective-permute-start | bytes 110600 | tf_op jit(solution)/shard_map/ppermute | solution.py:25
  25.6 1.6 %backproject.1.sums = f32[1024,128]{1,0:T(8,128)S(1)} custom-call(bf16[64,64]{1,0:T(8,128)(2,1)S(1)} %get-tuple-element.26.weight_ref, bf16[32,16384]{1,0:T(8,128)(2,1)S(1)} %get-tuple-element.21.own_images, bf16[32,16384]{1,0:T(8,128)(2,1)S(1)} %collective-permute-done.other_images, f32[8,8192]{1,0:T(8,128)S(1)} %get-tuple-element.23.cos_ref, ...), custom_call_target="tpu_custom_call" | custom-call | flops 20000000 | bytes 20000000 | tf_op jit(solution)/shard_map/backproject/pallas_call | solution.py:430
  27.1 0.9 %collective-permute-done.9.low_received = bf16[144,128]{1,0:T(8,128)(2,1)S(1)} collective-permute-done((bf16[144,128]{1,0:T(8,128)(2,1)S(1)}, bf16[144,128]{1,0:T(8,128)(2,1)S(1)}, u32[]{:S(2)}, u32[]{:S(2)}) %collective-permute-start.9) | collective-permute-done | bytes 36896 | tf_op jit(solution)/shard_map/ppermute | solution.py:25
  28.1 1.3 %collective-permute-start.10 = (bf16[272,128]{1,0:T(8,128)(2,1)S(1)}, bf16[272,128]{1,0:T(8,128)(2,1)S(1)}, u32[]{:S(2)}, u32[]{:S(2)}) collective-permute-start(bf16[272,128]{1,0:T(8,128)(2,1)S(1)} %get-tuple-element.32), channel_id=1, source_target_pairs={{0,4},{1,5},{2,6},{3,7},{4,0},{5,1},{6,2},{7,3},{8,12},{9,13},{10,... | collective-permute-start | bytes 208904 | tf_op jit(solution)/shard_map/ppermute | solution.py:25
  29.4 1.9 %collective-permute-start.11 = (bf16[272,128]{1,0:T(8,128)(2,1)S(1)}, bf16[272,128]{1,0:T(8,128)(2,1)S(1)}, u32[]{:S(2)}, u32[]{:S(2)}) collective-permute-start(bf16[272,128]{1,0:T(8,128)(2,1)S(1)} %get-tuple-element.33), channel_id=1, source_target_pairs={{0,8},{1,9},{2,10},{3,11},{4,12},{5,13},{6,14},{7,15},{8,0},{9,1},... | collective-permute-start | bytes 208904 | tf_op jit(solution)/shard_map/ppermute | solution.py:25
  31.2 1.3 %collective-permute-start.12 = (bf16[272,128]{1,0:T(8,128)(2,1)S(1)}, bf16[272,128]{1,0:T(8,128)(2,1)S(1)}, u32[]{:S(2)}, u32[]{:S(2)}) collective-permute-start(bf16[272,128]{1,0:T(8,128)(2,1)S(1)} %get-tuple-element.34), channel_id=1, source_target_pairs={{0,12},{1,13},{2,14},{3,15},{4,8},{5,9},{6,10},{7,11},{8,4},{9,5},... | collective-permute-start | bytes 208904 | tf_op jit(solution)/shard_map/ppermute | solution.py:25
  32.5 0.4 collective-permute-done.10.refs_0_
  32.9 3.1 %collective-permute-done.11.refs_1_ = bf16[272,128]{1,0:T(8,128)(2,1)S(1)} collective-permute-done((bf16[272,128]{1,0:T(8,128)(2,1)S(1)}, bf16[272,128]{1,0:T(8,128)(2,1)S(1)}, u32[]{:S(2)}, u32[]{:S(2)}) %collective-permute-start.11) | collective-permute-done | bytes 69664 | tf_op jit(solution)/shard_map/ppermute | solution.py:25
  36.1 1.4 %collective-permute-done.12.refs_2_ = bf16[272,128]{1,0:T(8,128)(2,1)S(1)} collective-permute-done((bf16[272,128]{1,0:T(8,128)(2,1)S(1)}, bf16[272,128]{1,0:T(8,128)(2,1)S(1)}, u32[]{:S(2)}, u32[]{:S(2)}) %collective-permute-start.12) | collective-permute-done | bytes 69664 | tf_op jit(solution)/shard_map/ppermute | solution.py:25
  37.6 1.2 %collective-permute-done.13.received = bf16[128,128]{1,0:T(8,128)(2,1)S(1)} collective-permute-done((bf16[128,128]{1,0:T(8,128)(2,1)S(1)}, bf16[128,128]{1,0:T(8,128)(2,1)S(1)}, u32[]{:S(2)}, u32[]{:S(2)}) %collective-permute-start.13) | collective-permute-done | bytes 32800 | tf_op jit(solution)/shard_map/ppermute | solution.py:25
  38.8 0.7 %finish.1 = (f32[256,128]{1,0:T(8,128)}, f32[8]{0:T(128)}) custom-call(f32[128,128]{1,0:T(8,128)S(1)} %get-tuple-element.35.own, bf16[128,128]{1,0:T(8,128)(2,1)S(1)} %collective-permute-done.13.received, f32[8,128]{1,0:T(8,128)S(1)} %get-tuple-element.37.mass), custom_call_target="tpu_custom_call" | custom-call | tf_op jit(solution)/shard_map/finish/pallas_call | solution.py:528
  (19 shorter events, 0.4 us)
Async XLA Ops:
  0.6 18.7 %copy-start.2 = (s32[8,2]{0,1:T(2,128)S(1)}, s32[8,2]{0,1:T(2,128)}, u32[]{:S(2)}) copy-start(s32[8,2]{0,1:T(2,128)} %param.13) | copy-start | bytes 196
  0.6 20.0 %copy-start = (f32[32]{0:T(128)S(1)}, f32[32]{0:T(128)}, u32[]{:S(2)}) copy-start(f32[32]{0:T(128)} %param.8) | copy-start | bytes 388
  0.7 20.0 %copy-start.1 = (s32[32]{0:T(128)S(1)}, s32[32]{0:T(128)}, u32[]{:S(2)}) copy-start(s32[32]{0:T(128)} %param.9) | copy-start | bytes 388
  7.5 13.1 %collective-permute-start = (bf16[32,16384]{1,0:T(8,128)(2,1)}, bf16[32,16384]{1,0:T(8,128)(2,1)S(1)}, u32[]{:S(2)}, u32[]{:S(2)}) collective-permute-start(bf16[32,16384]{1,0:T(8,128)(2,1)} %get-tuple-element.22), channel_id=1, source_target_pairs={{0,1},{1,0},{2,3},{3,2},{4,5},{5,4},{6,7},{7,6},{8,9},{9,8},{10,11... | collective-permute-start | bytes 3145736 | tf_op jit(solution)/shard_map/ppermute | solution.py:25
  8.0 5.3 %collective-permute-start.1 = (bf16[256,128]{1,0:T(8,128)(2,1)S(1)}, bf16[256,128]{1,0:T(8,128)(2,1)S(1)}, u32[]{:S(2)}, u32[]{:S(2)}) collective-permute-start(bf16[256,128]{1,0:T(8,128)(2,1)S(1)} %get-tuple-element.25.refs_0_), channel_id=1, source_target_pairs={{0,4},{1,5},{2,6},{3,7},{4,0},{5,1},{6,2},{7,3},{8,12},{9,13},{10,... | collective-permute-start | bytes 196616 | tf_op jit(solution)/shard_map/ppermute | solution.py:25
  10.6 7.7 %collective-permute-start.2 = (bf16[256,128]{1,0:T(8,128)(2,1)S(1)}, bf16[256,128]{1,0:T(8,128)(2,1)S(1)}, u32[]{:S(2)}, u32[]{:S(2)}) collective-permute-start(bf16[256,128]{1,0:T(8,128)(2,1)S(1)} %get-tuple-element.25.refs_0_), channel_id=1, source_target_pairs={{0,8},{1,9},{2,10},{3,11},{4,12},{5,13},{6,14},{7,15},{8,0},{9,1},... | collective-permute-start | bytes 196616 | tf_op jit(solution)/shard_map/ppermute | solution.py:25
  13.2 6.1 %collective-permute-start.3 = (bf16[256,128]{1,0:T(8,128)(2,1)S(1)}, bf16[256,128]{1,0:T(8,128)(2,1)S(1)}, u32[]{:S(2)}, u32[]{:S(2)}) collective-permute-start(bf16[256,128]{1,0:T(8,128)(2,1)S(1)} %get-tuple-element.25.refs_0_), channel_id=1, source_target_pairs={{0,12},{1,13},{2,14},{3,15},{4,8},{5,9},{6,10},{7,11},{8,4},{9,5},... | collective-permute-start | bytes 196616 | tf_op jit(solution)/shard_map/ppermute | solution.py:25
  13.2 6.6 %collective-permute-start.4 = (bf16[256,128]{1,0:T(8,128)(2,1)S(1)}, bf16[256,128]{1,0:T(8,128)(2,1)S(1)}, u32[]{:S(2)}, u32[]{:S(2)}) collective-permute-start(bf16[256,128]{1,0:T(8,128)(2,1)S(1)} %get-tuple-element.25.refs_0_), channel_id=1, source_target_pairs={{0,1},{1,0},{2,3},{3,2},{4,5},{5,4},{6,7},{7,6},{8,9},{9,8},{10,11... | collective-permute-start | bytes 196616 | tf_op jit(solution)/shard_map/ppermute | solution.py:25
  13.3 6.5 %collective-permute-start.5 = (bf16[256,128]{1,0:T(8,128)(2,1)S(1)}, bf16[256,128]{1,0:T(8,128)(2,1)S(1)}, u32[]{:S(2)}, u32[]{:S(2)}) collective-permute-start(bf16[256,128]{1,0:T(8,128)(2,1)S(1)} %collective-permute-done.1.refs_1_), channel_id=1, source_target_pairs={{0,1},{1,0},{2,3},{3,2},{4,5},{5,4},{6,7},{7,6},{8,9},{9,8},{10,11... | collective-permute-start | bytes 196616 | tf_op jit(solution)/shard_map/ppermute | solution.py:25
  18.4 1.5 %collective-permute-start.6 = (bf16[256,128]{1,0:T(8,128)(2,1)S(1)}, bf16[256,128]{1,0:T(8,128)(2,1)S(1)}, u32[]{:S(2)}, u32[]{:S(2)}) collective-permute-start(bf16[256,128]{1,0:T(8,128)(2,1)S(1)} %collective-permute-done.2.refs_2_), channel_id=1, source_target_pairs={{0,1},{1,0},{2,3},{3,2},{4,5},{5,4},{6,7},{7,6},{8,9},{9,8},{10,11... | collective-permute-start | bytes 196616 | tf_op jit(solution)/shard_map/ppermute | solution.py:25
  19.4 1.3 %collective-permute-start.7 = (bf16[256,128]{1,0:T(8,128)(2,1)S(1)}, bf16[256,128]{1,0:T(8,128)(2,1)S(1)}, u32[]{:S(2)}, u32[]{:S(2)}) collective-permute-start(bf16[256,128]{1,0:T(8,128)(2,1)S(1)} %collective-permute-done.3.refs_3_), channel_id=1, source_target_pairs={{0,1},{1,0},{2,3},{3,2},{4,5},{5,4},{6,7},{7,6},{8,9},{9,8},{10,11... | collective-permute-start | bytes 196616 | tf_op jit(solution)/shard_map/ppermute | solution.py:25
  22.4 1.3 %collective-permute-start.8 = (f32[80,128]{1,0:T(8,128)S(1)}, f32[80,128]{1,0:T(8,128)S(1)}, u32[]{:S(2)}, u32[]{:S(2)}) collective-permute-start(f32[80,128]{1,0:T(8,128)S(1)} %correlate.1.mine), channel_id=1, source_target_pairs={{0,1},{1,0},{2,3},{3,2},{4,5},{5,4},{6,7},{7,6},{8,9},{9,8},{10,11... | collective-permute-start | bytes 122888 | tf_op jit(solution)/shard_map/ppermute | solution.py:25
  24.0 4.0 %collective-permute-start.9 = (bf16[144,128]{1,0:T(8,128)(2,1)S(1)}, bf16[144,128]{1,0:T(8,128)(2,1)S(1)}, u32[]{:S(2)}, u32[]{:S(2)}) collective-permute-start(bf16[144,128]{1,0:T(8,128)(2,1)S(1)} %get-tuple-element.28), channel_id=1, source_target_pairs={{0,2},{1,3},{2,0},{3,1},{4,6},{5,7},{6,4},{7,5},{8,10},{9,11},{10,... | collective-permute-start | bytes 110600 | tf_op jit(solution)/shard_map/ppermute | solution.py:25
  28.1 4.8 %collective-permute-start.10 = (bf16[272,128]{1,0:T(8,128)(2,1)S(1)}, bf16[272,128]{1,0:T(8,128)(2,1)S(1)}, u32[]{:S(2)}, u32[]{:S(2)}) collective-permute-start(bf16[272,128]{1,0:T(8,128)(2,1)S(1)} %get-tuple-element.32), channel_id=1, source_target_pairs={{0,4},{1,5},{2,6},{3,7},{4,0},{5,1},{6,2},{7,3},{8,12},{9,13},{10,... | collective-permute-start | bytes 208904 | tf_op jit(solution)/shard_map/ppermute | solution.py:25
  29.4 6.7 %collective-permute-start.11 = (bf16[272,128]{1,0:T(8,128)(2,1)S(1)}, bf16[272,128]{1,0:T(8,128)(2,1)S(1)}, u32[]{:S(2)}, u32[]{:S(2)}) collective-permute-start(bf16[272,128]{1,0:T(8,128)(2,1)S(1)} %get-tuple-element.33), channel_id=1, source_target_pairs={{0,8},{1,9},{2,10},{3,11},{4,12},{5,13},{6,14},{7,15},{8,0},{9,1},... | collective-permute-start | bytes 208904 | tf_op jit(solution)/shard_map/ppermute | solution.py:25
  31.2 6.2 %collective-permute-start.12 = (bf16[272,128]{1,0:T(8,128)(2,1)S(1)}, bf16[272,128]{1,0:T(8,128)(2,1)S(1)}, u32[]{:S(2)}, u32[]{:S(2)}) collective-permute-start(bf16[272,128]{1,0:T(8,128)(2,1)S(1)} %get-tuple-element.34), channel_id=1, source_target_pairs={{0,12},{1,13},{2,14},{3,15},{4,8},{5,9},{6,10},{7,11},{8,4},{9,5},... | collective-permute-start | bytes 208904 | tf_op jit(solution)/shard_map/ppermute | solution.py:25
  37.5 1.3 %collective-permute-start.13 = (bf16[128,128]{1,0:T(8,128)(2,1)S(1)}, bf16[128,128]{1,0:T(8,128)(2,1)S(1)}, u32[]{:S(2)}, u32[]{:S(2)}) collective-permute-start(bf16[128,128]{1,0:T(8,128)(2,1)S(1)} %get-tuple-element.36), channel_id=1, source_target_pairs={{0,1},{1,0},{2,3},{3,2},{4,5},{5,4},{6,7},{7,6},{8,9},{9,8},{10,11... | collective-permute-start | bytes 98312 | tf_op jit(solution)/shard_map/ppermute | solution.py:25

commit v7 on v4

--- a/solution.py
+++ b/solution.py
@@ -366,13 +366,9 @@
     return real, imag
 
 
-def posterior_kernel(
-    mine, received, own_images, other_images, cos_ref, sin_ref,
-    weight_ref, low_ref, low_send, own_mass, *, slots
-):
+def posterior_kernel(mine, received, weight_ref, own_mass, *, slots, shifts, pixels):
     device = lax.axis_index("particle")
-    shifts, width = cos_ref.shape
-    parts = own_images.shape[0]
+    parts = weight_ref.shape[1] // 2
     combos = shifts * slots
     theirs = received[...]
     lane = lax.broadcasted_iota(jnp.int32, theirs.shape, 1)
@@ -385,7 +381,7 @@
     assigned = joint[combos + slots + 1 : combos + slots + 2].astype(jnp.int32)
     slot_class = slot_rows(device, slots) // (slots // CLASSES)
     match = (slot_class == assigned).astype(jnp.float32) * PRIOR_REWARD
-    likelihood_scale = 1.0 / math.sqrt(4 * width)
+    likelihood_scale = 1.0 / math.sqrt(2 * pixels)
     logits = [
         precision * (joint[s * slots : (s + 1) * slots] - 0.5 * power) * likelihood_scale + match
         for s in range(shifts)
@@ -407,38 +403,25 @@
     )
     own_mass[...] = jnp.broadcast_to(mass_row, own_mass.shape)
 
-    low = LOW_TILES * LANES
-    real, imag = rotate_back(
-        weights, own_images, other_images, cos_ref, sin_ref, slice(0, low), slice(width, width + low), slots
-    )
-    for k in range(LOW_TILES):
-        piece = slice(k * LANES, (k + 1) * LANES)
-        low_ref[pl.ds(k, slots, stride=2 * LOW_TILES), :] = real[:, piece]
-        low_ref[pl.ds(LOW_TILES + k, slots, stride=2 * LOW_TILES), :] = imag[:, piece]
-    low_body = low_ref.shape[0]
-    low_send[0:low_body, :] = low_ref[...].astype(jnp.bfloat16)
-    low_send[low_body:, :] = split_mass(mass_row)
-
-
-def posterior(mine, received, own_images, other_images, cos_table, sin_table, slots):
-    shifts = cos_table.shape[0]
-    low = slots * 2 * LOW_TILES
-    return pl.pallas_call(
-        functools.partial(posterior_kernel, slots=slots),
-        in_specs=whole_vmem(6),
-        out_specs=whole_vmem(4),
+
+def posterior(mine, received, slots, shifts, parts, pixels):
+    return pl.pallas_call(
+        functools.partial(posterior_kernel, slots=slots, shifts=shifts, pixels=pixels),
+        in_specs=whole_vmem(2),
+        out_specs=whole_vmem(2),
         out_shape=[
-            jax.ShapeDtypeStruct((shifts * slots, 2 * own_images.shape[0]), jnp.bfloat16),
-            jax.ShapeDtypeStruct((low, LANES), jnp.float32),
-            jax.ShapeDtypeStruct((low + MASS_ROWS, LANES), jnp.bfloat16),
+            jax.ShapeDtypeStruct((shifts * slots, 2 * parts), jnp.bfloat16),
             jax.ShapeDtypeStruct((8, LANES), jnp.float32),
         ],
         compiler_params=pltpu.CompilerParams(vmem_limit_bytes=(14 + slots // 2) * MIB),
         name="posterior",
-    )(mine, received, own_images, other_images, cos_table, sin_table)
-
-
-def backproject_kernel(weight_ref, own_images, other_images, cos_ref, sin_ref, sums, *, slots, chunk):
+    )(mine, received)
+
+
+def backproject_kernel(
+    weight_ref, mass, own_images, other_images, cos_ref, sin_ref, own, *refs, slots, chunk, unroll
+):
+    sends, sums = refs[:-1], refs[-1]
     width = cos_ref.shape[1]
     tiles = width // LANES
     per_row = 2 * tiles
@@ -446,10 +429,9 @@
     weights = weight_ref[...]
 
     def body(step, carry):
-        first = LOW_TILES + step * chunk_tiles
-        start = pl.multiple_of(first * LANES, LOW_TILES * LANES)
-        where = pl.ds(start, chunk)
-        imag_where = pl.ds(pl.multiple_of(width + start, LOW_TILES * LANES), chunk)
+        first = step * chunk_tiles
+        where = pl.ds(pl.multiple_of(step * chunk, chunk), chunk)
+        imag_where = pl.ds(pl.multiple_of(width + step * chunk, chunk), chunk)
         real, imag = rotate_back(
             weights, own_images, other_images, cos_ref, sin_ref, where, imag_where, slots
         )
@@ -459,112 +441,105 @@
             sums[pl.ds(tiles + first + k, slots, stride=per_row), :] = imag[:, piece]
         return carry
 
-    lax.fori_loop(0, (tiles - LOW_TILES) // chunk_tiles, body, 0)
-
-
-def backproject(weights, own_images, other_images, cos_table, sin_table, slots):
+    lax.fori_loop(0, width // chunk, body, 0, unroll=unroll)
+    own[...] = sums[0 : 2 * per_row, :]
+    block = split_mass(mass[0:1, :])
+    for m, send in enumerate(sends, start=1):
+        send[0 : 2 * per_row, :] = sums[2 * m * per_row : 2 * (m + 1) * per_row, :].astype(
+            jnp.bfloat16
+        )
+        send[2 * per_row :, :] = block
+
+
+def backproject(weights, mass, own_images, other_images, cos_table, sin_table, slots):
     width = cos_table.shape[1]
-    rows = slots * 2 * width // LANES
-    return pl.pallas_call(
-        functools.partial(backproject_kernel, slots=slots, chunk=LOW_TILES * LANES),
-        in_specs=whole_vmem(5),
-        out_specs=pl.BlockSpec(memory_space=pltpu.VMEM),
-        out_shape=jax.ShapeDtypeStruct((rows, LANES), jnp.float32),
+    rows = 2 * 2 * width // LANES
+    chips = slots // 2
+    return pl.pallas_call(
+        functools.partial(
+            backproject_kernel, slots=slots, chunk=BLOCK * LANES, unroll=8 if slots <= 8 else 1
+        ),
+        in_specs=whole_vmem(6),
+        out_specs=whole_vmem(chips),
+        out_shape=[jax.ShapeDtypeStruct((rows, LANES), jnp.float32)]
+        + [jax.ShapeDtypeStruct((rows + MASS_ROWS, LANES), jnp.bfloat16)] * (chips - 1),
+        scratch_shapes=[pltpu.VMEM((chips * rows, LANES), jnp.float32)],
         compiler_params=pltpu.CompilerParams(vmem_limit_bytes=(14 + slots // 2) * MIB),
-        cost_estimate=pl.CostEstimate(flops=20000000, bytes_accessed=20000000, transcendentals=0),
         name="backproject",
-    )(weights, own_images, other_images, cos_table, sin_table)
-
-
-def fold_kernel(sums, low_ref, low_received, mass, own, own_mass, *sends, slots):
-    per_row = sums.shape[0] // slots
-    tiles = per_row // 2
-    low_body = low_ref.shape[0]
-    total_mass = mass[0:1, :] + joined_mass(low_received[low_body:, :])
-    block = split_mass(total_mass)
-    own_mass[...] = jnp.broadcast_to(total_mass, own_mass.shape)
-    for slot in range(slots):
-        target = own if slot < 2 else sends[slot // 2 - 1]
-        for comp in range(2):
-            low = slice((2 * slot + comp) * LOW_TILES, (2 * slot + comp + 1) * LOW_TILES)
-            start = slot * per_row + comp * tiles
-            dest = (slot % 2) * per_row + comp * tiles
-            value = (low_ref[low, :] + low_received[low, :].astype(jnp.float32)) * 0.5
-            value = jnp.concatenate([value, sums[start + LOW_TILES : start + tiles, :]], axis=0)
-            target[dest : dest + tiles, :] = value.astype(target.dtype)
-    for send in sends:
-        send[2 * per_row :, :] = block
-
-
-def fold(sums, low, low_received, mass, slots):
-    rows = 2 * sums.shape[0] // slots
-    chips = slots // 2
-    return pl.pallas_call(
-        functools.partial(fold_kernel, slots=slots),
-        in_specs=whole_vmem(4),
-        out_specs=whole_vmem(1 + chips),
-        out_shape=[
-            jax.ShapeDtypeStruct((rows, LANES), jnp.float32),
-            jax.ShapeDtypeStruct((8, LANES), jnp.float32),
-        ]
-        + [jax.ShapeDtypeStruct((rows + MASS_ROWS, LANES), jnp.bfloat16)] * (chips - 1),
-        compiler_params=pltpu.CompilerParams(vmem_limit_bytes=(10 + slots // 2) * MIB),
-        name="fold",
-    )(sums, low, low_received, mass)
-
-
-def merge_kernel(own, mass, *refs, mass_scale):
-    received, (keep, send, mass_out) = refs[:-3], refs[-3:]
+    )(weights, mass, own_images, other_images, cos_table, sin_table)
+
+
+def low_blocks(tiles):
+    return [slice(comp * tiles, comp * tiles + LOW_TILES) for comp in range(2)]
+
+
+def merge_kernel(own, mass, *refs):
+    received, (keep, to_core, to_half, to_both, mass_out) = refs[:-5], refs[-5:]
     rows = own.shape[0]
     half = rows // 2
     core = own_half()
     total_mass = mass[0:1, :]
     for ref in received:
         total_mass = total_mass + joined_mass(ref[rows:, :])
-    for target, place in ((send, 1 - core), (keep, core)):
+    mass_out[...] = jnp.broadcast_to(total_mass, mass_out.shape)
+    for target, low, place in ((to_core, to_both, 1 - core), (keep, to_half, core)):
         where = pl.ds(pl.multiple_of(place * half, half), half)
         total = own[where, :]
         for ref in received:
             total = total + ref[where, :].astype(jnp.float32)
         target[...] = total.astype(target.dtype)
-    mass_out[...] = total_mass[0, :CLASSES] * mass_scale
-
-
-def merge(own, mass, received, mass_scale):
+        low[0 : 2 * LOW_TILES, :] = jnp.concatenate(
+            [total[block] for block in low_blocks(half // 2)], axis=0
+        ).astype(jnp.bfloat16)
+    to_half[2 * LOW_TILES :, :] = split_mass(total_mass)
+
+
+def merge(own, mass, received):
     rows = own.shape[0] // 2
     return pl.pallas_call(
-        functools.partial(merge_kernel, mass_scale=mass_scale),
+        merge_kernel,
         in_specs=whole_vmem(2 + len(received)),
-        out_specs=whole_vmem(3),
+        out_specs=whole_vmem(5),
         out_shape=[
             jax.ShapeDtypeStruct((rows, LANES), jnp.float32),
             jax.ShapeDtypeStruct((rows, LANES), jnp.bfloat16),
-            jax.ShapeDtypeStruct((CLASSES,), jnp.float32),
+            jax.ShapeDtypeStruct((2 * LOW_TILES + MASS_ROWS, LANES), jnp.bfloat16),
+            jax.ShapeDtypeStruct((2 * LOW_TILES, LANES), jnp.bfloat16),
+            jax.ShapeDtypeStruct((8, LANES), jnp.float32),
         ],
         compiler_params=pltpu.CompilerParams(vmem_limit_bytes=16 * MIB),
         name="merge",
     )(own, mass, *received)
 
 
-def finish_kernel(own, received, out, *, scale):
-    half = own_half()
-    for step in range(own.shape[0] // BLOCK):
-        rows = slice(step * BLOCK, (step + 1) * BLOCK)
-        own_rows = pl.ds(pl.multiple_of((2 * step + half) * BLOCK, BLOCK), BLOCK)
-        other_rows = pl.ds(pl.multiple_of((2 * step + 1 - half) * BLOCK, BLOCK), BLOCK)
-        out[own_rows, :] = own[rows, :] * scale
-        out[other_rows, :] = received[rows, :].astype(jnp.float32) * scale
-
-
-def finish(own, received, scale):
-    return pl.pallas_call(
-        functools.partial(finish_kernel, scale=scale),
-        in_specs=whole_vmem(2),
-        out_specs=pl.BlockSpec(memory_space=pltpu.VMEM),
-        out_shape=jax.ShapeDtypeStruct((2 * own.shape[0], LANES), jnp.float32),
+def finish_kernel(keep, from_core, from_half, from_both, mass, out, mass_out, *, scale, mass_scale):
+    core = own_half()
+    total_mass = mass[0:1, :] + joined_mass(from_half[2 * LOW_TILES :, :])
+    mass_out[...] = total_mass[0, :CLASSES] * mass_scale
+    steps = keep.shape[0] // BLOCK
+    low_steps = [block.start // BLOCK for block in low_blocks(keep.shape[0] // 2)]
+    for own, low, place in ((keep, from_half, core), (from_core, from_both, 1 - core)):
+        for step in range(steps):
+            value = own[step * BLOCK : (step + 1) * BLOCK, :].astype(jnp.float32)
+            if step in low_steps:
+                index = low_steps.index(step)
+                other = low[index * LOW_TILES : (index + 1) * LOW_TILES, :].astype(jnp.float32)
+                value = (value + other) * 0.5
+            out[pl.ds(pl.multiple_of((2 * step + place) * BLOCK, BLOCK), BLOCK), :] = value * scale
+
+
+def finish(keep, from_core, from_half, from_both, mass, scale, mass_scale):
+    return pl.pallas_call(
+        functools.partial(finish_kernel, scale=scale, mass_scale=mass_scale),
+        in_specs=whole_vmem(5),
+        out_specs=whole_vmem(2),
+        out_shape=[
+            jax.ShapeDtypeStruct((2 * keep.shape[0], LANES), jnp.float32),
+            jax.ShapeDtypeStruct((CLASSES,), jnp.float32),
+        ],
         compiler_params=pltpu.CompilerParams(vmem_limit_bytes=16 * MIB),
         name="finish",
-    )(own, received)
+    )(keep, from_core, from_half, from_both, mass)
 
 
 def local(
@@ -574,10 +549,12 @@
     slots = dev_count // 2
     chips = slots // 2
     parts, width = images.shape
+    shifts = shift_grid.shape[0]
     other_half, table, index, frac = project_other(class_refs, interp_index, interp_frac)
     from_core = exchange(other_half, 1)
     own, own_images, other_images = project_own(table, index, frac, images)
     pair = pair_rows(own, from_core)
+    pair, other_images = lax.optimization_barrier((pair, other_images))
     pairs = [pair] + [exchange(pair, 4 * m) for m in range(1, chips)]
     images_received = exchange(other_images, 1)
     cos_table, sin_table = phase_tables(shift_grid, width // 4)
@@ -590,18 +567,21 @@
         sin_table,
         pairs,
     )
-    weights, low, low_send, mass = posterior(
-        mine, exchange(mine, 1), own_images, images_received, cos_table, sin_table, slots
-    )
-    low_received = exchange(low_send, 2)
-    sums = backproject(weights, own_images, images_received, cos_table, sin_table, slots)
-    folded = fold(sums, low, low_received, mass, slots)
-    sends = folded[2:]
-    received = [exchange(sends[m - 1], 4 * m) for m in range(chips - 1, 0, -1)]
-    keep, send, class_mass = merge(
-        folded[0], folded[1], received, CLASSES / (parts * dev_count)
-    )
-    back = finish(keep, exchange(send, 1), 1.0 / math.sqrt(parts))
+    weights, mass = posterior(mine, exchange(mine, 1), slots, shifts, parts, width // 2)
+    sums = backproject(
+        weights, mass, own_images, images_received, cos_table, sin_table, slots
+    )
+    received = [exchange(send, 4 * m) for m, send in enumerate(sums[1:], start=1)]
+    keep, to_core, to_half, to_both, mass = merge(sums[0], mass, received)
+    back, class_mass = finish(
+        keep,
+        exchange(to_core, 1),
+        exchange(to_half, 2),
+        exchange(to_both, 3),
+        mass,
+        1.0 / math.sqrt(parts),
+        CLASSES / (parts * dev_count),
+    )
     return back.reshape(1, width), class_mass
 
 

time: 40.7 us -> 39.4 us (0.968)
  Pallas kernels: 11.9 us -> 11 us
  waiting for transfers between devices: 15.5 us -> 14.7 us
    pallas_call x5 -> x4, Pallas kernels: 3.63 us -> 2.75 us  [the longest x1 1.81 us: backproject(): pl.pallas_call(functools.partial(backproject_kernel, slots=slots, chunk=B...]
    ppermute x11 -> x12, waiting for transfers between devices: 15.5 us -> 14.7 us  [exchange(): return lax.ppermute(value, 'particle', pairs)]
    ppermute x11 -> x12, starting transfers between devices: 12.3 us -> 12.7 us  [exchange(): return lax.ppermute(value, 'particle', pairs)]
  transfers between devices with their start and end apart: 11 -> 12, of which waited for: 8 -> 6; matrix products, arithmetic and copies ran while one was open for 0% -> 0% of each run, Pallas kernels for 6% -> 8%
where the time goes in v7:
time: 39.4 us; the launch traced here: 39.2 us
  waiting for transfers between devices  14.7 us (37%)
  starting transfers between devices  12.7 us (32%)
  Pallas kernels  11 us (28%)
  between operations  0.73 us (2%)
    ppermute x12, waiting for transfers between devices, exchange(): return lax.ppermute(value, 'particle', pairs)  14.7 us
    ppermute x12, starting transfers between devices, exchange(): return lax.ppermute(value, 'particle', pairs)  12.7 us
    pallas_call x1, Pallas kernels, project_other(): pl.pallas_call(project_other_kernel, in_specs=[pl.BlockSpec(memory_space=...  3.56 us
    pallas_call x1, Pallas kernels, project_own(): pl.pallas_call(project_own_kernel, in_specs=whole_vmem(3) + [pl.BlockSpec...  2.59 us
    pallas_call x1, Pallas kernels, backproject(): pl.pallas_call(functools.partial(backproject_kernel, slots=slots, chunk=B...  1.81 us
    pallas_call x1, Pallas kernels, correlate(): pl.pallas_call(functools.partial(correlate_kernel, chunk=2048), in_specs=...  1.72 us
  transfers between devices with their start and end apart: 12, of which 6 were waited for; matrix products, arithmetic and copies ran while one was open for 0% of the time, Pallas kernels for 8%

profile of v7, /device:TPU:0, one launch (start us, length us, event | category | flops | bytes accessed | tf_op | source)
XLA Modules:
  0.0 39.2 jit_solution(6055305316062216427)
XLA Ops:
  0.6 3.6 %project_other.1 = (bf16[128,128]{1,0:T(8,128)(2,1)S(1)}, bf16[304,256]{1,0:T(8,128)(2,1)S(1)}, s32[1,16384]{1,0:T(1,128)S(1)}, f32[1,16384]{1,0:T(1,128)S(1)}) custom-call(bf16[2,8,2,32768]{3,2,1,0:T(2,128)(2,1)} %table_hbm.1, s32[1,16384]{1,0:T(1,128)} %index_hbm.1, f32[1,16384]{1,0:T(1,128)} %frac_hbm.1), custom_call_target="tpu_custom_call" | custom-call | tf_op jit(solution)/shard_map/project_other/pallas_call | solution.py:135
  4.2 0.5 %collective-permute-start = (bf16[128,128]{1,0:T(8,128)(2,1)S(1)}, bf16[128,128]{1,0:T(8,128)(2,1)S(1)}, u32[]{:S(2)}, u32[]{:S(2)}) collective-permute-start(bf16[128,128]{1,0:T(8,128)(2,1)S(1)} %get-tuple-element.31), channel_id=1, source_target_pairs={{0,1},{1,0},{2,3},{3,2},{4,5},{5,4},{6,7},{7,6},{8,9},{9,8},{10,11... | collective-permute-start | bytes 98312 | tf_op jit(solution)/shard_map/ppermute | solution.py:25
  4.7 2.6 %project_own.1 = (bf16[128,128]{1,0:T(8,128)(2,1)S(1)}, bf16[32,16384]{1,0:T(8,128)(2,1)S(1)}, bf16[32,16384]{1,0:T(8,128)(2,1)S(1)}) custom-call(bf16[304,256]{1,0:T(8,128)(2,1)S(1)} %get-tuple-element.26.table, s32[1,16384]{1,0:T(1,128)S(1)} %get-tuple-element.27.index_ref, f32[1,16384]{1,0:T(1,128)S(1)} %get-tuple-element.28.frac_ref, ...), custom_call_target="tpu_custom_call" | custom-call | flops 2000000000 | bytes 8000000 | tf_op jit(solution)/shard_map/project_own/pallas_call | solution.py:188
  7.4 0.1 collective-permute-start.1
  7.5 3.0 %collective-permute-start.2 = (bf16[256,128]{1,0:T(8,128)(2,1)S(1)}, bf16[256,128]{1,0:T(8,128)(2,1)S(1)}, u32[]{:S(2)}, u32[]{:S(2)}) collective-permute-start(bf16[256,128]{1,0:T(8,128)(2,1)S(1)} %pair_rows.1.refs_0_), channel_id=1, source_target_pairs={{0,4},{1,5},{2,6},{3,7},{4,0},{5,1},{6,2},{7,3},{8,12},{9,13},{10,... | collective-permute-start | bytes 196616 | tf_op jit(solution)/shard_map/ppermute | solution.py:25
  10.5 2.6 %collective-permute-start.3 = (bf16[256,128]{1,0:T(8,128)(2,1)S(1)}, bf16[256,128]{1,0:T(8,128)(2,1)S(1)}, u32[]{:S(2)}, u32[]{:S(2)}) collective-permute-start(bf16[256,128]{1,0:T(8,128)(2,1)S(1)} %pair_rows.1.refs_0_), channel_id=1, source_target_pairs={{0,8},{1,9},{2,10},{3,11},{4,12},{5,13},{6,14},{7,15},{8,0},{9,1},... | collective-permute-start | bytes 196616 | tf_op jit(solution)/shard_map/ppermute | solution.py:25
  13.1 0.1 copy.9.shift_ref
  13.2 0.4 %phase_tables.1 = (f32[8,8192]{1,0:T(8,128)S(1)}, f32[8,8192]{1,0:T(8,128)S(1)}) custom-call(s32[8,2]{1,0:T(8,128)S(1)} %copy.9.shift_ref), custom_call_target="tpu_custom_call" | custom-call | flops 2000000 | bytes 2000000 | tf_op jit(solution)/shard_map/phase_tables/pallas_call | solution.py:262
  13.6 4.4 %collective-permute-done.3.refs_2_ = bf16[256,128]{1,0:T(8,128)(2,1)S(1)} collective-permute-done((bf16[256,128]{1,0:T(8,128)(2,1)S(1)}, bf16[256,128]{1,0:T(8,128)(2,1)S(1)}, u32[]{:S(2)}, u32[]{:S(2)}) %collective-permute-start.3) | collective-permute-done | bytes 65568 | tf_op jit(solution)/shard_map/ppermute | solution.py:25
  18.0 1.3 %collective-permute-done.4.refs_3_ = bf16[256,128]{1,0:T(8,128)(2,1)S(1)} collective-permute-done((bf16[256,128]{1,0:T(8,128)(2,1)S(1)}, bf16[256,128]{1,0:T(8,128)(2,1)S(1)}, u32[]{:S(2)}, u32[]{:S(2)}) %collective-permute-start.4) | collective-permute-done | bytes 65568 | tf_op jit(solution)/shard_map/ppermute | solution.py:25
  19.3 1.7 %correlate.1.mine = f32[80,128]{1,0:T(8,128)S(1)} custom-call(bf16[32,16384]{1,0:T(8,128)(2,1)S(1)} %get-tuple-element.29.own_images, bf16[32,16384]{1,0:T(8,128)(2,1)S(1)} %collective-permute-done.1.other_images, f32[1,32]{1,0:T(1,128)S(1)} %bitcast.3, s32[1,32]{1,0:T(1,128)S(1)} %bitcast.4, f32[8,8192]{1,0:T(8,128)S(1)} %get-tuple-element.34.cos_ref, ...), custom_call_target="tpu_custom_call" | custom-call | tf_op jit(solution)/shard_map/correlate/pallas_call | solution.py:341
  21.0 0.1 collective-permute-start.5
  21.1 1.2 %collective-permute-done.5.received = f32[80,128]{1,0:T(8,128)S(1)} collective-permute-done((f32[80,128]{1,0:T(8,128)S(1)}, f32[80,128]{1,0:T(8,128)S(1)}, u32[]{:S(2)}, u32[]{:S(2)}) %collective-permute-start.5) | collective-permute-done | bytes 40992 | tf_op jit(solution)/shard_map/ppermute | solution.py:25
  22.3 0.2 posterior.1
  22.5 1.8 %backproject.1 = (f32[256,128]{1,0:T(8,128)S(1)}, bf16[272,128]{1,0:T(8,128)(2,1)S(1)}, bf16[272,128]{1,0:T(8,128)(2,1)S(1)}, bf16[272,128]{1,0:T(8,128)(2,1)S(1)}) custom-call(bf16[64,64]{1,0:T(8,128)(2,1)S(1)} %get-tuple-element.37.weight_ref, f32[8,128]{1,0:T(8,128)S(1)} %get-tuple-element.38.mass, bf16[32,16384]{1,0:T(8,128)(2,1)S(1)} %get-tuple-element.29.own_images, ...), custom_call_target="tpu_custom_call" | custom-call | tf_op jit(solution)/shard_map/backproject/pallas_call | solution.py:458
  24.3 0.8 %collective-permute-start.6 = (bf16[272,128]{1,0:T(8,128)(2,1)S(1)}, bf16[272,128]{1,0:T(8,128)(2,1)S(1)}, u32[]{:S(2)}, u32[]{:S(2)}) collective-permute-start(bf16[272,128]{1,0:T(8,128)(2,1)S(1)} %get-tuple-element.40), channel_id=1, source_target_pairs={{0,4},{1,5},{2,6},{3,7},{4,0},{5,1},{6,2},{7,3},{8,12},{9,13},{10,... | collective-permute-start | bytes 208904 | tf_op jit(solution)/shard_map/ppermute | solution.py:25
  25.2 1.7 %collective-permute-start.7 = (bf16[272,128]{1,0:T(8,128)(2,1)S(1)}, bf16[272,128]{1,0:T(8,128)(2,1)S(1)}, u32[]{:S(2)}, u32[]{:S(2)}) collective-permute-start(bf16[272,128]{1,0:T(8,128)(2,1)S(1)} %get-tuple-element.41), channel_id=1, source_target_pairs={{0,8},{1,9},{2,10},{3,11},{4,12},{5,13},{6,14},{7,15},{8,0},{9,1},... | collective-permute-start | bytes 208904 | tf_op jit(solution)/shard_map/ppermute | solution.py:25
  26.9 1.9 %collective-permute-start.8 = (bf16[272,128]{1,0:T(8,128)(2,1)S(1)}, bf16[272,128]{1,0:T(8,128)(2,1)S(1)}, u32[]{:S(2)}, u32[]{:S(2)}) collective-permute-start(bf16[272,128]{1,0:T(8,128)(2,1)S(1)} %get-tuple-element.42), channel_id=1, source_target_pairs={{0,12},{1,13},{2,14},{3,15},{4,8},{5,9},{6,10},{7,11},{8,4},{9,5},... | collective-permute-start | bytes 208904 | tf_op jit(solution)/shard_map/ppermute | solution.py:25
  28.8 0.7 %collective-permute-done.6.refs_0_ = bf16[272,128]{1,0:T(8,128)(2,1)S(1)} collective-permute-done((bf16[272,128]{1,0:T(8,128)(2,1)S(1)}, bf16[272,128]{1,0:T(8,128)(2,1)S(1)}, u32[]{:S(2)}, u32[]{:S(2)}) %collective-permute-start.6) | collective-permute-done | bytes 69664 | tf_op jit(solution)/shard_map/ppermute | solution.py:25
  29.4 4.4 %collective-permute-done.7.refs_1_ = bf16[272,128]{1,0:T(8,128)(2,1)S(1)} collective-permute-done((bf16[272,128]{1,0:T(8,128)(2,1)S(1)}, bf16[272,128]{1,0:T(8,128)(2,1)S(1)}, u32[]{:S(2)}, u32[]{:S(2)}) %collective-permute-start.7) | collective-permute-done | bytes 69664 | tf_op jit(solution)/shard_map/ppermute | solution.py:25
  34.0 1.6 %collective-permute-start.10 = (bf16[32,128]{1,0:T(8,128)(2,1)S(1)}, bf16[32,128]{1,0:T(8,128)(2,1)S(1)}, u32[]{:S(2)}, u32[]{:S(2)}) collective-permute-start(bf16[32,128]{1,0:T(8,128)(2,1)S(1)} %get-tuple-element.45), channel_id=1, source_target_pairs={{0,2},{1,3},{2,0},{3,1},{4,6},{5,7},{6,4},{7,5},{8,10},{9,11},{10,... | collective-permute-start | bytes 24584 | tf_op jit(solution)/shard_map/ppermute | solution.py:25
  35.5 0.3 collective-permute-start.11
  35.8 2.7 %collective-permute-done.11.from_both = bf16[16,128]{1,0:T(8,128)(2,1)S(1)} collective-permute-done((bf16[16,128]{1,0:T(8,128)(2,1)S(1)}, bf16[16,128]{1,0:T(8,128)(2,1)S(1)}, u32[]{:S(2)}, u32[]{:S(2)}) %collective-permute-start.11) | collective-permute-done | bytes 4128 | tf_op jit(solution)/shard_map/ppermute | solution.py:25
  38.5 0.7 %finish.1 = (f32[256,128]{1,0:T(8,128)}, f32[8]{0:T(128)}) custom-call(f32[128,128]{1,0:T(8,128)S(1)} %get-tuple-element.43.keep, bf16[128,128]{1,0:T(8,128)(2,1)S(1)} %collective-permute-done.9.from_core, bf16[32,128]{1,0:T(8,128)(2,1)S(1)} %collective-permute-done.10.from_half, bf16[16,128]{1,0:T(8,128)(2,1)S(1)} %collective-permute-done.11.from_both, ...), custom_call_target="tpu_custom_call" | custom-call | tf_op jit(solution)/shard_map/finish/pallas_call | solution.py:532
  (16 shorter events, 0.2 us)
Async XLA Ops:
  4.2 3.1 %collective-permute-start = (bf16[128,128]{1,0:T(8,128)(2,1)S(1)}, bf16[128,128]{1,0:T(8,128)(2,1)S(1)}, u32[]{:S(2)}, u32[]{:S(2)}) collective-permute-start(bf16[128,128]{1,0:T(8,128)(2,1)S(1)} %get-tuple-element.31), channel_id=1, source_target_pairs={{0,1},{1,0},{2,3},{3,2},{4,5},{5,4},{6,7},{7,6},{8,9},{9,8},{10,11... | collective-permute-start | bytes 98312 | tf_op jit(solution)/shard_map/ppermute | solution.py:25
  4.7 8.4 %copy-start.2 = (s32[8,2]{0,1:T(2,128)S(1)}, s32[8,2]{0,1:T(2,128)}, u32[]{:S(2)}) copy-start(s32[8,2]{0,1:T(2,128)} %param.13) | copy-start | bytes 196
  4.7 14.6 %copy-start = (f32[32]{0:T(128)S(1)}, f32[32]{0:T(128)}, u32[]{:S(2)}) copy-start(f32[32]{0:T(128)} %param.8) | copy-start | bytes 388
  4.7 14.6 %copy-start.1 = (s32[32]{0:T(128)S(1)}, s32[32]{0:T(128)}, u32[]{:S(2)}) copy-start(s32[32]{0:T(128)} %param.9) | copy-start | bytes 388
  7.4 11.9 %collective-permute-start.1 = (bf16[32,16384]{1,0:T(8,128)(2,1)S(1)}, bf16[32,16384]{1,0:T(8,128)(2,1)S(1)}, u32[]{:S(2)}, u32[]{:S(2)}) collective-permute-start(bf16[32,16384]{1,0:T(8,128)(2,1)S(1)} %get-tuple-element.33), channel_id=1, source_target_pairs={{0,1},{1,0},{2,3},{3,2},{4,5},{5,4},{6,7},{7,6},{8,9},{9,8},{10,11... | collective-permute-start | bytes 3145736 | tf_op jit(solution)/shard_map/ppermute | solution.py:25
  7.5 6.1 %collective-permute-start.2 = (bf16[256,128]{1,0:T(8,128)(2,1)S(1)}, bf16[256,128]{1,0:T(8,128)(2,1)S(1)}, u32[]{:S(2)}, u32[]{:S(2)}) collective-permute-start(bf16[256,128]{1,0:T(8,128)(2,1)S(1)} %pair_rows.1.refs_0_), channel_id=1, source_target_pairs={{0,4},{1,5},{2,6},{3,7},{4,0},{5,1},{6,2},{7,3},{8,12},{9,13},{10,... | collective-permute-start | bytes 196616 | tf_op jit(solution)/shard_map/ppermute | solution.py:25
  10.5 7.5 %collective-permute-start.3 = (bf16[256,128]{1,0:T(8,128)(2,1)S(1)}, bf16[256,128]{1,0:T(8,128)(2,1)S(1)}, u32[]{:S(2)}, u32[]{:S(2)}) collective-permute-start(bf16[256,128]{1,0:T(8,128)(2,1)S(1)} %pair_rows.1.refs_0_), channel_id=1, source_target_pairs={{0,8},{1,9},{2,10},{3,11},{4,12},{5,13},{6,14},{7,15},{8,0},{9,1},... | collective-permute-start | bytes 196616 | tf_op jit(solution)/shard_map/ppermute | solution.py:25
  13.1 6.2 %collective-permute-start.4 = (bf16[256,128]{1,0:T(8,128)(2,1)S(1)}, bf16[256,128]{1,0:T(8,128)(2,1)S(1)}, u32[]{:S(2)}, u32[]{:S(2)}) collective-permute-start(bf16[256,128]{1,0:T(8,128)(2,1)S(1)} %pair_rows.1.refs_0_), channel_id=1, source_target_pairs={{0,12},{1,13},{2,14},{3,15},{4,8},{5,9},{6,10},{7,11},{8,4},{9,5},... | collective-permute-start | bytes 196616 | tf_op jit(solution)/shard_map/ppermute | solution.py:25
  21.0 1.3 %collective-permute-start.5 = (f32[80,128]{1,0:T(8,128)S(1)}, f32[80,128]{1,0:T(8,128)S(1)}, u32[]{:S(2)}, u32[]{:S(2)}) collective-permute-start(f32[80,128]{1,0:T(8,128)S(1)} %correlate.1.mine), channel_id=1, source_target_pairs={{0,1},{1,0},{2,3},{3,2},{4,5},{5,4},{6,7},{7,6},{8,9},{9,8},{10,11... | collective-permute-start | bytes 122888 | tf_op jit(solution)/shard_map/ppermute | solution.py:25
  24.3 5.1 %collective-permute-start.6 = (bf16[272,128]{1,0:T(8,128)(2,1)S(1)}, bf16[272,128]{1,0:T(8,128)(2,1)S(1)}, u32[]{:S(2)}, u32[]{:S(2)}) collective-permute-start(bf16[272,128]{1,0:T(8,128)(2,1)S(1)} %get-tuple-element.40), channel_id=1, source_target_pairs={{0,4},{1,5},{2,6},{3,7},{4,0},{5,1},{6,2},{7,3},{8,12},{9,13},{10,... | collective-permute-start | bytes 208904 | tf_op jit(solution)/shard_map/ppermute | solution.py:25
  25.2 8.7 %collective-permute-start.7 = (bf16[272,128]{1,0:T(8,128)(2,1)S(1)}, bf16[272,128]{1,0:T(8,128)(2,1)S(1)}, u32[]{:S(2)}, u32[]{:S(2)}) collective-permute-start(bf16[272,128]{1,0:T(8,128)(2,1)S(1)} %get-tuple-element.41), channel_id=1, source_target_pairs={{0,8},{1,9},{2,10},{3,11},{4,12},{5,13},{6,14},{7,15},{8,0},{9,1},... | collective-permute-start | bytes 208904 | tf_op jit(solution)/shard_map/ppermute | solution.py:25
  26.9 6.9 %collective-permute-start.8 = (bf16[272,128]{1,0:T(8,128)(2,1)S(1)}, bf16[272,128]{1,0:T(8,128)(2,1)S(1)}, u32[]{:S(2)}, u32[]{:S(2)}) collective-permute-start(bf16[272,128]{1,0:T(8,128)(2,1)S(1)} %get-tuple-element.42), channel_id=1, source_target_pairs={{0,12},{1,13},{2,14},{3,15},{4,8},{5,9},{6,10},{7,11},{8,4},{9,5},... | collective-permute-start | bytes 208904 | tf_op jit(solution)/shard_map/ppermute | solution.py:25
  33.9 4.7 %collective-permute-start.9 = (bf16[128,128]{1,0:T(8,128)(2,1)S(1)}, bf16[128,128]{1,0:T(8,128)(2,1)S(1)}, u32[]{:S(2)}, u32[]{:S(2)}) collective-permute-start(bf16[128,128]{1,0:T(8,128)(2,1)S(1)} %get-tuple-element.44), channel_id=1, source_target_pairs={{0,1},{1,0},{2,3},{3,2},{4,5},{5,4},{6,7},{7,6},{8,9},{9,8},{10,11... | collective-permute-start | bytes 98312 | tf_op jit(solution)/shard_map/ppermute | solution.py:25
  34.0 4.6 %collective-permute-start.10 = (bf16[32,128]{1,0:T(8,128)(2,1)S(1)}, bf16[32,128]{1,0:T(8,128)(2,1)S(1)}, u32[]{:S(2)}, u32[]{:S(2)}) collective-permute-start(bf16[32,128]{1,0:T(8,128)(2,1)S(1)} %get-tuple-element.45), channel_id=1, source_target_pairs={{0,2},{1,3},{2,0},{3,1},{4,6},{5,7},{6,4},{7,5},{8,10},{9,11},{10,... | collective-permute-start | bytes 24584 | tf_op jit(solution)/shard_map/ppermute | solution.py:25
  35.5 3.0 %collective-permute-start.11 = (bf16[16,128]{1,0:T(8,128)(2,1)S(1)}, bf16[16,128]{1,0:T(8,128)(2,1)S(1)}, u32[]{:S(2)}, u32[]{:S(2)}) collective-permute-start(bf16[16,128]{1,0:T(8,128)(2,1)S(1)} %get-tuple-element.46), channel_id=1, source_target_pairs={{0,3},{1,2},{2,1},{3,0},{4,7},{5,6},{6,5},{7,4},{8,11},{9,10},{10,... | collective-permute-start | bytes 12296 | tf_op jit(solution)/shard_map/ppermute | solution.py:25

commit v8 on v4

--- a/solution.py
+++ b/solution.py
@@ -16,6 +16,7 @@
 PRIOR_REWARD = 1.0
 MASS_ROWS = 16
 BLOCK = 8
+PROJECT_CHUNK = 256
 LOW_TILES = LOWK * KY // LANES // 2
 MIB = 1 << 20
 
@@ -51,11 +52,14 @@
     highs = table.shape[1]
     groups = table.shape[0] // 16
     stride = 8 * groups
-    chunk = BLOCK * LANES
-    blocks = pixels // (2 * chunk)
+    chunk = PROJECT_CHUNK
+    tiles = chunk // LANES
+    per_block = BLOCK // tiles
+    half_tiles = pixels // (2 * LANES)
 
     def body(step, carry):
-        where = pl.ds(pl.multiple_of((2 * step + half) * chunk, chunk), chunk)
+        block = 2 * (step // per_block) + half
+        where = pl.ds(pl.multiple_of((block * per_block + step % per_block) * chunk, chunk), chunk)
         index = index_ref[:, where]
         frac = frac_ref[:, where]
         high = index >> 7
@@ -73,12 +77,12 @@
             start = comp * stride
             picked = tree_select([rows[start + 8 * g : start + 8 * g + 8] for g in range(groups)], masks)
             value = jnp.sum(picked * weight, axis=0, keepdims=True)
-            for k in range(BLOCK):
-                row = (comp * blocks + step) * BLOCK + k
+            for k in range(tiles):
+                row = comp * half_tiles + step * tiles + k
                 blended[pl.ds(row, 1), :] = value[:, k * LANES : (k + 1) * LANES]
         return carry
 
-    lax.fori_loop(0, blocks, body, 0, unroll=2)
+    lax.fori_loop(0, half_tiles // tiles, body, 0, unroll=8)
 
 
 def project_other_kernel(
@@ -438,16 +442,19 @@
     )(mine, received, own_images, other_images, cos_table, sin_table)
 
 
-def backproject_kernel(weight_ref, own_images, other_images, cos_ref, sin_ref, sums, *, slots, chunk):
+def backproject_kernel(
+    weight_ref, own_images, other_images, cos_ref, sin_ref, own, *refs, slots, chunk, unroll
+):
+    sends, sums = refs[:-1], refs[-1]
     width = cos_ref.shape[1]
-    tiles = width // LANES
+    tiles = width // LANES - LOW_TILES
     per_row = 2 * tiles
     chunk_tiles = chunk // LANES
     weights = weight_ref[...]
 
     def body(step, carry):
-        first = LOW_TILES + step * chunk_tiles
-        start = pl.multiple_of(first * LANES, LOW_TILES * LANES)
+        first = step * chunk_tiles
+        start = pl.multiple_of((LOW_TILES + first) * LANES, LOW_TILES * LANES)
         where = pl.ds(start, chunk)
         imag_where = pl.ds(pl.multiple_of(width + start, LOW_TILES * LANES), chunk)
         real, imag = rotate_back(
@@ -459,112 +466,124 @@
             sums[pl.ds(tiles + first + k, slots, stride=per_row), :] = imag[:, piece]
         return carry
 
-    lax.fori_loop(0, (tiles - LOW_TILES) // chunk_tiles, body, 0)
+    lax.fori_loop(0, tiles // chunk_tiles, body, 0, unroll=unroll)
+    own[...] = sums[0 : 2 * per_row, :]
+    for m, send in enumerate(sends, start=1):
+        send[...] = sums[2 * m * per_row : 2 * (m + 1) * per_row, :].astype(jnp.bfloat16)
 
 
 def backproject(weights, own_images, other_images, cos_table, sin_table, slots):
     width = cos_table.shape[1]
-    rows = slots * 2 * width // LANES
-    return pl.pallas_call(
-        functools.partial(backproject_kernel, slots=slots, chunk=LOW_TILES * LANES),
+    rows = 2 * 2 * (width // LANES - LOW_TILES)
+    chips = slots // 2
+    return pl.pallas_call(
+        functools.partial(
+            backproject_kernel, slots=slots, chunk=LOW_TILES * LANES, unroll=7 if slots <= 8 else 1
+        ),
         in_specs=whole_vmem(5),
-        out_specs=pl.BlockSpec(memory_space=pltpu.VMEM),
-        out_shape=jax.ShapeDtypeStruct((rows, LANES), jnp.float32),
+        out_specs=whole_vmem(chips),
+        out_shape=[jax.ShapeDtypeStruct((rows, LANES), jnp.float32)]
+        + [jax.ShapeDtypeStruct((rows, LANES), jnp.bfloat16)] * (chips - 1),
+        scratch_shapes=[pltpu.VMEM((chips * rows, LANES), jnp.float32)],
         compiler_params=pltpu.CompilerParams(vmem_limit_bytes=(14 + slots // 2) * MIB),
-        cost_estimate=pl.CostEstimate(flops=20000000, bytes_accessed=20000000, transcendentals=0),
+        cost_estimate=pl.CostEstimate(flops=2000000000, bytes_accessed=8000000, transcendentals=0),
         name="backproject",
     )(weights, own_images, other_images, cos_table, sin_table)
 
 
-def fold_kernel(sums, low_ref, low_received, mass, own, own_mass, *sends, slots):
-    per_row = sums.shape[0] // slots
-    tiles = per_row // 2
+def fold_kernel(low_ref, low_received, mass, own, own_mass, *sends):
+    rows = own.shape[0]
     low_body = low_ref.shape[0]
     total_mass = mass[0:1, :] + joined_mass(low_received[low_body:, :])
     block = split_mass(total_mass)
     own_mass[...] = jnp.broadcast_to(total_mass, own_mass.shape)
-    for slot in range(slots):
-        target = own if slot < 2 else sends[slot // 2 - 1]
-        for comp in range(2):
-            low = slice((2 * slot + comp) * LOW_TILES, (2 * slot + comp + 1) * LOW_TILES)
-            start = slot * per_row + comp * tiles
-            dest = (slot % 2) * per_row + comp * tiles
-            value = (low_ref[low, :] + low_received[low, :].astype(jnp.float32)) * 0.5
-            value = jnp.concatenate([value, sums[start + LOW_TILES : start + tiles, :]], axis=0)
-            target[dest : dest + tiles, :] = value.astype(target.dtype)
-    for send in sends:
-        send[2 * per_row :, :] = block
-
-
-def fold(sums, low, low_received, mass, slots):
-    rows = 2 * sums.shape[0] // slots
-    chips = slots // 2
-    return pl.pallas_call(
-        functools.partial(fold_kernel, slots=slots),
-        in_specs=whole_vmem(4),
+    for m, target in enumerate((own,) + sends):
+        part = slice(m * rows, (m + 1) * rows)
+        value = (low_ref[part, :] + low_received[part, :].astype(jnp.float32)) * 0.5
+        target[0:rows, :] = value.astype(target.dtype)
+        if m > 0:
+            target[rows:, :] = block
+
+
+def fold(low, low_received, mass, chips):
+    rows = low.shape[0] // chips
+    return pl.pallas_call(
+        fold_kernel,
+        in_specs=whole_vmem(3),
         out_specs=whole_vmem(1 + chips),
         out_shape=[
             jax.ShapeDtypeStruct((rows, LANES), jnp.float32),
             jax.ShapeDtypeStruct((8, LANES), jnp.float32),
         ]
         + [jax.ShapeDtypeStruct((rows + MASS_ROWS, LANES), jnp.bfloat16)] * (chips - 1),
-        compiler_params=pltpu.CompilerParams(vmem_limit_bytes=(10 + slots // 2) * MIB),
+        compiler_params=pltpu.CompilerParams(vmem_limit_bytes=16 * MIB),
         name="fold",
-    )(sums, low, low_received, mass)
-
-
-def merge_kernel(own, mass, *refs, mass_scale):
-    received, (keep, send, mass_out) = refs[:-3], refs[-3:]
-    rows = own.shape[0]
-    half = rows // 2
+    )(low, low_received, mass)
+
+
+def merge_kernel(own, own_low, mass, *refs, others):
+    received, low_received = refs[:others], refs[others : 2 * others]
+    keep, to_core, mass_out = refs[2 * others :]
     core = own_half()
+    low_half = own_low.shape[0] // 2
+    half = own.shape[0] // 2
     total_mass = mass[0:1, :]
-    for ref in received:
-        total_mass = total_mass + joined_mass(ref[rows:, :])
-    for target, place in ((send, 1 - core), (keep, core)):
+    for ref in low_received:
+        total_mass = total_mass + joined_mass(ref[2 * low_half :, :])
+    mass_out[...] = jnp.broadcast_to(total_mass, mass_out.shape)
+    for target, place in ((to_core, 1 - core), (keep, core)):
         where = pl.ds(pl.multiple_of(place * half, half), half)
         total = own[where, :]
         for ref in received:
             total = total + ref[where, :].astype(jnp.float32)
-        target[...] = total.astype(target.dtype)
-    mass_out[...] = total_mass[0, :CLASSES] * mass_scale
-
-
-def merge(own, mass, received, mass_scale):
-    rows = own.shape[0] // 2
-    return pl.pallas_call(
-        functools.partial(merge_kernel, mass_scale=mass_scale),
-        in_specs=whole_vmem(2 + len(received)),
+        where = pl.ds(pl.multiple_of(place * low_half, low_half), low_half)
+        low = own_low[where, :]
+        for ref in low_received:
+            low = low + ref[where, :].astype(jnp.float32)
+        target[...] = jnp.concatenate(
+            [low[0:LOW_TILES], total[0 : half // 2], low[LOW_TILES:], total[half // 2 :]], axis=0
+        ).astype(target.dtype)
+
+
+def merge(own, own_low, mass, received, low_received):
+    rows = (own.shape[0] + own_low.shape[0]) // 2
+    return pl.pallas_call(
+        functools.partial(merge_kernel, others=len(received)),
+        in_specs=whole_vmem(3 + 2 * len(received)),
         out_specs=whole_vmem(3),
         out_shape=[
             jax.ShapeDtypeStruct((rows, LANES), jnp.float32),
             jax.ShapeDtypeStruct((rows, LANES), jnp.bfloat16),
+            jax.ShapeDtypeStruct((8, LANES), jnp.float32),
+        ],
+        compiler_params=pltpu.CompilerParams(vmem_limit_bytes=16 * MIB),
+        name="merge",
+    )(own, own_low, mass, *received, *low_received)
+
+
+def finish_kernel(own, received, mass, out, mass_out, *, scale, mass_scale):
+    core = own_half()
+    mass_out[...] = mass[0, :CLASSES] * mass_scale
+    for step in range(own.shape[0] // BLOCK):
+        rows = slice(step * BLOCK, (step + 1) * BLOCK)
+        own_rows = pl.ds(pl.multiple_of((2 * step + core) * BLOCK, BLOCK), BLOCK)
+        other_rows = pl.ds(pl.multiple_of((2 * step + 1 - core) * BLOCK, BLOCK), BLOCK)
+        out[own_rows, :] = own[rows, :] * scale
+        out[other_rows, :] = received[rows, :].astype(jnp.float32) * scale
+
+
+def finish(own, received, mass, scale, mass_scale):
+    return pl.pallas_call(
+        functools.partial(finish_kernel, scale=scale, mass_scale=mass_scale),
+        in_specs=whole_vmem(3),
+        out_specs=whole_vmem(2),
+        out_shape=[
+            jax.ShapeDtypeStruct((2 * own.shape[0], LANES), jnp.float32),
             jax.ShapeDtypeStruct((CLASSES,), jnp.float32),
         ],
         compiler_params=pltpu.CompilerParams(vmem_limit_bytes=16 * MIB),
-        name="merge",
-    )(own, mass, *received)
-
-
-def finish_kernel(own, received, out, *, scale):
-    half = own_half()
-    for step in range(own.shape[0] // BLOCK):
-        rows = slice(step * BLOCK, (step + 1) * BLOCK)
-        own_rows = pl.ds(pl.multiple_of((2 * step + half) * BLOCK, BLOCK), BLOCK)
-        other_rows = pl.ds(pl.multiple_of((2 * step + 1 - half) * BLOCK, BLOCK), BLOCK)
-        out[own_rows, :] = own[rows, :] * scale
-        out[other_rows, :] = received[rows, :].astype(jnp.float32) * scale
-
-
-def finish(own, received, scale):
-    return pl.pallas_call(
-        functools.partial(finish_kernel, scale=scale),
-        in_specs=whole_vmem(2),
-        out_specs=pl.BlockSpec(memory_space=pltpu.VMEM),
-        out_shape=jax.ShapeDtypeStruct((2 * own.shape[0], LANES), jnp.float32),
-        compiler_params=pltpu.CompilerParams(vmem_limit_bytes=16 * MIB),
         name="finish",
-    )(own, received)
+    )(own, received, mass)
 
 
 def local(
@@ -578,6 +597,7 @@
     from_core = exchange(other_half, 1)
     own, own_images, other_images = project_own(table, index, frac, images)
     pair = pair_rows(own, from_core)
+    pair, other_images = lax.optimization_barrier((pair, other_images))
     pairs = [pair] + [exchange(pair, 4 * m) for m in range(1, chips)]
     images_received = exchange(other_images, 1)
     cos_table, sin_table = phase_tables(shift_grid, width // 4)
@@ -593,15 +613,15 @@
     weights, low, low_send, mass = posterior(
         mine, exchange(mine, 1), own_images, images_received, cos_table, sin_table, slots
     )
-    low_received = exchange(low_send, 2)
+    low_from_half = exchange(low_send, 2)
     sums = backproject(weights, own_images, images_received, cos_table, sin_table, slots)
-    folded = fold(sums, low, low_received, mass, slots)
-    sends = folded[2:]
-    received = [exchange(sends[m - 1], 4 * m) for m in range(chips - 1, 0, -1)]
-    keep, send, class_mass = merge(
-        folded[0], folded[1], received, CLASSES / (parts * dev_count)
-    )
-    back = finish(keep, exchange(send, 1), 1.0 / math.sqrt(parts))
+    received = [exchange(send, 4 * m) for m, send in enumerate(sums[1:], start=1)]
+    folded = fold(low, low_from_half, mass, chips)
+    low_received = [exchange(send, 4 * m) for m, send in enumerate(folded[2:], start=1)]
+    keep, send, mass = merge(sums[0], folded[0], folded[1], received, low_received)
+    back, class_mass = finish(
+        keep, exchange(send, 1), mass, 1.0 / math.sqrt(parts), CLASSES / (parts * dev_count)
+    )
     return back.reshape(1, width), class_mass
 
 

time: 40.7 us -> 41.7 us (1.025)
  starting transfers between devices: 12.3 us -> 16.8 us
  waiting for transfers between devices: 15.5 us -> 13.3 us
  Pallas kernels: 11.9 us -> 10.6 us
    ppermute x11 -> x14, starting transfers between devices: 12.3 us -> 16.8 us  [exchange(): return lax.ppermute(value, 'particle', pairs)]
    ppermute x11 -> x14, waiting for transfers between devices: 15.5 us -> 13.3 us  [exchange(): return lax.ppermute(value, 'particle', pairs)]
    pallas_call x1, Pallas kernels: 2.02 us -> 1.31 us  [backproject(): pl.pallas_call(functools.partial(backproject_kernel, slots=slots, chunk=L...]
    pallas_call x3, Pallas kernels: 1.23 us -> 0.75 us  [the longest x1 0.68 us: finish(): pl.pallas_call(functools.partial(finish_kernel, scale=scale, mass_scale=m...]
  transfers between devices with their start and end apart: 11 -> 14, of which waited for: 8 -> 6; matrix products, arithmetic and copies ran while one was open for 0% -> 0% of each run, Pallas kernels for 6% -> 10%
where the time goes in v8:
time: 41.7 us; the launch traced here: 41.6 us
  starting transfers between devices  16.8 us (40%)
  waiting for transfers between devices  13.3 us (32%)
  Pallas kernels  10.6 us (25%)
  between operations  0.74 us (2%)
    ppermute x14, starting transfers between devices, exchange(): return lax.ppermute(value, 'particle', pairs)  16.8 us
    ppermute x14, waiting for transfers between devices, exchange(): return lax.ppermute(value, 'particle', pairs)  13.3 us
    pallas_call x1, Pallas kernels, project_other(): pl.pallas_call(project_other_kernel, in_specs=[pl.BlockSpec(memory_space=...  3.5 us
    pallas_call x1, Pallas kernels, project_own(): pl.pallas_call(project_own_kernel, in_specs=whole_vmem(3) + [pl.BlockSpec...  2.54 us
    pallas_call x1, Pallas kernels, correlate(): pl.pallas_call(functools.partial(correlate_kernel, chunk=2048), in_specs=...  1.72 us
    pallas_call x1, Pallas kernels, backproject(): pl.pallas_call(functools.partial(backproject_kernel, slots=slots, chunk=L...  1.31 us
  transfers between devices with their start and end apart: 14, of which 6 were waited for; matrix products, arithmetic and copies ran while one was open for 0% of the time, Pallas kernels for 10%

profile of v8, /device:TPU:0, one launch (start us, length us, event | category | flops | bytes accessed | tf_op | source)
XLA Modules:
  0.0 41.6 jit_solution(11879136610368373029)
XLA Ops:
  0.6 3.5 %project_other.1 = (bf16[128,128]{1,0:T(8,128)(2,1)S(1)}, bf16[304,256]{1,0:T(8,128)(2,1)S(1)}, s32[1,16384]{1,0:T(1,128)S(1)}, f32[1,16384]{1,0:T(1,128)S(1)}) custom-call(bf16[2,8,2,32768]{3,2,1,0:T(2,128)(2,1)} %table_hbm.1, s32[1,16384]{1,0:T(1,128)} %index_hbm.1, f32[1,16384]{1,0:T(1,128)} %frac_hbm.1), custom_call_target="tpu_custom_call" | custom-call | tf_op jit(solution)/shard_map/project_other/pallas_call | solution.py:139
  4.1 0.5 %collective-permute-start = (bf16[128,128]{1,0:T(8,128)(2,1)S(1)}, bf16[128,128]{1,0:T(8,128)(2,1)S(1)}, u32[]{:S(2)}, u32[]{:S(2)}) collective-permute-start(bf16[128,128]{1,0:T(8,128)(2,1)S(1)} %get-tuple-element.36), channel_id=1, source_target_pairs={{0,1},{1,0},{2,3},{3,2},{4,5},{5,4},{6,7},{7,6},{8,9},{9,8},{10,11... | collective-permute-start | bytes 98312 | tf_op jit(solution)/shard_map/ppermute | solution.py:26
  4.7 2.5 %project_own.1 = (bf16[128,128]{1,0:T(8,128)(2,1)S(1)}, bf16[32,16384]{1,0:T(8,128)(2,1)S(1)}, bf16[32,16384]{1,0:T(8,128)(2,1)S(1)}) custom-call(bf16[304,256]{1,0:T(8,128)(2,1)S(1)} %get-tuple-element.31.table, s32[1,16384]{1,0:T(1,128)S(1)} %get-tuple-element.32.index_ref, f32[1,16384]{1,0:T(1,128)S(1)} %get-tuple-element.33.frac_ref, ...), custom_call_target="tpu_custom_call" | custom-call | flops 2000000000 | bytes 8000000 | tf_op jit(solution)/shard_map/project_own/pallas_call | solution.py:192
  7.2 0.1 collective-permute-start.1
  7.4 3.0 %collective-permute-start.2 = (bf16[256,128]{1,0:T(8,128)(2,1)S(1)}, bf16[256,128]{1,0:T(8,128)(2,1)S(1)}, u32[]{:S(2)}, u32[]{:S(2)}) collective-permute-start(bf16[256,128]{1,0:T(8,128)(2,1)S(1)} %pair_rows.1.refs_0_), channel_id=1, source_target_pairs={{0,4},{1,5},{2,6},{3,7},{4,0},{5,1},{6,2},{7,3},{8,12},{9,13},{10,... | collective-permute-start | bytes 196616 | tf_op jit(solution)/shard_map/ppermute | solution.py:26
  10.4 2.6 %collective-permute-start.3 = (bf16[256,128]{1,0:T(8,128)(2,1)S(1)}, bf16[256,128]{1,0:T(8,128)(2,1)S(1)}, u32[]{:S(2)}, u32[]{:S(2)}) collective-permute-start(bf16[256,128]{1,0:T(8,128)(2,1)S(1)} %pair_rows.1.refs_0_), channel_id=1, source_target_pairs={{0,8},{1,9},{2,10},{3,11},{4,12},{5,13},{6,14},{7,15},{8,0},{9,1},... | collective-permute-start | bytes 196616 | tf_op jit(solution)/shard_map/ppermute | solution.py:26
  13.0 0.1 copy.9.shift_ref
  13.1 0.4 phase_tables.1
  13.5 4.4 %collective-permute-done.3.refs_2_ = bf16[256,128]{1,0:T(8,128)(2,1)S(1)} collective-permute-done((bf16[256,128]{1,0:T(8,128)(2,1)S(1)}, bf16[256,128]{1,0:T(8,128)(2,1)S(1)}, u32[]{:S(2)}, u32[]{:S(2)}) %collective-permute-start.3) | collective-permute-done | bytes 65568 | tf_op jit(solution)/shard_map/ppermute | solution.py:26
  17.9 1.3 %collective-permute-done.4.refs_3_ = bf16[256,128]{1,0:T(8,128)(2,1)S(1)} collective-permute-done((bf16[256,128]{1,0:T(8,128)(2,1)S(1)}, bf16[256,128]{1,0:T(8,128)(2,1)S(1)}, u32[]{:S(2)}, u32[]{:S(2)}) %collective-permute-start.4) | collective-permute-done | bytes 65568 | tf_op jit(solution)/shard_map/ppermute | solution.py:26
  19.2 1.7 %correlate.1.mine = f32[80,128]{1,0:T(8,128)S(1)} custom-call(bf16[32,16384]{1,0:T(8,128)(2,1)S(1)} %get-tuple-element.34.own_images, bf16[32,16384]{1,0:T(8,128)(2,1)S(1)} %collective-permute-done.1.other_images, f32[1,32]{1,0:T(1,128)S(1)} %bitcast.3, s32[1,32]{1,0:T(1,128)S(1)} %bitcast.4, f32[8,8192]{1,0:T(8,128)S(1)} %get-tuple-element.39.cos_ref, ...), custom_call_target="tpu_custom_call" | custom-call | tf_op jit(solution)/shard_map/correlate/pallas_call | solution.py:345
  21.0 1.2 %collective-permute-done.5.received = f32[80,128]{1,0:T(8,128)S(1)} collective-permute-done((f32[80,128]{1,0:T(8,128)S(1)}, f32[80,128]{1,0:T(8,128)S(1)}, u32[]{:S(2)}, u32[]{:S(2)}) %collective-permute-start.5) | collective-permute-done | bytes 40992 | tf_op jit(solution)/shard_map/ppermute | solution.py:26
  22.2 0.4 posterior.1
  22.6 1.6 %collective-permute-start.6 = (bf16[144,128]{1,0:T(8,128)(2,1)S(1)}, bf16[144,128]{1,0:T(8,128)(2,1)S(1)}, u32[]{:S(2)}, u32[]{:S(2)}) collective-permute-start(bf16[144,128]{1,0:T(8,128)(2,1)S(1)} %get-tuple-element.45), channel_id=1, source_target_pairs={{0,2},{1,3},{2,0},{3,1},{4,6},{5,7},{6,4},{7,5},{8,10},{9,11},{10,... | collective-permute-start | bytes 110600 | tf_op jit(solution)/shard_map/ppermute | solution.py:26
  24.1 1.3 %backproject.1 = (f32[224,128]{1,0:T(8,128)S(1)}, bf16[224,128]{1,0:T(8,128)(2,1)S(1)}, bf16[224,128]{1,0:T(8,128)(2,1)S(1)}, bf16[224,128]{1,0:T(8,128)(2,1)S(1)}) custom-call(bf16[64,64]{1,0:T(8,128)(2,1)S(1)} %get-tuple-element.42.weight_ref, bf16[32,16384]{1,0:T(8,128)(2,1)S(1)} %get-tuple-element.34.own_images, ...), custom_call_target="tpu_custom_call" | custom-call | flops 2000000000 | bytes 8000000 | tf_op jit(solution)/shard_map/backproject/pallas_call | solution.py:479
  25.4 0.8 %collective-permute-start.7 = (bf16[224,128]{1,0:T(8,128)(2,1)S(1)}, bf16[224,128]{1,0:T(8,128)(2,1)S(1)}, u32[]{:S(2)}, u32[]{:S(2)}) collective-permute-start(bf16[224,128]{1,0:T(8,128)(2,1)S(1)} %get-tuple-element.49), channel_id=1, source_target_pairs={{0,4},{1,5},{2,6},{3,7},{4,0},{5,1},{6,2},{7,3},{8,12},{9,13},{10,... | collective-permute-start | bytes 172040 | tf_op jit(solution)/shard_map/ppermute | solution.py:26
  26.3 1.7 %collective-permute-start.8 = (bf16[224,128]{1,0:T(8,128)(2,1)S(1)}, bf16[224,128]{1,0:T(8,128)(2,1)S(1)}, u32[]{:S(2)}, u32[]{:S(2)}) collective-permute-start(bf16[224,128]{1,0:T(8,128)(2,1)S(1)} %get-tuple-element.50), channel_id=1, source_target_pairs={{0,8},{1,9},{2,10},{3,11},{4,12},{5,13},{6,14},{7,15},{8,0},{9,1},... | collective-permute-start | bytes 172040 | tf_op jit(solution)/shard_map/ppermute | solution.py:26
  28.0 1.9 %collective-permute-start.9 = (bf16[224,128]{1,0:T(8,128)(2,1)S(1)}, bf16[224,128]{1,0:T(8,128)(2,1)S(1)}, u32[]{:S(2)}, u32[]{:S(2)}) collective-permute-start(bf16[224,128]{1,0:T(8,128)(2,1)S(1)} %get-tuple-element.51), channel_id=1, source_target_pairs={{0,12},{1,13},{2,14},{3,15},{4,8},{5,9},{6,10},{7,11},{8,4},{9,5},... | collective-permute-start | bytes 172040 | tf_op jit(solution)/shard_map/ppermute | solution.py:26
  30.0 2.5 %collective-permute-start.11 = (bf16[48,128]{1,0:T(8,128)(2,1)S(1)}, bf16[48,128]{1,0:T(8,128)(2,1)S(1)}, u32[]{:S(2)}, u32[]{:S(2)}) collective-permute-start(bf16[48,128]{1,0:T(8,128)(2,1)S(1)} %get-tuple-element.53), channel_id=1, source_target_pairs={{0,8},{1,9},{2,10},{3,11},{4,12},{5,13},{6,14},{7,15},{8,0},{9,1},... | collective-permute-start | bytes 36872 | tf_op jit(solution)/shard_map/ppermute | solution.py:26
  32.5 1.6 %collective-permute-done.10.refs_3_ = bf16[48,128]{1,0:T(8,128)(2,1)S(1)} collective-permute-done((bf16[48,128]{1,0:T(8,128)(2,1)S(1)}, bf16[48,128]{1,0:T(8,128)(2,1)S(1)}, u32[]{:S(2)}, u32[]{:S(2)}) %collective-permute-start.10) | collective-permute-done | bytes 12320 | tf_op jit(solution)/shard_map/ppermute | solution.py:26
  34.1 1.8 %collective-permute-start.12 = (bf16[48,128]{1,0:T(8,128)(2,1)S(1)}, bf16[48,128]{1,0:T(8,128)(2,1)S(1)}, u32[]{:S(2)}, u32[]{:S(2)}) collective-permute-start(bf16[48,128]{1,0:T(8,128)(2,1)S(1)} %get-tuple-element.54), channel_id=1, source_target_pairs={{0,12},{1,13},{2,14},{3,15},{4,8},{5,9},{6,10},{7,11},{8,4},{9,5},... | collective-permute-start | bytes 36872 | tf_op jit(solution)/shard_map/ppermute | solution.py:26
  35.9 3.7 %collective-permute-done.12.refs_5_ = bf16[48,128]{1,0:T(8,128)(2,1)S(1)} collective-permute-done((bf16[48,128]{1,0:T(8,128)(2,1)S(1)}, bf16[48,128]{1,0:T(8,128)(2,1)S(1)}, u32[]{:S(2)}, u32[]{:S(2)}) %collective-permute-start.12) | collective-permute-done | bytes 12320 | tf_op jit(solution)/shard_map/ppermute | solution.py:26
  39.7 1.2 %collective-permute-done.13.received = bf16[128,128]{1,0:T(8,128)(2,1)S(1)} collective-permute-done((bf16[128,128]{1,0:T(8,128)(2,1)S(1)}, bf16[128,128]{1,0:T(8,128)(2,1)S(1)}, u32[]{:S(2)}, u32[]{:S(2)}) %collective-permute-start.13) | collective-permute-done | bytes 32800 | tf_op jit(solution)/shard_map/ppermute | solution.py:26
  40.9 0.7 %finish.1 = (f32[256,128]{1,0:T(8,128)}, f32[8]{0:T(128)}) custom-call(f32[128,128]{1,0:T(8,128)S(1)} %get-tuple-element.55.own, bf16[128,128]{1,0:T(8,128)(2,1)S(1)} %collective-permute-done.13.received, f32[8,128]{1,0:T(8,128)S(1)} %get-tuple-element.57.mass), custom_call_target="tpu_custom_call" | custom-call | tf_op jit(solution)/shard_map/finish/pallas_call | solution.py:576
  (21 shorter events, 0.3 us)
Async XLA Ops:
  4.1 3.1 %collective-permute-start = (bf16[128,128]{1,0:T(8,128)(2,1)S(1)}, bf16[128,128]{1,0:T(8,128)(2,1)S(1)}, u32[]{:S(2)}, u32[]{:S(2)}) collective-permute-start(bf16[128,128]{1,0:T(8,128)(2,1)S(1)} %get-tuple-element.36), channel_id=1, source_target_pairs={{0,1},{1,0},{2,3},{3,2},{4,5},{5,4},{6,7},{7,6},{8,9},{9,8},{10,11... | collective-permute-start | bytes 98312 | tf_op jit(solution)/shard_map/ppermute | solution.py:26
  4.7 8.3 %copy-start.2 = (s32[8,2]{0,1:T(2,128)S(1)}, s32[8,2]{0,1:T(2,128)}, u32[]{:S(2)}) copy-start(s32[8,2]{0,1:T(2,128)} %param.13) | copy-start | bytes 196
  4.7 14.5 %copy-start = (f32[32]{0:T(128)S(1)}, f32[32]{0:T(128)}, u32[]{:S(2)}) copy-start(f32[32]{0:T(128)} %param.8) | copy-start | bytes 388
  4.7 14.5 %copy-start.1 = (s32[32]{0:T(128)S(1)}, s32[32]{0:T(128)}, u32[]{:S(2)}) copy-start(s32[32]{0:T(128)} %param.9) | copy-start | bytes 388
  7.2 11.9 %collective-permute-start.1 = (bf16[32,16384]{1,0:T(8,128)(2,1)S(1)}, bf16[32,16384]{1,0:T(8,128)(2,1)S(1)}, u32[]{:S(2)}, u32[]{:S(2)}) collective-permute-start(bf16[32,16384]{1,0:T(8,128)(2,1)S(1)} %get-tuple-element.38), channel_id=1, source_target_pairs={{0,1},{1,0},{2,3},{3,2},{4,5},{5,4},{6,7},{7,6},{8,9},{9,8},{10,11... | collective-permute-start | bytes 3145736 | tf_op jit(solution)/shard_map/ppermute | solution.py:26
  7.4 6.1 %collective-permute-start.2 = (bf16[256,128]{1,0:T(8,128)(2,1)S(1)}, bf16[256,128]{1,0:T(8,128)(2,1)S(1)}, u32[]{:S(2)}, u32[]{:S(2)}) collective-permute-start(bf16[256,128]{1,0:T(8,128)(2,1)S(1)} %pair_rows.1.refs_0_), channel_id=1, source_target_pairs={{0,4},{1,5},{2,6},{3,7},{4,0},{5,1},{6,2},{7,3},{8,12},{9,13},{10,... | collective-permute-start | bytes 196616 | tf_op jit(solution)/shard_map/ppermute | solution.py:26
  10.4 7.5 %collective-permute-start.3 = (bf16[256,128]{1,0:T(8,128)(2,1)S(1)}, bf16[256,128]{1,0:T(8,128)(2,1)S(1)}, u32[]{:S(2)}, u32[]{:S(2)}) collective-permute-start(bf16[256,128]{1,0:T(8,128)(2,1)S(1)} %pair_rows.1.refs_0_), channel_id=1, source_target_pairs={{0,8},{1,9},{2,10},{3,11},{4,12},{5,13},{6,14},{7,15},{8,0},{9,1},... | collective-permute-start | bytes 196616 | tf_op jit(solution)/shard_map/ppermute | solution.py:26
  13.0 6.2 %collective-permute-start.4 = (bf16[256,128]{1,0:T(8,128)(2,1)S(1)}, bf16[256,128]{1,0:T(8,128)(2,1)S(1)}, u32[]{:S(2)}, u32[]{:S(2)}) collective-permute-start(bf16[256,128]{1,0:T(8,128)(2,1)S(1)} %pair_rows.1.refs_0_), channel_id=1, source_target_pairs={{0,12},{1,13},{2,14},{3,15},{4,8},{5,9},{6,10},{7,11},{8,4},{9,5},... | collective-permute-start | bytes 196616 | tf_op jit(solution)/shard_map/ppermute | solution.py:26
  20.9 1.3 %collective-permute-start.5 = (f32[80,128]{1,0:T(8,128)S(1)}, f32[80,128]{1,0:T(8,128)S(1)}, u32[]{:S(2)}, u32[]{:S(2)}) collective-permute-start(f32[80,128]{1,0:T(8,128)S(1)} %correlate.1.mine), channel_id=1, source_target_pairs={{0,1},{1,0},{2,3},{3,2},{4,5},{5,4},{6,7},{7,6},{8,9},{9,8},{10,11... | collective-permute-start | bytes 122888 | tf_op jit(solution)/shard_map/ppermute | solution.py:26
  22.6 7.3 %collective-permute-start.6 = (bf16[144,128]{1,0:T(8,128)(2,1)S(1)}, bf16[144,128]{1,0:T(8,128)(2,1)S(1)}, u32[]{:S(2)}, u32[]{:S(2)}) collective-permute-start(bf16[144,128]{1,0:T(8,128)(2,1)S(1)} %get-tuple-element.45), channel_id=1, source_target_pairs={{0,2},{1,3},{2,0},{3,1},{4,6},{5,7},{6,4},{7,5},{8,10},{9,11},{10,... | collective-permute-start | bytes 110600 | tf_op jit(solution)/shard_map/ppermute | solution.py:26
  25.4 14.1 %collective-permute-start.7 = (bf16[224,128]{1,0:T(8,128)(2,1)S(1)}, bf16[224,128]{1,0:T(8,128)(2,1)S(1)}, u32[]{:S(2)}, u32[]{:S(2)}) collective-permute-start(bf16[224,128]{1,0:T(8,128)(2,1)S(1)} %get-tuple-element.49), channel_id=1, source_target_pairs={{0,4},{1,5},{2,6},{3,7},{4,0},{5,1},{6,2},{7,3},{8,12},{9,13},{10,... | collective-permute-start | bytes 172040 | tf_op jit(solution)/shard_map/ppermute | solution.py:26
  26.3 13.3 %collective-permute-start.8 = (bf16[224,128]{1,0:T(8,128)(2,1)S(1)}, bf16[224,128]{1,0:T(8,128)(2,1)S(1)}, u32[]{:S(2)}, u32[]{:S(2)}) collective-permute-start(bf16[224,128]{1,0:T(8,128)(2,1)S(1)} %get-tuple-element.50), channel_id=1, source_target_pairs={{0,8},{1,9},{2,10},{3,11},{4,12},{5,13},{6,14},{7,15},{8,0},{9,1},... | collective-permute-start | bytes 172040 | tf_op jit(solution)/shard_map/ppermute | solution.py:26
  28.0 11.6 %collective-permute-start.9 = (bf16[224,128]{1,0:T(8,128)(2,1)S(1)}, bf16[224,128]{1,0:T(8,128)(2,1)S(1)}, u32[]{:S(2)}, u32[]{:S(2)}) collective-permute-start(bf16[224,128]{1,0:T(8,128)(2,1)S(1)} %get-tuple-element.51), channel_id=1, source_target_pairs={{0,12},{1,13},{2,14},{3,15},{4,8},{5,9},{6,10},{7,11},{8,4},{9,5},... | collective-permute-start | bytes 172040 | tf_op jit(solution)/shard_map/ppermute | solution.py:26
  29.9 4.1 %collective-permute-start.10 = (bf16[48,128]{1,0:T(8,128)(2,1)S(1)}, bf16[48,128]{1,0:T(8,128)(2,1)S(1)}, u32[]{:S(2)}, u32[]{:S(2)}) collective-permute-start(bf16[48,128]{1,0:T(8,128)(2,1)S(1)} %get-tuple-element.52), channel_id=1, source_target_pairs={{0,4},{1,5},{2,6},{3,7},{4,0},{5,1},{6,2},{7,3},{8,12},{9,13},{10,... | collective-permute-start | bytes 36872 | tf_op jit(solution)/shard_map/ppermute | solution.py:26
  30.0 5.9 %collective-permute-start.11 = (bf16[48,128]{1,0:T(8,128)(2,1)S(1)}, bf16[48,128]{1,0:T(8,128)(2,1)S(1)}, u32[]{:S(2)}, u32[]{:S(2)}) collective-permute-start(bf16[48,128]{1,0:T(8,128)(2,1)S(1)} %get-tuple-element.53), channel_id=1, source_target_pairs={{0,8},{1,9},{2,10},{3,11},{4,12},{5,13},{6,14},{7,15},{8,0},{9,1},... | collective-permute-start | bytes 36872 | tf_op jit(solution)/shard_map/ppermute | solution.py:26
  34.1 5.5 %collective-permute-start.12 = (bf16[48,128]{1,0:T(8,128)(2,1)S(1)}, bf16[48,128]{1,0:T(8,128)(2,1)S(1)}, u32[]{:S(2)}, u32[]{:S(2)}) collective-permute-start(bf16[48,128]{1,0:T(8,128)(2,1)S(1)} %get-tuple-element.54), channel_id=1, source_target_pairs={{0,12},{1,13},{2,14},{3,15},{4,8},{5,9},{6,10},{7,11},{8,4},{9,5},... | collective-permute-start | bytes 36872 | tf_op jit(solution)/shard_map/ppermute | solution.py:26
  39.6 1.3 %collective-permute-start.13 = (bf16[128,128]{1,0:T(8,128)(2,1)S(1)}, bf16[128,128]{1,0:T(8,128)(2,1)S(1)}, u32[]{:S(2)}, u32[]{:S(2)}) collective-permute-start(bf16[128,128]{1,0:T(8,128)(2,1)S(1)} %get-tuple-element.56), channel_id=1, source_target_pairs={{0,1},{1,0},{2,3},{3,2},{4,5},{5,4},{6,7},{7,6},{8,9},{9,8},{10,11... | collective-permute-start | bytes 98312 | tf_op jit(solution)/shard_map/ppermute | solution.py:26

commit v9 on v8

--- a/solution.py
+++ b/solution.py
@@ -226,9 +226,12 @@
     )(own, other)
 
 
-def slot_rows(device, slots):
-    ids = lax.broadcasted_iota(jnp.int32, (slots, 1), 0)
-    return 2 * ((device // 4) ^ (ids // 2)) + ids % 2
+def chip_order(chips):
+    return [0, chips - 1] + list(range(1, chips - 1))
+
+
+def slot_orientation(device, slot, slots):
+    return 2 * ((device // 4) ^ chip_order(slots // 2)[slot // 2]) + slot % 2
 
 
 def split_mass(mass_row):
@@ -274,7 +277,7 @@
     )(shift_grid)
 
 
-def correlate_kernel(own_images, other_images, precision_ref, assigned_ref, cos_ref, sin_ref, *refs, chunk):
+def correlate_kernel(own_images, other_images, cos_ref, sin_ref, *refs, chunk):
     pair_refs, (out_ref, proj) = refs[:-2], refs[-2:]
     shifts = cos_ref.shape[0]
     parts = own_images.shape[0]
@@ -282,29 +285,32 @@
     width = own_images.shape[1] // 2
     tiles = width // LANES
     per_row = 2 * tiles
-    for m, ref in enumerate(pair_refs):
-        proj[2 * m * per_row : 2 * (m + 1) * per_row, :] = ref[...].astype(jnp.float32)
+    combos = shifts * slots
+    for slot in range(slots):
+        place = slice(slot % 2 * per_row, (slot % 2 + 1) * per_row)
+        row = pair_refs[slot // 2][place, :].astype(jnp.float32)
+        proj[slot * per_row : (slot + 1) * per_row, :] = row
+        out_ref[combos + slot : combos + slot + 1, :] = jnp.sum(row * row, axis=0, keepdims=True)
 
     chunk_tiles = chunk // LANES
     contract_lanes = (((1,), (1,)), ((), ()))
 
-    def body(step, carry):
-        total, power = carry
+    def body(step, total):
         first = step * chunk_tiles
-        real = jnp.concatenate(
-            [proj[pl.ds(first + k, slots, stride=per_row), :] for k in range(chunk_tiles)], axis=1
-        )
-        imag = jnp.concatenate(
-            [proj[pl.ds(tiles + first + k, slots, stride=per_row), :] for k in range(chunk_tiles)],
-            axis=1,
-        )
         where = pl.ds(pl.multiple_of(step * chunk, chunk), chunk)
         imag_where = pl.ds(pl.multiple_of(width + step * chunk, chunk), chunk)
+        cos_part, sin_part = cos_ref[:, where], sin_ref[:, where]
         reals, imags = [], []
-        for s in range(shifts):
-            cos_s, sin_s = cos_ref[s : s + 1, where], sin_ref[s : s + 1, where]
-            reals.append(real * cos_s - imag * sin_s)
-            imags.append(real * sin_s + imag * cos_s)
+        for slot in range(slots):
+            start = slot * per_row + first
+            real = jnp.concatenate(
+                [proj[pl.ds(start + k, 1), :] for k in range(chunk_tiles)], axis=1
+            )
+            imag = jnp.concatenate(
+                [proj[pl.ds(start + tiles + k, 1), :] for k in range(chunk_tiles)], axis=1
+            )
+            reals.append(real * cos_part - imag * sin_part)
+            imags.append(real * sin_part + imag * cos_part)
         turned_real = jnp.concatenate(reals, axis=0).astype(jnp.bfloat16)
         turned_imag = jnp.concatenate(imags, axis=0).astype(jnp.bfloat16)
         image_real = jnp.concatenate([own_images[:, where], other_images[:, where]], axis=0)
@@ -312,45 +318,55 @@
         total = total + lax.dot_general(
             turned_real, image_real, contract_lanes, preferred_element_type=jnp.float32
         )
-        total = total + lax.dot_general(
+        return total + lax.dot_general(
             turned_imag, image_imag, contract_lanes, preferred_element_type=jnp.float32
         )
-        squares = real * real + imag * imag
-        for k in range(chunk_tiles):
-            power = power + squares[:, k * LANES : (k + 1) * LANES]
-        return total, power
-
-    total, power = lax.fori_loop(
-        0,
-        width // chunk,
-        body,
-        (
-            jnp.zeros((shifts * slots, 2 * parts), jnp.float32),
-            jnp.zeros((slots, LANES), jnp.float32),
-        ),
-    )
-    combos = shifts * slots
-    out_ref[...] = jnp.zeros_like(out_ref)
+
+    total = lax.fori_loop(
+        0, width // chunk, body, jnp.zeros((combos, 2 * parts), jnp.float32), unroll=2
+    )
+    out_ref[0:combos, :] = jnp.zeros((combos, LANES), jnp.float32)
     out_ref[0:combos, 0 : 2 * parts] = total
-    out_ref[combos : combos + slots, :] = jnp.broadcast_to(
-        jnp.sum(power, axis=1, keepdims=True), (slots, LANES)
-    )
-    out_ref[combos + slots : combos + slots + 1, 0:parts] = precision_ref[...]
-    out_ref[combos + slots + 1 : combos + slots + 2, 0:parts] = assigned_ref[...].astype(jnp.float32)
-
-
-def correlate(own_images, other_images, precision, assigned, cos_table, sin_table, pairs):
+
+
+def correlate(own_images, other_images, cos_table, sin_table, pairs):
     slots = 2 * len(pairs)
     shifts, width = cos_table.shape
     return pl.pallas_call(
         functools.partial(correlate_kernel, chunk=2048),
-        in_specs=whole_vmem(6 + len(pairs)),
+        in_specs=whole_vmem(4 + len(pairs)),
         out_specs=pl.BlockSpec(memory_space=pltpu.VMEM),
-        out_shape=jax.ShapeDtypeStruct((shifts * slots + slots + 8, LANES), jnp.float32),
+        out_shape=jax.ShapeDtypeStruct((shifts * slots + slots, LANES), jnp.float32),
         scratch_shapes=[pltpu.VMEM((slots * 2 * width // LANES, LANES), jnp.float32)],
-        compiler_params=pltpu.CompilerParams(vmem_limit_bytes=(14 + slots // 2) * MIB),
+        compiler_params=pltpu.CompilerParams(vmem_limit_bytes=(14 + slots) * MIB),
+        cost_estimate=pl.CostEstimate(flops=1500000000, bytes_accessed=6000000, transcendentals=0),
         name="correlate",
-    )(own_images, other_images, precision, assigned, cos_table, sin_table, *pairs)
+    )(own_images, other_images, cos_table, sin_table, *pairs)
+
+
+def collect_kernel(near, far, precision_ref, assigned_ref, out_ref, *, combos):
+    slots = near.shape[0] - combos
+    parts = precision_ref.shape[1]
+    for index, ref in enumerate((near, far)):
+        out_ref[index * combos : (index + 1) * combos, :] = ref[0:combos, :]
+        power = 2 * combos + index * slots
+        out_ref[power : power + slots, :] = ref[combos:, :]
+    rest = 2 * combos + 2 * slots
+    out_ref[rest:, :] = jnp.zeros((8, LANES), jnp.float32)
+    out_ref[rest : rest + 1, 0:parts] = precision_ref[...]
+    out_ref[rest + 1 : rest + 2, 0:parts] = assigned_ref[...].astype(jnp.float32)
+
+
+def collect(near, far, precision, assigned, combos):
+    rows = 2 * near.shape[0] + 8
+    return pl.pallas_call(
+        functools.partial(collect_kernel, combos=combos),
+        in_specs=whole_vmem(4),
+        out_specs=pl.BlockSpec(memory_space=pltpu.VMEM),
+        out_shape=jax.ShapeDtypeStruct((rows, LANES), jnp.float32),
+        compiler_params=pltpu.CompilerParams(vmem_limit_bytes=16 * MIB),
+        name="collect",
+    )(near, far, precision, assigned)
 
 
 def rotate_back(weights, own_images, other_images, cos_ref, sin_ref, where, imag_where, slots):
@@ -372,7 +388,7 @@
 
 def posterior_kernel(
     mine, received, own_images, other_images, cos_ref, sin_ref,
-    weight_ref, low_ref, low_send, own_mass, *, slots
+    weight_ref, low_ref, low_send, own_mass, ordered, *, slots
 ):
     device = lax.axis_index("particle")
     shifts, width = cos_ref.shape
@@ -384,31 +400,35 @@
         lane < parts, pltpu.roll(theirs, LANES - parts, 1), pltpu.roll(theirs, parts, 1)
     )
     joint = mine[...] + swapped
-    power = mine[combos : combos + slots, :] + received[combos : combos + slots, :]
+    power = jnp.sum(
+        mine[combos : combos + slots, :] + received[combos : combos + slots, :], axis=1, keepdims=True
+    )
     precision = joint[combos + slots : combos + slots + 1]
     assigned = joint[combos + slots + 1 : combos + slots + 2].astype(jnp.int32)
-    slot_class = slot_rows(device, slots) // (slots // CLASSES)
-    match = (slot_class == assigned).astype(jnp.float32) * PRIOR_REWARD
     likelihood_scale = 1.0 / math.sqrt(4 * width)
-    logits = [
-        precision * (joint[s * slots : (s + 1) * slots] - 0.5 * power) * likelihood_scale + match
-        for s in range(shifts)
-    ]
-    peak = functools.reduce(jnp.maximum, logits)
-    peak = jnp.max(peak, axis=0, keepdims=True)
+    classes = [slot_orientation(device, slot, slots) // (slots // CLASSES) for slot in range(slots)]
+    logits = []
+    for slot in range(slots):
+        match = (assigned == classes[slot]).astype(jnp.float32) * PRIOR_REWARD
+        part = joint[slot * shifts : (slot + 1) * shifts]
+        logits.append(precision * (part - 0.5 * power[slot : slot + 1]) * likelihood_scale + match)
+    peak = jnp.max(functools.reduce(jnp.maximum, logits), axis=0, keepdims=True)
     terms = [jnp.exp(value - peak) for value in logits]
-    mass = functools.reduce(jnp.add, terms)
-    norm = jnp.sum(mass, axis=0, keepdims=True)
-    weights = jnp.concatenate([term / norm for term in terms], axis=0)
+    norm = jnp.sum(functools.reduce(jnp.add, terms), axis=0, keepdims=True)
+    counted = lax.broadcasted_iota(jnp.int32, (1, LANES), 1) < 2 * parts
+    class_lane = lax.broadcasted_iota(jnp.int32, (1, LANES), 1)
+    mass_row = jnp.zeros((1, LANES), jnp.float32)
+    for slot in range(slots):
+        value = terms[slot] / norm
+        ordered[slot * shifts : (slot + 1) * shifts, :] = value
+        share = jnp.where(counted, jnp.sum(value, axis=0, keepdims=True) * precision, 0.0)
+        share = jnp.sum(share, axis=1, keepdims=True)
+        mass_row = mass_row + jnp.where(class_lane == classes[slot], share, 0.0)
+    weights = jnp.concatenate(
+        [ordered[pl.ds(s, slots, stride=shifts), :] for s in range(shifts)], axis=0
+    )
     weights = weights[:, 0 : 2 * parts].astype(jnp.bfloat16)
     weight_ref[...] = weights
-    counted = lax.broadcasted_iota(jnp.int32, (1, LANES), 1) < 2 * parts
-    share = jnp.where(counted, mass / norm * precision, 0.0)
-    slot_mass = jnp.sum(share, axis=1, keepdims=True)
-    class_lane = lax.broadcasted_iota(jnp.int32, (slots, LANES), 1)
-    mass_row = jnp.sum(
-        jnp.where(class_lane == slot_class, slot_mass, 0.0), axis=0, keepdims=True
-    )
     own_mass[...] = jnp.broadcast_to(mass_row, own_mass.shape)
 
     low = LOW_TILES * LANES
@@ -437,6 +457,7 @@
             jax.ShapeDtypeStruct((low + MASS_ROWS, LANES), jnp.bfloat16),
             jax.ShapeDtypeStruct((8, LANES), jnp.float32),
         ],
+        scratch_shapes=[pltpu.VMEM((shifts * slots, LANES), jnp.float32)],
         compiler_params=pltpu.CompilerParams(vmem_limit_bytes=(14 + slots // 2) * MIB),
         name="posterior",
     )(mine, received, own_images, other_images, cos_table, sin_table)
@@ -491,65 +512,72 @@
     )(weights, own_images, other_images, cos_table, sin_table)
 
 
-def fold_kernel(low_ref, low_received, mass, own, own_mass, *sends):
+def fold_kernel(low_ref, low_received, mass, *refs, chips):
+    mains, (own, own_mass), sends = refs[: chips - 1], refs[chips - 1 : chips + 1], refs[chips + 1 :]
     rows = own.shape[0]
     low_body = low_ref.shape[0]
     total_mass = mass[0:1, :] + joined_mass(low_received[low_body:, :])
     block = split_mass(total_mass)
     own_mass[...] = jnp.broadcast_to(total_mass, own_mass.shape)
-    for m, target in enumerate((own,) + sends):
+    for m, target in enumerate((own,) + tuple(sends)):
         part = slice(m * rows, (m + 1) * rows)
         value = (low_ref[part, :] + low_received[part, :].astype(jnp.float32)) * 0.5
         target[0:rows, :] = value.astype(target.dtype)
         if m > 0:
-            target[rows:, :] = block
-
-
-def fold(low, low_received, mass, chips):
+            target[rows : rows + MASS_ROWS, :] = block
+            target[rows + MASS_ROWS :, :] = mains[m - 1][...]
+
+
+def fold(low, low_received, mass, mains):
+    chips = len(mains) + 1
     rows = low.shape[0] // chips
     return pl.pallas_call(
-        fold_kernel,
-        in_specs=whole_vmem(3),
+        functools.partial(fold_kernel, chips=chips),
+        in_specs=whole_vmem(2 + chips),
         out_specs=whole_vmem(1 + chips),
         out_shape=[
             jax.ShapeDtypeStruct((rows, LANES), jnp.float32),
             jax.ShapeDtypeStruct((8, LANES), jnp.float32),
         ]
-        + [jax.ShapeDtypeStruct((rows + MASS_ROWS, LANES), jnp.bfloat16)] * (chips - 1),
+        + [
+            jax.ShapeDtypeStruct((rows + MASS_ROWS + main.shape[0], LANES), jnp.bfloat16)
+            for main in mains
+        ],
         compiler_params=pltpu.CompilerParams(vmem_limit_bytes=16 * MIB),
         name="fold",
-    )(low, low_received, mass)
-
-
-def merge_kernel(own, own_low, mass, *refs, others):
-    received, low_received = refs[:others], refs[others : 2 * others]
-    keep, to_core, mass_out = refs[2 * others :]
+    )(low, low_received, mass, *mains)
+
+
+def merge_kernel(own, own_low, mass, *refs):
+    received, (keep, to_core, mass_out) = refs[:-3], refs[-3:]
     core = own_half()
-    low_half = own_low.shape[0] // 2
+    low_rows = own_low.shape[0]
+    low_half = low_rows // 2
+    head = low_rows + MASS_ROWS
     half = own.shape[0] // 2
     total_mass = mass[0:1, :]
-    for ref in low_received:
-        total_mass = total_mass + joined_mass(ref[2 * low_half :, :])
+    for ref in received:
+        total_mass = total_mass + joined_mass(ref[low_rows:head, :])
     mass_out[...] = jnp.broadcast_to(total_mass, mass_out.shape)
     for target, place in ((to_core, 1 - core), (keep, core)):
-        where = pl.ds(pl.multiple_of(place * half, half), half)
-        total = own[where, :]
+        start = pl.multiple_of(place * half, half)
+        total = own[pl.ds(start, half), :]
         for ref in received:
-            total = total + ref[where, :].astype(jnp.float32)
+            total = total + ref[pl.ds(head + start, half), :].astype(jnp.float32)
         where = pl.ds(pl.multiple_of(place * low_half, low_half), low_half)
         low = own_low[where, :]
-        for ref in low_received:
+        for ref in received:
             low = low + ref[where, :].astype(jnp.float32)
         target[...] = jnp.concatenate(
             [low[0:LOW_TILES], total[0 : half // 2], low[LOW_TILES:], total[half // 2 :]], axis=0
         ).astype(target.dtype)
 
 
-def merge(own, own_low, mass, received, low_received):
+def merge(own, own_low, mass, received):
     rows = (own.shape[0] + own_low.shape[0]) // 2
     return pl.pallas_call(
-        functools.partial(merge_kernel, others=len(received)),
-        in_specs=whole_vmem(3 + 2 * len(received)),
+        merge_kernel,
+        in_specs=whole_vmem(3 + len(received)),
         out_specs=whole_vmem(3),
         out_shape=[
             jax.ShapeDtypeStruct((rows, LANES), jnp.float32),
@@ -558,7 +586,7 @@
         ],
         compiler_params=pltpu.CompilerParams(vmem_limit_bytes=16 * MIB),
         name="merge",
-    )(own, own_low, mass, *received, *low_received)
+    )(own, own_low, mass, *received)
 
 
 def finish_kernel(own, received, mass, out, mass_out, *, scale, mass_scale):
@@ -598,27 +626,29 @@
     own, own_images, other_images = project_own(table, index, frac, images)
     pair = pair_rows(own, from_core)
     pair, other_images = lax.optimization_barrier((pair, other_images))
-    pairs = [pair] + [exchange(pair, 4 * m) for m in range(1, chips)]
+    others = chip_order(chips)[1:]
+    pairs = [pair] + [exchange(pair, 4 * m) for m in others]
     images_received = exchange(other_images, 1)
     cos_table, sin_table = phase_tables(shift_grid, width // 4)
-    mine = correlate(
-        own_images,
-        images_received,
+    near, far = (
+        correlate(own_images, images_received, cos_table, sin_table, part)
+        for part in (pairs[: chips // 2], pairs[chips // 2 :])
+    )
+    mine = collect(
+        near,
+        far,
         noise_precision.reshape(1, parts),
         assigned_class.reshape(1, parts),
-        cos_table,
-        sin_table,
-        pairs,
+        shift_grid.shape[0] * slots // 2,
     )
     weights, low, low_send, mass = posterior(
         mine, exchange(mine, 1), own_images, images_received, cos_table, sin_table, slots
     )
     low_from_half = exchange(low_send, 2)
     sums = backproject(weights, own_images, images_received, cos_table, sin_table, slots)
-    received = [exchange(send, 4 * m) for m, send in enumerate(sums[1:], start=1)]
-    folded = fold(low, low_from_half, mass, chips)
-    low_received = [exchange(send, 4 * m) for m, send in enumerate(folded[2:], start=1)]
-    keep, send, mass = merge(sums[0], folded[0], folded[1], received, low_received)
+    folded = fold(low, low_from_half, mass, sums[1:])
+    chip_sums = [exchange(send, 4 * m) for m, send in zip(others, folded[2:])]
+    keep, send, mass = merge(sums[0], folded[0], folded[1], chip_sums)
     back, class_mass = finish(
         keep, exchange(send, 1), mass, 1.0 / math.sqrt(parts), CLASSES / (parts * dev_count)
     )

time: 41.7 us -> 35.8 us (0.86)
  starting transfers between devices: 16.8 us -> 12.5 us
  waiting for transfers between devices: 13.3 us -> 11.7 us
    ppermute x14 -> x11, starting transfers between devices: 16.8 us -> 12.5 us  [exchange(): return lax.ppermute(value, 'particle', pairs)]
    ppermute x14 -> x11, waiting for transfers between devices: 13.3 us -> 11.7 us  [exchange(): return lax.ppermute(value, 'particle', pairs)]
    pallas_call x1 -> x2, Pallas kernels: 1.72 us -> 1.69 us  [correlate(): pl.pallas_call(functools.partial(correlate_kernel, chunk=2048), in_specs=...]
  transfers between devices with their start and end apart: 14 -> 11, of which waited for: 6 -> 9; matrix products, arithmetic and copies ran while one was open for 0% -> 0% of each run, Pallas kernels for 10% -> 14%
where the time goes in v9:
time: 35.8 us; the launch traced here: 35.6 us
  starting transfers between devices  12.5 us (35%)
  waiting for transfers between devices  11.7 us (33%)
  Pallas kernels  10.6 us (30%)
  between operations  0.77 us (2%)
    ppermute x11, starting transfers between devices, exchange(): return lax.ppermute(value, 'particle', pairs)  12.5 us
    ppermute x11, waiting for transfers between devices, exchange(): return lax.ppermute(value, 'particle', pairs)  11.7 us
    pallas_call x1, Pallas kernels, project_other(): pl.pallas_call(project_other_kernel, in_specs=[pl.BlockSpec(memory_space=...  3.5 us
    pallas_call x1, Pallas kernels, project_own(): pl.pallas_call(project_own_kernel, in_specs=whole_vmem(3) + [pl.BlockSpec...  2.54 us
    pallas_call x2, Pallas kernels, correlate(): pl.pallas_call(functools.partial(correlate_kernel, chunk=2048), in_specs=...  1.69 us
    pallas_call x1, Pallas kernels, backproject(): pl.pallas_call(functools.partial(backproject_kernel, slots=slots, chunk=L...  1.3 us
  transfers between devices with their start and end apart: 11, of which 9 were waited for; matrix products, arithmetic and copies ran while one was open for 0% of the time, Pallas kernels for 14%

profile of v9, /device:TPU:0, one launch (start us, length us, event | category | flops | bytes accessed | tf_op | source)
XLA Modules:
  0.0 35.6 jit_solution(18439962619635699028)
XLA Ops:
  0.6 3.5 %project_other.1 = (bf16[128,128]{1,0:T(8,128)(2,1)S(1)}, bf16[304,256]{1,0:T(8,128)(2,1)S(1)}, s32[1,16384]{1,0:T(1,128)S(1)}, f32[1,16384]{1,0:T(1,128)S(1)}) custom-call(bf16[2,8,2,32768]{3,2,1,0:T(2,128)(2,1)} %table_hbm.1, s32[1,16384]{1,0:T(1,128)} %index_hbm.1, f32[1,16384]{1,0:T(1,128)} %frac_hbm.1), custom_call_target="tpu_custom_call" | custom-call | tf_op jit(solution)/shard_map/project_other/pallas_call | solution.py:139
  4.1 0.5 %collective-permute-start = (bf16[128,128]{1,0:T(8,128)(2,1)S(1)}, bf16[128,128]{1,0:T(8,128)(2,1)S(1)}, u32[]{:S(2)}, u32[]{:S(2)}) collective-permute-start(bf16[128,128]{1,0:T(8,128)(2,1)S(1)} %get-tuple-element.36), channel_id=1, source_target_pairs={{0,1},{1,0},{2,3},{3,2},{4,5},{5,4},{6,7},{7,6},{8,9},{9,8},{10,11... | collective-permute-start | bytes 98312 | tf_op jit(solution)/shard_map/ppermute | solution.py:26
  4.7 2.5 %project_own.1 = (bf16[128,128]{1,0:T(8,128)(2,1)S(1)}, bf16[32,16384]{1,0:T(8,128)(2,1)S(1)}, bf16[32,16384]{1,0:T(8,128)(2,1)S(1)}) custom-call(bf16[304,256]{1,0:T(8,128)(2,1)S(1)} %get-tuple-element.31.table, s32[1,16384]{1,0:T(1,128)S(1)} %get-tuple-element.32.index_ref, f32[1,16384]{1,0:T(1,128)S(1)} %get-tuple-element.33.frac_ref, ...), custom_call_target="tpu_custom_call" | custom-call | flops 2000000000 | bytes 8000000 | tf_op jit(solution)/shard_map/project_own/pallas_call | solution.py:192
  7.2 0.1 collective-permute-start.1
  7.4 5.0 %collective-permute-start.2 = (bf16[256,128]{1,0:T(8,128)(2,1)S(1)}, bf16[256,128]{1,0:T(8,128)(2,1)S(1)}, u32[]{:S(2)}, u32[]{:S(2)}) collective-permute-start(bf16[256,128]{1,0:T(8,128)(2,1)S(1)} %pair_rows.1.refs_0_), channel_id=1, source_target_pairs={{0,12},{1,13},{2,14},{3,15},{4,8},{5,9},{6,10},{7,11},{8,4},{9,5},... | collective-permute-start | bytes 196616 | tf_op jit(solution)/shard_map/ppermute | solution.py:26
  12.5 0.4 %phase_tables.1 = (f32[8,8192]{1,0:T(8,128)S(1)}, f32[8,8192]{1,0:T(8,128)S(1)}) custom-call(s32[8,2]{1,0:T(8,128)S(1)} %copy.9.shift_ref), custom_call_target="tpu_custom_call" | custom-call | flops 2000000 | bytes 2000000 | tf_op jit(solution)/shard_map/phase_tables/pallas_call | solution.py:269
  13.0 0.6 %collective-permute-start.4 = (bf16[256,128]{1,0:T(8,128)(2,1)S(1)}, bf16[256,128]{1,0:T(8,128)(2,1)S(1)}, u32[]{:S(2)}, u32[]{:S(2)}) collective-permute-start(bf16[256,128]{1,0:T(8,128)(2,1)S(1)} %pair_rows.1.refs_0_), channel_id=1, source_target_pairs={{0,8},{1,9},{2,10},{3,11},{4,12},{5,13},{6,14},{7,15},{8,0},{9,1},... | collective-permute-start | bytes 196616 | tf_op jit(solution)/shard_map/ppermute | solution.py:26
  13.5 1.7 %collective-permute-done.2.refs_1_ = bf16[256,128]{1,0:T(8,128)(2,1)S(1)} collective-permute-done((bf16[256,128]{1,0:T(8,128)(2,1)S(1)}, bf16[256,128]{1,0:T(8,128)(2,1)S(1)}, u32[]{:S(2)}, u32[]{:S(2)}) %collective-permute-start.2) | collective-permute-done | bytes 65568 | tf_op jit(solution)/shard_map/ppermute | solution.py:26
  15.3 0.8 %correlate.2.near = f32[36,128]{1,0:T(8,128)S(1)} custom-call(bf16[32,16384]{1,0:T(8,128)(2,1)S(1)} %get-tuple-element.34.own_images, bf16[32,16384]{1,0:T(8,128)(2,1)S(1)} %collective-permute-done.1.other_images, f32[8,8192]{1,0:T(8,128)S(1)} %get-tuple-element.39.cos_ref, f32[8,8192]{1,0:T(8,128)S(1)} %get-tuple-element.40.sin_ref, ...), custom_call_target="tpu_custom_call" | custom-call | flops 1500000000 | bytes 6000000 | tf_op jit(solution)/shard_map/correlate/pallas_call | solution.py:335
  16.1 1.6 %collective-permute-done.3.refs_0_ = bf16[256,128]{1,0:T(8,128)(2,1)S(1)} collective-permute-done((bf16[256,128]{1,0:T(8,128)(2,1)S(1)}, bf16[256,128]{1,0:T(8,128)(2,1)S(1)}, u32[]{:S(2)}, u32[]{:S(2)}) %collective-permute-start.3) | collective-permute-done | bytes 65568 | tf_op jit(solution)/shard_map/ppermute | solution.py:26
  17.8 1.1 %collective-permute-done.4.refs_1_ = bf16[256,128]{1,0:T(8,128)(2,1)S(1)} collective-permute-done((bf16[256,128]{1,0:T(8,128)(2,1)S(1)}, bf16[256,128]{1,0:T(8,128)(2,1)S(1)}, u32[]{:S(2)}, u32[]{:S(2)}) %collective-permute-start.4) | collective-permute-done | bytes 65568 | tf_op jit(solution)/shard_map/ppermute | solution.py:26
  18.8 0.8 %correlate.3.far = f32[36,128]{1,0:T(8,128)S(1)} custom-call(bf16[32,16384]{1,0:T(8,128)(2,1)S(1)} %get-tuple-element.34.own_images, bf16[32,16384]{1,0:T(8,128)(2,1)S(1)} %collective-permute-done.1.other_images, f32[8,8192]{1,0:T(8,128)S(1)} %get-tuple-element.39.cos_ref, f32[8,8192]{1,0:T(8,128)S(1)} %get-tuple-element.40.sin_ref, ...), custom_call_target="tpu_custom_call" | custom-call | flops 1500000000 | bytes 6000000 | tf_op jit(solution)/shard_map/correlate/pallas_call | solution.py:335
  19.8 1.2 %collective-permute-done.5.received = f32[80,128]{1,0:T(8,128)S(1)} collective-permute-done((f32[80,128]{1,0:T(8,128)S(1)}, f32[80,128]{1,0:T(8,128)S(1)}, u32[]{:S(2)}, u32[]{:S(2)}) %collective-permute-start.5) | collective-permute-done | bytes 40992 | tf_op jit(solution)/shard_map/ppermute | solution.py:26
  21.0 0.4 %posterior.1 = (bf16[64,64]{1,0:T(8,128)(2,1)S(1)}, f32[128,128]{1,0:T(8,128)S(1)}, bf16[144,128]{1,0:T(8,128)(2,1)S(1)}, f32[8,128]{1,0:T(8,128)S(1)}) custom-call(f32[80,128]{1,0:T(8,128)S(1)} %collect.1.mine, f32[80,128]{1,0:T(8,128)S(1)} %collective-permute-done.5.received, bf16[32,16384]{1,0:T(8,128)(2,1)S(1)} %get-tuple-element.34.own_images, ...), custom_call_target="tpu_custom_call" | custom-call | tf_op jit(solution)/shard_map/posterior/pallas_call | solution.py:450
  21.4 1.6 %collective-permute-start.6 = (bf16[144,128]{1,0:T(8,128)(2,1)S(1)}, bf16[144,128]{1,0:T(8,128)(2,1)S(1)}, u32[]{:S(2)}, u32[]{:S(2)}) collective-permute-start(bf16[144,128]{1,0:T(8,128)(2,1)S(1)} %get-tuple-element.45), channel_id=1, source_target_pairs={{0,2},{1,3},{2,0},{3,1},{4,6},{5,7},{6,4},{7,5},{8,10},{9,11},{10,... | collective-permute-start | bytes 110600 | tf_op jit(solution)/shard_map/ppermute | solution.py:26
  23.0 1.3 %backproject.1 = (f32[224,128]{1,0:T(8,128)S(1)}, bf16[224,128]{1,0:T(8,128)(2,1)S(1)}, bf16[224,128]{1,0:T(8,128)(2,1)S(1)}, bf16[224,128]{1,0:T(8,128)(2,1)S(1)}) custom-call(bf16[64,64]{1,0:T(8,128)(2,1)S(1)} %get-tuple-element.42.weight_ref, bf16[32,16384]{1,0:T(8,128)(2,1)S(1)} %get-tuple-element.34.own_images, ...), custom_call_target="tpu_custom_call" | custom-call | flops 2000000000 | bytes 8000000 | tf_op jit(solution)/shard_map/backproject/pallas_call | solution.py:500
  24.3 1.2 %collective-permute-done.6.low_received = bf16[144,128]{1,0:T(8,128)(2,1)S(1)} collective-permute-done((bf16[144,128]{1,0:T(8,128)(2,1)S(1)}, bf16[144,128]{1,0:T(8,128)(2,1)S(1)}, u32[]{:S(2)}, u32[]{:S(2)}) %collective-permute-start.6) | collective-permute-done | bytes 36896 | tf_op jit(solution)/shard_map/ppermute | solution.py:26
  25.5 2.5 %collective-permute-start.7 = (bf16[272,128]{1,0:T(8,128)(2,1)S(1)}, bf16[272,128]{1,0:T(8,128)(2,1)S(1)}, u32[]{:S(2)}, u32[]{:S(2)}) collective-permute-start(bf16[272,128]{1,0:T(8,128)(2,1)S(1)} %get-tuple-element.52), channel_id=1, source_target_pairs={{0,12},{1,13},{2,14},{3,15},{4,8},{5,9},{6,10},{7,11},{8,4},{9,5},... | collective-permute-start | bytes 208904 | tf_op jit(solution)/shard_map/ppermute | solution.py:26
  27.9 2.0 %collective-permute-start.9 = (bf16[272,128]{1,0:T(8,128)(2,1)S(1)}, bf16[272,128]{1,0:T(8,128)(2,1)S(1)}, u32[]{:S(2)}, u32[]{:S(2)}) collective-permute-start(bf16[272,128]{1,0:T(8,128)(2,1)S(1)} %get-tuple-element.54), channel_id=1, source_target_pairs={{0,8},{1,9},{2,10},{3,11},{4,12},{5,13},{6,14},{7,15},{8,0},{9,1},... | collective-permute-start | bytes 208904 | tf_op jit(solution)/shard_map/ppermute | solution.py:26
  29.9 2.2 %collective-permute-done.7.refs_0_ = bf16[272,128]{1,0:T(8,128)(2,1)S(1)} collective-permute-done((bf16[272,128]{1,0:T(8,128)(2,1)S(1)}, bf16[272,128]{1,0:T(8,128)(2,1)S(1)}, u32[]{:S(2)}, u32[]{:S(2)}) %collective-permute-start.7) | collective-permute-done | bytes 69664 | tf_op jit(solution)/shard_map/ppermute | solution.py:26
  32.1 1.0 %collective-permute-done.8.refs_1_ = bf16[272,128]{1,0:T(8,128)(2,1)S(1)} collective-permute-done((bf16[272,128]{1,0:T(8,128)(2,1)S(1)}, bf16[272,128]{1,0:T(8,128)(2,1)S(1)}, u32[]{:S(2)}, u32[]{:S(2)}) %collective-permute-start.8) | collective-permute-done | bytes 69664 | tf_op jit(solution)/shard_map/ppermute | solution.py:26
  33.1 0.5 %collective-permute-done.9.refs_2_ = bf16[272,128]{1,0:T(8,128)(2,1)S(1)} collective-permute-done((bf16[272,128]{1,0:T(8,128)(2,1)S(1)}, bf16[272,128]{1,0:T(8,128)(2,1)S(1)}, u32[]{:S(2)}, u32[]{:S(2)}) %collective-permute-start.9) | collective-permute-done | bytes 69664 | tf_op jit(solution)/shard_map/ppermute | solution.py:26
  33.7 1.2 %collective-permute-done.10.received = bf16[128,128]{1,0:T(8,128)(2,1)S(1)} collective-permute-done((bf16[128,128]{1,0:T(8,128)(2,1)S(1)}, bf16[128,128]{1,0:T(8,128)(2,1)S(1)}, u32[]{:S(2)}, u32[]{:S(2)}) %collective-permute-start.10) | collective-permute-done | bytes 32800 | tf_op jit(solution)/shard_map/ppermute | solution.py:26
  34.9 0.7 %finish.1 = (f32[256,128]{1,0:T(8,128)}, f32[8]{0:T(128)}) custom-call(f32[128,128]{1,0:T(8,128)S(1)} %get-tuple-element.55.own, bf16[128,128]{1,0:T(8,128)(2,1)S(1)} %collective-permute-done.10.received, f32[8,128]{1,0:T(8,128)S(1)} %get-tuple-element.57.mass), custom_call_target="tpu_custom_call" | custom-call | tf_op jit(solution)/shard_map/finish/pallas_call | solution.py:604
  (17 shorter events, 0.4 us)
Async XLA Ops:
  4.1 3.1 %collective-permute-start = (bf16[128,128]{1,0:T(8,128)(2,1)S(1)}, bf16[128,128]{1,0:T(8,128)(2,1)S(1)}, u32[]{:S(2)}, u32[]{:S(2)}) collective-permute-start(bf16[128,128]{1,0:T(8,128)(2,1)S(1)} %get-tuple-element.36), channel_id=1, source_target_pairs={{0,1},{1,0},{2,3},{3,2},{4,5},{5,4},{6,7},{7,6},{8,9},{9,8},{10,11... | collective-permute-start | bytes 98312 | tf_op jit(solution)/shard_map/ppermute | solution.py:26
  4.7 7.8 %copy-start.2 = (s32[8,2]{0,1:T(2,128)S(1)}, s32[8,2]{0,1:T(2,128)}, u32[]{:S(2)}) copy-start(s32[8,2]{0,1:T(2,128)} %param.13) | copy-start | bytes 196
  7.2 8.0 %collective-permute-start.1 = (bf16[32,16384]{1,0:T(8,128)(2,1)S(1)}, bf16[32,16384]{1,0:T(8,128)(2,1)S(1)}, u32[]{:S(2)}, u32[]{:S(2)}) collective-permute-start(bf16[32,16384]{1,0:T(8,128)(2,1)S(1)} %get-tuple-element.38), channel_id=1, source_target_pairs={{0,1},{1,0},{2,3},{3,2},{4,5},{5,4},{6,7},{7,6},{8,9},{9,8},{10,11... | collective-permute-start | bytes 3145736 | tf_op jit(solution)/shard_map/ppermute | solution.py:26
  7.4 7.9 %collective-permute-start.2 = (bf16[256,128]{1,0:T(8,128)(2,1)S(1)}, bf16[256,128]{1,0:T(8,128)(2,1)S(1)}, u32[]{:S(2)}, u32[]{:S(2)}) collective-permute-start(bf16[256,128]{1,0:T(8,128)(2,1)S(1)} %pair_rows.1.refs_0_), channel_id=1, source_target_pairs={{0,12},{1,13},{2,14},{3,15},{4,8},{5,9},{6,10},{7,11},{8,4},{9,5},... | collective-permute-start | bytes 196616 | tf_op jit(solution)/shard_map/ppermute | solution.py:26
  12.9 4.9 %collective-permute-start.3 = (bf16[256,128]{1,0:T(8,128)(2,1)S(1)}, bf16[256,128]{1,0:T(8,128)(2,1)S(1)}, u32[]{:S(2)}, u32[]{:S(2)}) collective-permute-start(bf16[256,128]{1,0:T(8,128)(2,1)S(1)} %pair_rows.1.refs_0_), channel_id=1, source_target_pairs={{0,4},{1,5},{2,6},{3,7},{4,0},{5,1},{6,2},{7,3},{8,12},{9,13},{10,... | collective-permute-start | bytes 196616 | tf_op jit(solution)/shard_map/ppermute | solution.py:26
  13.0 5.9 %collective-permute-start.4 = (bf16[256,128]{1,0:T(8,128)(2,1)S(1)}, bf16[256,128]{1,0:T(8,128)(2,1)S(1)}, u32[]{:S(2)}, u32[]{:S(2)}) collective-permute-start(bf16[256,128]{1,0:T(8,128)(2,1)S(1)} %pair_rows.1.refs_0_), channel_id=1, source_target_pairs={{0,8},{1,9},{2,10},{3,11},{4,12},{5,13},{6,14},{7,15},{8,0},{9,1},... | collective-permute-start | bytes 196616 | tf_op jit(solution)/shard_map/ppermute | solution.py:26
  16.1 3.6 %copy-start = (f32[32]{0:T(128)S(1)}, f32[32]{0:T(128)}, u32[]{:S(2)}) copy-start(f32[32]{0:T(128)} %param.8) | copy-start | bytes 388
  16.1 3.6 %copy-start.1 = (s32[32]{0:T(128)S(1)}, s32[32]{0:T(128)}, u32[]{:S(2)}) copy-start(s32[32]{0:T(128)} %param.9) | copy-start | bytes 388
  19.7 1.3 %collective-permute-start.5 = (f32[80,128]{1,0:T(8,128)S(1)}, f32[80,128]{1,0:T(8,128)S(1)}, u32[]{:S(2)}, u32[]{:S(2)}) collective-permute-start(f32[80,128]{1,0:T(8,128)S(1)} %collect.1.mine), channel_id=1, source_target_pairs={{0,1},{1,0},{2,3},{3,2},{4,5},{5,4},{6,7},{7,6},{8,9},{9,8},{10,11... | collective-permute-start | bytes 122888 | tf_op jit(solution)/shard_map/ppermute | solution.py:26
  21.4 4.0 %collective-permute-start.6 = (bf16[144,128]{1,0:T(8,128)(2,1)S(1)}, bf16[144,128]{1,0:T(8,128)(2,1)S(1)}, u32[]{:S(2)}, u32[]{:S(2)}) collective-permute-start(bf16[144,128]{1,0:T(8,128)(2,1)S(1)} %get-tuple-element.45), channel_id=1, source_target_pairs={{0,2},{1,3},{2,0},{3,1},{4,6},{5,7},{6,4},{7,5},{8,10},{9,11},{10,... | collective-permute-start | bytes 110600 | tf_op jit(solution)/shard_map/ppermute | solution.py:26
  25.5 6.7 %collective-permute-start.7 = (bf16[272,128]{1,0:T(8,128)(2,1)S(1)}, bf16[272,128]{1,0:T(8,128)(2,1)S(1)}, u32[]{:S(2)}, u32[]{:S(2)}) collective-permute-start(bf16[272,128]{1,0:T(8,128)(2,1)S(1)} %get-tuple-element.52), channel_id=1, source_target_pairs={{0,12},{1,13},{2,14},{3,15},{4,8},{5,9},{6,10},{7,11},{8,4},{9,5},... | collective-permute-start | bytes 208904 | tf_op jit(solution)/shard_map/ppermute | solution.py:26
  27.9 5.2 %collective-permute-start.8 = (bf16[272,128]{1,0:T(8,128)(2,1)S(1)}, bf16[272,128]{1,0:T(8,128)(2,1)S(1)}, u32[]{:S(2)}, u32[]{:S(2)}) collective-permute-start(bf16[272,128]{1,0:T(8,128)(2,1)S(1)} %get-tuple-element.53), channel_id=1, source_target_pairs={{0,4},{1,5},{2,6},{3,7},{4,0},{5,1},{6,2},{7,3},{8,12},{9,13},{10,... | collective-permute-start | bytes 208904 | tf_op jit(solution)/shard_map/ppermute | solution.py:26
  27.9 5.7 %collective-permute-start.9 = (bf16[272,128]{1,0:T(8,128)(2,1)S(1)}, bf16[272,128]{1,0:T(8,128)(2,1)S(1)}, u32[]{:S(2)}, u32[]{:S(2)}) collective-permute-start(bf16[272,128]{1,0:T(8,128)(2,1)S(1)} %get-tuple-element.54), channel_id=1, source_target_pairs={{0,8},{1,9},{2,10},{3,11},{4,12},{5,13},{6,14},{7,15},{8,0},{9,1},... | collective-permute-start | bytes 208904 | tf_op jit(solution)/shard_map/ppermute | solution.py:26
  33.6 1.3 %collective-permute-start.10 = (bf16[128,128]{1,0:T(8,128)(2,1)S(1)}, bf16[128,128]{1,0:T(8,128)(2,1)S(1)}, u32[]{:S(2)}, u32[]{:S(2)}) collective-permute-start(bf16[128,128]{1,0:T(8,128)(2,1)S(1)} %get-tuple-element.56), channel_id=1, source_target_pairs={{0,1},{1,0},{2,3},{3,2},{4,5},{5,4},{6,7},{7,6},{8,9},{9,8},{10,11... | collective-permute-start | bytes 98312 | tf_op jit(solution)/shard_map/ppermute | solution.py:26

commit v10 on v9

--- a/solution.py
+++ b/solution.py
@@ -86,7 +86,8 @@
 
 
 def project_other_kernel(
-    table_hbm, index_hbm, frac_hbm, out_ref, table, index_ref, frac_ref,
+    table_hbm, index_hbm, frac_hbm, images_hbm,
+    out_ref, table, index_ref, frac_ref, own_images, other_images,
     table_in, flat, wide, blended, sems
 ):
     device = lax.axis_index("particle")
@@ -100,9 +101,26 @@
         pltpu.make_async_copy(index_hbm, index_ref, sems.at[1]),
         pltpu.make_async_copy(frac_hbm, frac_ref, sems.at[2]),
     ]
-    for copy in copies:
+    pixels = index_ref.shape[1]
+    chunk = BLOCK * LANES
+    blocks = pixels // (2 * chunk)
+    for target, half in ((other_images, 1 - own_half()), (own_images, own_half())):
+        for comp in range(2):
+            for step in range(blocks):
+                source = pl.multiple_of(comp * pixels + (2 * step + half) * chunk, chunk)
+                dest = (comp * blocks + step) * chunk
+                copies.append(
+                    pltpu.make_async_copy(
+                        images_hbm.at[:, pl.ds(source, chunk)],
+                        target.at[:, pl.ds(dest, chunk)],
+                        sems.at[len(copies)],
+                    )
+                )
+    for copy in copies[:3]:
         copy.start()
     copies[0].wait()
+    for copy in copies[3:]:
+        copy.start()
     highs = flat.shape[1]
     groups = table.shape[0] // 16
 
@@ -128,84 +146,59 @@
     copies[2].wait()
     project_half(table, index_ref, frac_ref, 1 - own_half(), blended)
     out_ref[...] = blended[...].astype(jnp.bfloat16)
-
-
-def project_other(class_refs, interp_index, interp_frac):
+    for copy in copies[3:]:
+        copy.wait()
+
+
+def project_other(class_refs, interp_index, interp_frac, images):
     vox = class_refs.shape[3]
     pixels = interp_index.shape[1]
     highs = vox // LANES
     half_rows = pixels // LANES
     groups = -(-LANES // 7)
+    half_images = jax.ShapeDtypeStruct((images.shape[0], pixels), jnp.bfloat16)
+    copies = 3 + 2 * pixels // (BLOCK * LANES)
     return pl.pallas_call(
         project_other_kernel,
-        in_specs=[pl.BlockSpec(memory_space=pltpu.HBM)] * 3,
-        out_specs=whole_vmem(4),
+        in_specs=[pl.BlockSpec(memory_space=pltpu.HBM)] * 4,
+        out_specs=whole_vmem(6),
         out_shape=[
             jax.ShapeDtypeStruct((half_rows, LANES), jnp.bfloat16),
             jax.ShapeDtypeStruct((16 * groups, highs), jnp.bfloat16),
             jax.ShapeDtypeStruct((1, pixels), jnp.int32),
             jax.ShapeDtypeStruct((1, pixels), jnp.float32),
+            half_images,
+            half_images,
         ],
         scratch_shapes=[
             pltpu.VMEM((1, 1, 2, vox), jnp.bfloat16),
             pltpu.VMEM((2, highs, LANES), jnp.float32),
             pltpu.VMEM((LANES + 8, highs), jnp.float32),
             pltpu.VMEM((half_rows, LANES), jnp.float32),
-            pltpu.SemaphoreType.DMA((3,)),
+            pltpu.SemaphoreType.DMA((copies,)),
         ],
         compiler_params=pltpu.CompilerParams(vmem_limit_bytes=16 * MIB),
         name="project_other",
-    )(*(in_hbm(value) for value in (class_refs, interp_index, interp_frac)))
-
-
-def project_own_kernel(
-    table, index_ref, frac_ref, images_hbm, out_ref, own_images, other_images, blended, sems
-):
-    pixels = index_ref.shape[1]
-    chunk = BLOCK * LANES
-    blocks = pixels // (2 * chunk)
-    copies = []
-    for target, half in ((other_images, 1 - own_half()), (own_images, own_half())):
-        for comp in range(2):
-            for step in range(blocks):
-                source = pl.multiple_of(comp * pixels + (2 * step + half) * chunk, chunk)
-                dest = (comp * blocks + step) * chunk
-                copies.append(
-                    pltpu.make_async_copy(
-                        images_hbm.at[:, pl.ds(source, chunk)],
-                        target.at[:, pl.ds(dest, chunk)],
-                        sems.at[len(copies)],
-                    )
-                )
-    for copy in copies:
-        copy.start()
+    )(*(in_hbm(value) for value in (class_refs, interp_index, interp_frac, images)))
+
+
+def project_own_kernel(table, index_ref, frac_ref, out_ref, blended):
     project_half(table, index_ref, frac_ref, own_half(), blended)
     out_ref[...] = blended[...].astype(jnp.bfloat16)
-    for copy in copies:
-        copy.wait()
-
-
-def project_own(table, index, frac, images):
-    parts, width = images.shape
+
+
+def project_own(table, index, frac):
     half_rows = index.shape[1] // LANES
-    half_images = jax.ShapeDtypeStruct((parts, width // 2), jnp.bfloat16)
     return pl.pallas_call(
         project_own_kernel,
-        in_specs=whole_vmem(3) + [pl.BlockSpec(memory_space=pltpu.HBM)],
-        out_specs=whole_vmem(3),
-        out_shape=[
-            jax.ShapeDtypeStruct((half_rows, LANES), jnp.bfloat16),
-            half_images,
-            half_images,
-        ],
-        scratch_shapes=[
-            pltpu.VMEM((half_rows, LANES), jnp.float32),
-            pltpu.SemaphoreType.DMA((2 * width // (2 * BLOCK * LANES),)),
-        ],
+        in_specs=whole_vmem(3),
+        out_specs=pl.BlockSpec(memory_space=pltpu.VMEM),
+        out_shape=jax.ShapeDtypeStruct((half_rows, LANES), jnp.bfloat16),
+        scratch_shapes=[pltpu.VMEM((half_rows, LANES), jnp.float32)],
         compiler_params=pltpu.CompilerParams(vmem_limit_bytes=16 * MIB),
         cost_estimate=pl.CostEstimate(flops=2000000000, bytes_accessed=8000000, transcendentals=0),
         name="project_own",
-    )(table, index, frac, in_hbm(images))
+    )(table, index, frac)
 
 
 def pair_kernel(own, other, out_ref):
@@ -227,7 +220,7 @@
 
 
 def chip_order(chips):
-    return [0, chips - 1] + list(range(1, chips - 1))
+    return [0] + list(range(chips - 1, 0, -1))
 
 
 def slot_orientation(device, slot, slots):
@@ -245,7 +238,7 @@
     return jnp.sum(block.astype(jnp.float32), axis=0, keepdims=True)
 
 
-def table_kernel(shift_ref, cos_ref, sin_ref):
+def fill_tables(shift_ref, cos_ref, sin_ref):
     shifts, width = cos_ref.shape
     grid_x = shift_ref[:, 0:1]
     grid_y = shift_ref[:, 1:2]
@@ -264,20 +257,15 @@
         sin_ref[:, where] = sin_j * cos_y + cos_j * sin_y
 
 
-def phase_tables(shift_grid, width):
-    shape = jax.ShapeDtypeStruct((shift_grid.shape[0], width), jnp.float32)
-    return pl.pallas_call(
-        table_kernel,
-        in_specs=whole_vmem(1),
-        out_specs=whole_vmem(2),
-        out_shape=[shape, shape],
-        compiler_params=pltpu.CompilerParams(vmem_limit_bytes=16 * MIB),
-        cost_estimate=pl.CostEstimate(flops=2000000, bytes_accessed=2000000, transcendentals=0),
-        name="phase_tables",
-    )(shift_grid)
-
-
-def correlate_kernel(own_images, other_images, cos_ref, sin_ref, *refs, chunk):
+def correlate_first_kernel(shift_ref, own_images, other_images, *refs, chunk):
+    pair_refs, (out_ref, cos_ref, sin_ref, proj) = refs[:-4], refs[-4:]
+    fill_tables(shift_ref, cos_ref, sin_ref)
+    correlate_kernel(
+        cos_ref, sin_ref, own_images, other_images, *pair_refs, out_ref, proj, chunk=chunk
+    )
+
+
+def correlate_kernel(cos_ref, sin_ref, own_images, other_images, *refs, chunk):
     pair_refs, (out_ref, proj) = refs[:-2], refs[-2:]
     shifts = cos_ref.shape[0]
     parts = own_images.shape[0]
@@ -329,44 +317,52 @@
     out_ref[0:combos, 0 : 2 * parts] = total
 
 
-def correlate(own_images, other_images, cos_table, sin_table, pairs):
+def correlate(own_images, other_images, pairs, shift_grid=None, tables=None):
     slots = 2 * len(pairs)
-    shifts, width = cos_table.shape
-    return pl.pallas_call(
-        functools.partial(correlate_kernel, chunk=2048),
-        in_specs=whole_vmem(4 + len(pairs)),
-        out_specs=pl.BlockSpec(memory_space=pltpu.VMEM),
-        out_shape=jax.ShapeDtypeStruct((shifts * slots + slots, LANES), jnp.float32),
+    width = own_images.shape[1] // 2
+    shifts = shift_grid.shape[0] if tables is None else tables[0].shape[0]
+    first = (shift_grid,) if tables is None else tuple(tables)
+    table = jax.ShapeDtypeStruct((shifts, width), jnp.float32)
+    outs = [jax.ShapeDtypeStruct((shifts * slots + slots, LANES), jnp.float32)]
+    outs += [table, table] if tables is None else []
+    kernel = correlate_first_kernel if tables is None else correlate_kernel
+    return pl.pallas_call(
+        functools.partial(kernel, chunk=2048),
+        in_specs=whole_vmem(len(first) + 2 + len(pairs)),
+        out_specs=whole_vmem(len(outs)),
+        out_shape=outs,
         scratch_shapes=[pltpu.VMEM((slots * 2 * width // LANES, LANES), jnp.float32)],
         compiler_params=pltpu.CompilerParams(vmem_limit_bytes=(14 + slots) * MIB),
-        cost_estimate=pl.CostEstimate(flops=1500000000, bytes_accessed=6000000, transcendentals=0),
+        cost_estimate=pl.CostEstimate(flops=1000000000, bytes_accessed=4000000, transcendentals=0),
         name="correlate",
-    )(own_images, other_images, cos_table, sin_table, *pairs)
-
-
-def collect_kernel(near, far, precision_ref, assigned_ref, out_ref, *, combos):
-    slots = near.shape[0] - combos
+    )(*first, own_images, other_images, *pairs)
+
+
+def collect_kernel(*refs, combos):
+    parts_refs, (precision_ref, assigned_ref, out_ref) = refs[:-3], refs[-3:]
+    count = len(parts_refs)
+    slots = parts_refs[0].shape[0] - combos
     parts = precision_ref.shape[1]
-    for index, ref in enumerate((near, far)):
+    for index, ref in enumerate(parts_refs[::-1]):
         out_ref[index * combos : (index + 1) * combos, :] = ref[0:combos, :]
-        power = 2 * combos + index * slots
+        power = count * combos + index * slots
         out_ref[power : power + slots, :] = ref[combos:, :]
-    rest = 2 * combos + 2 * slots
+    rest = count * (combos + slots)
     out_ref[rest:, :] = jnp.zeros((8, LANES), jnp.float32)
     out_ref[rest : rest + 1, 0:parts] = precision_ref[...]
     out_ref[rest + 1 : rest + 2, 0:parts] = assigned_ref[...].astype(jnp.float32)
 
 
-def collect(near, far, precision, assigned, combos):
-    rows = 2 * near.shape[0] + 8
+def collect(passes, precision, assigned, combos):
+    rows = len(passes) * passes[0].shape[0] + 8
     return pl.pallas_call(
         functools.partial(collect_kernel, combos=combos),
-        in_specs=whole_vmem(4),
+        in_specs=whole_vmem(2 + len(passes)),
         out_specs=pl.BlockSpec(memory_space=pltpu.VMEM),
         out_shape=jax.ShapeDtypeStruct((rows, LANES), jnp.float32),
         compiler_params=pltpu.CompilerParams(vmem_limit_bytes=16 * MIB),
         name="collect",
-    )(near, far, precision, assigned)
+    )(*passes[::-1], precision, assigned)
 
 
 def rotate_back(weights, own_images, other_images, cos_ref, sin_ref, where, imag_where, slots):
@@ -621,25 +617,31 @@
     slots = dev_count // 2
     chips = slots // 2
     parts, width = images.shape
-    other_half, table, index, frac = project_other(class_refs, interp_index, interp_frac)
+    other_half, table, index, frac, own_images, other_images = project_other(
+        class_refs, interp_index, interp_frac, images
+    )
     from_core = exchange(other_half, 1)
-    own, own_images, other_images = project_own(table, index, frac, images)
-    pair = pair_rows(own, from_core)
-    pair, other_images = lax.optimization_barrier((pair, other_images))
+    images_received = exchange(other_images, 1)
+    pair = pair_rows(project_own(table, index, frac), from_core)
     others = chip_order(chips)[1:]
     pairs = [pair] + [exchange(pair, 4 * m) for m in others]
-    images_received = exchange(other_images, 1)
-    cos_table, sin_table = phase_tables(shift_grid, width // 4)
-    near, far = (
-        correlate(own_images, images_received, cos_table, sin_table, part)
-        for part in (pairs[: chips // 2], pairs[chips // 2 :])
-    )
+    group = chips // 4
+    first, cos_table, sin_table = correlate(
+        own_images, images_received, pairs[:group], shift_grid=shift_grid
+    )
+    passes = [first]
+    for start in range(group, chips, group):
+        passes += correlate(
+            own_images,
+            images_received,
+            pairs[start : start + group],
+            tables=(cos_table, sin_table),
+        )
     mine = collect(
-        near,
-        far,
+        passes,
         noise_precision.reshape(1, parts),
         assigned_class.reshape(1, parts),
-        shift_grid.shape[0] * slots // 2,
+        shift_grid.shape[0] * 2 * group,
     )
     weights, low, low_send, mass = posterior(
         mine, exchange(mine, 1), own_images, images_received, cos_table, sin_table, slots

time: 35.8 us -> 36.6 us (1.022)
  Pallas kernels: 10.6 us -> 12 us
  waiting for transfers between devices: 11.7 us -> 11.1 us
    pallas_call x4 -> x5, Pallas kernels: 4.62 us -> 5.67 us  [the longest x4 3.55 us: correlate(): pl.pallas_call(functools.partial(kernel, chunk=2048), in_specs=whole_vmem...]
    ppermute x11, waiting for transfers between devices: 11.7 us -> 11.1 us  [exchange(): return lax.ppermute(value, 'particle', pairs)]
    pallas_call x1, Pallas kernels: 3.5 us -> 3.91 us  [project_other(): pl.pallas_call(project_other_kernel, in_specs=[pl.BlockSpec(memory_space=...]
  transfers between devices with their start and end apart: 11 -> 11, of which waited for: 9 -> 7; matrix products, arithmetic and copies ran while one was open for 0% -> 0% of each run, Pallas kernels for 14% -> 17%
where the time goes in v10:
time: 36.6 us; the launch traced here: 36.4 us
  starting transfers between devices  12.5 us (34%)
  Pallas kernels  12 us (33%)
  waiting for transfers between devices  11.1 us (30%)
  between operations  0.73 us (2%)
    ppermute x11, starting transfers between devices, exchange(): return lax.ppermute(value, 'particle', pairs)  12.5 us
    ppermute x11, waiting for transfers between devices, exchange(): return lax.ppermute(value, 'particle', pairs)  11.1 us
    pallas_call x1, Pallas kernels, project_other(): pl.pallas_call(project_other_kernel, in_specs=[pl.BlockSpec(memory_space=...  3.91 us
    pallas_call x4, Pallas kernels, correlate(): pl.pallas_call(functools.partial(kernel, chunk=2048), in_specs=whole_vmem...  3.55 us
    pallas_call x1, Pallas kernels, project_own(): pl.pallas_call(project_own_kernel, in_specs=whole_vmem(3), out_specs=pl.B...  2.13 us
    pallas_call x1, Pallas kernels, backproject(): pl.pallas_call(functools.partial(backproject_kernel, slots=slots, chunk=L...  1.29 us
  transfers between devices with their start and end apart: 11, of which 7 were waited for; matrix products, arithmetic and copies ran while one was open for 0% of the time, Pallas kernels for 17%

profile of v10, /device:TPU:0, one launch (start us, length us, event | category | flops | bytes accessed | tf_op | source)
XLA Modules:
  0.0 36.4 jit_solution(9977378338863319054)
XLA Ops:
  0.6 3.9 %project_other.1 = (bf16[128,128]{1,0:T(8,128)(2,1)S(1)}, bf16[304,256]{1,0:T(8,128)(2,1)S(1)}, s32[1,16384]{1,0:T(1,128)S(1)}, f32[1,16384]{1,0:T(1,128)S(1)}, ...) custom-call(bf16[2,8,2,32768]{3,2,1,0:T(2,128)(2,1)} %table_hbm.1, s32[1,16384]{1,0:T(1,128)} %index_hbm.1, ...), custom_call_target="tpu_custom_call" | custom-call | tf_op jit(solution)/shard_map/project_other/pallas_call | solution.py:161
  4.5 0.5 %collective-permute-start = (bf16[32,16384]{1,0:T(8,128)(2,1)S(1)}, bf16[32,16384]{1,0:T(8,128)(2,1)S(1)}, u32[]{:S(2)}, u32[]{:S(2)}) collective-permute-start(bf16[32,16384]{1,0:T(8,128)(2,1)S(1)} %get-tuple-element.30), channel_id=1, source_target_pairs={{0,1},{1,0},{2,3},{3,2},{4,5},{5,4},{6,7},{7,6},{8,9},{9,8},{10,11... | collective-permute-start | bytes 3145736 | tf_op jit(solution)/shard_map/ppermute | solution.py:26
  5.1 0.1 collective-permute-start.1
  5.1 2.1 %project_own.1.own = bf16[128,128]{1,0:T(8,128)(2,1)S(1)} custom-call(bf16[304,256]{1,0:T(8,128)(2,1)S(1)} %get-tuple-element.31.table, s32[1,16384]{1,0:T(1,128)S(1)} %get-tuple-element.32.index_ref, f32[1,16384]{1,0:T(1,128)S(1)} %get-tuple-element.33.frac_ref), custom_call_target="tpu_custom_call" | custom-call | flops 2000000000 | bytes 8000000 | tf_op jit(solution)/shard_map/project_own/pallas_call | solution.py:192
  7.3 0.1 copy.9.shift_ref
  7.4 5.1 %collective-permute-start.4 = (bf16[256,128]{1,0:T(8,128)(2,1)S(1)}, bf16[256,128]{1,0:T(8,128)(2,1)S(1)}, u32[]{:S(2)}, u32[]{:S(2)}) collective-permute-start(bf16[256,128]{1,0:T(8,128)(2,1)S(1)} %pair_rows.1.refs_0_), channel_id=1, source_target_pairs={{0,12},{1,13},{2,14},{3,15},{4,8},{5,9},{6,10},{7,11},{8,4},{9,5},... | collective-permute-start | bytes 196616 | tf_op jit(solution)/shard_map/ppermute | solution.py:26
  12.5 0.6 %collective-permute-start.2 = (bf16[256,128]{1,0:T(8,128)(2,1)S(1)}, bf16[256,128]{1,0:T(8,128)(2,1)S(1)}, u32[]{:S(2)}, u32[]{:S(2)}) collective-permute-start(bf16[256,128]{1,0:T(8,128)(2,1)S(1)} %pair_rows.1.refs_0_), channel_id=1, source_target_pairs={{0,4},{1,5},{2,6},{3,7},{4,0},{5,1},{6,2},{7,3},{8,12},{9,13},{10,... | collective-permute-start | bytes 196616 | tf_op jit(solution)/shard_map/ppermute | solution.py:26
  13.1 1.2 %correlate.4 = (f32[18,128]{1,0:T(8,128)S(1)}, f32[8,8192]{1,0:T(8,128)S(1)}, f32[8,8192]{1,0:T(8,128)S(1)}) custom-call(s32[8,2]{1,0:T(8,128)S(1)} %copy.9.shift_ref, bf16[32,16384]{1,0:T(8,128)(2,1)S(1)} %get-tuple-element.29.own_images, bf16[32,16384]{1,0:T(8,128)(2,1)S(1)} %collective-permute-done.other_images, bf16[256,128]{1,0:T(8,128)(2,1)S(1)} %pair_rows.1.refs_0_), custom_call_target="tpu_custom_call" | custom-call | flops 1000000000 | bytes 4000000 | tf_op jit(solution)/shard_map/correlate/pallas_call | solution.py:329
  14.3 0.7 %collective-permute-done.4.refs_0_ = bf16[256,128]{1,0:T(8,128)(2,1)S(1)} collective-permute-done((bf16[256,128]{1,0:T(8,128)(2,1)S(1)}, bf16[256,128]{1,0:T(8,128)(2,1)S(1)}, u32[]{:S(2)}, u32[]{:S(2)}) %collective-permute-start.4) | collective-permute-done | bytes 65568 | tf_op jit(solution)/shard_map/ppermute | solution.py:26
  15.0 0.8 %correlate.7.refs_2_ = f32[18,128]{1,0:T(8,128)S(1)} custom-call(f32[8,8192]{1,0:T(8,128)S(1)} %get-tuple-element.35.cos_ref, f32[8,8192]{1,0:T(8,128)S(1)} %get-tuple-element.36.sin_ref, bf16[32,16384]{1,0:T(8,128)(2,1)S(1)} %get-tuple-element.29.own_images, bf16[32,16384]{1,0:T(8,128)(2,1)S(1)} %collective-permute-done.other_images, ...), custom_call_target="tpu_custom_call" | custom-call | flops 1000000000 | bytes 4000000 | tf_op jit(solution)/shard_map/correlate/pallas_call | solution.py:329
  15.8 2.5 %collective-permute-done.3.refs_0_ = bf16[256,128]{1,0:T(8,128)(2,1)S(1)} collective-permute-done((bf16[256,128]{1,0:T(8,128)(2,1)S(1)}, bf16[256,128]{1,0:T(8,128)(2,1)S(1)}, u32[]{:S(2)}, u32[]{:S(2)}) %collective-permute-start.3) | collective-permute-done | bytes 65568 | tf_op jit(solution)/shard_map/ppermute | solution.py:26
  18.3 0.8 %correlate.6.refs_1_ = f32[18,128]{1,0:T(8,128)S(1)} custom-call(f32[8,8192]{1,0:T(8,128)S(1)} %get-tuple-element.35.cos_ref, f32[8,8192]{1,0:T(8,128)S(1)} %get-tuple-element.36.sin_ref, bf16[32,16384]{1,0:T(8,128)(2,1)S(1)} %get-tuple-element.29.own_images, bf16[32,16384]{1,0:T(8,128)(2,1)S(1)} %collective-permute-done.other_images, ...), custom_call_target="tpu_custom_call" | custom-call | flops 1000000000 | bytes 4000000 | tf_op jit(solution)/shard_map/correlate/pallas_call | solution.py:329
  19.2 0.8 %correlate.5.refs_0_ = f32[18,128]{1,0:T(8,128)S(1)} custom-call(f32[8,8192]{1,0:T(8,128)S(1)} %get-tuple-element.35.cos_ref, f32[8,8192]{1,0:T(8,128)S(1)} %get-tuple-element.36.sin_ref, bf16[32,16384]{1,0:T(8,128)(2,1)S(1)} %get-tuple-element.29.own_images, bf16[32,16384]{1,0:T(8,128)(2,1)S(1)} %collective-permute-done.other_images, ...), custom_call_target="tpu_custom_call" | custom-call | flops 1000000000 | bytes 4000000 | tf_op jit(solution)/shard_map/correlate/pallas_call | solution.py:329
  20.1 1.2 %collective-permute-done.5.received = f32[80,128]{1,0:T(8,128)S(1)} collective-permute-done((f32[80,128]{1,0:T(8,128)S(1)}, f32[80,128]{1,0:T(8,128)S(1)}, u32[]{:S(2)}, u32[]{:S(2)}) %collective-permute-start.5) | collective-permute-done | bytes 40992 | tf_op jit(solution)/shard_map/ppermute | solution.py:26
  21.3 0.4 %posterior.1 = (bf16[64,64]{1,0:T(8,128)(2,1)S(1)}, f32[128,128]{1,0:T(8,128)S(1)}, bf16[144,128]{1,0:T(8,128)(2,1)S(1)}, f32[8,128]{1,0:T(8,128)S(1)}) custom-call(f32[80,128]{1,0:T(8,128)S(1)} %collect.1.mine, f32[80,128]{1,0:T(8,128)S(1)} %collective-permute-done.5.received, bf16[32,16384]{1,0:T(8,128)(2,1)S(1)} %get-tuple-element.29.own_images, ...), custom_call_target="tpu_custom_call" | custom-call | tf_op jit(solution)/shard_map/posterior/pallas_call | solution.py:446
  21.7 1.6 %collective-permute-start.6 = (bf16[144,128]{1,0:T(8,128)(2,1)S(1)}, bf16[144,128]{1,0:T(8,128)(2,1)S(1)}, u32[]{:S(2)}, u32[]{:S(2)}) collective-permute-start(bf16[144,128]{1,0:T(8,128)(2,1)S(1)} %get-tuple-element.41), channel_id=1, source_target_pairs={{0,2},{1,3},{2,0},{3,1},{4,6},{5,7},{6,4},{7,5},{8,10},{9,11},{10,... | collective-permute-start | bytes 110600 | tf_op jit(solution)/shard_map/ppermute | solution.py:26
  23.2 1.3 %backproject.1 = (f32[224,128]{1,0:T(8,128)S(1)}, bf16[224,128]{1,0:T(8,128)(2,1)S(1)}, bf16[224,128]{1,0:T(8,128)(2,1)S(1)}, bf16[224,128]{1,0:T(8,128)(2,1)S(1)}) custom-call(bf16[64,64]{1,0:T(8,128)(2,1)S(1)} %get-tuple-element.38.weight_ref, bf16[32,16384]{1,0:T(8,128)(2,1)S(1)} %get-tuple-element.29.own_images, ...), custom_call_target="tpu_custom_call" | custom-call | flops 2000000000 | bytes 8000000 | tf_op jit(solution)/shard_map/backproject/pallas_call | solution.py:496
  24.5 1.2 %collective-permute-done.6.low_received = bf16[144,128]{1,0:T(8,128)(2,1)S(1)} collective-permute-done((bf16[144,128]{1,0:T(8,128)(2,1)S(1)}, bf16[144,128]{1,0:T(8,128)(2,1)S(1)}, u32[]{:S(2)}, u32[]{:S(2)}) %collective-permute-start.6) | collective-permute-done | bytes 36896 | tf_op jit(solution)/shard_map/ppermute | solution.py:26
  25.7 2.6 %collective-permute-start.7 = (bf16[272,128]{1,0:T(8,128)(2,1)S(1)}, bf16[272,128]{1,0:T(8,128)(2,1)S(1)}, u32[]{:S(2)}, u32[]{:S(2)}) collective-permute-start(bf16[272,128]{1,0:T(8,128)(2,1)S(1)} %get-tuple-element.48), channel_id=1, source_target_pairs={{0,12},{1,13},{2,14},{3,15},{4,8},{5,9},{6,10},{7,11},{8,4},{9,5},... | collective-permute-start | bytes 208904 | tf_op jit(solution)/shard_map/ppermute | solution.py:26
  28.3 1.9 %collective-permute-start.9 = (bf16[272,128]{1,0:T(8,128)(2,1)S(1)}, bf16[272,128]{1,0:T(8,128)(2,1)S(1)}, u32[]{:S(2)}, u32[]{:S(2)}) collective-permute-start(bf16[272,128]{1,0:T(8,128)(2,1)S(1)} %get-tuple-element.50), channel_id=1, source_target_pairs={{0,4},{1,5},{2,6},{3,7},{4,0},{5,1},{6,2},{7,3},{8,12},{9,13},{10,... | collective-permute-start | bytes 208904 | tf_op jit(solution)/shard_map/ppermute | solution.py:26
  30.2 2.0 %collective-permute-done.7.refs_0_ = bf16[272,128]{1,0:T(8,128)(2,1)S(1)} collective-permute-done((bf16[272,128]{1,0:T(8,128)(2,1)S(1)}, bf16[272,128]{1,0:T(8,128)(2,1)S(1)}, u32[]{:S(2)}, u32[]{:S(2)}) %collective-permute-start.7) | collective-permute-done | bytes 69664 | tf_op jit(solution)/shard_map/ppermute | solution.py:26
  32.2 2.2 %collective-permute-done.8.refs_1_ = bf16[272,128]{1,0:T(8,128)(2,1)S(1)} collective-permute-done((bf16[272,128]{1,0:T(8,128)(2,1)S(1)}, bf16[272,128]{1,0:T(8,128)(2,1)S(1)}, u32[]{:S(2)}, u32[]{:S(2)}) %collective-permute-start.8) | collective-permute-done | bytes 69664 | tf_op jit(solution)/shard_map/ppermute | solution.py:26
  34.6 1.2 %collective-permute-done.10.received = bf16[128,128]{1,0:T(8,128)(2,1)S(1)} collective-permute-done((bf16[128,128]{1,0:T(8,128)(2,1)S(1)}, bf16[128,128]{1,0:T(8,128)(2,1)S(1)}, u32[]{:S(2)}, u32[]{:S(2)}) %collective-permute-start.10) | collective-permute-done | bytes 32800 | tf_op jit(solution)/shard_map/ppermute | solution.py:26
  35.8 0.7 %finish.1 = (f32[256,128]{1,0:T(8,128)}, f32[8]{0:T(128)}) custom-call(f32[128,128]{1,0:T(8,128)S(1)} %get-tuple-element.51.own, bf16[128,128]{1,0:T(8,128)(2,1)S(1)} %collective-permute-done.10.received, f32[8,128]{1,0:T(8,128)S(1)} %get-tuple-element.53.mass), custom_call_target="tpu_custom_call" | custom-call | tf_op jit(solution)/shard_map/finish/pallas_call | solution.py:600
  (18 shorter events, 0.3 us)
Async XLA Ops:
  4.5 8.6 %collective-permute-start = (bf16[32,16384]{1,0:T(8,128)(2,1)S(1)}, bf16[32,16384]{1,0:T(8,128)(2,1)S(1)}, u32[]{:S(2)}, u32[]{:S(2)}) collective-permute-start(bf16[32,16384]{1,0:T(8,128)(2,1)S(1)} %get-tuple-element.30), channel_id=1, source_target_pairs={{0,1},{1,0},{2,3},{3,2},{4,5},{5,4},{6,7},{7,6},{8,9},{9,8},{10,11... | collective-permute-start | bytes 3145736 | tf_op jit(solution)/shard_map/ppermute | solution.py:26
  5.1 2.3 %collective-permute-start.1 = (bf16[128,128]{1,0:T(8,128)(2,1)S(1)}, bf16[128,128]{1,0:T(8,128)(2,1)S(1)}, u32[]{:S(2)}, u32[]{:S(2)}) collective-permute-start(bf16[128,128]{1,0:T(8,128)(2,1)S(1)} %get-tuple-element.34), channel_id=1, source_target_pairs={{0,1},{1,0},{2,3},{3,2},{4,5},{5,4},{6,7},{7,6},{8,9},{9,8},{10,11... | collective-permute-start | bytes 98312 | tf_op jit(solution)/shard_map/ppermute | solution.py:26
  5.1 2.1 %copy-start.2 = (s32[8,2]{0,1:T(2,128)S(1)}, s32[8,2]{0,1:T(2,128)}, u32[]{:S(2)}) copy-start(s32[8,2]{0,1:T(2,128)} %param.13) | copy-start | bytes 196
  7.4 7.6 %collective-permute-start.4 = (bf16[256,128]{1,0:T(8,128)(2,1)S(1)}, bf16[256,128]{1,0:T(8,128)(2,1)S(1)}, u32[]{:S(2)}, u32[]{:S(2)}) collective-permute-start(bf16[256,128]{1,0:T(8,128)(2,1)S(1)} %pair_rows.1.refs_0_), channel_id=1, source_target_pairs={{0,12},{1,13},{2,14},{3,15},{4,8},{5,9},{6,10},{7,11},{8,4},{9,5},... | collective-permute-start | bytes 196616 | tf_op jit(solution)/shard_map/ppermute | solution.py:26
  12.5 5.9 %collective-permute-start.3 = (bf16[256,128]{1,0:T(8,128)(2,1)S(1)}, bf16[256,128]{1,0:T(8,128)(2,1)S(1)}, u32[]{:S(2)}, u32[]{:S(2)}) collective-permute-start(bf16[256,128]{1,0:T(8,128)(2,1)S(1)} %pair_rows.1.refs_0_), channel_id=1, source_target_pairs={{0,8},{1,9},{2,10},{3,11},{4,12},{5,13},{6,14},{7,15},{8,0},{9,1},... | collective-permute-start | bytes 196616 | tf_op jit(solution)/shard_map/ppermute | solution.py:26
  12.5 6.7 %collective-permute-start.2 = (bf16[256,128]{1,0:T(8,128)(2,1)S(1)}, bf16[256,128]{1,0:T(8,128)(2,1)S(1)}, u32[]{:S(2)}, u32[]{:S(2)}) collective-permute-start(bf16[256,128]{1,0:T(8,128)(2,1)S(1)} %pair_rows.1.refs_0_), channel_id=1, source_target_pairs={{0,4},{1,5},{2,6},{3,7},{4,0},{5,1},{6,2},{7,3},{8,12},{9,13},{10,... | collective-permute-start | bytes 196616 | tf_op jit(solution)/shard_map/ppermute | solution.py:26
  19.1 0.8 %copy-start = (f32[32]{0:T(128)S(1)}, f32[32]{0:T(128)}, u32[]{:S(2)}) copy-start(f32[32]{0:T(128)} %param.8) | copy-start | bytes 388
  19.1 0.8 %copy-start.1 = (s32[32]{0:T(128)S(1)}, s32[32]{0:T(128)}, u32[]{:S(2)}) copy-start(s32[32]{0:T(128)} %param.9) | copy-start | bytes 388
  20.0 1.3 %collective-permute-start.5 = (f32[80,128]{1,0:T(8,128)S(1)}, f32[80,128]{1,0:T(8,128)S(1)}, u32[]{:S(2)}, u32[]{:S(2)}) collective-permute-start(f32[80,128]{1,0:T(8,128)S(1)} %collect.1.mine), channel_id=1, source_target_pairs={{0,1},{1,0},{2,3},{3,2},{4,5},{5,4},{6,7},{7,6},{8,9},{9,8},{10,11... | collective-permute-start | bytes 122888 | tf_op jit(solution)/shard_map/ppermute | solution.py:26
  21.7 4.0 %collective-permute-start.6 = (bf16[144,128]{1,0:T(8,128)(2,1)S(1)}, bf16[144,128]{1,0:T(8,128)(2,1)S(1)}, u32[]{:S(2)}, u32[]{:S(2)}) collective-permute-start(bf16[144,128]{1,0:T(8,128)(2,1)S(1)} %get-tuple-element.41), channel_id=1, source_target_pairs={{0,2},{1,3},{2,0},{3,1},{4,6},{5,7},{6,4},{7,5},{8,10},{9,11},{10,... | collective-permute-start | bytes 110600 | tf_op jit(solution)/shard_map/ppermute | solution.py:26
  25.7 6.5 %collective-permute-start.7 = (bf16[272,128]{1,0:T(8,128)(2,1)S(1)}, bf16[272,128]{1,0:T(8,128)(2,1)S(1)}, u32[]{:S(2)}, u32[]{:S(2)}) collective-permute-start(bf16[272,128]{1,0:T(8,128)(2,1)S(1)} %get-tuple-element.48), channel_id=1, source_target_pairs={{0,12},{1,13},{2,14},{3,15},{4,8},{5,9},{6,10},{7,11},{8,4},{9,5},... | collective-permute-start | bytes 208904 | tf_op jit(solution)/shard_map/ppermute | solution.py:26
  28.3 6.1 %collective-permute-start.8 = (bf16[272,128]{1,0:T(8,128)(2,1)S(1)}, bf16[272,128]{1,0:T(8,128)(2,1)S(1)}, u32[]{:S(2)}, u32[]{:S(2)}) collective-permute-start(bf16[272,128]{1,0:T(8,128)(2,1)S(1)} %get-tuple-element.49), channel_id=1, source_target_pairs={{0,8},{1,9},{2,10},{3,11},{4,12},{5,13},{6,14},{7,15},{8,0},{9,1},... | collective-permute-start | bytes 208904 | tf_op jit(solution)/shard_map/ppermute | solution.py:26
  28.3 6.1 %collective-permute-start.9 = (bf16[272,128]{1,0:T(8,128)(2,1)S(1)}, bf16[272,128]{1,0:T(8,128)(2,1)S(1)}, u32[]{:S(2)}, u32[]{:S(2)}) collective-permute-start(bf16[272,128]{1,0:T(8,128)(2,1)S(1)} %get-tuple-element.50), channel_id=1, source_target_pairs={{0,4},{1,5},{2,6},{3,7},{4,0},{5,1},{6,2},{7,3},{8,12},{9,13},{10,... | collective-permute-start | bytes 208904 | tf_op jit(solution)/shard_map/ppermute | solution.py:26
  34.5 1.3 %collective-permute-start.10 = (bf16[128,128]{1,0:T(8,128)(2,1)S(1)}, bf16[128,128]{1,0:T(8,128)(2,1)S(1)}, u32[]{:S(2)}, u32[]{:S(2)}) collective-permute-start(bf16[128,128]{1,0:T(8,128)(2,1)S(1)} %get-tuple-element.52), channel_id=1, source_target_pairs={{0,1},{1,0},{2,3},{3,2},{4,5},{5,4},{6,7},{7,6},{8,9},{9,8},{10,11... | collective-permute-start | bytes 98312 | tf_op jit(solution)/shard_map/ppermute | solution.py:26

commit v11 on v10

--- a/solution.py
+++ b/solution.py
@@ -106,9 +106,10 @@
     blocks = pixels // (2 * chunk)
     for target, half in ((other_images, 1 - own_half()), (own_images, own_half())):
         for comp in range(2):
-            for step in range(blocks):
-                source = pl.multiple_of(comp * pixels + (2 * step + half) * chunk, chunk)
-                dest = (comp * blocks + step) * chunk
+            for step in range(blocks + 1):
+                block = 2 * step + half if step < blocks else 1 - half
+                source = pl.multiple_of(comp * pixels + block * chunk, chunk)
+                dest = (comp * (blocks + 1) + step) * chunk
                 copies.append(
                     pltpu.make_async_copy(
                         images_hbm.at[:, pl.ds(source, chunk)],
@@ -156,8 +157,10 @@
     highs = vox // LANES
     half_rows = pixels // LANES
     groups = -(-LANES // 7)
-    half_images = jax.ShapeDtypeStruct((images.shape[0], pixels), jnp.bfloat16)
-    copies = 3 + 2 * pixels // (BLOCK * LANES)
+    half_images = jax.ShapeDtypeStruct(
+        (images.shape[0], pixels + 2 * LOW_TILES * LANES), jnp.bfloat16
+    )
+    copies = 3 + 2 * half_images.shape[1] // (BLOCK * LANES)
     return pl.pallas_call(
         project_other_kernel,
         in_specs=[pl.BlockSpec(memory_space=pltpu.HBM)] * 4,
@@ -243,7 +246,9 @@
     grid_x = shift_ref[:, 0:1]
     grid_y = shift_ref[:, 1:2]
     lane = lax.broadcasted_iota(jnp.int32, (shifts, LANES), 1)
+    main = width // LANES - LOW_TILES
     freq_x = (lane // BLOCK) * (2 * BLOCK) + own_half() * BLOCK + lane % BLOCK
+    freq_x = jnp.where(lane < main, freq_x, (1 - own_half()) * BLOCK + lane - main)
     turn_x = (freq_x * grid_x) & (BOX - 1)
     turn_y = ((lane - KY // 2) * grid_y) & (BOX - 1)
     angle_x = turn_x.astype(jnp.float32) * (2.0 * math.pi / BOX)
@@ -270,7 +275,8 @@
     shifts = cos_ref.shape[0]
     parts = own_images.shape[0]
     slots = 2 * len(pair_refs)
-    width = own_images.shape[1] // 2
+    full = own_images.shape[1] // 2
+    width = full - LOW_TILES * LANES
     tiles = width // LANES
     per_row = 2 * tiles
     combos = shifts * slots
@@ -286,7 +292,7 @@
     def body(step, total):
         first = step * chunk_tiles
         where = pl.ds(pl.multiple_of(step * chunk, chunk), chunk)
-        imag_where = pl.ds(pl.multiple_of(width + step * chunk, chunk), chunk)
+        imag_where = pl.ds(pl.multiple_of(full + step * chunk, LOW_TILES * LANES), chunk)
         cos_part, sin_part = cos_ref[:, where], sin_ref[:, where]
         reals, imags = [], []
         for slot in range(slots):
@@ -319,10 +325,10 @@
 
 def correlate(own_images, other_images, pairs, shift_grid=None, tables=None):
     slots = 2 * len(pairs)
-    width = own_images.shape[1] // 2
+    width = own_images.shape[1] // 2 - LOW_TILES * LANES
     shifts = shift_grid.shape[0] if tables is None else tables[0].shape[0]
     first = (shift_grid,) if tables is None else tuple(tables)
-    table = jax.ShapeDtypeStruct((shifts, width), jnp.float32)
+    table = jax.ShapeDtypeStruct((shifts, width + LOW_TILES * LANES), jnp.float32)
     outs = [jax.ShapeDtypeStruct((shifts * slots + slots, LANES), jnp.float32)]
     outs += [table, table] if tables is None else []
     kernel = correlate_first_kernel if tables is None else correlate_kernel
@@ -343,7 +349,7 @@
     count = len(parts_refs)
     slots = parts_refs[0].shape[0] - combos
     parts = precision_ref.shape[1]
-    for index, ref in enumerate(parts_refs[::-1]):
+    for index, ref in enumerate(parts_refs):
         out_ref[index * combos : (index + 1) * combos, :] = ref[0:combos, :]
         power = count * combos + index * slots
         out_ref[power : power + slots, :] = ref[combos:, :]
@@ -362,7 +368,7 @@
         out_shape=jax.ShapeDtypeStruct((rows, LANES), jnp.float32),
         compiler_params=pltpu.CompilerParams(vmem_limit_bytes=16 * MIB),
         name="collect",
-    )(*passes[::-1], precision, assigned)
+    )(*passes, precision, assigned)
 
 
 def rotate_back(weights, own_images, other_images, cos_ref, sin_ref, where, imag_where, slots):
@@ -382,13 +388,9 @@
     return real, imag
 
 
-def posterior_kernel(
-    mine, received, own_images, other_images, cos_ref, sin_ref,
-    weight_ref, low_ref, low_send, own_mass, ordered, *, slots
-):
+def posterior_kernel(mine, received, weight_ref, own_mass, ordered, *, slots, shifts, pixels):
     device = lax.axis_index("particle")
-    shifts, width = cos_ref.shape
-    parts = own_images.shape[0]
+    parts = weight_ref.shape[1] // 2
     combos = shifts * slots
     theirs = received[...]
     lane = lax.broadcasted_iota(jnp.int32, theirs.shape, 1)
@@ -401,7 +403,7 @@
     )
     precision = joint[combos + slots : combos + slots + 1]
     assigned = joint[combos + slots + 1 : combos + slots + 2].astype(jnp.int32)
-    likelihood_scale = 1.0 / math.sqrt(4 * width)
+    likelihood_scale = 1.0 / math.sqrt(2 * pixels)
     classes = [slot_orientation(device, slot, slots) // (slots // CLASSES) for slot in range(slots)]
     logits = []
     for slot in range(slots):
@@ -427,53 +429,38 @@
     weight_ref[...] = weights
     own_mass[...] = jnp.broadcast_to(mass_row, own_mass.shape)
 
-    low = LOW_TILES * LANES
-    real, imag = rotate_back(
-        weights, own_images, other_images, cos_ref, sin_ref, slice(0, low), slice(width, width + low), slots
-    )
-    for k in range(LOW_TILES):
-        piece = slice(k * LANES, (k + 1) * LANES)
-        low_ref[pl.ds(k, slots, stride=2 * LOW_TILES), :] = real[:, piece]
-        low_ref[pl.ds(LOW_TILES + k, slots, stride=2 * LOW_TILES), :] = imag[:, piece]
-    low_body = low_ref.shape[0]
-    low_send[0:low_body, :] = low_ref[...].astype(jnp.bfloat16)
-    low_send[low_body:, :] = split_mass(mass_row)
-
-
-def posterior(mine, received, own_images, other_images, cos_table, sin_table, slots):
-    shifts = cos_table.shape[0]
-    low = slots * 2 * LOW_TILES
-    return pl.pallas_call(
-        functools.partial(posterior_kernel, slots=slots),
-        in_specs=whole_vmem(6),
-        out_specs=whole_vmem(4),
+
+def posterior(mine, received, slots, shifts, parts, pixels):
+    return pl.pallas_call(
+        functools.partial(posterior_kernel, slots=slots, shifts=shifts, pixels=pixels),
+        in_specs=whole_vmem(2),
+        out_specs=whole_vmem(2),
         out_shape=[
-            jax.ShapeDtypeStruct((shifts * slots, 2 * own_images.shape[0]), jnp.bfloat16),
-            jax.ShapeDtypeStruct((low, LANES), jnp.float32),
-            jax.ShapeDtypeStruct((low + MASS_ROWS, LANES), jnp.bfloat16),
+            jax.ShapeDtypeStruct((shifts * slots, 2 * parts), jnp.bfloat16),
             jax.ShapeDtypeStruct((8, LANES), jnp.float32),
         ],
         scratch_shapes=[pltpu.VMEM((shifts * slots, LANES), jnp.float32)],
         compiler_params=pltpu.CompilerParams(vmem_limit_bytes=(14 + slots // 2) * MIB),
         name="posterior",
-    )(mine, received, own_images, other_images, cos_table, sin_table)
+    )(mine, received)
 
 
 def backproject_kernel(
-    weight_ref, own_images, other_images, cos_ref, sin_ref, own, *refs, slots, chunk, unroll
+    weight_ref, mass, own_images, other_images, cos_ref, sin_ref, own, *refs, slots, chunk, unroll
 ):
     sends, sums = refs[:-1], refs[-1]
+    core = own_half()
     width = cos_ref.shape[1]
-    tiles = width // LANES - LOW_TILES
+    tiles = width // LANES
+    main = tiles - 2 * LOW_TILES
     per_row = 2 * tiles
     chunk_tiles = chunk // LANES
     weights = weight_ref[...]
 
     def body(step, carry):
         first = step * chunk_tiles
-        start = pl.multiple_of((LOW_TILES + first) * LANES, LOW_TILES * LANES)
-        where = pl.ds(start, chunk)
-        imag_where = pl.ds(pl.multiple_of(width + start, LOW_TILES * LANES), chunk)
+        where = pl.ds(pl.multiple_of(step * chunk, chunk), chunk)
+        imag_where = pl.ds(pl.multiple_of(width + step * chunk, chunk), chunk)
         real, imag = rotate_back(
             weights, own_images, other_images, cos_ref, sin_ref, where, imag_where, slots
         )
@@ -483,131 +470,116 @@
             sums[pl.ds(tiles + first + k, slots, stride=per_row), :] = imag[:, piece]
         return carry
 
-    lax.fori_loop(0, tiles // chunk_tiles, body, 0, unroll=unroll)
-    own[...] = sums[0 : 2 * per_row, :]
-    for m, send in enumerate(sends, start=1):
-        send[...] = sums[2 * m * per_row : 2 * (m + 1) * per_row, :].astype(jnp.bfloat16)
-
-
-def backproject(weights, own_images, other_images, cos_table, sin_table, slots):
-    width = cos_table.shape[1]
-    rows = 2 * 2 * (width // LANES - LOW_TILES)
+    lax.fori_loop(0, width // chunk, body, 0, unroll=unroll)
+    block = split_mass(mass[0:1, :])
+    for index, target in enumerate((own,) + sends):
+        for row in range(2):
+            for comp in range(2):
+                start = (2 * index + row) * per_row + comp * tiles + LOW_TILES
+                dest = (2 * row + comp) * main
+                target[dest : dest + main, :] = sums[start : start + main, :].astype(target.dtype)
+        low = []
+        for offset in (0, tiles, tiles - LOW_TILES, 2 * tiles - LOW_TILES):
+            start = pl.multiple_of((2 * index + core) * per_row + offset, LOW_TILES)
+            low.append(sums[pl.ds(start, LOW_TILES), :])
+        head = 4 * main
+        target[head : head + 4 * LOW_TILES, :] = jnp.concatenate(low, axis=0).astype(target.dtype)
+        if index > 0:
+            target[head + 4 * LOW_TILES :, :] = block
+
+
+def backproject(weights, mass, own_images, other_images, cos_table, sin_table, slots):
+    tiles = cos_table.shape[1] // LANES
     chips = slots // 2
+    rows = 4 * (tiles - LOW_TILES)
     return pl.pallas_call(
         functools.partial(
-            backproject_kernel, slots=slots, chunk=LOW_TILES * LANES, unroll=7 if slots <= 8 else 1
+            backproject_kernel, slots=slots, chunk=BLOCK * LANES, unroll=9 if slots <= 8 else 1
         ),
-        in_specs=whole_vmem(5),
+        in_specs=whole_vmem(6),
         out_specs=whole_vmem(chips),
         out_shape=[jax.ShapeDtypeStruct((rows, LANES), jnp.float32)]
-        + [jax.ShapeDtypeStruct((rows, LANES), jnp.bfloat16)] * (chips - 1),
-        scratch_shapes=[pltpu.VMEM((chips * rows, LANES), jnp.float32)],
+        + [jax.ShapeDtypeStruct((rows + MASS_ROWS, LANES), jnp.bfloat16)] * (chips - 1),
+        scratch_shapes=[pltpu.VMEM((slots * 2 * tiles, LANES), jnp.float32)],
         compiler_params=pltpu.CompilerParams(vmem_limit_bytes=(14 + slots // 2) * MIB),
-        cost_estimate=pl.CostEstimate(flops=2000000000, bytes_accessed=8000000, transcendentals=0),
         name="backproject",
-    )(weights, own_images, other_images, cos_table, sin_table)
-
-
-def fold_kernel(low_ref, low_received, mass, *refs, chips):
-    mains, (own, own_mass), sends = refs[: chips - 1], refs[chips - 1 : chips + 1], refs[chips + 1 :]
+    )(weights, mass, own_images, other_images, cos_table, sin_table)
+
+
+def merge_kernel(own, mass, *refs):
+    received, (keep, to_core, low, to_half, mass_out) = refs[:-5], refs[-5:]
+    core = own_half()
+    half = keep.shape[0]
     rows = own.shape[0]
-    low_body = low_ref.shape[0]
-    total_mass = mass[0:1, :] + joined_mass(low_received[low_body:, :])
-    block = split_mass(total_mass)
-    own_mass[...] = jnp.broadcast_to(total_mass, own_mass.shape)
-    for m, target in enumerate((own,) + tuple(sends)):
-        part = slice(m * rows, (m + 1) * rows)
-        value = (low_ref[part, :] + low_received[part, :].astype(jnp.float32)) * 0.5
-        target[0:rows, :] = value.astype(target.dtype)
-        if m > 0:
-            target[rows : rows + MASS_ROWS, :] = block
-            target[rows + MASS_ROWS :, :] = mains[m - 1][...]
-
-
-def fold(low, low_received, mass, mains):
-    chips = len(mains) + 1
-    rows = low.shape[0] // chips
-    return pl.pallas_call(
-        functools.partial(fold_kernel, chips=chips),
-        in_specs=whole_vmem(2 + chips),
-        out_specs=whole_vmem(1 + chips),
+    total_mass = mass[0:1, :]
+    total_low = own[2 * half :, :]
+    for ref in received:
+        total_mass = total_mass + joined_mass(ref[rows:, :])
+        total_low = total_low + ref[2 * half : rows, :].astype(jnp.float32)
+    mass_out[...] = jnp.broadcast_to(total_mass, mass_out.shape)
+    low[...] = total_low
+    to_half[0 : rows - 2 * half, :] = total_low.astype(jnp.bfloat16)
+    to_half[rows - 2 * half :, :] = split_mass(total_mass)
+    for target, place in ((to_core, 1 - core), (keep, core)):
+        where = pl.ds(pl.multiple_of(place * half, half), half)
+        total = own[where, :]
+        for ref in received:
+            total = total + ref[where, :].astype(jnp.float32)
+        target[...] = total.astype(target.dtype)
+
+
+def merge(own, mass, received):
+    low = 4 * LOW_TILES
+    half = (own.shape[0] - low) // 2
+    return pl.pallas_call(
+        merge_kernel,
+        in_specs=whole_vmem(2 + len(received)),
+        out_specs=whole_vmem(5),
         out_shape=[
-            jax.ShapeDtypeStruct((rows, LANES), jnp.float32),
-            jax.ShapeDtypeStruct((8, LANES), jnp.float32),
-        ]
-        + [
-            jax.ShapeDtypeStruct((rows + MASS_ROWS + main.shape[0], LANES), jnp.bfloat16)
-            for main in mains
-        ],
-        compiler_params=pltpu.CompilerParams(vmem_limit_bytes=16 * MIB),
-        name="fold",
-    )(low, low_received, mass, *mains)
-
-
-def merge_kernel(own, own_low, mass, *refs):
-    received, (keep, to_core, mass_out) = refs[:-3], refs[-3:]
-    core = own_half()
-    low_rows = own_low.shape[0]
-    low_half = low_rows // 2
-    head = low_rows + MASS_ROWS
-    half = own.shape[0] // 2
-    total_mass = mass[0:1, :]
-    for ref in received:
-        total_mass = total_mass + joined_mass(ref[low_rows:head, :])
-    mass_out[...] = jnp.broadcast_to(total_mass, mass_out.shape)
-    for target, place in ((to_core, 1 - core), (keep, core)):
-        start = pl.multiple_of(place * half, half)
-        total = own[pl.ds(start, half), :]
-        for ref in received:
-            total = total + ref[pl.ds(head + start, half), :].astype(jnp.float32)
-        where = pl.ds(pl.multiple_of(place * low_half, low_half), low_half)
-        low = own_low[where, :]
-        for ref in received:
-            low = low + ref[where, :].astype(jnp.float32)
-        target[...] = jnp.concatenate(
-            [low[0:LOW_TILES], total[0 : half // 2], low[LOW_TILES:], total[half // 2 :]], axis=0
-        ).astype(target.dtype)
-
-
-def merge(own, own_low, mass, received):
-    rows = (own.shape[0] + own_low.shape[0]) // 2
-    return pl.pallas_call(
-        merge_kernel,
-        in_specs=whole_vmem(3 + len(received)),
-        out_specs=whole_vmem(3),
-        out_shape=[
-            jax.ShapeDtypeStruct((rows, LANES), jnp.float32),
-            jax.ShapeDtypeStruct((rows, LANES), jnp.bfloat16),
+            jax.ShapeDtypeStruct((half, LANES), jnp.float32),
+            jax.ShapeDtypeStruct((half, LANES), jnp.bfloat16),
+            jax.ShapeDtypeStruct((low, LANES), jnp.float32),
+            jax.ShapeDtypeStruct((low + MASS_ROWS, LANES), jnp.bfloat16),
             jax.ShapeDtypeStruct((8, LANES), jnp.float32),
         ],
         compiler_params=pltpu.CompilerParams(vmem_limit_bytes=16 * MIB),
         name="merge",
-    )(own, own_low, mass, *received)
-
-
-def finish_kernel(own, received, mass, out, mass_out, *, scale, mass_scale):
+    )(own, mass, *received)
+
+
+def finish_kernel(keep, from_core, low, from_half, mass, out, mass_out, *, scale, mass_scale):
     core = own_half()
-    mass_out[...] = mass[0, :CLASSES] * mass_scale
-    for step in range(own.shape[0] // BLOCK):
-        rows = slice(step * BLOCK, (step + 1) * BLOCK)
-        own_rows = pl.ds(pl.multiple_of((2 * step + core) * BLOCK, BLOCK), BLOCK)
-        other_rows = pl.ds(pl.multiple_of((2 * step + 1 - core) * BLOCK, BLOCK), BLOCK)
-        out[own_rows, :] = own[rows, :] * scale
-        out[other_rows, :] = received[rows, :].astype(jnp.float32) * scale
-
-
-def finish(own, received, mass, scale, mass_scale):
+    low_rows = low.shape[0]
+    total_mass = mass[0:1, :] + joined_mass(from_half[low_rows:, :])
+    mass_out[...] = total_mass[0, :CLASSES] * mass_scale
+    mean = (low[...] + from_half[0:low_rows, :].astype(jnp.float32)) * (0.5 * scale)
+    main = keep.shape[0] // 2
+    blocks = main // BLOCK + 1
+    for index, (source, place) in enumerate(((keep, core), (from_core, 1 - core))):
+        for comp in range(2):
+            for block in range(blocks):
+                if block == 0:
+                    start = (2 * index + comp) * LOW_TILES
+                    value = mean[start : start + LOW_TILES]
+                else:
+                    start = comp * main + (block - 1) * BLOCK
+                    value = source[start : start + BLOCK, :].astype(jnp.float32) * scale
+                dest = pl.multiple_of((2 * (comp * blocks + block) + place) * BLOCK, BLOCK)
+                out[pl.ds(dest, BLOCK), :] = value
+
+
+def finish(keep, from_core, low, from_half, mass, scale, mass_scale):
     return pl.pallas_call(
         functools.partial(finish_kernel, scale=scale, mass_scale=mass_scale),
-        in_specs=whole_vmem(3),
+        in_specs=whole_vmem(5),
         out_specs=whole_vmem(2),
         out_shape=[
-            jax.ShapeDtypeStruct((2 * own.shape[0], LANES), jnp.float32),
+            jax.ShapeDtypeStruct((2 * keep.shape[0] + low.shape[0], LANES), jnp.float32),
             jax.ShapeDtypeStruct((CLASSES,), jnp.float32),
         ],
         compiler_params=pltpu.CompilerParams(vmem_limit_bytes=16 * MIB),
         name="finish",
-    )(own, received, mass)
+    )(keep, from_core, low, from_half, mass)
 
 
 def local(
@@ -625,7 +597,7 @@
     pair = pair_rows(project_own(table, index, frac), from_core)
     others = chip_order(chips)[1:]
     pairs = [pair] + [exchange(pair, 4 * m) for m in others]
-    group = chips // 4
+    group = chips // 2
     first, cos_table, sin_table = correlate(
         own_images, images_received, pairs[:group], shift_grid=shift_grid
     )
@@ -643,16 +615,22 @@
         assigned_class.reshape(1, parts),
         shift_grid.shape[0] * 2 * group,
     )
-    weights, low, low_send, mass = posterior(
-        mine, exchange(mine, 1), own_images, images_received, cos_table, sin_table, slots
-    )
-    low_from_half = exchange(low_send, 2)
-    sums = backproject(weights, own_images, images_received, cos_table, sin_table, slots)
-    folded = fold(low, low_from_half, mass, sums[1:])
-    chip_sums = [exchange(send, 4 * m) for m, send in zip(others, folded[2:])]
-    keep, send, mass = merge(sums[0], folded[0], folded[1], chip_sums)
+    weights, mass = posterior(
+        mine, exchange(mine, 1), slots, shift_grid.shape[0], parts, width // 2
+    )
+    sums = backproject(
+        weights, mass, own_images, images_received, cos_table, sin_table, slots
+    )
+    received = [exchange(send, 4 * m) for m, send in zip(others, sums[1:])]
+    keep, to_core, low, to_half, mass = merge(sums[0], mass, received)
     back, class_mass = finish(
-        keep, exchange(send, 1), mass, 1.0 / math.sqrt(parts), CLASSES / (parts * dev_count)
+        keep,
+        exchange(to_core, 1),
+        low,
+        exchange(to_half, 2),
+        mass,
+        1.0 / math.sqrt(parts),
+        CLASSES / (parts * dev_count),
     )
     return back.reshape(1, width), class_mass
 

time: 36.6 us -> 37.7 us (1.030)
  waiting for transfers between devices: 11.1 us -> 12.6 us
    ppermute x11, waiting for transfers between devices: 11.1 us -> 12.6 us  [exchange(): return lax.ppermute(value, 'particle', pairs)]
    pallas_call x4 -> x2, Pallas kernels: 3.55 us -> 2.18 us  [correlate(): pl.pallas_call(functools.partial(kernel, chunk=2048), in_specs=whole_vmem...]
    pallas_call x1, Pallas kernels: 3.91 us -> 5 us  [project_other(): pl.pallas_call(project_other_kernel, in_specs=[pl.BlockSpec(memory_space=...]
    pallas_call x4 -> x3, Pallas kernels: 1.76 us -> 1.93 us  [the longest x1 1.66 us: backproject(): pl.pallas_call(functools.partial(backproject_kernel, slots=slots, chunk=B...]
  transfers between devices with their start and end apart: 11 -> 11, of which waited for: 7 -> 7; matrix products, arithmetic and copies ran while one was open for 0% -> 0% of each run, Pallas kernels for 17% -> 9%
where the time goes in v11:
time: 37.7 us; the launch traced here: 37.6 us
  waiting for transfers between devices  12.6 us (33%)
  starting transfers between devices  12.3 us (33%)
  Pallas kernels  12 us (32%)
  between operations  0.72 us (2%)
    ppermute x11, waiting for transfers between devices, exchange(): return lax.ppermute(value, 'particle', pairs)  12.6 us
    ppermute x11, starting transfers between devices, exchange(): return lax.ppermute(value, 'particle', pairs)  12.3 us
    pallas_call x1, Pallas kernels, project_other(): pl.pallas_call(project_other_kernel, in_specs=[pl.BlockSpec(memory_space=...  5 us
    pallas_call x2, Pallas kernels, correlate(): pl.pallas_call(functools.partial(kernel, chunk=2048), in_specs=whole_vmem...  2.18 us
    pallas_call x1, Pallas kernels, project_own(): pl.pallas_call(project_own_kernel, in_specs=whole_vmem(3), out_specs=pl.B...  2.14 us
    pallas_call x1, Pallas kernels, backproject(): pl.pallas_call(functools.partial(backproject_kernel, slots=slots, chunk=B...  1.66 us
  transfers between devices with their start and end apart: 11, of which 7 were waited for; matrix products, arithmetic and copies ran while one was open for 0% of the time, Pallas kernels for 9%

profile of v11, /device:TPU:0, one launch (start us, length us, event | category | flops | bytes accessed | tf_op | source)
XLA Modules:
  0.0 37.6 jit_solution(12120281424909084339)
XLA Ops:
  0.6 5.0 %project_other.1 = (bf16[128,128]{1,0:T(8,128)(2,1)S(1)}, bf16[304,256]{1,0:T(8,128)(2,1)S(1)}, s32[1,16384]{1,0:T(1,128)S(1)}, f32[1,16384]{1,0:T(1,128)S(1)}, ...) custom-call(bf16[2,8,2,32768]{3,2,1,0:T(2,128)(2,1)} %table_hbm.1, s32[1,16384]{1,0:T(1,128)} %index_hbm.1, ...), custom_call_target="tpu_custom_call" | custom-call | tf_op jit(solution)/shard_map/project_other/pallas_call | solution.py:164
  5.6 0.5 %collective-permute-start = (bf16[32,18432]{1,0:T(8,128)(2,1)}, bf16[32,18432]{1,0:T(8,128)(2,1)S(1)}, u32[]{:S(2)}, u32[]{:S(2)}) collective-permute-start(bf16[32,18432]{1,0:T(8,128)(2,1)} %get-tuple-element.25), channel_id=1, source_target_pairs={{0,1},{1,0},{2,3},{3,2},{4,5},{5,4},{6,7},{7,6},{8,9},{9,8},{10,11... | collective-permute-start | bytes 3538952 | tf_op jit(solution)/shard_map/ppermute | solution.py:26
  6.2 0.1 collective-permute-start.1
  6.2 2.1 %project_own.1.own = bf16[128,128]{1,0:T(8,128)(2,1)S(1)} custom-call(bf16[304,256]{1,0:T(8,128)(2,1)S(1)} %get-tuple-element.26.table, s32[1,16384]{1,0:T(1,128)S(1)} %get-tuple-element.27.index_ref, f32[1,16384]{1,0:T(1,128)S(1)} %get-tuple-element.28.frac_ref), custom_call_target="tpu_custom_call" | custom-call | flops 2000000000 | bytes 8000000 | tf_op jit(solution)/shard_map/project_own/pallas_call | solution.py:195
  8.4 0.2 collective-permute-done.1.other
  8.6 4.9 %collective-permute-start.2 = (bf16[256,128]{1,0:T(8,128)(2,1)S(1)}, bf16[256,128]{1,0:T(8,128)(2,1)S(1)}, u32[]{:S(2)}, u32[]{:S(2)}) collective-permute-start(bf16[256,128]{1,0:T(8,128)(2,1)S(1)} %pair_rows.1.refs_0_), channel_id=1, source_target_pairs={{0,12},{1,13},{2,14},{3,15},{4,8},{5,9},{6,10},{7,11},{8,4},{9,5},... | collective-permute-start | bytes 196616 | tf_op jit(solution)/shard_map/ppermute | solution.py:26
  13.5 0.1 copy.9.shift_ref
  13.6 0.6 %collective-permute-start.4 = (bf16[256,128]{1,0:T(8,128)(2,1)S(1)}, bf16[256,128]{1,0:T(8,128)(2,1)S(1)}, u32[]{:S(2)}, u32[]{:S(2)}) collective-permute-start(bf16[256,128]{1,0:T(8,128)(2,1)S(1)} %pair_rows.1.refs_0_), channel_id=1, source_target_pairs={{0,4},{1,5},{2,6},{3,7},{4,0},{5,1},{6,2},{7,3},{8,12},{9,13},{10,... | collective-permute-start | bytes 196616 | tf_op jit(solution)/shard_map/ppermute | solution.py:26
  14.2 1.9 %collective-permute-done.2.refs_1_ = bf16[256,128]{1,0:T(8,128)(2,1)S(1)} collective-permute-done((bf16[256,128]{1,0:T(8,128)(2,1)S(1)}, bf16[256,128]{1,0:T(8,128)(2,1)S(1)}, u32[]{:S(2)}, u32[]{:S(2)}) %collective-permute-start.2) | collective-permute-done | bytes 65568 | tf_op jit(solution)/shard_map/ppermute | solution.py:26
  16.1 1.3 %correlate.2 = (f32[36,128]{1,0:T(8,128)S(1)}, f32[8,9216]{1,0:T(8,128)S(1)}, f32[8,9216]{1,0:T(8,128)S(1)}) custom-call(s32[8,2]{1,0:T(8,128)S(1)} %copy.9.shift_ref, bf16[32,18432]{1,0:T(8,128)(2,1)S(1)} %get-tuple-element.24.own_images, bf16[32,18432]{1,0:T(8,128)(2,1)S(1)} %collective-permute-done.other_images, bf16[256,128]{1,0:T(8,128)(2,1)S(1)} %pair_rows.1.refs_0_, ...), custom_call_target="tpu_custom_call" | custom-call | flops 1000000000 | bytes 4000000 | tf_op jit(solution)/shard_map/correlate/pallas_call | solution.py:335
  17.4 2.0 %collective-permute-done.3.refs_0_ = bf16[256,128]{1,0:T(8,128)(2,1)S(1)} collective-permute-done((bf16[256,128]{1,0:T(8,128)(2,1)S(1)}, bf16[256,128]{1,0:T(8,128)(2,1)S(1)}, u32[]{:S(2)}, u32[]{:S(2)}) %collective-permute-start.3) | collective-permute-done | bytes 65568 | tf_op jit(solution)/shard_map/ppermute | solution.py:26
  19.4 0.9 %correlate.3.refs_1_ = f32[36,128]{1,0:T(8,128)S(1)} custom-call(f32[8,9216]{1,0:T(8,128)S(1)} %get-tuple-element.31.cos_ref, f32[8,9216]{1,0:T(8,128)S(1)} %get-tuple-element.32.sin_ref, bf16[32,18432]{1,0:T(8,128)(2,1)S(1)} %get-tuple-element.24.own_images, bf16[32,18432]{1,0:T(8,128)(2,1)S(1)} %collective-permute-done.other_images, ...), custom_call_target="tpu_custom_call" | custom-call | flops 1000000000 | bytes 4000000 | tf_op jit(solution)/shard_map/correlate/pallas_call | solution.py:335
  20.4 0.1 collective-permute-start.5
  20.4 1.2 %collective-permute-done.5.received = f32[80,128]{1,0:T(8,128)S(1)} collective-permute-done((f32[80,128]{1,0:T(8,128)S(1)}, f32[80,128]{1,0:T(8,128)S(1)}, u32[]{:S(2)}, u32[]{:S(2)}) %collective-permute-start.5) | collective-permute-done | bytes 40992 | tf_op jit(solution)/shard_map/ppermute | solution.py:26
  21.6 0.2 posterior.1
  21.9 1.7 %backproject.1 = (f32[256,128]{1,0:T(8,128)S(1)}, bf16[272,128]{1,0:T(8,128)(2,1)S(1)}, bf16[272,128]{1,0:T(8,128)(2,1)S(1)}, bf16[272,128]{1,0:T(8,128)(2,1)S(1)}) custom-call(bf16[64,64]{1,0:T(8,128)(2,1)S(1)} %get-tuple-element.33.weight_ref, f32[8,128]{1,0:T(8,128)S(1)} %get-tuple-element.34.mass, bf16[32,18432]{1,0:T(8,128)(2,1)S(1)} %get-tuple-element.24.own_images, ...), custom_call_target="tpu_custom_call" | custom-call | tf_op jit(solution)/shard_map/backproject/pallas_call | solution.py:495
  23.5 2.5 %collective-permute-start.6 = (bf16[272,128]{1,0:T(8,128)(2,1)S(1)}, bf16[272,128]{1,0:T(8,128)(2,1)S(1)}, u32[]{:S(2)}, u32[]{:S(2)}) collective-permute-start(bf16[272,128]{1,0:T(8,128)(2,1)S(1)} %get-tuple-element.36), channel_id=1, source_target_pairs={{0,12},{1,13},{2,14},{3,15},{4,8},{5,9},{6,10},{7,11},{8,4},{9,5},... | collective-permute-start | bytes 208904 | tf_op jit(solution)/shard_map/ppermute | solution.py:26
  26.1 0.2 collective-permute-start.7
  26.2 1.7 %collective-permute-start.8 = (bf16[272,128]{1,0:T(8,128)(2,1)S(1)}, bf16[272,128]{1,0:T(8,128)(2,1)S(1)}, u32[]{:S(2)}, u32[]{:S(2)}) collective-permute-start(bf16[272,128]{1,0:T(8,128)(2,1)S(1)} %get-tuple-element.38), channel_id=1, source_target_pairs={{0,4},{1,5},{2,6},{3,7},{4,0},{5,1},{6,2},{7,3},{8,12},{9,13},{10,... | collective-permute-start | bytes 208904 | tf_op jit(solution)/shard_map/ppermute | solution.py:26
  28.0 2.5 %collective-permute-done.6.refs_0_ = bf16[272,128]{1,0:T(8,128)(2,1)S(1)} collective-permute-done((bf16[272,128]{1,0:T(8,128)(2,1)S(1)}, bf16[272,128]{1,0:T(8,128)(2,1)S(1)}, u32[]{:S(2)}, u32[]{:S(2)}) %collective-permute-start.6) | collective-permute-done | bytes 69664 | tf_op jit(solution)/shard_map/ppermute | solution.py:26
  30.5 2.5 %collective-permute-done.7.refs_1_ = bf16[272,128]{1,0:T(8,128)(2,1)S(1)} collective-permute-done((bf16[272,128]{1,0:T(8,128)(2,1)S(1)}, bf16[272,128]{1,0:T(8,128)(2,1)S(1)}, u32[]{:S(2)}, u32[]{:S(2)}) %collective-permute-start.7) | collective-permute-done | bytes 69664 | tf_op jit(solution)/shard_map/ppermute | solution.py:26
  33.1 1.6 %collective-permute-start.10 = (bf16[48,128]{1,0:T(8,128)(2,1)S(1)}, bf16[48,128]{1,0:T(8,128)(2,1)S(1)}, u32[]{:S(2)}, u32[]{:S(2)}) collective-permute-start(bf16[48,128]{1,0:T(8,128)(2,1)S(1)} %get-tuple-element.42), channel_id=1, source_target_pairs={{0,2},{1,3},{2,0},{3,1},{4,6},{5,7},{6,4},{7,5},{8,10},{9,11},{10,... | collective-permute-start | bytes 36872 | tf_op jit(solution)/shard_map/ppermute | solution.py:26
  34.7 2.2 %collective-permute-done.10.from_half = bf16[48,128]{1,0:T(8,128)(2,1)S(1)} collective-permute-done((bf16[48,128]{1,0:T(8,128)(2,1)S(1)}, bf16[48,128]{1,0:T(8,128)(2,1)S(1)}, u32[]{:S(2)}, u32[]{:S(2)}) %collective-permute-start.10) | collective-permute-done | bytes 12320 | tf_op jit(solution)/shard_map/ppermute | solution.py:26
  36.9 0.7 %finish.1 = (f32[256,128]{1,0:T(8,128)}, f32[8]{0:T(128)}) custom-call(f32[112,128]{1,0:T(8,128)S(1)} %get-tuple-element.39.keep, bf16[112,128]{1,0:T(8,128)(2,1)S(1)} %collective-permute-done.9.from_core, f32[32,128]{1,0:T(8,128)S(1)} %get-tuple-element.41.low, bf16[48,128]{1,0:T(8,128)(2,1)S(1)} %collective-permute-done.10.from_half, ...), custom_call_target="tpu_custom_call" | custom-call | tf_op jit(solution)/shard_map/finish/pallas_call | solution.py:572
  (15 shorter events, 0.2 us)
Async XLA Ops:
  5.6 10.5 %collective-permute-start = (bf16[32,18432]{1,0:T(8,128)(2,1)}, bf16[32,18432]{1,0:T(8,128)(2,1)S(1)}, u32[]{:S(2)}, u32[]{:S(2)}) collective-permute-start(bf16[32,18432]{1,0:T(8,128)(2,1)} %get-tuple-element.25), channel_id=1, source_target_pairs={{0,1},{1,0},{2,3},{3,2},{4,5},{5,4},{6,7},{7,6},{8,9},{9,8},{10,11... | collective-permute-start | bytes 3538952 | tf_op jit(solution)/shard_map/ppermute | solution.py:26
  6.2 2.4 %collective-permute-start.1 = (bf16[128,128]{1,0:T(8,128)(2,1)S(1)}, bf16[128,128]{1,0:T(8,128)(2,1)S(1)}, u32[]{:S(2)}, u32[]{:S(2)}) collective-permute-start(bf16[128,128]{1,0:T(8,128)(2,1)S(1)} %get-tuple-element.29), channel_id=1, source_target_pairs={{0,1},{1,0},{2,3},{3,2},{4,5},{5,4},{6,7},{7,6},{8,9},{9,8},{10,11... | collective-permute-start | bytes 98312 | tf_op jit(solution)/shard_map/ppermute | solution.py:26
  6.2 7.3 %copy-start.2 = (s32[8,2]{0,1:T(2,128)S(1)}, s32[8,2]{0,1:T(2,128)}, u32[]{:S(2)}) copy-start(s32[8,2]{0,1:T(2,128)} %param.13) | copy-start | bytes 196
  8.6 7.5 %collective-permute-start.2 = (bf16[256,128]{1,0:T(8,128)(2,1)S(1)}, bf16[256,128]{1,0:T(8,128)(2,1)S(1)}, u32[]{:S(2)}, u32[]{:S(2)}) collective-permute-start(bf16[256,128]{1,0:T(8,128)(2,1)S(1)} %pair_rows.1.refs_0_), channel_id=1, source_target_pairs={{0,12},{1,13},{2,14},{3,15},{4,8},{5,9},{6,10},{7,11},{8,4},{9,5},... | collective-permute-start | bytes 196616 | tf_op jit(solution)/shard_map/ppermute | solution.py:26
  13.6 5.8 %collective-permute-start.3 = (bf16[256,128]{1,0:T(8,128)(2,1)S(1)}, bf16[256,128]{1,0:T(8,128)(2,1)S(1)}, u32[]{:S(2)}, u32[]{:S(2)}) collective-permute-start(bf16[256,128]{1,0:T(8,128)(2,1)S(1)} %pair_rows.1.refs_0_), channel_id=1, source_target_pairs={{0,8},{1,9},{2,10},{3,11},{4,12},{5,13},{6,14},{7,15},{8,0},{9,1},... | collective-permute-start | bytes 196616 | tf_op jit(solution)/shard_map/ppermute | solution.py:26
  13.6 5.8 %collective-permute-start.4 = (bf16[256,128]{1,0:T(8,128)(2,1)S(1)}, bf16[256,128]{1,0:T(8,128)(2,1)S(1)}, u32[]{:S(2)}, u32[]{:S(2)}) collective-permute-start(bf16[256,128]{1,0:T(8,128)(2,1)S(1)} %pair_rows.1.refs_0_), channel_id=1, source_target_pairs={{0,4},{1,5},{2,6},{3,7},{4,0},{5,1},{6,2},{7,3},{8,12},{9,13},{10,... | collective-permute-start | bytes 196616 | tf_op jit(solution)/shard_map/ppermute | solution.py:26
  19.4 0.9 %copy-start = (f32[32]{0:T(128)S(1)}, f32[32]{0:T(128)}, u32[]{:S(2)}) copy-start(f32[32]{0:T(128)} %param.8) | copy-start | bytes 388
  19.4 0.9 %copy-start.1 = (s32[32]{0:T(128)S(1)}, s32[32]{0:T(128)}, u32[]{:S(2)}) copy-start(s32[32]{0:T(128)} %param.9) | copy-start | bytes 388
  20.4 1.3 %collective-permute-start.5 = (f32[80,128]{1,0:T(8,128)S(1)}, f32[80,128]{1,0:T(8,128)S(1)}, u32[]{:S(2)}, u32[]{:S(2)}) collective-permute-start(f32[80,128]{1,0:T(8,128)S(1)} %collect.1.mine), channel_id=1, source_target_pairs={{0,1},{1,0},{2,3},{3,2},{4,5},{5,4},{6,7},{7,6},{8,9},{9,8},{10,11... | collective-permute-start | bytes 122888 | tf_op jit(solution)/shard_map/ppermute | solution.py:26
  23.5 7.0 %collective-permute-start.6 = (bf16[272,128]{1,0:T(8,128)(2,1)S(1)}, bf16[272,128]{1,0:T(8,128)(2,1)S(1)}, u32[]{:S(2)}, u32[]{:S(2)}) collective-permute-start(bf16[272,128]{1,0:T(8,128)(2,1)S(1)} %get-tuple-element.36), channel_id=1, source_target_pairs={{0,12},{1,13},{2,14},{3,15},{4,8},{5,9},{6,10},{7,11},{8,4},{9,5},... | collective-permute-start | bytes 208904 | tf_op jit(solution)/shard_map/ppermute | solution.py:26
  26.1 6.9 %collective-permute-start.7 = (bf16[272,128]{1,0:T(8,128)(2,1)S(1)}, bf16[272,128]{1,0:T(8,128)(2,1)S(1)}, u32[]{:S(2)}, u32[]{:S(2)}) collective-permute-start(bf16[272,128]{1,0:T(8,128)(2,1)S(1)} %get-tuple-element.37), channel_id=1, source_target_pairs={{0,8},{1,9},{2,10},{3,11},{4,12},{5,13},{6,14},{7,15},{8,0},{9,1},... | collective-permute-start | bytes 208904 | tf_op jit(solution)/shard_map/ppermute | solution.py:26
  26.2 6.8 %collective-permute-start.8 = (bf16[272,128]{1,0:T(8,128)(2,1)S(1)}, bf16[272,128]{1,0:T(8,128)(2,1)S(1)}, u32[]{:S(2)}, u32[]{:S(2)}) collective-permute-start(bf16[272,128]{1,0:T(8,128)(2,1)S(1)} %get-tuple-element.38), channel_id=1, source_target_pairs={{0,4},{1,5},{2,6},{3,7},{4,0},{5,1},{6,2},{7,3},{8,12},{9,13},{10,... | collective-permute-start | bytes 208904 | tf_op jit(solution)/shard_map/ppermute | solution.py:26
  33.1 3.8 %collective-permute-start.9 = (bf16[112,128]{1,0:T(8,128)(2,1)S(1)}, bf16[112,128]{1,0:T(8,128)(2,1)S(1)}, u32[]{:S(2)}, u32[]{:S(2)}) collective-permute-start(bf16[112,128]{1,0:T(8,128)(2,1)S(1)} %get-tuple-element.40), channel_id=1, source_target_pairs={{0,1},{1,0},{2,3},{3,2},{4,5},{5,4},{6,7},{7,6},{8,9},{9,8},{10,11... | collective-permute-start | bytes 86024 | tf_op jit(solution)/shard_map/ppermute | solution.py:26
  33.1 3.8 %collective-permute-start.10 = (bf16[48,128]{1,0:T(8,128)(2,1)S(1)}, bf16[48,128]{1,0:T(8,128)(2,1)S(1)}, u32[]{:S(2)}, u32[]{:S(2)}) collective-permute-start(bf16[48,128]{1,0:T(8,128)(2,1)S(1)} %get-tuple-element.42), channel_id=1, source_target_pairs={{0,2},{1,3},{2,0},{3,1},{4,6},{5,7},{6,4},{7,5},{8,10},{9,11},{10,... | collective-permute-start | bytes 36872 | tf_op jit(solution)/shard_map/ppermute | solution.py:26

commit v12 on v10

--- a/solution.py
+++ b/solution.py
@@ -85,10 +85,27 @@
     lax.fori_loop(0, half_tiles // tiles, body, 0, unroll=8)
 
 
+def image_copies(images_hbm, target, sems, first, half, pixels):
+    chunk = BLOCK * LANES
+    blocks = pixels // (2 * chunk)
+    copies = []
+    for comp in range(2):
+        for step in range(blocks):
+            source = pl.multiple_of(comp * pixels + (2 * step + half) * chunk, chunk)
+            dest = (comp * blocks + step) * chunk
+            copies.append(
+                pltpu.make_async_copy(
+                    images_hbm.at[:, pl.ds(source, chunk)],
+                    target.at[:, pl.ds(dest, chunk)],
+                    sems.at[first + len(copies)],
+                )
+            )
+    return copies
+
+
 def project_other_kernel(
     table_hbm, index_hbm, frac_hbm, images_hbm,
-    out_ref, table, index_ref, frac_ref, own_images, other_images,
-    table_in, flat, wide, blended, sems
+    out_ref, table, index_ref, frac_ref, table_in, flat, wide, blended, sems
 ):
     device = lax.axis_index("particle")
     row_count = lax.axis_size("particle") // 2
@@ -102,20 +119,7 @@
         pltpu.make_async_copy(frac_hbm, frac_ref, sems.at[2]),
     ]
     pixels = index_ref.shape[1]
-    chunk = BLOCK * LANES
-    blocks = pixels // (2 * chunk)
-    for target, half in ((other_images, 1 - own_half()), (own_images, own_half())):
-        for comp in range(2):
-            for step in range(blocks):
-                source = pl.multiple_of(comp * pixels + (2 * step + half) * chunk, chunk)
-                dest = (comp * blocks + step) * chunk
-                copies.append(
-                    pltpu.make_async_copy(
-                        images_hbm.at[:, pl.ds(source, chunk)],
-                        target.at[:, pl.ds(dest, chunk)],
-                        sems.at[len(copies)],
-                    )
-                )
+    copies += image_copies(images_hbm, out_ref, sems, 3, 1 - own_half(), pixels)
     for copy in copies[:3]:
         copy.start()
     copies[0].wait()
@@ -145,7 +149,11 @@
     copies[1].wait()
     copies[2].wait()
     project_half(table, index_ref, frac_ref, 1 - own_half(), blended)
-    out_ref[...] = blended[...].astype(jnp.bfloat16)
+    parts = out_ref.shape[0]
+    for k in range(blended.shape[0] // parts):
+        out_ref[:, pixels + k * LANES : pixels + (k + 1) * LANES] = blended[
+            k * parts : (k + 1) * parts, :
+        ].astype(jnp.bfloat16)
     for copy in copies[3:]:
         copy.wait()
 
@@ -156,19 +164,17 @@
     highs = vox // LANES
     half_rows = pixels // LANES
     groups = -(-LANES // 7)
-    half_images = jax.ShapeDtypeStruct((images.shape[0], pixels), jnp.bfloat16)
-    copies = 3 + 2 * pixels // (BLOCK * LANES)
+    parts = images.shape[0]
+    copies = 3 + pixels // (BLOCK * LANES)
     return pl.pallas_call(
         project_other_kernel,
         in_specs=[pl.BlockSpec(memory_space=pltpu.HBM)] * 4,
-        out_specs=whole_vmem(6),
+        out_specs=whole_vmem(4),
         out_shape=[
-            jax.ShapeDtypeStruct((half_rows, LANES), jnp.bfloat16),
+            jax.ShapeDtypeStruct((parts, pixels + half_rows * LANES // parts), jnp.bfloat16),
             jax.ShapeDtypeStruct((16 * groups, highs), jnp.bfloat16),
             jax.ShapeDtypeStruct((1, pixels), jnp.int32),
             jax.ShapeDtypeStruct((1, pixels), jnp.float32),
-            half_images,
-            half_images,
         ],
         scratch_shapes=[
             pltpu.VMEM((1, 1, 2, vox), jnp.bfloat16),
@@ -182,30 +188,47 @@
     )(*(in_hbm(value) for value in (class_refs, interp_index, interp_frac, images)))
 
 
-def project_own_kernel(table, index_ref, frac_ref, out_ref, blended):
+def project_own_kernel(table, index_ref, frac_ref, images_hbm, out_ref, own_images, blended, sems):
+    copies = image_copies(images_hbm, own_images, sems, 0, own_half(), index_ref.shape[1])
+    for copy in copies:
+        copy.start()
     project_half(table, index_ref, frac_ref, own_half(), blended)
     out_ref[...] = blended[...].astype(jnp.bfloat16)
-
-
-def project_own(table, index, frac):
-    half_rows = index.shape[1] // LANES
+    for copy in copies:
+        copy.wait()
+
+
+def project_own(table, index, frac, images):
+    pixels = index.shape[1]
+    half_rows = pixels // LANES
     return pl.pallas_call(
         project_own_kernel,
-        in_specs=whole_vmem(3),
-        out_specs=pl.BlockSpec(memory_space=pltpu.VMEM),
-        out_shape=jax.ShapeDtypeStruct((half_rows, LANES), jnp.bfloat16),
-        scratch_shapes=[pltpu.VMEM((half_rows, LANES), jnp.float32)],
+        in_specs=whole_vmem(3) + [pl.BlockSpec(memory_space=pltpu.HBM)],
+        out_specs=whole_vmem(2),
+        out_shape=[
+            jax.ShapeDtypeStruct((half_rows, LANES), jnp.bfloat16),
+            jax.ShapeDtypeStruct((images.shape[0], pixels), jnp.bfloat16),
+        ],
+        scratch_shapes=[
+            pltpu.VMEM((half_rows, LANES), jnp.float32),
+            pltpu.SemaphoreType.DMA((pixels // (BLOCK * LANES),)),
+        ],
         compiler_params=pltpu.CompilerParams(vmem_limit_bytes=16 * MIB),
         cost_estimate=pl.CostEstimate(flops=2000000000, bytes_accessed=8000000, transcendentals=0),
         name="project_own",
-    )(table, index, frac)
+    )(table, index, frac, in_hbm(images))
 
 
 def pair_kernel(own, other, out_ref):
     count = own.shape[0]
+    parts, width = other.shape
+    tiles = count // parts
     core = own_half()
     out_ref[pl.ds(pl.multiple_of(core * count, count), count), :] = own[...]
-    out_ref[pl.ds(pl.multiple_of((1 - core) * count, count), count), :] = other[...]
+    for k in range(tiles):
+        lanes = slice(width - (tiles - k) * LANES, width - (tiles - k - 1) * LANES)
+        rows = pl.ds(pl.multiple_of((1 - core) * count + k * parts, parts), parts)
+        out_ref[rows, :] = other[:, lanes]
 
 
 def pair_rows(own, other):
@@ -343,7 +366,7 @@
     count = len(parts_refs)
     slots = parts_refs[0].shape[0] - combos
     parts = precision_ref.shape[1]
-    for index, ref in enumerate(parts_refs[::-1]):
+    for index, ref in enumerate(parts_refs):
         out_ref[index * combos : (index + 1) * combos, :] = ref[0:combos, :]
         power = count * combos + index * slots
         out_ref[power : power + slots, :] = ref[combos:, :]
@@ -362,7 +385,7 @@
         out_shape=jax.ShapeDtypeStruct((rows, LANES), jnp.float32),
         compiler_params=pltpu.CompilerParams(vmem_limit_bytes=16 * MIB),
         name="collect",
-    )(*passes[::-1], precision, assigned)
+    )(*passes, precision, assigned)
 
 
 def rotate_back(weights, own_images, other_images, cos_ref, sin_ref, where, imag_where, slots):
@@ -617,15 +640,13 @@
     slots = dev_count // 2
     chips = slots // 2
     parts, width = images.shape
-    other_half, table, index, frac, own_images, other_images = project_other(
-        class_refs, interp_index, interp_frac, images
-    )
-    from_core = exchange(other_half, 1)
-    images_received = exchange(other_images, 1)
-    pair = pair_rows(project_own(table, index, frac), from_core)
+    to_core, table, index, frac = project_other(class_refs, interp_index, interp_frac, images)
+    images_received = exchange(to_core, 1)
+    own, own_images = project_own(table, index, frac, images)
+    pair = pair_rows(own, images_received)
     others = chip_order(chips)[1:]
     pairs = [pair] + [exchange(pair, 4 * m) for m in others]
-    group = chips // 4
+    group = chips // 2
     first, cos_table, sin_table = correlate(
         own_images, images_received, pairs[:group], shift_grid=shift_grid
     )
@@ -650,6 +671,7 @@
     sums = backproject(weights, own_images, images_received, cos_table, sin_table, slots)
     folded = fold(low, low_from_half, mass, sums[1:])
     chip_sums = [exchange(send, 4 * m) for m, send in zip(others, folded[2:])]
+    chip_sums = chip_sums[:1] + chip_sums[:0:-1]
     keep, send, mass = merge(sums[0], folded[0], folded[1], chip_sums)
     back, class_mass = finish(
         keep, exchange(send, 1), mass, 1.0 / math.sqrt(parts), CLASSES / (parts * dev_count)

time: 36.6 us -> 34.9 us (0.954)
  Pallas kernels: 12 us -> 10.6 us
    pallas_call x4 -> x2, Pallas kernels: 3.55 us -> 2.05 us  [correlate(): pl.pallas_call(functools.partial(kernel, chunk=2048), in_specs=whole_vmem...]
    ppermute x11 -> x10, starting transfers between devices: 12.5 us -> 12.3 us  [exchange(): return lax.ppermute(value, 'particle', pairs)]
    ppermute x11 -> x10, waiting for transfers between devices: 11.1 us -> 11.1 us  [exchange(): return lax.ppermute(value, 'particle', pairs)]
  transfers between devices with their start and end apart: 11 -> 10, of which waited for: 7 -> 8; matrix products, arithmetic and copies ran while one was open for 0% -> 0% of each run, Pallas kernels for 17% -> 14%
where the time goes in v12:
time: 34.9 us; the launch traced here: 34.8 us
  starting transfers between devices  12.3 us (35%)
  waiting for transfers between devices  11.1 us (32%)
  Pallas kernels  10.6 us (30%)
  between operations  0.76 us (2%)
    ppermute x10, starting transfers between devices, exchange(): return lax.ppermute(value, 'particle', pairs)  12.3 us
    ppermute x10, waiting for transfers between devices, exchange(): return lax.ppermute(value, 'particle', pairs)  11.1 us
    pallas_call x1, Pallas kernels, project_other(): pl.pallas_call(project_other_kernel, in_specs=[pl.BlockSpec(memory_space=...  3.7 us
    pallas_call x1, Pallas kernels, project_own(): pl.pallas_call(project_own_kernel, in_specs=whole_vmem(3) + [pl.BlockSpec...  2.33 us
    pallas_call x2, Pallas kernels, correlate(): pl.pallas_call(functools.partial(kernel, chunk=2048), in_specs=whole_vmem...  2.05 us
    pallas_call x1, Pallas kernels, backproject(): pl.pallas_call(functools.partial(backproject_kernel, slots=slots, chunk=L...  1.32 us
  transfers between devices with their start and end apart: 10, of which 8 were waited for; matrix products, arithmetic and copies ran while one was open for 0% of the time, Pallas kernels for 14%

profile of v12, /device:TPU:0, one launch (start us, length us, event | category | flops | bytes accessed | tf_op | source)
XLA Modules:
  0.0 34.8 jit_solution(13175982665818563390)
XLA Ops:
  0.6 3.7 %project_other.1 = (bf16[32,16896]{1,0:T(8,128)(2,1)S(1)}, bf16[304,256]{1,0:T(8,128)(2,1)S(1)}, s32[1,16384]{1,0:T(1,128)S(1)}, f32[1,16384]{1,0:T(1,128)S(1)}) custom-call(bf16[2,8,2,32768]{3,2,1,0:T(2,128)(2,1)} %table_hbm.1, s32[1,16384]{1,0:T(1,128)} %index_hbm.1, f32[1,16384]{1,0:T(1,128)} %frac_hbm.1, bf16[32,32768]{1,0:T(8,128)(2,1)} %images_hbm.3), custom_call_target="tpu_custom_call" | custom-call | tf_op jit(solution)/shard_map/project_other/pallas_call | solution.py:169
  4.3 0.5 %collective-permute-start = (bf16[32,16896]{1,0:T(8,128)(2,1)S(1)}, bf16[32,16896]{1,0:T(8,128)(2,1)S(1)}, u32[]{:S(2)}, u32[]{:S(2)}) collective-permute-start(bf16[32,16896]{1,0:T(8,128)(2,1)S(1)} %get-tuple-element.33), channel_id=1, source_target_pairs={{0,1},{1,0},{2,3},{3,2},{4,5},{5,4},{6,7},{7,6},{8,9},{9,8},{10,11... | collective-permute-start | bytes 3244040 | tf_op jit(solution)/shard_map/ppermute | solution.py:26
  4.9 2.3 %project_own.1 = (bf16[128,128]{1,0:T(8,128)(2,1)S(1)}, bf16[32,16384]{1,0:T(8,128)(2,1)S(1)}) custom-call(bf16[304,256]{1,0:T(8,128)(2,1)S(1)} %get-tuple-element.29.table, s32[1,16384]{1,0:T(1,128)S(1)} %get-tuple-element.30.index_ref, f32[1,16384]{1,0:T(1,128)S(1)} %get-tuple-element.31.frac_ref, bf16[32,32768]{1,0:T(8,128)(2,1)} %images_hbm.3), custom_call_target="tpu_custom_call" | custom-call | flops 2000000000 | bytes 8000000 | tf_op jit(solution)/shard_map/project_own/pallas_call | solution.py:204
  7.2 5.0 %collective-permute-start.1 = (bf16[256,128]{1,0:T(8,128)(2,1)S(1)}, bf16[256,128]{1,0:T(8,128)(2,1)S(1)}, u32[]{:S(2)}, u32[]{:S(2)}) collective-permute-start(bf16[256,128]{1,0:T(8,128)(2,1)S(1)} %pair_rows.1.refs_0_), channel_id=1, source_target_pairs={{0,12},{1,13},{2,14},{3,15},{4,8},{5,9},{6,10},{7,11},{8,4},{9,5},... | collective-permute-start | bytes 196616 | tf_op jit(solution)/shard_map/ppermute | solution.py:26
  12.2 0.1 copy.9.shift_ref
  12.3 0.6 %collective-permute-start.3 = (bf16[256,128]{1,0:T(8,128)(2,1)S(1)}, bf16[256,128]{1,0:T(8,128)(2,1)S(1)}, u32[]{:S(2)}, u32[]{:S(2)}) collective-permute-start(bf16[256,128]{1,0:T(8,128)(2,1)S(1)} %pair_rows.1.refs_0_), channel_id=1, source_target_pairs={{0,4},{1,5},{2,6},{3,7},{4,0},{5,1},{6,2},{7,3},{8,12},{9,13},{10,... | collective-permute-start | bytes 196616 | tf_op jit(solution)/shard_map/ppermute | solution.py:26
  12.9 1.9 %collective-permute-done.1.refs_1_ = bf16[256,128]{1,0:T(8,128)(2,1)S(1)} collective-permute-done((bf16[256,128]{1,0:T(8,128)(2,1)S(1)}, bf16[256,128]{1,0:T(8,128)(2,1)S(1)}, u32[]{:S(2)}, u32[]{:S(2)}) %collective-permute-start.1) | collective-permute-done | bytes 65568 | tf_op jit(solution)/shard_map/ppermute | solution.py:26
  14.8 1.2 %correlate.2 = (f32[36,128]{1,0:T(8,128)S(1)}, f32[8,8192]{1,0:T(8,128)S(1)}, f32[8,8192]{1,0:T(8,128)S(1)}) custom-call(s32[8,2]{1,0:T(8,128)S(1)} %copy.9.shift_ref, bf16[32,16384]{1,0:T(8,128)(2,1)S(1)} %get-tuple-element.32.own_images, bf16[32,16896]{1,0:T(8,128)(2,1)S(1)} %collective-permute-done.other.other_images, ...), custom_call_target="tpu_custom_call" | custom-call | flops 1000000000 | bytes 4000000 | tf_op jit(solution)/shard_map/correlate/pallas_call | solution.py:352
  16.0 2.1 %collective-permute-done.2.refs_0_ = bf16[256,128]{1,0:T(8,128)(2,1)S(1)} collective-permute-done((bf16[256,128]{1,0:T(8,128)(2,1)S(1)}, bf16[256,128]{1,0:T(8,128)(2,1)S(1)}, u32[]{:S(2)}, u32[]{:S(2)}) %collective-permute-start.2) | collective-permute-done | bytes 65568 | tf_op jit(solution)/shard_map/ppermute | solution.py:26
  18.1 0.8 %correlate.3.refs_1_ = f32[36,128]{1,0:T(8,128)S(1)} custom-call(f32[8,8192]{1,0:T(8,128)S(1)} %get-tuple-element.36.cos_ref, f32[8,8192]{1,0:T(8,128)S(1)} %get-tuple-element.37.sin_ref, bf16[32,16384]{1,0:T(8,128)(2,1)S(1)} %get-tuple-element.32.own_images, bf16[32,16896]{1,0:T(8,128)(2,1)S(1)} %collective-permute-done.other.other_images, ...), custom_call_target="tpu_custom_call" | custom-call | flops 1000000000 | bytes 4000000 | tf_op jit(solution)/shard_map/correlate/pallas_call | solution.py:352
  19.0 0.1 collective-permute-start.4
  19.1 1.2 %collective-permute-done.4.received = f32[80,128]{1,0:T(8,128)S(1)} collective-permute-done((f32[80,128]{1,0:T(8,128)S(1)}, f32[80,128]{1,0:T(8,128)S(1)}, u32[]{:S(2)}, u32[]{:S(2)}) %collective-permute-start.4) | collective-permute-done | bytes 40992 | tf_op jit(solution)/shard_map/ppermute | solution.py:26
  20.3 0.4 %posterior.1 = (bf16[64,64]{1,0:T(8,128)(2,1)S(1)}, f32[128,128]{1,0:T(8,128)S(1)}, bf16[144,128]{1,0:T(8,128)(2,1)S(1)}, f32[8,128]{1,0:T(8,128)S(1)}) custom-call(f32[80,128]{1,0:T(8,128)S(1)} %collect.1.mine, f32[80,128]{1,0:T(8,128)S(1)} %collective-permute-done.4.received, bf16[32,16384]{1,0:T(8,128)(2,1)S(1)} %get-tuple-element.32.own_images, ...), custom_call_target="tpu_custom_call" | custom-call | tf_op jit(solution)/shard_map/posterior/pallas_call | solution.py:469
  20.7 1.6 %collective-permute-start.5 = (bf16[144,128]{1,0:T(8,128)(2,1)S(1)}, bf16[144,128]{1,0:T(8,128)(2,1)S(1)}, u32[]{:S(2)}, u32[]{:S(2)}) collective-permute-start(bf16[144,128]{1,0:T(8,128)(2,1)S(1)} %get-tuple-element.41), channel_id=1, source_target_pairs={{0,2},{1,3},{2,0},{3,1},{4,6},{5,7},{6,4},{7,5},{8,10},{9,11},{10,... | collective-permute-start | bytes 110600 | tf_op jit(solution)/shard_map/ppermute | solution.py:26
  22.3 1.3 %backproject.1 = (f32[224,128]{1,0:T(8,128)S(1)}, bf16[224,128]{1,0:T(8,128)(2,1)S(1)}, bf16[224,128]{1,0:T(8,128)(2,1)S(1)}, bf16[224,128]{1,0:T(8,128)(2,1)S(1)}) custom-call(bf16[64,64]{1,0:T(8,128)(2,1)S(1)} %get-tuple-element.38.weight_ref, bf16[32,16384]{1,0:T(8,128)(2,1)S(1)} %get-tuple-element.32.own_images, ...), custom_call_target="tpu_custom_call" | custom-call | flops 2000000000 | bytes 8000000 | tf_op jit(solution)/shard_map/backproject/pallas_call | solution.py:519
  23.6 1.1 %collective-permute-done.5.low_received = bf16[144,128]{1,0:T(8,128)(2,1)S(1)} collective-permute-done((bf16[144,128]{1,0:T(8,128)(2,1)S(1)}, bf16[144,128]{1,0:T(8,128)(2,1)S(1)}, u32[]{:S(2)}, u32[]{:S(2)}) %collective-permute-start.5) | collective-permute-done | bytes 36896 | tf_op jit(solution)/shard_map/ppermute | solution.py:26
  24.7 2.5 %collective-permute-start.6 = (bf16[272,128]{1,0:T(8,128)(2,1)S(1)}, bf16[272,128]{1,0:T(8,128)(2,1)S(1)}, u32[]{:S(2)}, u32[]{:S(2)}) collective-permute-start(bf16[272,128]{1,0:T(8,128)(2,1)S(1)} %get-tuple-element.48), channel_id=1, source_target_pairs={{0,12},{1,13},{2,14},{3,15},{4,8},{5,9},{6,10},{7,11},{8,4},{9,5},... | collective-permute-start | bytes 208904 | tf_op jit(solution)/shard_map/ppermute | solution.py:26
  27.3 1.9 %collective-permute-start.8 = (bf16[272,128]{1,0:T(8,128)(2,1)S(1)}, bf16[272,128]{1,0:T(8,128)(2,1)S(1)}, u32[]{:S(2)}, u32[]{:S(2)}) collective-permute-start(bf16[272,128]{1,0:T(8,128)(2,1)S(1)} %get-tuple-element.50), channel_id=1, source_target_pairs={{0,8},{1,9},{2,10},{3,11},{4,12},{5,13},{6,14},{7,15},{8,0},{9,1},... | collective-permute-start | bytes 208904 | tf_op jit(solution)/shard_map/ppermute | solution.py:26
  29.2 2.1 %collective-permute-done.6.refs_0_ = bf16[272,128]{1,0:T(8,128)(2,1)S(1)} collective-permute-done((bf16[272,128]{1,0:T(8,128)(2,1)S(1)}, bf16[272,128]{1,0:T(8,128)(2,1)S(1)}, u32[]{:S(2)}, u32[]{:S(2)}) %collective-permute-start.6) | collective-permute-done | bytes 69664 | tf_op jit(solution)/shard_map/ppermute | solution.py:26
  31.3 1.2 %collective-permute-done.7.refs_1_ = bf16[272,128]{1,0:T(8,128)(2,1)S(1)} collective-permute-done((bf16[272,128]{1,0:T(8,128)(2,1)S(1)}, bf16[272,128]{1,0:T(8,128)(2,1)S(1)}, u32[]{:S(2)}, u32[]{:S(2)}) %collective-permute-start.7) | collective-permute-done | bytes 69664 | tf_op jit(solution)/shard_map/ppermute | solution.py:26
  32.5 0.2 collective-permute-done.8.refs_2_
  32.8 0.1 collective-permute-start.9
  32.9 1.2 %collective-permute-done.9.received = bf16[128,128]{1,0:T(8,128)(2,1)S(1)} collective-permute-done((bf16[128,128]{1,0:T(8,128)(2,1)S(1)}, bf16[128,128]{1,0:T(8,128)(2,1)S(1)}, u32[]{:S(2)}, u32[]{:S(2)}) %collective-permute-start.9) | collective-permute-done | bytes 32800 | tf_op jit(solution)/shard_map/ppermute | solution.py:26
  34.1 0.7 %finish.1 = (f32[256,128]{1,0:T(8,128)}, f32[8]{0:T(128)}) custom-call(f32[128,128]{1,0:T(8,128)S(1)} %get-tuple-element.51.own, bf16[128,128]{1,0:T(8,128)(2,1)S(1)} %collective-permute-done.9.received, f32[8,128]{1,0:T(8,128)S(1)} %get-tuple-element.53.mass), custom_call_target="tpu_custom_call" | custom-call | tf_op jit(solution)/shard_map/finish/pallas_call | solution.py:623
  (14 shorter events, 0.1 us)
Async XLA Ops:
  4.3 2.9 %collective-permute-start = (bf16[32,16896]{1,0:T(8,128)(2,1)S(1)}, bf16[32,16896]{1,0:T(8,128)(2,1)S(1)}, u32[]{:S(2)}, u32[]{:S(2)}) collective-permute-start(bf16[32,16896]{1,0:T(8,128)(2,1)S(1)} %get-tuple-element.33), channel_id=1, source_target_pairs={{0,1},{1,0},{2,3},{3,2},{4,5},{5,4},{6,7},{7,6},{8,9},{9,8},{10,11... | collective-permute-start | bytes 3244040 | tf_op jit(solution)/shard_map/ppermute | solution.py:26
  4.8 7.4 %copy-start.2 = (s32[8,2]{0,1:T(2,128)S(1)}, s32[8,2]{0,1:T(2,128)}, u32[]{:S(2)}) copy-start(s32[8,2]{0,1:T(2,128)} %param.13) | copy-start | bytes 196
  7.2 7.6 %collective-permute-start.1 = (bf16[256,128]{1,0:T(8,128)(2,1)S(1)}, bf16[256,128]{1,0:T(8,128)(2,1)S(1)}, u32[]{:S(2)}, u32[]{:S(2)}) collective-permute-start(bf16[256,128]{1,0:T(8,128)(2,1)S(1)} %pair_rows.1.refs_0_), channel_id=1, source_target_pairs={{0,12},{1,13},{2,14},{3,15},{4,8},{5,9},{6,10},{7,11},{8,4},{9,5},... | collective-permute-start | bytes 196616 | tf_op jit(solution)/shard_map/ppermute | solution.py:26
  12.3 5.8 %collective-permute-start.2 = (bf16[256,128]{1,0:T(8,128)(2,1)S(1)}, bf16[256,128]{1,0:T(8,128)(2,1)S(1)}, u32[]{:S(2)}, u32[]{:S(2)}) collective-permute-start(bf16[256,128]{1,0:T(8,128)(2,1)S(1)} %pair_rows.1.refs_0_), channel_id=1, source_target_pairs={{0,8},{1,9},{2,10},{3,11},{4,12},{5,13},{6,14},{7,15},{8,0},{9,1},... | collective-permute-start | bytes 196616 | tf_op jit(solution)/shard_map/ppermute | solution.py:26
  12.3 5.8 %collective-permute-start.3 = (bf16[256,128]{1,0:T(8,128)(2,1)S(1)}, bf16[256,128]{1,0:T(8,128)(2,1)S(1)}, u32[]{:S(2)}, u32[]{:S(2)}) collective-permute-start(bf16[256,128]{1,0:T(8,128)(2,1)S(1)} %pair_rows.1.refs_0_), channel_id=1, source_target_pairs={{0,4},{1,5},{2,6},{3,7},{4,0},{5,1},{6,2},{7,3},{8,12},{9,13},{10,... | collective-permute-start | bytes 196616 | tf_op jit(solution)/shard_map/ppermute | solution.py:26
  16.0 3.0 %copy-start = (f32[32]{0:T(128)S(1)}, f32[32]{0:T(128)}, u32[]{:S(2)}) copy-start(f32[32]{0:T(128)} %param.8) | copy-start | bytes 388
  16.0 3.0 %copy-start.1 = (s32[32]{0:T(128)S(1)}, s32[32]{0:T(128)}, u32[]{:S(2)}) copy-start(s32[32]{0:T(128)} %param.9) | copy-start | bytes 388
  19.0 1.3 %collective-permute-start.4 = (f32[80,128]{1,0:T(8,128)S(1)}, f32[80,128]{1,0:T(8,128)S(1)}, u32[]{:S(2)}, u32[]{:S(2)}) collective-permute-start(f32[80,128]{1,0:T(8,128)S(1)} %collect.1.mine), channel_id=1, source_target_pairs={{0,1},{1,0},{2,3},{3,2},{4,5},{5,4},{6,7},{7,6},{8,9},{9,8},{10,11... | collective-permute-start | bytes 122888 | tf_op jit(solution)/shard_map/ppermute | solution.py:26
  20.7 4.0 %collective-permute-start.5 = (bf16[144,128]{1,0:T(8,128)(2,1)S(1)}, bf16[144,128]{1,0:T(8,128)(2,1)S(1)}, u32[]{:S(2)}, u32[]{:S(2)}) collective-permute-start(bf16[144,128]{1,0:T(8,128)(2,1)S(1)} %get-tuple-element.41), channel_id=1, source_target_pairs={{0,2},{1,3},{2,0},{3,1},{4,6},{5,7},{6,4},{7,5},{8,10},{9,11},{10,... | collective-permute-start | bytes 110600 | tf_op jit(solution)/shard_map/ppermute | solution.py:26
  24.7 6.6 %collective-permute-start.6 = (bf16[272,128]{1,0:T(8,128)(2,1)S(1)}, bf16[272,128]{1,0:T(8,128)(2,1)S(1)}, u32[]{:S(2)}, u32[]{:S(2)}) collective-permute-start(bf16[272,128]{1,0:T(8,128)(2,1)S(1)} %get-tuple-element.48), channel_id=1, source_target_pairs={{0,12},{1,13},{2,14},{3,15},{4,8},{5,9},{6,10},{7,11},{8,4},{9,5},... | collective-permute-start | bytes 208904 | tf_op jit(solution)/shard_map/ppermute | solution.py:26
  27.3 5.3 %collective-permute-start.7 = (bf16[272,128]{1,0:T(8,128)(2,1)S(1)}, bf16[272,128]{1,0:T(8,128)(2,1)S(1)}, u32[]{:S(2)}, u32[]{:S(2)}) collective-permute-start(bf16[272,128]{1,0:T(8,128)(2,1)S(1)} %get-tuple-element.49), channel_id=1, source_target_pairs={{0,4},{1,5},{2,6},{3,7},{4,0},{5,1},{6,2},{7,3},{8,12},{9,13},{10,... | collective-permute-start | bytes 208904 | tf_op jit(solution)/shard_map/ppermute | solution.py:26
  27.3 5.5 %collective-permute-start.8 = (bf16[272,128]{1,0:T(8,128)(2,1)S(1)}, bf16[272,128]{1,0:T(8,128)(2,1)S(1)}, u32[]{:S(2)}, u32[]{:S(2)}) collective-permute-start(bf16[272,128]{1,0:T(8,128)(2,1)S(1)} %get-tuple-element.50), channel_id=1, source_target_pairs={{0,8},{1,9},{2,10},{3,11},{4,12},{5,13},{6,14},{7,15},{8,0},{9,1},... | collective-permute-start | bytes 208904 | tf_op jit(solution)/shard_map/ppermute | solution.py:26
  32.8 1.3 %collective-permute-start.9 = (bf16[128,128]{1,0:T(8,128)(2,1)S(1)}, bf16[128,128]{1,0:T(8,128)(2,1)S(1)}, u32[]{:S(2)}, u32[]{:S(2)}) collective-permute-start(bf16[128,128]{1,0:T(8,128)(2,1)S(1)} %get-tuple-element.52), channel_id=1, source_target_pairs={{0,1},{1,0},{2,3},{3,2},{4,5},{5,4},{6,7},{7,6},{8,9},{9,8},{10,11... | collective-permute-start | bytes 98312 | tf_op jit(solution)/shard_map/ppermute | solution.py:26

commit v13 on v12

--- a/solution.py
+++ b/solution.py
@@ -327,17 +327,17 @@
         image_real = jnp.concatenate([own_images[:, where], other_images[:, where]], axis=0)
         image_imag = jnp.concatenate([own_images[:, imag_where], other_images[:, imag_where]], axis=0)
         total = total + lax.dot_general(
-            turned_real, image_real, contract_lanes, preferred_element_type=jnp.float32
+            image_real, turned_real, contract_lanes, preferred_element_type=jnp.float32
         )
         return total + lax.dot_general(
-            turned_imag, image_imag, contract_lanes, preferred_element_type=jnp.float32
+            image_imag, turned_imag, contract_lanes, preferred_element_type=jnp.float32
         )
 
     total = lax.fori_loop(
-        0, width // chunk, body, jnp.zeros((combos, 2 * parts), jnp.float32), unroll=2
+        0, width // chunk, body, jnp.zeros((2 * parts, combos), jnp.float32), unroll=2
     )
     out_ref[0:combos, :] = jnp.zeros((combos, LANES), jnp.float32)
-    out_ref[0:combos, 0 : 2 * parts] = total
+    out_ref[0:combos, 0 : 2 * parts] = total.T
 
 
 def correlate(own_images, other_images, pairs, shift_grid=None, tables=None):
@@ -532,7 +532,7 @@
 
 
 def fold_kernel(low_ref, low_received, mass, *refs, chips):
-    mains, (own, own_mass), sends = refs[: chips - 1], refs[chips - 1 : chips + 1], refs[chips + 1 :]
+    mains, (own, own_mass), sends = refs[: chips - 2], refs[chips - 2 : chips], refs[chips:]
     rows = own.shape[0]
     low_body = low_ref.shape[0]
     total_mass = mass[0:1, :] + joined_mass(low_received[low_body:, :])
@@ -544,27 +544,44 @@
         target[0:rows, :] = value.astype(target.dtype)
         if m > 0:
             target[rows : rows + MASS_ROWS, :] = block
-            target[rows + MASS_ROWS :, :] = mains[m - 1][...]
+        if m > 1:
+            target[rows + MASS_ROWS :, :] = mains[m - 2][...]
 
 
 def fold(low, low_received, mass, mains):
-    chips = len(mains) + 1
+    chips = len(mains) + 2
     rows = low.shape[0] // chips
+    head = rows + MASS_ROWS
     return pl.pallas_call(
         functools.partial(fold_kernel, chips=chips),
-        in_specs=whole_vmem(2 + chips),
+        in_specs=whole_vmem(1 + chips),
         out_specs=whole_vmem(1 + chips),
         out_shape=[
             jax.ShapeDtypeStruct((rows, LANES), jnp.float32),
             jax.ShapeDtypeStruct((8, LANES), jnp.float32),
+            jax.ShapeDtypeStruct((head, LANES), jnp.bfloat16),
         ]
-        + [
-            jax.ShapeDtypeStruct((rows + MASS_ROWS + main.shape[0], LANES), jnp.bfloat16)
-            for main in mains
-        ],
+        + [jax.ShapeDtypeStruct((head + main.shape[0], LANES), jnp.bfloat16) for main in mains],
         compiler_params=pltpu.CompilerParams(vmem_limit_bytes=16 * MIB),
+        cost_estimate=pl.CostEstimate(flops=4000000000, bytes_accessed=16000000, transcendentals=0),
         name="fold",
     )(low, low_received, mass, *mains)
+
+
+def add_far_kernel(own, received, out):
+    out[...] = own[...] + received[...].astype(jnp.float32)
+
+
+def add_far(own, received):
+    return pl.pallas_call(
+        add_far_kernel,
+        in_specs=whole_vmem(2),
+        out_specs=pl.BlockSpec(memory_space=pltpu.VMEM),
+        out_shape=jax.ShapeDtypeStruct(own.shape, jnp.float32),
+        compiler_params=pltpu.CompilerParams(vmem_limit_bytes=16 * MIB),
+        cost_estimate=pl.CostEstimate(flops=1000000000, bytes_accessed=4000000, transcendentals=0),
+        name="add_far",
+    )(own, received)
 
 
 def merge_kernel(own, own_low, mass, *refs):
@@ -581,7 +598,7 @@
     for target, place in ((to_core, 1 - core), (keep, core)):
         start = pl.multiple_of(place * half, half)
         total = own[pl.ds(start, half), :]
-        for ref in received:
+        for ref in received[:-1]:
             total = total + ref[pl.ds(head + start, half), :].astype(jnp.float32)
         where = pl.ds(pl.multiple_of(place * low_half, low_half), low_half)
         low = own_low[where, :]
@@ -669,10 +686,11 @@
     )
     low_from_half = exchange(low_send, 2)
     sums = backproject(weights, own_images, images_received, cos_table, sin_table, slots)
-    folded = fold(low, low_from_half, mass, sums[1:])
-    chip_sums = [exchange(send, 4 * m) for m, send in zip(others, folded[2:])]
-    chip_sums = chip_sums[:1] + chip_sums[:0:-1]
-    keep, send, mass = merge(sums[0], folded[0], folded[1], chip_sums)
+    far_sum = add_far(sums[0], exchange(sums[1], 4 * others[0]))
+    folded = fold(low, low_from_half, mass, sums[2:])
+    received = [exchange(send, 4 * m) for m, send in zip(others[1:], folded[3:])]
+    received.append(exchange(folded[2], 4 * others[0]))
+    keep, send, mass = merge(far_sum, folded[0], folded[1], received)
     back, class_mass = finish(
         keep, exchange(send, 1), mass, 1.0 / math.sqrt(parts), CLASSES / (parts * dev_count)
     )

time: 34.9 us -> 35.9 us (1.029)
  starting transfers between devices: 12.3 us -> 14.8 us
  waiting for transfers between devices: 11.1 us -> 9.3 us
    ppermute x10 -> x11, starting transfers between devices: 12.3 us -> 14.8 us  [exchange(): return lax.ppermute(value, 'particle', pairs)]
    ppermute x10 -> x11, waiting for transfers between devices: 11.1 us -> 9.3 us  [exchange(): return lax.ppermute(value, 'particle', pairs)]
  transfers between devices with their start and end apart: 10 -> 11, of which waited for: 8 -> 5; matrix products, arithmetic and copies ran while one was open for 0% -> 0% of each run, Pallas kernels for 14% -> 14%
where the time goes in v13:
time: 35.9 us; the launch traced here: 35.7 us
  starting transfers between devices  14.8 us (41%)
  Pallas kernels  10.8 us (30%)
  waiting for transfers between devices  9.3 us (26%)
  between operations  0.72 us (2%)
    ppermute x11, starting transfers between devices, exchange(): return lax.ppermute(value, 'particle', pairs)  14.8 us
    ppermute x11, waiting for transfers between devices, exchange(): return lax.ppermute(value, 'particle', pairs)  9.3 us
    pallas_call x1, Pallas kernels, project_other(): pl.pallas_call(project_other_kernel, in_specs=[pl.BlockSpec(memory_space=...  3.7 us
    pallas_call x1, Pallas kernels, project_own(): pl.pallas_call(project_own_kernel, in_specs=whole_vmem(3) + [pl.BlockSpec...  2.33 us
    pallas_call x2, Pallas kernels, correlate(): pl.pallas_call(functools.partial(kernel, chunk=2048), in_specs=whole_vmem...  2.28 us
    pallas_call x1, Pallas kernels, backproject(): pl.pallas_call(functools.partial(backproject_kernel, slots=slots, chunk=L...  1.32 us
  transfers between devices with their start and end apart: 11, of which 5 were waited for; matrix products, arithmetic and copies ran while one was open for 0% of the time, Pallas kernels for 14%

profile of v13, /device:TPU:0, one launch (start us, length us, event | category | flops | bytes accessed | tf_op | source)
XLA Modules:
  0.0 35.7 jit_solution(8661569315243724477)
XLA Ops:
  0.6 3.7 %project_other.1 = (bf16[32,16896]{1,0:T(8,128)(2,1)S(1)}, bf16[304,256]{1,0:T(8,128)(2,1)S(1)}, s32[1,16384]{1,0:T(1,128)S(1)}, f32[1,16384]{1,0:T(1,128)S(1)}) custom-call(bf16[2,8,2,32768]{3,2,1,0:T(2,128)(2,1)} %table_hbm.1, s32[1,16384]{1,0:T(1,128)} %index_hbm.1, f32[1,16384]{1,0:T(1,128)} %frac_hbm.1, bf16[32,32768]{1,0:T(8,128)(2,1)} %images_hbm.3), custom_call_target="tpu_custom_call" | custom-call | tf_op jit(solution)/shard_map/project_other/pallas_call | solution.py:169
  4.3 0.5 %collective-permute-start = (bf16[32,16896]{1,0:T(8,128)(2,1)S(1)}, bf16[32,16896]{1,0:T(8,128)(2,1)S(1)}, u32[]{:S(2)}, u32[]{:S(2)}) collective-permute-start(bf16[32,16896]{1,0:T(8,128)(2,1)S(1)} %get-tuple-element.33), channel_id=1, source_target_pairs={{0,1},{1,0},{2,3},{3,2},{4,5},{5,4},{6,7},{7,6},{8,9},{9,8},{10,11... | collective-permute-start | bytes 3244040 | tf_op jit(solution)/shard_map/ppermute | solution.py:26
  4.9 2.3 %project_own.1 = (bf16[128,128]{1,0:T(8,128)(2,1)S(1)}, bf16[32,16384]{1,0:T(8,128)(2,1)S(1)}) custom-call(bf16[304,256]{1,0:T(8,128)(2,1)S(1)} %get-tuple-element.29.table, s32[1,16384]{1,0:T(1,128)S(1)} %get-tuple-element.30.index_ref, f32[1,16384]{1,0:T(1,128)S(1)} %get-tuple-element.31.frac_ref, bf16[32,32768]{1,0:T(8,128)(2,1)} %images_hbm.3), custom_call_target="tpu_custom_call" | custom-call | flops 2000000000 | bytes 8000000 | tf_op jit(solution)/shard_map/project_own/pallas_call | solution.py:204
  7.2 0.0 collective-permute-done.other.other_images
  7.2 5.0 %collective-permute-start.1 = (bf16[256,128]{1,0:T(8,128)(2,1)S(1)}, bf16[256,128]{1,0:T(8,128)(2,1)S(1)}, u32[]{:S(2)}, u32[]{:S(2)}) collective-permute-start(bf16[256,128]{1,0:T(8,128)(2,1)S(1)} %pair_rows.1.refs_0_), channel_id=1, source_target_pairs={{0,12},{1,13},{2,14},{3,15},{4,8},{5,9},{6,10},{7,11},{8,4},{9,5},... | collective-permute-start | bytes 196616 | tf_op jit(solution)/shard_map/ppermute | solution.py:26
  12.2 0.1 copy.9.shift_ref
  12.3 0.6 %collective-permute-start.3 = (bf16[256,128]{1,0:T(8,128)(2,1)S(1)}, bf16[256,128]{1,0:T(8,128)(2,1)S(1)}, u32[]{:S(2)}, u32[]{:S(2)}) collective-permute-start(bf16[256,128]{1,0:T(8,128)(2,1)S(1)} %pair_rows.1.refs_0_), channel_id=1, source_target_pairs={{0,4},{1,5},{2,6},{3,7},{4,0},{5,1},{6,2},{7,3},{8,12},{9,13},{10,... | collective-permute-start | bytes 196616 | tf_op jit(solution)/shard_map/ppermute | solution.py:26
  12.9 1.9 %collective-permute-done.1.refs_1_ = bf16[256,128]{1,0:T(8,128)(2,1)S(1)} collective-permute-done((bf16[256,128]{1,0:T(8,128)(2,1)S(1)}, bf16[256,128]{1,0:T(8,128)(2,1)S(1)}, u32[]{:S(2)}, u32[]{:S(2)}) %collective-permute-start.1) | collective-permute-done | bytes 65568 | tf_op jit(solution)/shard_map/ppermute | solution.py:26
  14.8 1.3 %correlate.2 = (f32[36,128]{1,0:T(8,128)S(1)}, f32[8,8192]{1,0:T(8,128)S(1)}, f32[8,8192]{1,0:T(8,128)S(1)}) custom-call(s32[8,2]{1,0:T(8,128)S(1)} %copy.9.shift_ref, bf16[32,16384]{1,0:T(8,128)(2,1)S(1)} %get-tuple-element.32.own_images, bf16[32,16896]{1,0:T(8,128)(2,1)S(1)} %collective-permute-done.other.other_images, ...), custom_call_target="tpu_custom_call" | custom-call | flops 1000000000 | bytes 4000000 | tf_op jit(solution)/shard_map/correlate/pallas_call | solution.py:352
  16.1 2.0 %collective-permute-done.2.refs_0_ = bf16[256,128]{1,0:T(8,128)(2,1)S(1)} collective-permute-done((bf16[256,128]{1,0:T(8,128)(2,1)S(1)}, bf16[256,128]{1,0:T(8,128)(2,1)S(1)}, u32[]{:S(2)}, u32[]{:S(2)}) %collective-permute-start.2) | collective-permute-done | bytes 65568 | tf_op jit(solution)/shard_map/ppermute | solution.py:26
  18.1 1.0 %correlate.3.refs_1_ = f32[36,128]{1,0:T(8,128)S(1)} custom-call(f32[8,8192]{1,0:T(8,128)S(1)} %get-tuple-element.36.cos_ref, f32[8,8192]{1,0:T(8,128)S(1)} %get-tuple-element.37.sin_ref, bf16[32,16384]{1,0:T(8,128)(2,1)S(1)} %get-tuple-element.32.own_images, bf16[32,16896]{1,0:T(8,128)(2,1)S(1)} %collective-permute-done.other.other_images, ...), custom_call_target="tpu_custom_call" | custom-call | flops 1000000000 | bytes 4000000 | tf_op jit(solution)/shard_map/correlate/pallas_call | solution.py:352
  19.1 0.1 collective-permute-start.4
  19.2 1.2 %collective-permute-done.4.received = f32[80,128]{1,0:T(8,128)S(1)} collective-permute-done((f32[80,128]{1,0:T(8,128)S(1)}, f32[80,128]{1,0:T(8,128)S(1)}, u32[]{:S(2)}, u32[]{:S(2)}) %collective-permute-start.4) | collective-permute-done | bytes 40992 | tf_op jit(solution)/shard_map/ppermute | solution.py:26
  20.4 0.4 %posterior.1 = (bf16[64,64]{1,0:T(8,128)(2,1)S(1)}, f32[128,128]{1,0:T(8,128)S(1)}, bf16[144,128]{1,0:T(8,128)(2,1)S(1)}, f32[8,128]{1,0:T(8,128)S(1)}) custom-call(f32[80,128]{1,0:T(8,128)S(1)} %collect.1.mine, f32[80,128]{1,0:T(8,128)S(1)} %collective-permute-done.4.received, bf16[32,16384]{1,0:T(8,128)(2,1)S(1)} %get-tuple-element.32.own_images, ...), custom_call_target="tpu_custom_call" | custom-call | tf_op jit(solution)/shard_map/posterior/pallas_call | solution.py:469
  20.8 1.6 %collective-permute-start.6 = (bf16[144,128]{1,0:T(8,128)(2,1)S(1)}, bf16[144,128]{1,0:T(8,128)(2,1)S(1)}, u32[]{:S(2)}, u32[]{:S(2)}) collective-permute-start(bf16[144,128]{1,0:T(8,128)(2,1)S(1)} %get-tuple-element.42), channel_id=1, source_target_pairs={{0,2},{1,3},{2,0},{3,1},{4,6},{5,7},{6,4},{7,5},{8,10},{9,11},{10,... | collective-permute-start | bytes 110600 | tf_op jit(solution)/shard_map/ppermute | solution.py:26
  22.4 1.3 %backproject.1 = (f32[224,128]{1,0:T(8,128)S(1)}, bf16[224,128]{1,0:T(8,128)(2,1)S(1)}, bf16[224,128]{1,0:T(8,128)(2,1)S(1)}, bf16[224,128]{1,0:T(8,128)(2,1)S(1)}) custom-call(bf16[64,64]{1,0:T(8,128)(2,1)S(1)} %get-tuple-element.38.weight_ref, bf16[32,16384]{1,0:T(8,128)(2,1)S(1)} %get-tuple-element.32.own_images, ...), custom_call_target="tpu_custom_call" | custom-call | flops 2000000000 | bytes 8000000 | tf_op jit(solution)/shard_map/backproject/pallas_call | solution.py:519
  23.7 2.5 %collective-permute-start.5 = (bf16[224,128]{1,0:T(8,128)(2,1)S(1)}, bf16[224,128]{1,0:T(8,128)(2,1)S(1)}, u32[]{:S(2)}, u32[]{:S(2)}) collective-permute-start(bf16[224,128]{1,0:T(8,128)(2,1)S(1)} %get-tuple-element.40), channel_id=1, source_target_pairs={{0,12},{1,13},{2,14},{3,15},{4,8},{5,9},{6,10},{7,11},{8,4},{9,5},... | collective-permute-start | bytes 172040 | tf_op jit(solution)/shard_map/ppermute | solution.py:26
  26.3 0.2 collective-permute-start.7
  26.4 1.8 %collective-permute-start.8 = (bf16[272,128]{1,0:T(8,128)(2,1)S(1)}, bf16[272,128]{1,0:T(8,128)(2,1)S(1)}, u32[]{:S(2)}, u32[]{:S(2)}) collective-permute-start(bf16[272,128]{1,0:T(8,128)(2,1)S(1)} %get-tuple-element.49), channel_id=1, source_target_pairs={{0,4},{1,5},{2,6},{3,7},{4,0},{5,1},{6,2},{7,3},{8,12},{9,13},{10,... | collective-permute-start | bytes 208904 | tf_op jit(solution)/shard_map/ppermute | solution.py:26
  28.2 2.5 %collective-permute-start.9 = (bf16[48,128]{1,0:T(8,128)(2,1)S(1)}, bf16[48,128]{1,0:T(8,128)(2,1)S(1)}, u32[]{:S(2)}, u32[]{:S(2)}) collective-permute-start(bf16[48,128]{1,0:T(8,128)(2,1)S(1)} %get-tuple-element.50), channel_id=1, source_target_pairs={{0,12},{1,13},{2,14},{3,15},{4,8},{5,9},{6,10},{7,11},{8,4},{9,5},... | collective-permute-start | bytes 36872 | tf_op jit(solution)/shard_map/ppermute | solution.py:26
  30.7 3.0 %collective-permute-done.9.refs_2_ = bf16[48,128]{1,0:T(8,128)(2,1)S(1)} collective-permute-done((bf16[48,128]{1,0:T(8,128)(2,1)S(1)}, bf16[48,128]{1,0:T(8,128)(2,1)S(1)}, u32[]{:S(2)}, u32[]{:S(2)}) %collective-permute-start.9) | collective-permute-done | bytes 12320 | tf_op jit(solution)/shard_map/ppermute | solution.py:26
  33.8 0.1 collective-permute-start.10
  33.8 1.2 %collective-permute-done.10.received = bf16[128,128]{1,0:T(8,128)(2,1)S(1)} collective-permute-done((bf16[128,128]{1,0:T(8,128)(2,1)S(1)}, bf16[128,128]{1,0:T(8,128)(2,1)S(1)}, u32[]{:S(2)}, u32[]{:S(2)}) %collective-permute-start.10) | collective-permute-done | bytes 32800 | tf_op jit(solution)/shard_map/ppermute | solution.py:26
  35.0 0.7 %finish.1 = (f32[256,128]{1,0:T(8,128)}, f32[8]{0:T(128)}) custom-call(f32[128,128]{1,0:T(8,128)S(1)} %get-tuple-element.51.own, bf16[128,128]{1,0:T(8,128)(2,1)S(1)} %collective-permute-done.10.received, f32[8,128]{1,0:T(8,128)S(1)} %get-tuple-element.53.mass), custom_call_target="tpu_custom_call" | custom-call | tf_op jit(solution)/shard_map/finish/pallas_call | solution.py:640
  (17 shorter events, 0.1 us)
Async XLA Ops:
  4.3 2.9 %collective-permute-start = (bf16[32,16896]{1,0:T(8,128)(2,1)S(1)}, bf16[32,16896]{1,0:T(8,128)(2,1)S(1)}, u32[]{:S(2)}, u32[]{:S(2)}) collective-permute-start(bf16[32,16896]{1,0:T(8,128)(2,1)S(1)} %get-tuple-element.33), channel_id=1, source_target_pairs={{0,1},{1,0},{2,3},{3,2},{4,5},{5,4},{6,7},{7,6},{8,9},{9,8},{10,11... | collective-permute-start | bytes 3244040 | tf_op jit(solution)/shard_map/ppermute | solution.py:26
  4.8 7.4 %copy-start.2 = (s32[8,2]{0,1:T(2,128)S(1)}, s32[8,2]{0,1:T(2,128)}, u32[]{:S(2)}) copy-start(s32[8,2]{0,1:T(2,128)} %param.13) | copy-start | bytes 196
  7.2 7.6 %collective-permute-start.1 = (bf16[256,128]{1,0:T(8,128)(2,1)S(1)}, bf16[256,128]{1,0:T(8,128)(2,1)S(1)}, u32[]{:S(2)}, u32[]{:S(2)}) collective-permute-start(bf16[256,128]{1,0:T(8,128)(2,1)S(1)} %pair_rows.1.refs_0_), channel_id=1, source_target_pairs={{0,12},{1,13},{2,14},{3,15},{4,8},{5,9},{6,10},{7,11},{8,4},{9,5},... | collective-permute-start | bytes 196616 | tf_op jit(solution)/shard_map/ppermute | solution.py:26
  12.3 5.8 %collective-permute-start.2 = (bf16[256,128]{1,0:T(8,128)(2,1)S(1)}, bf16[256,128]{1,0:T(8,128)(2,1)S(1)}, u32[]{:S(2)}, u32[]{:S(2)}) collective-permute-start(bf16[256,128]{1,0:T(8,128)(2,1)S(1)} %pair_rows.1.refs_0_), channel_id=1, source_target_pairs={{0,8},{1,9},{2,10},{3,11},{4,12},{5,13},{6,14},{7,15},{8,0},{9,1},... | collective-permute-start | bytes 196616 | tf_op jit(solution)/shard_map/ppermute | solution.py:26
  12.3 5.8 %collective-permute-start.3 = (bf16[256,128]{1,0:T(8,128)(2,1)S(1)}, bf16[256,128]{1,0:T(8,128)(2,1)S(1)}, u32[]{:S(2)}, u32[]{:S(2)}) collective-permute-start(bf16[256,128]{1,0:T(8,128)(2,1)S(1)} %pair_rows.1.refs_0_), channel_id=1, source_target_pairs={{0,4},{1,5},{2,6},{3,7},{4,0},{5,1},{6,2},{7,3},{8,12},{9,13},{10,... | collective-permute-start | bytes 196616 | tf_op jit(solution)/shard_map/ppermute | solution.py:26
  16.1 3.0 %copy-start = (f32[32]{0:T(128)S(1)}, f32[32]{0:T(128)}, u32[]{:S(2)}) copy-start(f32[32]{0:T(128)} %param.8) | copy-start | bytes 388
  16.1 3.0 %copy-start.1 = (s32[32]{0:T(128)S(1)}, s32[32]{0:T(128)}, u32[]{:S(2)}) copy-start(s32[32]{0:T(128)} %param.9) | copy-start | bytes 388
  19.1 1.3 %collective-permute-start.4 = (f32[80,128]{1,0:T(8,128)S(1)}, f32[80,128]{1,0:T(8,128)S(1)}, u32[]{:S(2)}, u32[]{:S(2)}) collective-permute-start(f32[80,128]{1,0:T(8,128)S(1)} %collect.1.mine), channel_id=1, source_target_pairs={{0,1},{1,0},{2,3},{3,2},{4,5},{5,4},{6,7},{7,6},{8,9},{9,8},{10,11... | collective-permute-start | bytes 122888 | tf_op jit(solution)/shard_map/ppermute | solution.py:26
  20.8 5.4 %collective-permute-start.6 = (bf16[144,128]{1,0:T(8,128)(2,1)S(1)}, bf16[144,128]{1,0:T(8,128)(2,1)S(1)}, u32[]{:S(2)}, u32[]{:S(2)}) collective-permute-start(bf16[144,128]{1,0:T(8,128)(2,1)S(1)} %get-tuple-element.42), channel_id=1, source_target_pairs={{0,2},{1,3},{2,0},{3,1},{4,6},{5,7},{6,4},{7,5},{8,10},{9,11},{10,... | collective-permute-start | bytes 110600 | tf_op jit(solution)/shard_map/ppermute | solution.py:26
  23.7 7.0 %collective-permute-start.5 = (bf16[224,128]{1,0:T(8,128)(2,1)S(1)}, bf16[224,128]{1,0:T(8,128)(2,1)S(1)}, u32[]{:S(2)}, u32[]{:S(2)}) collective-permute-start(bf16[224,128]{1,0:T(8,128)(2,1)S(1)} %get-tuple-element.40), channel_id=1, source_target_pairs={{0,12},{1,13},{2,14},{3,15},{4,8},{5,9},{6,10},{7,11},{8,4},{9,5},... | collective-permute-start | bytes 172040 | tf_op jit(solution)/shard_map/ppermute | solution.py:26
  26.3 7.5 %collective-permute-start.7 = (bf16[272,128]{1,0:T(8,128)(2,1)S(1)}, bf16[272,128]{1,0:T(8,128)(2,1)S(1)}, u32[]{:S(2)}, u32[]{:S(2)}) collective-permute-start(bf16[272,128]{1,0:T(8,128)(2,1)S(1)} %get-tuple-element.48), channel_id=1, source_target_pairs={{0,8},{1,9},{2,10},{3,11},{4,12},{5,13},{6,14},{7,15},{8,0},{9,1},... | collective-permute-start | bytes 208904 | tf_op jit(solution)/shard_map/ppermute | solution.py:26
  26.4 7.3 %collective-permute-start.8 = (bf16[272,128]{1,0:T(8,128)(2,1)S(1)}, bf16[272,128]{1,0:T(8,128)(2,1)S(1)}, u32[]{:S(2)}, u32[]{:S(2)}) collective-permute-start(bf16[272,128]{1,0:T(8,128)(2,1)S(1)} %get-tuple-element.49), channel_id=1, source_target_pairs={{0,4},{1,5},{2,6},{3,7},{4,0},{5,1},{6,2},{7,3},{8,12},{9,13},{10,... | collective-permute-start | bytes 208904 | tf_op jit(solution)/shard_map/ppermute | solution.py:26
  28.2 5.5 %collective-permute-start.9 = (bf16[48,128]{1,0:T(8,128)(2,1)S(1)}, bf16[48,128]{1,0:T(8,128)(2,1)S(1)}, u32[]{:S(2)}, u32[]{:S(2)}) collective-permute-start(bf16[48,128]{1,0:T(8,128)(2,1)S(1)} %get-tuple-element.50), channel_id=1, source_target_pairs={{0,12},{1,13},{2,14},{3,15},{4,8},{5,9},{6,10},{7,11},{8,4},{9,5},... | collective-permute-start | bytes 36872 | tf_op jit(solution)/shard_map/ppermute | solution.py:26
  33.8 1.3 %collective-permute-start.10 = (bf16[128,128]{1,0:T(8,128)(2,1)S(1)}, bf16[128,128]{1,0:T(8,128)(2,1)S(1)}, u32[]{:S(2)}, u32[]{:S(2)}) collective-permute-start(bf16[128,128]{1,0:T(8,128)(2,1)S(1)} %get-tuple-element.52), channel_id=1, source_target_pairs={{0,1},{1,0},{2,3},{3,2},{4,5},{5,4},{6,7},{7,6},{8,9},{9,8},{10,11... | collective-permute-start | bytes 98312 | tf_op jit(solution)/shard_map/ppermute | solution.py:26

commit v14 on v12

--- a/solution.py
+++ b/solution.py
@@ -135,7 +135,7 @@
                 flat[comp, pl.ds(step * 8 + k, 1), :] = piece[comp : comp + 1, k * LANES : (k + 1) * LANES]
         return carry
 
-    lax.fori_loop(0, highs // 8, unfold, 0, unroll=4)
+    lax.fori_loop(0, highs // 8, unfold, 0, unroll=16)
     picked = []
     for comp in range(2):
         turned = flat[comp].T
@@ -243,7 +243,7 @@
 
 
 def chip_order(chips):
-    return [0] + list(range(chips - 1, 0, -1))
+    return [0, chips - 1] + list(range(1, chips - 1))
 
 
 def slot_orientation(device, slot, slots):
@@ -263,8 +263,17 @@
 
 def fill_tables(shift_ref, cos_ref, sin_ref):
     shifts, width = cos_ref.shape
-    grid_x = shift_ref[:, 0:1]
-    grid_y = shift_ref[:, 1:2]
+    same = lax.broadcasted_iota(jnp.int32, (shifts, shifts), 0) == lax.broadcasted_iota(
+        jnp.int32, (shifts, shifts), 1
+    )
+    grid_x, grid_y = (
+        jnp.sum(
+            jnp.where(same, shift_ref[axis : axis + 1, :].astype(jnp.float32), 0.0),
+            axis=1,
+            keepdims=True,
+        ).astype(jnp.int32)
+        for axis in range(2)
+    )
     lane = lax.broadcasted_iota(jnp.int32, (shifts, LANES), 1)
     freq_x = (lane // BLOCK) * (2 * BLOCK) + own_half() * BLOCK + lane % BLOCK
     turn_x = (freq_x * grid_x) & (BOX - 1)
@@ -344,13 +353,13 @@
     slots = 2 * len(pairs)
     width = own_images.shape[1] // 2
     shifts = shift_grid.shape[0] if tables is None else tables[0].shape[0]
-    first = (shift_grid,) if tables is None else tuple(tables)
+    first = (shift_grid.T,) if tables is None else tuple(tables)
     table = jax.ShapeDtypeStruct((shifts, width), jnp.float32)
     outs = [jax.ShapeDtypeStruct((shifts * slots + slots, LANES), jnp.float32)]
     outs += [table, table] if tables is None else []
     kernel = correlate_first_kernel if tables is None else correlate_kernel
     return pl.pallas_call(
-        functools.partial(kernel, chunk=2048),
+        functools.partial(kernel, chunk=4096),
         in_specs=whole_vmem(len(first) + 2 + len(pairs)),
         out_specs=whole_vmem(len(outs)),
         out_shape=outs,
@@ -671,7 +680,6 @@
     sums = backproject(weights, own_images, images_received, cos_table, sin_table, slots)
     folded = fold(low, low_from_half, mass, sums[1:])
     chip_sums = [exchange(send, 4 * m) for m, send in zip(others, folded[2:])]
-    chip_sums = chip_sums[:1] + chip_sums[:0:-1]
     keep, send, mass = merge(sums[0], folded[0], folded[1], chip_sums)
     back, class_mass = finish(
         keep, exchange(send, 1), mass, 1.0 / math.sqrt(parts), CLASSES / (parts * dev_count)

time: 34.9 us -> 34.7 us (level)
  Pallas kernels: 10.6 us -> 10.1 us
    pallas_call x2, Pallas kernels: 2.05 us -> 1.56 us  [correlate(): pl.pallas_call(functools.partial(kernel, chunk=4096), in_specs=whole_vmem...]
  transfers between devices with their start and end apart: 10 -> 10, of which waited for: 8 -> 8; matrix products, arithmetic and copies ran while one was open for 0% -> 0% of each run, Pallas kernels for 14% -> 13%
where the time goes in v14:
time: 34.7 us; the launch traced here: 34.5 us
  starting transfers between devices  12.3 us (35%)
  waiting for transfers between devices  11.4 us (33%)
  Pallas kernels  10.1 us (29%)
  between operations  0.75 us (2%)
    ppermute x10, starting transfers between devices, exchange(): return lax.ppermute(value, 'particle', pairs)  12.3 us
    ppermute x10, waiting for transfers between devices, exchange(): return lax.ppermute(value, 'particle', pairs)  11.4 us
    pallas_call x1, Pallas kernels, project_other(): pl.pallas_call(project_other_kernel, in_specs=[pl.BlockSpec(memory_space=...  3.67 us
    pallas_call x1, Pallas kernels, project_own(): pl.pallas_call(project_own_kernel, in_specs=whole_vmem(3) + [pl.BlockSpec...  2.33 us
    pallas_call x2, Pallas kernels, correlate(): pl.pallas_call(functools.partial(kernel, chunk=4096), in_specs=whole_vmem...  1.56 us
    pallas_call x1, Pallas kernels, backproject(): pl.pallas_call(functools.partial(backproject_kernel, slots=slots, chunk=L...  1.34 us
  transfers between devices with their start and end apart: 10, of which 8 were waited for; matrix products, arithmetic and copies ran while one was open for 0% of the time, Pallas kernels for 13%

profile of v14, /device:TPU:0, one launch (start us, length us, event | category | flops | bytes accessed | tf_op | source)
XLA Modules:
  0.0 34.5 jit_solution(14954539009071119677)
XLA Ops:
  0.6 3.7 %project_other.1 = (bf16[32,16896]{1,0:T(8,128)(2,1)S(1)}, bf16[304,256]{1,0:T(8,128)(2,1)S(1)}, s32[1,16384]{1,0:T(1,128)S(1)}, f32[1,16384]{1,0:T(1,128)S(1)}) custom-call(bf16[2,8,2,32768]{3,2,1,0:T(2,128)(2,1)} %table_hbm.1, s32[1,16384]{1,0:T(1,128)} %index_hbm.1, f32[1,16384]{1,0:T(1,128)} %frac_hbm.1, bf16[32,32768]{1,0:T(8,128)(2,1)} %images_hbm.3), custom_call_target="tpu_custom_call" | custom-call | tf_op jit(solution)/shard_map/project_other/pallas_call | solution.py:169
  4.3 0.5 %collective-permute-start = (bf16[32,16896]{1,0:T(8,128)(2,1)S(1)}, bf16[32,16896]{1,0:T(8,128)(2,1)S(1)}, u32[]{:S(2)}, u32[]{:S(2)}) collective-permute-start(bf16[32,16896]{1,0:T(8,128)(2,1)S(1)} %get-tuple-element.33), channel_id=1, source_target_pairs={{0,1},{1,0},{2,3},{3,2},{4,5},{5,4},{6,7},{7,6},{8,9},{9,8},{10,11... | collective-permute-start | bytes 3244040 | tf_op jit(solution)/shard_map/ppermute | solution.py:26
  4.8 2.3 %project_own.1 = (bf16[128,128]{1,0:T(8,128)(2,1)S(1)}, bf16[32,16384]{1,0:T(8,128)(2,1)S(1)}) custom-call(bf16[304,256]{1,0:T(8,128)(2,1)S(1)} %get-tuple-element.29.table, s32[1,16384]{1,0:T(1,128)S(1)} %get-tuple-element.30.index_ref, f32[1,16384]{1,0:T(1,128)S(1)} %get-tuple-element.31.frac_ref, bf16[32,32768]{1,0:T(8,128)(2,1)} %images_hbm.3), custom_call_target="tpu_custom_call" | custom-call | flops 2000000000 | bytes 8000000 | tf_op jit(solution)/shard_map/project_own/pallas_call | solution.py:204
  7.2 5.0 %collective-permute-start.1 = (bf16[256,128]{1,0:T(8,128)(2,1)S(1)}, bf16[256,128]{1,0:T(8,128)(2,1)S(1)}, u32[]{:S(2)}, u32[]{:S(2)}) collective-permute-start(bf16[256,128]{1,0:T(8,128)(2,1)S(1)} %pair_rows.1.refs_0_), channel_id=1, source_target_pairs={{0,12},{1,13},{2,14},{3,15},{4,8},{5,9},{6,10},{7,11},{8,4},{9,5},... | collective-permute-start | bytes 196616 | tf_op jit(solution)/shard_map/ppermute | solution.py:26
  12.2 0.6 %collective-permute-start.2 = (bf16[256,128]{1,0:T(8,128)(2,1)S(1)}, bf16[256,128]{1,0:T(8,128)(2,1)S(1)}, u32[]{:S(2)}, u32[]{:S(2)}) collective-permute-start(bf16[256,128]{1,0:T(8,128)(2,1)S(1)} %pair_rows.1.refs_0_), channel_id=1, source_target_pairs={{0,4},{1,5},{2,6},{3,7},{4,0},{5,1},{6,2},{7,3},{8,12},{9,13},{10,... | collective-permute-start | bytes 196616 | tf_op jit(solution)/shard_map/ppermute | solution.py:26
  12.9 2.0 %collective-permute-done.1.refs_1_ = bf16[256,128]{1,0:T(8,128)(2,1)S(1)} collective-permute-done((bf16[256,128]{1,0:T(8,128)(2,1)S(1)}, bf16[256,128]{1,0:T(8,128)(2,1)S(1)}, u32[]{:S(2)}, u32[]{:S(2)}) %collective-permute-start.1) | collective-permute-done | bytes 65568 | tf_op jit(solution)/shard_map/ppermute | solution.py:26
  14.9 0.9 %correlate.2 = (f32[36,128]{1,0:T(8,128)S(1)}, f32[8,8192]{1,0:T(8,128)S(1)}, f32[8,8192]{1,0:T(8,128)S(1)}) custom-call(s32[2,8]{1,0:T(2,128)S(1)} %bitcast.6, bf16[32,16384]{1,0:T(8,128)(2,1)S(1)} %get-tuple-element.32.own_images, bf16[32,16896]{1,0:T(8,128)(2,1)S(1)} %collective-permute-done.other.other_images, bf16[256,128]{1,0:T(8,128)(2,1)S(1)} %pair_rows.1.refs_0_, ...), custom_call_target="tpu_custom_call" | custom-call | flops 1000000000 | bytes 4000000 | tf_op jit(solution)/shard_map/correlate/pallas_call | solution.py:361
  15.8 2.3 %collective-permute-done.3.refs_1_ = bf16[256,128]{1,0:T(8,128)(2,1)S(1)} collective-permute-done((bf16[256,128]{1,0:T(8,128)(2,1)S(1)}, bf16[256,128]{1,0:T(8,128)(2,1)S(1)}, u32[]{:S(2)}, u32[]{:S(2)}) %collective-permute-start.3) | collective-permute-done | bytes 65568 | tf_op jit(solution)/shard_map/ppermute | solution.py:26
  18.1 0.7 %correlate.3.refs_1_ = f32[36,128]{1,0:T(8,128)S(1)} custom-call(f32[8,8192]{1,0:T(8,128)S(1)} %get-tuple-element.36.cos_ref, f32[8,8192]{1,0:T(8,128)S(1)} %get-tuple-element.37.sin_ref, bf16[32,16384]{1,0:T(8,128)(2,1)S(1)} %get-tuple-element.32.own_images, bf16[32,16896]{1,0:T(8,128)(2,1)S(1)} %collective-permute-done.other.other_images, ...), custom_call_target="tpu_custom_call" | custom-call | flops 1000000000 | bytes 4000000 | tf_op jit(solution)/shard_map/correlate/pallas_call | solution.py:361
  18.8 0.0 copy-done
  18.8 0.1 collective-permute-start.4
  18.9 1.2 %collective-permute-done.4.received = f32[80,128]{1,0:T(8,128)S(1)} collective-permute-done((f32[80,128]{1,0:T(8,128)S(1)}, f32[80,128]{1,0:T(8,128)S(1)}, u32[]{:S(2)}, u32[]{:S(2)}) %collective-permute-start.4) | collective-permute-done | bytes 40992 | tf_op jit(solution)/shard_map/ppermute | solution.py:26
  20.1 0.4 %posterior.1 = (bf16[64,64]{1,0:T(8,128)(2,1)S(1)}, f32[128,128]{1,0:T(8,128)S(1)}, bf16[144,128]{1,0:T(8,128)(2,1)S(1)}, f32[8,128]{1,0:T(8,128)S(1)}) custom-call(f32[80,128]{1,0:T(8,128)S(1)} %collect.1.mine, f32[80,128]{1,0:T(8,128)S(1)} %collective-permute-done.4.received, bf16[32,16384]{1,0:T(8,128)(2,1)S(1)} %get-tuple-element.32.own_images, ...), custom_call_target="tpu_custom_call" | custom-call | tf_op jit(solution)/shard_map/posterior/pallas_call | solution.py:478
  20.5 1.6 %collective-permute-start.5 = (bf16[144,128]{1,0:T(8,128)(2,1)S(1)}, bf16[144,128]{1,0:T(8,128)(2,1)S(1)}, u32[]{:S(2)}, u32[]{:S(2)}) collective-permute-start(bf16[144,128]{1,0:T(8,128)(2,1)S(1)} %get-tuple-element.41), channel_id=1, source_target_pairs={{0,2},{1,3},{2,0},{3,1},{4,6},{5,7},{6,4},{7,5},{8,10},{9,11},{10,... | collective-permute-start | bytes 110600 | tf_op jit(solution)/shard_map/ppermute | solution.py:26
  22.1 1.3 %backproject.1 = (f32[224,128]{1,0:T(8,128)S(1)}, bf16[224,128]{1,0:T(8,128)(2,1)S(1)}, bf16[224,128]{1,0:T(8,128)(2,1)S(1)}, bf16[224,128]{1,0:T(8,128)(2,1)S(1)}) custom-call(bf16[64,64]{1,0:T(8,128)(2,1)S(1)} %get-tuple-element.38.weight_ref, bf16[32,16384]{1,0:T(8,128)(2,1)S(1)} %get-tuple-element.32.own_images, ...), custom_call_target="tpu_custom_call" | custom-call | flops 2000000000 | bytes 8000000 | tf_op jit(solution)/shard_map/backproject/pallas_call | solution.py:528
  23.4 1.1 %collective-permute-done.5.low_received = bf16[144,128]{1,0:T(8,128)(2,1)S(1)} collective-permute-done((bf16[144,128]{1,0:T(8,128)(2,1)S(1)}, bf16[144,128]{1,0:T(8,128)(2,1)S(1)}, u32[]{:S(2)}, u32[]{:S(2)}) %collective-permute-start.5) | collective-permute-done | bytes 36896 | tf_op jit(solution)/shard_map/ppermute | solution.py:26
  24.5 2.5 %collective-permute-start.6 = (bf16[272,128]{1,0:T(8,128)(2,1)S(1)}, bf16[272,128]{1,0:T(8,128)(2,1)S(1)}, u32[]{:S(2)}, u32[]{:S(2)}) collective-permute-start(bf16[272,128]{1,0:T(8,128)(2,1)S(1)} %get-tuple-element.48), channel_id=1, source_target_pairs={{0,12},{1,13},{2,14},{3,15},{4,8},{5,9},{6,10},{7,11},{8,4},{9,5},... | collective-permute-start | bytes 208904 | tf_op jit(solution)/shard_map/ppermute | solution.py:26
  27.1 1.9 %collective-permute-start.8 = (bf16[272,128]{1,0:T(8,128)(2,1)S(1)}, bf16[272,128]{1,0:T(8,128)(2,1)S(1)}, u32[]{:S(2)}, u32[]{:S(2)}) collective-permute-start(bf16[272,128]{1,0:T(8,128)(2,1)S(1)} %get-tuple-element.50), channel_id=1, source_target_pairs={{0,8},{1,9},{2,10},{3,11},{4,12},{5,13},{6,14},{7,15},{8,0},{9,1},... | collective-permute-start | bytes 208904 | tf_op jit(solution)/shard_map/ppermute | solution.py:26
  29.0 2.1 %collective-permute-done.6.refs_0_ = bf16[272,128]{1,0:T(8,128)(2,1)S(1)} collective-permute-done((bf16[272,128]{1,0:T(8,128)(2,1)S(1)}, bf16[272,128]{1,0:T(8,128)(2,1)S(1)}, u32[]{:S(2)}, u32[]{:S(2)}) %collective-permute-start.6) | collective-permute-done | bytes 69664 | tf_op jit(solution)/shard_map/ppermute | solution.py:26
  31.1 1.1 %collective-permute-done.7.refs_1_ = bf16[272,128]{1,0:T(8,128)(2,1)S(1)} collective-permute-done((bf16[272,128]{1,0:T(8,128)(2,1)S(1)}, bf16[272,128]{1,0:T(8,128)(2,1)S(1)}, u32[]{:S(2)}, u32[]{:S(2)}) %collective-permute-start.7) | collective-permute-done | bytes 69664 | tf_op jit(solution)/shard_map/ppermute | solution.py:26
  32.2 0.3 collective-permute-done.8.refs_2_
  32.6 0.1 collective-permute-start.9
  32.7 1.2 %collective-permute-done.9.received = bf16[128,128]{1,0:T(8,128)(2,1)S(1)} collective-permute-done((bf16[128,128]{1,0:T(8,128)(2,1)S(1)}, bf16[128,128]{1,0:T(8,128)(2,1)S(1)}, u32[]{:S(2)}, u32[]{:S(2)}) %collective-permute-start.9) | collective-permute-done | bytes 32800 | tf_op jit(solution)/shard_map/ppermute | solution.py:26
  33.9 0.7 %finish.1 = (f32[256,128]{1,0:T(8,128)}, f32[8]{0:T(128)}) custom-call(f32[128,128]{1,0:T(8,128)S(1)} %get-tuple-element.51.own, bf16[128,128]{1,0:T(8,128)(2,1)S(1)} %collective-permute-done.9.received, f32[8,128]{1,0:T(8,128)S(1)} %get-tuple-element.53.mass), custom_call_target="tpu_custom_call" | custom-call | tf_op jit(solution)/shard_map/finish/pallas_call | solution.py:632
  (13 shorter events, 0.1 us)
Async XLA Ops:
  4.3 2.9 %collective-permute-start = (bf16[32,16896]{1,0:T(8,128)(2,1)S(1)}, bf16[32,16896]{1,0:T(8,128)(2,1)S(1)}, u32[]{:S(2)}, u32[]{:S(2)}) collective-permute-start(bf16[32,16896]{1,0:T(8,128)(2,1)S(1)} %get-tuple-element.33), channel_id=1, source_target_pairs={{0,1},{1,0},{2,3},{3,2},{4,5},{5,4},{6,7},{7,6},{8,9},{9,8},{10,11... | collective-permute-start | bytes 3244040 | tf_op jit(solution)/shard_map/ppermute | solution.py:26
  4.8 10.0 %copy-start.2 = (s32[8,2]{0,1:T(2,128)S(1)}, s32[8,2]{0,1:T(2,128)}, u32[]{:S(2)}) copy-start(s32[8,2]{0,1:T(2,128)} %param.13) | copy-start | bytes 196
  7.2 7.7 %collective-permute-start.1 = (bf16[256,128]{1,0:T(8,128)(2,1)S(1)}, bf16[256,128]{1,0:T(8,128)(2,1)S(1)}, u32[]{:S(2)}, u32[]{:S(2)}) collective-permute-start(bf16[256,128]{1,0:T(8,128)(2,1)S(1)} %pair_rows.1.refs_0_), channel_id=1, source_target_pairs={{0,12},{1,13},{2,14},{3,15},{4,8},{5,9},{6,10},{7,11},{8,4},{9,5},... | collective-permute-start | bytes 196616 | tf_op jit(solution)/shard_map/ppermute | solution.py:26
  12.2 5.9 %collective-permute-start.3 = (bf16[256,128]{1,0:T(8,128)(2,1)S(1)}, bf16[256,128]{1,0:T(8,128)(2,1)S(1)}, u32[]{:S(2)}, u32[]{:S(2)}) collective-permute-start(bf16[256,128]{1,0:T(8,128)(2,1)S(1)} %pair_rows.1.refs_0_), channel_id=1, source_target_pairs={{0,8},{1,9},{2,10},{3,11},{4,12},{5,13},{6,14},{7,15},{8,0},{9,1},... | collective-permute-start | bytes 196616 | tf_op jit(solution)/shard_map/ppermute | solution.py:26
  12.2 5.9 %collective-permute-start.2 = (bf16[256,128]{1,0:T(8,128)(2,1)S(1)}, bf16[256,128]{1,0:T(8,128)(2,1)S(1)}, u32[]{:S(2)}, u32[]{:S(2)}) collective-permute-start(bf16[256,128]{1,0:T(8,128)(2,1)S(1)} %pair_rows.1.refs_0_), channel_id=1, source_target_pairs={{0,4},{1,5},{2,6},{3,7},{4,0},{5,1},{6,2},{7,3},{8,12},{9,13},{10,... | collective-permute-start | bytes 196616 | tf_op jit(solution)/shard_map/ppermute | solution.py:26
  15.7 3.0 %copy-start = (f32[32]{0:T(128)S(1)}, f32[32]{0:T(128)}, u32[]{:S(2)}) copy-start(f32[32]{0:T(128)} %param.8) | copy-start | bytes 388
  15.8 3.0 %copy-start.1 = (s32[32]{0:T(128)S(1)}, s32[32]{0:T(128)}, u32[]{:S(2)}) copy-start(s32[32]{0:T(128)} %param.9) | copy-start | bytes 388
  18.8 1.3 %collective-permute-start.4 = (f32[80,128]{1,0:T(8,128)S(1)}, f32[80,128]{1,0:T(8,128)S(1)}, u32[]{:S(2)}, u32[]{:S(2)}) collective-permute-start(f32[80,128]{1,0:T(8,128)S(1)} %collect.1.mine), channel_id=1, source_target_pairs={{0,1},{1,0},{2,3},{3,2},{4,5},{5,4},{6,7},{7,6},{8,9},{9,8},{10,11... | collective-permute-start | bytes 122888 | tf_op jit(solution)/shard_map/ppermute | solution.py:26
  20.5 4.0 %collective-permute-start.5 = (bf16[144,128]{1,0:T(8,128)(2,1)S(1)}, bf16[144,128]{1,0:T(8,128)(2,1)S(1)}, u32[]{:S(2)}, u32[]{:S(2)}) collective-permute-start(bf16[144,128]{1,0:T(8,128)(2,1)S(1)} %get-tuple-element.41), channel_id=1, source_target_pairs={{0,2},{1,3},{2,0},{3,1},{4,6},{5,7},{6,4},{7,5},{8,10},{9,11},{10,... | collective-permute-start | bytes 110600 | tf_op jit(solution)/shard_map/ppermute | solution.py:26
  24.5 6.6 %collective-permute-start.6 = (bf16[272,128]{1,0:T(8,128)(2,1)S(1)}, bf16[272,128]{1,0:T(8,128)(2,1)S(1)}, u32[]{:S(2)}, u32[]{:S(2)}) collective-permute-start(bf16[272,128]{1,0:T(8,128)(2,1)S(1)} %get-tuple-element.48), channel_id=1, source_target_pairs={{0,12},{1,13},{2,14},{3,15},{4,8},{5,9},{6,10},{7,11},{8,4},{9,5},... | collective-permute-start | bytes 208904 | tf_op jit(solution)/shard_map/ppermute | solution.py:26
  27.1 5.2 %collective-permute-start.7 = (bf16[272,128]{1,0:T(8,128)(2,1)S(1)}, bf16[272,128]{1,0:T(8,128)(2,1)S(1)}, u32[]{:S(2)}, u32[]{:S(2)}) collective-permute-start(bf16[272,128]{1,0:T(8,128)(2,1)S(1)} %get-tuple-element.49), channel_id=1, source_target_pairs={{0,4},{1,5},{2,6},{3,7},{4,0},{5,1},{6,2},{7,3},{8,12},{9,13},{10,... | collective-permute-start | bytes 208904 | tf_op jit(solution)/shard_map/ppermute | solution.py:26
  27.1 5.4 %collective-permute-start.8 = (bf16[272,128]{1,0:T(8,128)(2,1)S(1)}, bf16[272,128]{1,0:T(8,128)(2,1)S(1)}, u32[]{:S(2)}, u32[]{:S(2)}) collective-permute-start(bf16[272,128]{1,0:T(8,128)(2,1)S(1)} %get-tuple-element.50), channel_id=1, source_target_pairs={{0,8},{1,9},{2,10},{3,11},{4,12},{5,13},{6,14},{7,15},{8,0},{9,1},... | collective-permute-start | bytes 208904 | tf_op jit(solution)/shard_map/ppermute | solution.py:26
  32.6 1.3 %collective-permute-start.9 = (bf16[128,128]{1,0:T(8,128)(2,1)S(1)}, bf16[128,128]{1,0:T(8,128)(2,1)S(1)}, u32[]{:S(2)}, u32[]{:S(2)}) collective-permute-start(bf16[128,128]{1,0:T(8,128)(2,1)S(1)} %get-tuple-element.52), channel_id=1, source_target_pairs={{0,1},{1,0},{2,3},{3,2},{4,5},{5,4},{6,7},{7,6},{8,9},{9,8},{10,11... | collective-permute-start | bytes 98312 | tf_op jit(solution)/shard_map/ppermute | solution.py:26

commit v15 on v14

--- a/solution.py
+++ b/solution.py
@@ -16,7 +16,7 @@
 PRIOR_REWARD = 1.0
 MASS_ROWS = 16
 BLOCK = 8
-PROJECT_CHUNK = 256
+PROJECT_CHUNK = 512
 LOW_TILES = LOWK * KY // LANES // 2
 MIB = 1 << 20
 
@@ -82,7 +82,7 @@
                 blended[pl.ds(row, 1), :] = value[:, k * LANES : (k + 1) * LANES]
         return carry
 
-    lax.fori_loop(0, half_tiles // tiles, body, 0, unroll=8)
+    lax.fori_loop(0, half_tiles // tiles, body, 0, unroll=16)
 
 
 def image_copies(images_hbm, target, sems, first, half, pixels):

time: 34.7 us -> 35.9 us (1.035)
  Pallas kernels: 10.1 us -> 11.2 us
    pallas_call x1, Pallas kernels: 2.33 us -> 3.43 us  [project_own(): pl.pallas_call(project_own_kernel, in_specs=whole_vmem(3) + [pl.BlockSpec...]
  transfers between devices with their start and end apart: 10 -> 10, of which waited for: 8 -> 8; matrix products, arithmetic and copies ran while one was open for 0% -> 0% of each run, Pallas kernels for 13% -> 16%
where the time goes in v15:
time: 35.9 us; the launch traced here: 35.7 us
  starting transfers between devices  12 us (33%)
  waiting for transfers between devices  11.7 us (33%)
  Pallas kernels  11.2 us (31%)
  between operations  0.75 us (2%)
    ppermute x10, starting transfers between devices, exchange(): return lax.ppermute(value, 'particle', pairs)  12 us
    ppermute x10, waiting for transfers between devices, exchange(): return lax.ppermute(value, 'particle', pairs)  11.7 us
    pallas_call x1, Pallas kernels, project_other(): pl.pallas_call(project_other_kernel, in_specs=[pl.BlockSpec(memory_space=...  3.71 us
    pallas_call x1, Pallas kernels, project_own(): pl.pallas_call(project_own_kernel, in_specs=whole_vmem(3) + [pl.BlockSpec...  3.43 us
    pallas_call x2, Pallas kernels, correlate(): pl.pallas_call(functools.partial(kernel, chunk=4096), in_specs=whole_vmem...  1.56 us
    pallas_call x1, Pallas kernels, backproject(): pl.pallas_call(functools.partial(backproject_kernel, slots=slots, chunk=L...  1.34 us
  transfers between devices with their start and end apart: 10, of which 8 were waited for; matrix products, arithmetic and copies ran while one was open for 0% of the time, Pallas kernels for 16%

profile of v15, /device:TPU:0, one launch (start us, length us, event | category | flops | bytes accessed | tf_op | source)
XLA Modules:
  0.0 35.7 jit_solution(16854850973308335334)
XLA Ops:
  0.6 3.7 %project_other.1 = (bf16[32,16896]{1,0:T(8,128)(2,1)S(1)}, bf16[304,256]{1,0:T(8,128)(2,1)S(1)}, s32[1,16384]{1,0:T(1,128)S(1)}, f32[1,16384]{1,0:T(1,128)S(1)}) custom-call(bf16[2,8,2,32768]{3,2,1,0:T(2,128)(2,1)} %table_hbm.1, s32[1,16384]{1,0:T(1,128)} %index_hbm.1, f32[1,16384]{1,0:T(1,128)} %frac_hbm.1, bf16[32,32768]{1,0:T(8,128)(2,1)} %images_hbm.3), custom_call_target="tpu_custom_call" | custom-call | tf_op jit(solution)/shard_map/project_other/pallas_call | solution.py:169
  4.3 0.5 %collective-permute-start = (bf16[32,16896]{1,0:T(8,128)(2,1)S(1)}, bf16[32,16896]{1,0:T(8,128)(2,1)S(1)}, u32[]{:S(2)}, u32[]{:S(2)}) collective-permute-start(bf16[32,16896]{1,0:T(8,128)(2,1)S(1)} %get-tuple-element.33), channel_id=1, source_target_pairs={{0,1},{1,0},{2,3},{3,2},{4,5},{5,4},{6,7},{7,6},{8,9},{9,8},{10,11... | collective-permute-start | bytes 3244040 | tf_op jit(solution)/shard_map/ppermute | solution.py:26
  4.9 3.4 %project_own.1 = (bf16[128,128]{1,0:T(8,128)(2,1)S(1)}, bf16[32,16384]{1,0:T(8,128)(2,1)S(1)}) custom-call(bf16[304,256]{1,0:T(8,128)(2,1)S(1)} %get-tuple-element.29.table, s32[1,16384]{1,0:T(1,128)S(1)} %get-tuple-element.30.index_ref, f32[1,16384]{1,0:T(1,128)S(1)} %get-tuple-element.31.frac_ref, bf16[32,32768]{1,0:T(8,128)(2,1)} %images_hbm.3), custom_call_target="tpu_custom_call" | custom-call | flops 2000000000 | bytes 8000000 | tf_op jit(solution)/shard_map/project_own/pallas_call | solution.py:204
  8.3 4.7 %collective-permute-start.1 = (bf16[256,128]{1,0:T(8,128)(2,1)S(1)}, bf16[256,128]{1,0:T(8,128)(2,1)S(1)}, u32[]{:S(2)}, u32[]{:S(2)}) collective-permute-start(bf16[256,128]{1,0:T(8,128)(2,1)S(1)} %pair_rows.1.refs_0_), channel_id=1, source_target_pairs={{0,12},{1,13},{2,14},{3,15},{4,8},{5,9},{6,10},{7,11},{8,4},{9,5},... | collective-permute-start | bytes 196616 | tf_op jit(solution)/shard_map/ppermute | solution.py:26
  13.0 0.6 %collective-permute-start.2 = (bf16[256,128]{1,0:T(8,128)(2,1)S(1)}, bf16[256,128]{1,0:T(8,128)(2,1)S(1)}, u32[]{:S(2)}, u32[]{:S(2)}) collective-permute-start(bf16[256,128]{1,0:T(8,128)(2,1)S(1)} %pair_rows.1.refs_0_), channel_id=1, source_target_pairs={{0,4},{1,5},{2,6},{3,7},{4,0},{5,1},{6,2},{7,3},{8,12},{9,13},{10,... | collective-permute-start | bytes 196616 | tf_op jit(solution)/shard_map/ppermute | solution.py:26
  13.7 2.3 %collective-permute-done.1.refs_1_ = bf16[256,128]{1,0:T(8,128)(2,1)S(1)} collective-permute-done((bf16[256,128]{1,0:T(8,128)(2,1)S(1)}, bf16[256,128]{1,0:T(8,128)(2,1)S(1)}, u32[]{:S(2)}, u32[]{:S(2)}) %collective-permute-start.1) | collective-permute-done | bytes 65568 | tf_op jit(solution)/shard_map/ppermute | solution.py:26
  16.0 0.9 %correlate.2 = (f32[36,128]{1,0:T(8,128)S(1)}, f32[8,8192]{1,0:T(8,128)S(1)}, f32[8,8192]{1,0:T(8,128)S(1)}) custom-call(s32[2,8]{1,0:T(2,128)S(1)} %bitcast.6, bf16[32,16384]{1,0:T(8,128)(2,1)S(1)} %get-tuple-element.32.own_images, bf16[32,16896]{1,0:T(8,128)(2,1)S(1)} %collective-permute-done.other.other_images, bf16[256,128]{1,0:T(8,128)(2,1)S(1)} %pair_rows.1.refs_0_, ...), custom_call_target="tpu_custom_call" | custom-call | flops 1000000000 | bytes 4000000 | tf_op jit(solution)/shard_map/correlate/pallas_call | solution.py:361
  16.9 0.0 copy-start.1
  16.9 2.3 %collective-permute-done.3.refs_1_ = bf16[256,128]{1,0:T(8,128)(2,1)S(1)} collective-permute-done((bf16[256,128]{1,0:T(8,128)(2,1)S(1)}, bf16[256,128]{1,0:T(8,128)(2,1)S(1)}, u32[]{:S(2)}, u32[]{:S(2)}) %collective-permute-start.3) | collective-permute-done | bytes 65568 | tf_op jit(solution)/shard_map/ppermute | solution.py:26
  19.1 0.7 %correlate.3.refs_1_ = f32[36,128]{1,0:T(8,128)S(1)} custom-call(f32[8,8192]{1,0:T(8,128)S(1)} %get-tuple-element.36.cos_ref, f32[8,8192]{1,0:T(8,128)S(1)} %get-tuple-element.37.sin_ref, bf16[32,16384]{1,0:T(8,128)(2,1)S(1)} %get-tuple-element.32.own_images, bf16[32,16896]{1,0:T(8,128)(2,1)S(1)} %collective-permute-done.other.other_images, ...), custom_call_target="tpu_custom_call" | custom-call | flops 1000000000 | bytes 4000000 | tf_op jit(solution)/shard_map/correlate/pallas_call | solution.py:361
  19.8 0.1 collective-permute-start.4
  19.9 1.2 %collective-permute-done.4.received = f32[80,128]{1,0:T(8,128)S(1)} collective-permute-done((f32[80,128]{1,0:T(8,128)S(1)}, f32[80,128]{1,0:T(8,128)S(1)}, u32[]{:S(2)}, u32[]{:S(2)}) %collective-permute-start.4) | collective-permute-done | bytes 40992 | tf_op jit(solution)/shard_map/ppermute | solution.py:26
  21.1 0.4 %posterior.1 = (bf16[64,64]{1,0:T(8,128)(2,1)S(1)}, f32[128,128]{1,0:T(8,128)S(1)}, bf16[144,128]{1,0:T(8,128)(2,1)S(1)}, f32[8,128]{1,0:T(8,128)S(1)}) custom-call(f32[80,128]{1,0:T(8,128)S(1)} %collect.1.mine, f32[80,128]{1,0:T(8,128)S(1)} %collective-permute-done.4.received, bf16[32,16384]{1,0:T(8,128)(2,1)S(1)} %get-tuple-element.32.own_images, ...), custom_call_target="tpu_custom_call" | custom-call | tf_op jit(solution)/shard_map/posterior/pallas_call | solution.py:478
  21.5 1.6 %collective-permute-start.5 = (bf16[144,128]{1,0:T(8,128)(2,1)S(1)}, bf16[144,128]{1,0:T(8,128)(2,1)S(1)}, u32[]{:S(2)}, u32[]{:S(2)}) collective-permute-start(bf16[144,128]{1,0:T(8,128)(2,1)S(1)} %get-tuple-element.41), channel_id=1, source_target_pairs={{0,2},{1,3},{2,0},{3,1},{4,6},{5,7},{6,4},{7,5},{8,10},{9,11},{10,... | collective-permute-start | bytes 110600 | tf_op jit(solution)/shard_map/ppermute | solution.py:26
  23.1 1.3 %backproject.1 = (f32[224,128]{1,0:T(8,128)S(1)}, bf16[224,128]{1,0:T(8,128)(2,1)S(1)}, bf16[224,128]{1,0:T(8,128)(2,1)S(1)}, bf16[224,128]{1,0:T(8,128)(2,1)S(1)}) custom-call(bf16[64,64]{1,0:T(8,128)(2,1)S(1)} %get-tuple-element.38.weight_ref, bf16[32,16384]{1,0:T(8,128)(2,1)S(1)} %get-tuple-element.32.own_images, ...), custom_call_target="tpu_custom_call" | custom-call | flops 2000000000 | bytes 8000000 | tf_op jit(solution)/shard_map/backproject/pallas_call | solution.py:528
  24.4 1.1 %collective-permute-done.5.low_received = bf16[144,128]{1,0:T(8,128)(2,1)S(1)} collective-permute-done((bf16[144,128]{1,0:T(8,128)(2,1)S(1)}, bf16[144,128]{1,0:T(8,128)(2,1)S(1)}, u32[]{:S(2)}, u32[]{:S(2)}) %collective-permute-start.5) | collective-permute-done | bytes 36896 | tf_op jit(solution)/shard_map/ppermute | solution.py:26
  25.6 2.5 %collective-permute-start.6 = (bf16[272,128]{1,0:T(8,128)(2,1)S(1)}, bf16[272,128]{1,0:T(8,128)(2,1)S(1)}, u32[]{:S(2)}, u32[]{:S(2)}) collective-permute-start(bf16[272,128]{1,0:T(8,128)(2,1)S(1)} %get-tuple-element.48), channel_id=1, source_target_pairs={{0,12},{1,13},{2,14},{3,15},{4,8},{5,9},{6,10},{7,11},{8,4},{9,5},... | collective-permute-start | bytes 208904 | tf_op jit(solution)/shard_map/ppermute | solution.py:26
  28.1 1.9 %collective-permute-start.8 = (bf16[272,128]{1,0:T(8,128)(2,1)S(1)}, bf16[272,128]{1,0:T(8,128)(2,1)S(1)}, u32[]{:S(2)}, u32[]{:S(2)}) collective-permute-start(bf16[272,128]{1,0:T(8,128)(2,1)S(1)} %get-tuple-element.50), channel_id=1, source_target_pairs={{0,8},{1,9},{2,10},{3,11},{4,12},{5,13},{6,14},{7,15},{8,0},{9,1},... | collective-permute-start | bytes 208904 | tf_op jit(solution)/shard_map/ppermute | solution.py:26
  30.0 2.1 %collective-permute-done.6.refs_0_ = bf16[272,128]{1,0:T(8,128)(2,1)S(1)} collective-permute-done((bf16[272,128]{1,0:T(8,128)(2,1)S(1)}, bf16[272,128]{1,0:T(8,128)(2,1)S(1)}, u32[]{:S(2)}, u32[]{:S(2)}) %collective-permute-start.6) | collective-permute-done | bytes 69664 | tf_op jit(solution)/shard_map/ppermute | solution.py:26
  32.1 1.3 %collective-permute-done.7.refs_1_ = bf16[272,128]{1,0:T(8,128)(2,1)S(1)} collective-permute-done((bf16[272,128]{1,0:T(8,128)(2,1)S(1)}, bf16[272,128]{1,0:T(8,128)(2,1)S(1)}, u32[]{:S(2)}, u32[]{:S(2)}) %collective-permute-start.7) | collective-permute-done | bytes 69664 | tf_op jit(solution)/shard_map/ppermute | solution.py:26
  33.5 0.2 collective-permute-done.8.refs_2_
  33.7 0.1 collective-permute-start.9
  33.8 1.2 %collective-permute-done.9.received = bf16[128,128]{1,0:T(8,128)(2,1)S(1)} collective-permute-done((bf16[128,128]{1,0:T(8,128)(2,1)S(1)}, bf16[128,128]{1,0:T(8,128)(2,1)S(1)}, u32[]{:S(2)}, u32[]{:S(2)}) %collective-permute-start.9) | collective-permute-done | bytes 32800 | tf_op jit(solution)/shard_map/ppermute | solution.py:26
  35.0 0.7 %finish.1 = (f32[256,128]{1,0:T(8,128)}, f32[8]{0:T(128)}) custom-call(f32[128,128]{1,0:T(8,128)S(1)} %get-tuple-element.51.own, bf16[128,128]{1,0:T(8,128)(2,1)S(1)} %collective-permute-done.9.received, f32[8,128]{1,0:T(8,128)S(1)} %get-tuple-element.53.mass), custom_call_target="tpu_custom_call" | custom-call | tf_op jit(solution)/shard_map/finish/pallas_call | solution.py:632
  (13 shorter events, 0.1 us)
Async XLA Ops:
  4.3 4.0 %collective-permute-start = (bf16[32,16896]{1,0:T(8,128)(2,1)S(1)}, bf16[32,16896]{1,0:T(8,128)(2,1)S(1)}, u32[]{:S(2)}, u32[]{:S(2)}) collective-permute-start(bf16[32,16896]{1,0:T(8,128)(2,1)S(1)} %get-tuple-element.33), channel_id=1, source_target_pairs={{0,1},{1,0},{2,3},{3,2},{4,5},{5,4},{6,7},{7,6},{8,9},{9,8},{10,11... | collective-permute-start | bytes 3244040 | tf_op jit(solution)/shard_map/ppermute | solution.py:26
  4.9 11.1 %copy-start.2 = (s32[8,2]{0,1:T(2,128)S(1)}, s32[8,2]{0,1:T(2,128)}, u32[]{:S(2)}) copy-start(s32[8,2]{0,1:T(2,128)} %param.13) | copy-start | bytes 196
  8.3 7.6 %collective-permute-start.1 = (bf16[256,128]{1,0:T(8,128)(2,1)S(1)}, bf16[256,128]{1,0:T(8,128)(2,1)S(1)}, u32[]{:S(2)}, u32[]{:S(2)}) collective-permute-start(bf16[256,128]{1,0:T(8,128)(2,1)S(1)} %pair_rows.1.refs_0_), channel_id=1, source_target_pairs={{0,12},{1,13},{2,14},{3,15},{4,8},{5,9},{6,10},{7,11},{8,4},{9,5},... | collective-permute-start | bytes 196616 | tf_op jit(solution)/shard_map/ppermute | solution.py:26
  13.0 6.1 %collective-permute-start.3 = (bf16[256,128]{1,0:T(8,128)(2,1)S(1)}, bf16[256,128]{1,0:T(8,128)(2,1)S(1)}, u32[]{:S(2)}, u32[]{:S(2)}) collective-permute-start(bf16[256,128]{1,0:T(8,128)(2,1)S(1)} %pair_rows.1.refs_0_), channel_id=1, source_target_pairs={{0,8},{1,9},{2,10},{3,11},{4,12},{5,13},{6,14},{7,15},{8,0},{9,1},... | collective-permute-start | bytes 196616 | tf_op jit(solution)/shard_map/ppermute | solution.py:26
  13.0 6.1 %collective-permute-start.2 = (bf16[256,128]{1,0:T(8,128)(2,1)S(1)}, bf16[256,128]{1,0:T(8,128)(2,1)S(1)}, u32[]{:S(2)}, u32[]{:S(2)}) collective-permute-start(bf16[256,128]{1,0:T(8,128)(2,1)S(1)} %pair_rows.1.refs_0_), channel_id=1, source_target_pairs={{0,4},{1,5},{2,6},{3,7},{4,0},{5,1},{6,2},{7,3},{8,12},{9,13},{10,... | collective-permute-start | bytes 196616 | tf_op jit(solution)/shard_map/ppermute | solution.py:26
  16.8 3.0 %copy-start = (f32[32]{0:T(128)S(1)}, f32[32]{0:T(128)}, u32[]{:S(2)}) copy-start(f32[32]{0:T(128)} %param.8) | copy-start | bytes 388
  16.9 3.0 %copy-start.1 = (s32[32]{0:T(128)S(1)}, s32[32]{0:T(128)}, u32[]{:S(2)}) copy-start(s32[32]{0:T(128)} %param.9) | copy-start | bytes 388
  19.8 1.3 %collective-permute-start.4 = (f32[80,128]{1,0:T(8,128)S(1)}, f32[80,128]{1,0:T(8,128)S(1)}, u32[]{:S(2)}, u32[]{:S(2)}) collective-permute-start(f32[80,128]{1,0:T(8,128)S(1)} %collect.1.mine), channel_id=1, source_target_pairs={{0,1},{1,0},{2,3},{3,2},{4,5},{5,4},{6,7},{7,6},{8,9},{9,8},{10,11... | collective-permute-start | bytes 122888 | tf_op jit(solution)/shard_map/ppermute | solution.py:26
  21.5 4.0 %collective-permute-start.5 = (bf16[144,128]{1,0:T(8,128)(2,1)S(1)}, bf16[144,128]{1,0:T(8,128)(2,1)S(1)}, u32[]{:S(2)}, u32[]{:S(2)}) collective-permute-start(bf16[144,128]{1,0:T(8,128)(2,1)S(1)} %get-tuple-element.41), channel_id=1, source_target_pairs={{0,2},{1,3},{2,0},{3,1},{4,6},{5,7},{6,4},{7,5},{8,10},{9,11},{10,... | collective-permute-start | bytes 110600 | tf_op jit(solution)/shard_map/ppermute | solution.py:26
  25.6 6.6 %collective-permute-start.6 = (bf16[272,128]{1,0:T(8,128)(2,1)S(1)}, bf16[272,128]{1,0:T(8,128)(2,1)S(1)}, u32[]{:S(2)}, u32[]{:S(2)}) collective-permute-start(bf16[272,128]{1,0:T(8,128)(2,1)S(1)} %get-tuple-element.48), channel_id=1, source_target_pairs={{0,12},{1,13},{2,14},{3,15},{4,8},{5,9},{6,10},{7,11},{8,4},{9,5},... | collective-permute-start | bytes 208904 | tf_op jit(solution)/shard_map/ppermute | solution.py:26
  28.1 5.4 %collective-permute-start.7 = (bf16[272,128]{1,0:T(8,128)(2,1)S(1)}, bf16[272,128]{1,0:T(8,128)(2,1)S(1)}, u32[]{:S(2)}, u32[]{:S(2)}) collective-permute-start(bf16[272,128]{1,0:T(8,128)(2,1)S(1)} %get-tuple-element.49), channel_id=1, source_target_pairs={{0,4},{1,5},{2,6},{3,7},{4,0},{5,1},{6,2},{7,3},{8,12},{9,13},{10,... | collective-permute-start | bytes 208904 | tf_op jit(solution)/shard_map/ppermute | solution.py:26
  28.1 5.5 %collective-permute-start.8 = (bf16[272,128]{1,0:T(8,128)(2,1)S(1)}, bf16[272,128]{1,0:T(8,128)(2,1)S(1)}, u32[]{:S(2)}, u32[]{:S(2)}) collective-permute-start(bf16[272,128]{1,0:T(8,128)(2,1)S(1)} %get-tuple-element.50), channel_id=1, source_target_pairs={{0,8},{1,9},{2,10},{3,11},{4,12},{5,13},{6,14},{7,15},{8,0},{9,1},... | collective-permute-start | bytes 208904 | tf_op jit(solution)/shard_map/ppermute | solution.py:26
  33.7 1.3 %collective-permute-start.9 = (bf16[128,128]{1,0:T(8,128)(2,1)S(1)}, bf16[128,128]{1,0:T(8,128)(2,1)S(1)}, u32[]{:S(2)}, u32[]{:S(2)}) collective-permute-start(bf16[128,128]{1,0:T(8,128)(2,1)S(1)} %get-tuple-element.52), channel_id=1, source_target_pairs={{0,1},{1,0},{2,3},{3,2},{4,5},{5,4},{6,7},{7,6},{8,9},{9,8},{10,11... | collective-permute-start | bytes 98312 | tf_op jit(solution)/shard_map/ppermute | solution.py:26

commit v16 on v14

--- a/solution.py
+++ b/solution.py
@@ -82,7 +82,7 @@
                 blended[pl.ds(row, 1), :] = value[:, k * LANES : (k + 1) * LANES]
         return carry
 
-    lax.fori_loop(0, half_tiles // tiles, body, 0, unroll=8)
+    lax.fori_loop(0, half_tiles // tiles, body, 0, unroll=4)
 
 
 def image_copies(images_hbm, target, sems, first, half, pixels):

time: 34.7 us -> 36.1 us (1.040)
  Pallas kernels: 10.1 us -> 11.5 us
    pallas_call x1, Pallas kernels: 3.67 us -> 4.4 us  [project_other(): pl.pallas_call(project_other_kernel, in_specs=[pl.BlockSpec(memory_space=...]
    pallas_call x1, Pallas kernels: 2.33 us -> 3.05 us  [project_own(): pl.pallas_call(project_own_kernel, in_specs=whole_vmem(3) + [pl.BlockSpec...]
  transfers between devices with their start and end apart: 10 -> 10, of which waited for: 8 -> 8; matrix products, arithmetic and copies ran while one was open for 0% -> 0% of each run, Pallas kernels for 13% -> 15%
where the time goes in v16:
time: 36.1 us; the launch traced here: 36 us
  starting transfers between devices  12 us (33%)
  waiting for transfers between devices  11.7 us (32%)
  Pallas kernels  11.5 us (32%)
  between operations  0.75 us (2%)
    ppermute x10, starting transfers between devices, exchange(): return lax.ppermute(value, 'particle', pairs)  12 us
    ppermute x10, waiting for transfers between devices, exchange(): return lax.ppermute(value, 'particle', pairs)  11.7 us
    pallas_call x1, Pallas kernels, project_other(): pl.pallas_call(project_other_kernel, in_specs=[pl.BlockSpec(memory_space=...  4.4 us
    pallas_call x1, Pallas kernels, project_own(): pl.pallas_call(project_own_kernel, in_specs=whole_vmem(3) + [pl.BlockSpec...  3.05 us
    pallas_call x2, Pallas kernels, correlate(): pl.pallas_call(functools.partial(kernel, chunk=4096), in_specs=whole_vmem...  1.56 us
    pallas_call x1, Pallas kernels, backproject(): pl.pallas_call(functools.partial(backproject_kernel, slots=slots, chunk=L...  1.34 us
  transfers between devices with their start and end apart: 10, of which 8 were waited for; matrix products, arithmetic and copies ran while one was open for 0% of the time, Pallas kernels for 15%

profile of v16, /device:TPU:0, one launch (start us, length us, event | category | flops | bytes accessed | tf_op | source)
XLA Modules:
  0.0 36.0 jit_solution(12567588605526364149)
XLA Ops:
  0.6 4.4 %project_other.1 = (bf16[32,16896]{1,0:T(8,128)(2,1)S(1)}, bf16[304,256]{1,0:T(8,128)(2,1)S(1)}, s32[1,16384]{1,0:T(1,128)S(1)}, f32[1,16384]{1,0:T(1,128)S(1)}) custom-call(bf16[2,8,2,32768]{3,2,1,0:T(2,128)(2,1)} %table_hbm.1, s32[1,16384]{1,0:T(1,128)} %index_hbm.1, f32[1,16384]{1,0:T(1,128)} %frac_hbm.1, bf16[32,32768]{1,0:T(8,128)(2,1)} %images_hbm.3), custom_call_target="tpu_custom_call" | custom-call | tf_op jit(solution)/shard_map/project_other/pallas_call | solution.py:169
  5.0 0.5 %collective-permute-start = (bf16[32,16896]{1,0:T(8,128)(2,1)S(1)}, bf16[32,16896]{1,0:T(8,128)(2,1)S(1)}, u32[]{:S(2)}, u32[]{:S(2)}) collective-permute-start(bf16[32,16896]{1,0:T(8,128)(2,1)S(1)} %get-tuple-element.33), channel_id=1, source_target_pairs={{0,1},{1,0},{2,3},{3,2},{4,5},{5,4},{6,7},{7,6},{8,9},{9,8},{10,11... | collective-permute-start | bytes 3244040 | tf_op jit(solution)/shard_map/ppermute | solution.py:26
  5.6 3.1 %project_own.1 = (bf16[128,128]{1,0:T(8,128)(2,1)S(1)}, bf16[32,16384]{1,0:T(8,128)(2,1)S(1)}) custom-call(bf16[304,256]{1,0:T(8,128)(2,1)S(1)} %get-tuple-element.29.table, s32[1,16384]{1,0:T(1,128)S(1)} %get-tuple-element.30.index_ref, f32[1,16384]{1,0:T(1,128)S(1)} %get-tuple-element.31.frac_ref, bf16[32,32768]{1,0:T(8,128)(2,1)} %images_hbm.3), custom_call_target="tpu_custom_call" | custom-call | flops 2000000000 | bytes 8000000 | tf_op jit(solution)/shard_map/project_own/pallas_call | solution.py:204
  8.7 4.7 %collective-permute-start.1 = (bf16[256,128]{1,0:T(8,128)(2,1)S(1)}, bf16[256,128]{1,0:T(8,128)(2,1)S(1)}, u32[]{:S(2)}, u32[]{:S(2)}) collective-permute-start(bf16[256,128]{1,0:T(8,128)(2,1)S(1)} %pair_rows.1.refs_0_), channel_id=1, source_target_pairs={{0,12},{1,13},{2,14},{3,15},{4,8},{5,9},{6,10},{7,11},{8,4},{9,5},... | collective-permute-start | bytes 196616 | tf_op jit(solution)/shard_map/ppermute | solution.py:26
  13.4 0.6 %collective-permute-start.2 = (bf16[256,128]{1,0:T(8,128)(2,1)S(1)}, bf16[256,128]{1,0:T(8,128)(2,1)S(1)}, u32[]{:S(2)}, u32[]{:S(2)}) collective-permute-start(bf16[256,128]{1,0:T(8,128)(2,1)S(1)} %pair_rows.1.refs_0_), channel_id=1, source_target_pairs={{0,4},{1,5},{2,6},{3,7},{4,0},{5,1},{6,2},{7,3},{8,12},{9,13},{10,... | collective-permute-start | bytes 196616 | tf_op jit(solution)/shard_map/ppermute | solution.py:26
  14.0 2.3 %collective-permute-done.1.refs_1_ = bf16[256,128]{1,0:T(8,128)(2,1)S(1)} collective-permute-done((bf16[256,128]{1,0:T(8,128)(2,1)S(1)}, bf16[256,128]{1,0:T(8,128)(2,1)S(1)}, u32[]{:S(2)}, u32[]{:S(2)}) %collective-permute-start.1) | collective-permute-done | bytes 65568 | tf_op jit(solution)/shard_map/ppermute | solution.py:26
  16.3 0.9 %correlate.2 = (f32[36,128]{1,0:T(8,128)S(1)}, f32[8,8192]{1,0:T(8,128)S(1)}, f32[8,8192]{1,0:T(8,128)S(1)}) custom-call(s32[2,8]{1,0:T(2,128)S(1)} %bitcast.6, bf16[32,16384]{1,0:T(8,128)(2,1)S(1)} %get-tuple-element.32.own_images, bf16[32,16896]{1,0:T(8,128)(2,1)S(1)} %collective-permute-done.other.other_images, bf16[256,128]{1,0:T(8,128)(2,1)S(1)} %pair_rows.1.refs_0_, ...), custom_call_target="tpu_custom_call" | custom-call | flops 1000000000 | bytes 4000000 | tf_op jit(solution)/shard_map/correlate/pallas_call | solution.py:361
  17.2 0.0 copy-start.1
  17.2 2.3 %collective-permute-done.3.refs_1_ = bf16[256,128]{1,0:T(8,128)(2,1)S(1)} collective-permute-done((bf16[256,128]{1,0:T(8,128)(2,1)S(1)}, bf16[256,128]{1,0:T(8,128)(2,1)S(1)}, u32[]{:S(2)}, u32[]{:S(2)}) %collective-permute-start.3) | collective-permute-done | bytes 65568 | tf_op jit(solution)/shard_map/ppermute | solution.py:26
  19.5 0.7 %correlate.3.refs_1_ = f32[36,128]{1,0:T(8,128)S(1)} custom-call(f32[8,8192]{1,0:T(8,128)S(1)} %get-tuple-element.36.cos_ref, f32[8,8192]{1,0:T(8,128)S(1)} %get-tuple-element.37.sin_ref, bf16[32,16384]{1,0:T(8,128)(2,1)S(1)} %get-tuple-element.32.own_images, bf16[32,16896]{1,0:T(8,128)(2,1)S(1)} %collective-permute-done.other.other_images, ...), custom_call_target="tpu_custom_call" | custom-call | flops 1000000000 | bytes 4000000 | tf_op jit(solution)/shard_map/correlate/pallas_call | solution.py:361
  20.2 0.1 collective-permute-start.4
  20.2 1.2 %collective-permute-done.4.received = f32[80,128]{1,0:T(8,128)S(1)} collective-permute-done((f32[80,128]{1,0:T(8,128)S(1)}, f32[80,128]{1,0:T(8,128)S(1)}, u32[]{:S(2)}, u32[]{:S(2)}) %collective-permute-start.4) | collective-permute-done | bytes 40992 | tf_op jit(solution)/shard_map/ppermute | solution.py:26
  21.4 0.4 %posterior.1 = (bf16[64,64]{1,0:T(8,128)(2,1)S(1)}, f32[128,128]{1,0:T(8,128)S(1)}, bf16[144,128]{1,0:T(8,128)(2,1)S(1)}, f32[8,128]{1,0:T(8,128)S(1)}) custom-call(f32[80,128]{1,0:T(8,128)S(1)} %collect.1.mine, f32[80,128]{1,0:T(8,128)S(1)} %collective-permute-done.4.received, bf16[32,16384]{1,0:T(8,128)(2,1)S(1)} %get-tuple-element.32.own_images, ...), custom_call_target="tpu_custom_call" | custom-call | tf_op jit(solution)/shard_map/posterior/pallas_call | solution.py:478
  21.8 1.6 %collective-permute-start.5 = (bf16[144,128]{1,0:T(8,128)(2,1)S(1)}, bf16[144,128]{1,0:T(8,128)(2,1)S(1)}, u32[]{:S(2)}, u32[]{:S(2)}) collective-permute-start(bf16[144,128]{1,0:T(8,128)(2,1)S(1)} %get-tuple-element.41), channel_id=1, source_target_pairs={{0,2},{1,3},{2,0},{3,1},{4,6},{5,7},{6,4},{7,5},{8,10},{9,11},{10,... | collective-permute-start | bytes 110600 | tf_op jit(solution)/shard_map/ppermute | solution.py:26
  23.4 1.3 %backproject.1 = (f32[224,128]{1,0:T(8,128)S(1)}, bf16[224,128]{1,0:T(8,128)(2,1)S(1)}, bf16[224,128]{1,0:T(8,128)(2,1)S(1)}, bf16[224,128]{1,0:T(8,128)(2,1)S(1)}) custom-call(bf16[64,64]{1,0:T(8,128)(2,1)S(1)} %get-tuple-element.38.weight_ref, bf16[32,16384]{1,0:T(8,128)(2,1)S(1)} %get-tuple-element.32.own_images, ...), custom_call_target="tpu_custom_call" | custom-call | flops 2000000000 | bytes 8000000 | tf_op jit(solution)/shard_map/backproject/pallas_call | solution.py:528
  24.8 1.1 %collective-permute-done.5.low_received = bf16[144,128]{1,0:T(8,128)(2,1)S(1)} collective-permute-done((bf16[144,128]{1,0:T(8,128)(2,1)S(1)}, bf16[144,128]{1,0:T(8,128)(2,1)S(1)}, u32[]{:S(2)}, u32[]{:S(2)}) %collective-permute-start.5) | collective-permute-done | bytes 36896 | tf_op jit(solution)/shard_map/ppermute | solution.py:26
  25.9 2.5 %collective-permute-start.6 = (bf16[272,128]{1,0:T(8,128)(2,1)S(1)}, bf16[272,128]{1,0:T(8,128)(2,1)S(1)}, u32[]{:S(2)}, u32[]{:S(2)}) collective-permute-start(bf16[272,128]{1,0:T(8,128)(2,1)S(1)} %get-tuple-element.48), channel_id=1, source_target_pairs={{0,12},{1,13},{2,14},{3,15},{4,8},{5,9},{6,10},{7,11},{8,4},{9,5},... | collective-permute-start | bytes 208904 | tf_op jit(solution)/shard_map/ppermute | solution.py:26
  28.4 1.9 %collective-permute-start.8 = (bf16[272,128]{1,0:T(8,128)(2,1)S(1)}, bf16[272,128]{1,0:T(8,128)(2,1)S(1)}, u32[]{:S(2)}, u32[]{:S(2)}) collective-permute-start(bf16[272,128]{1,0:T(8,128)(2,1)S(1)} %get-tuple-element.50), channel_id=1, source_target_pairs={{0,8},{1,9},{2,10},{3,11},{4,12},{5,13},{6,14},{7,15},{8,0},{9,1},... | collective-permute-start | bytes 208904 | tf_op jit(solution)/shard_map/ppermute | solution.py:26
  30.4 2.1 %collective-permute-done.6.refs_0_ = bf16[272,128]{1,0:T(8,128)(2,1)S(1)} collective-permute-done((bf16[272,128]{1,0:T(8,128)(2,1)S(1)}, bf16[272,128]{1,0:T(8,128)(2,1)S(1)}, u32[]{:S(2)}, u32[]{:S(2)}) %collective-permute-start.6) | collective-permute-done | bytes 69664 | tf_op jit(solution)/shard_map/ppermute | solution.py:26
  32.5 1.3 %collective-permute-done.7.refs_1_ = bf16[272,128]{1,0:T(8,128)(2,1)S(1)} collective-permute-done((bf16[272,128]{1,0:T(8,128)(2,1)S(1)}, bf16[272,128]{1,0:T(8,128)(2,1)S(1)}, u32[]{:S(2)}, u32[]{:S(2)}) %collective-permute-start.7) | collective-permute-done | bytes 69664 | tf_op jit(solution)/shard_map/ppermute | solution.py:26
  33.8 0.2 collective-permute-done.8.refs_2_
  34.0 0.1 collective-permute-start.9
  34.1 1.2 %collective-permute-done.9.received = bf16[128,128]{1,0:T(8,128)(2,1)S(1)} collective-permute-done((bf16[128,128]{1,0:T(8,128)(2,1)S(1)}, bf16[128,128]{1,0:T(8,128)(2,1)S(1)}, u32[]{:S(2)}, u32[]{:S(2)}) %collective-permute-start.9) | collective-permute-done | bytes 32800 | tf_op jit(solution)/shard_map/ppermute | solution.py:26
  35.3 0.7 %finish.1 = (f32[256,128]{1,0:T(8,128)}, f32[8]{0:T(128)}) custom-call(f32[128,128]{1,0:T(8,128)S(1)} %get-tuple-element.51.own, bf16[128,128]{1,0:T(8,128)(2,1)S(1)} %collective-permute-done.9.received, f32[8,128]{1,0:T(8,128)S(1)} %get-tuple-element.53.mass), custom_call_target="tpu_custom_call" | custom-call | tf_op jit(solution)/shard_map/finish/pallas_call | solution.py:632
  (13 shorter events, 0.1 us)
Async XLA Ops:
  5.0 3.6 %collective-permute-start = (bf16[32,16896]{1,0:T(8,128)(2,1)S(1)}, bf16[32,16896]{1,0:T(8,128)(2,1)S(1)}, u32[]{:S(2)}, u32[]{:S(2)}) collective-permute-start(bf16[32,16896]{1,0:T(8,128)(2,1)S(1)} %get-tuple-element.33), channel_id=1, source_target_pairs={{0,1},{1,0},{2,3},{3,2},{4,5},{5,4},{6,7},{7,6},{8,9},{9,8},{10,11... | collective-permute-start | bytes 3244040 | tf_op jit(solution)/shard_map/ppermute | solution.py:26
  5.6 10.7 %copy-start.2 = (s32[8,2]{0,1:T(2,128)S(1)}, s32[8,2]{0,1:T(2,128)}, u32[]{:S(2)}) copy-start(s32[8,2]{0,1:T(2,128)} %param.13) | copy-start | bytes 196
  8.7 7.6 %collective-permute-start.1 = (bf16[256,128]{1,0:T(8,128)(2,1)S(1)}, bf16[256,128]{1,0:T(8,128)(2,1)S(1)}, u32[]{:S(2)}, u32[]{:S(2)}) collective-permute-start(bf16[256,128]{1,0:T(8,128)(2,1)S(1)} %pair_rows.1.refs_0_), channel_id=1, source_target_pairs={{0,12},{1,13},{2,14},{3,15},{4,8},{5,9},{6,10},{7,11},{8,4},{9,5},... | collective-permute-start | bytes 196616 | tf_op jit(solution)/shard_map/ppermute | solution.py:26
  13.4 6.1 %collective-permute-start.3 = (bf16[256,128]{1,0:T(8,128)(2,1)S(1)}, bf16[256,128]{1,0:T(8,128)(2,1)S(1)}, u32[]{:S(2)}, u32[]{:S(2)}) collective-permute-start(bf16[256,128]{1,0:T(8,128)(2,1)S(1)} %pair_rows.1.refs_0_), channel_id=1, source_target_pairs={{0,8},{1,9},{2,10},{3,11},{4,12},{5,13},{6,14},{7,15},{8,0},{9,1},... | collective-permute-start | bytes 196616 | tf_op jit(solution)/shard_map/ppermute | solution.py:26
  13.4 6.1 %collective-permute-start.2 = (bf16[256,128]{1,0:T(8,128)(2,1)S(1)}, bf16[256,128]{1,0:T(8,128)(2,1)S(1)}, u32[]{:S(2)}, u32[]{:S(2)}) collective-permute-start(bf16[256,128]{1,0:T(8,128)(2,1)S(1)} %pair_rows.1.refs_0_), channel_id=1, source_target_pairs={{0,4},{1,5},{2,6},{3,7},{4,0},{5,1},{6,2},{7,3},{8,12},{9,13},{10,... | collective-permute-start | bytes 196616 | tf_op jit(solution)/shard_map/ppermute | solution.py:26
  17.2 3.0 %copy-start = (f32[32]{0:T(128)S(1)}, f32[32]{0:T(128)}, u32[]{:S(2)}) copy-start(f32[32]{0:T(128)} %param.8) | copy-start | bytes 388
  17.2 3.0 %copy-start.1 = (s32[32]{0:T(128)S(1)}, s32[32]{0:T(128)}, u32[]{:S(2)}) copy-start(s32[32]{0:T(128)} %param.9) | copy-start | bytes 388
  20.2 1.3 %collective-permute-start.4 = (f32[80,128]{1,0:T(8,128)S(1)}, f32[80,128]{1,0:T(8,128)S(1)}, u32[]{:S(2)}, u32[]{:S(2)}) collective-permute-start(f32[80,128]{1,0:T(8,128)S(1)} %collect.1.mine), channel_id=1, source_target_pairs={{0,1},{1,0},{2,3},{3,2},{4,5},{5,4},{6,7},{7,6},{8,9},{9,8},{10,11... | collective-permute-start | bytes 122888 | tf_op jit(solution)/shard_map/ppermute | solution.py:26
  21.8 4.0 %collective-permute-start.5 = (bf16[144,128]{1,0:T(8,128)(2,1)S(1)}, bf16[144,128]{1,0:T(8,128)(2,1)S(1)}, u32[]{:S(2)}, u32[]{:S(2)}) collective-permute-start(bf16[144,128]{1,0:T(8,128)(2,1)S(1)} %get-tuple-element.41), channel_id=1, source_target_pairs={{0,2},{1,3},{2,0},{3,1},{4,6},{5,7},{6,4},{7,5},{8,10},{9,11},{10,... | collective-permute-start | bytes 110600 | tf_op jit(solution)/shard_map/ppermute | solution.py:26
  25.9 6.6 %collective-permute-start.6 = (bf16[272,128]{1,0:T(8,128)(2,1)S(1)}, bf16[272,128]{1,0:T(8,128)(2,1)S(1)}, u32[]{:S(2)}, u32[]{:S(2)}) collective-permute-start(bf16[272,128]{1,0:T(8,128)(2,1)S(1)} %get-tuple-element.48), channel_id=1, source_target_pairs={{0,12},{1,13},{2,14},{3,15},{4,8},{5,9},{6,10},{7,11},{8,4},{9,5},... | collective-permute-start | bytes 208904 | tf_op jit(solution)/shard_map/ppermute | solution.py:26
  28.4 5.4 %collective-permute-start.7 = (bf16[272,128]{1,0:T(8,128)(2,1)S(1)}, bf16[272,128]{1,0:T(8,128)(2,1)S(1)}, u32[]{:S(2)}, u32[]{:S(2)}) collective-permute-start(bf16[272,128]{1,0:T(8,128)(2,1)S(1)} %get-tuple-element.49), channel_id=1, source_target_pairs={{0,4},{1,5},{2,6},{3,7},{4,0},{5,1},{6,2},{7,3},{8,12},{9,13},{10,... | collective-permute-start | bytes 208904 | tf_op jit(solution)/shard_map/ppermute | solution.py:26
  28.4 5.5 %collective-permute-start.8 = (bf16[272,128]{1,0:T(8,128)(2,1)S(1)}, bf16[272,128]{1,0:T(8,128)(2,1)S(1)}, u32[]{:S(2)}, u32[]{:S(2)}) collective-permute-start(bf16[272,128]{1,0:T(8,128)(2,1)S(1)} %get-tuple-element.50), channel_id=1, source_target_pairs={{0,8},{1,9},{2,10},{3,11},{4,12},{5,13},{6,14},{7,15},{8,0},{9,1},... | collective-permute-start | bytes 208904 | tf_op jit(solution)/shard_map/ppermute | solution.py:26
  34.0 1.3 %collective-permute-start.9 = (bf16[128,128]{1,0:T(8,128)(2,1)S(1)}, bf16[128,128]{1,0:T(8,128)(2,1)S(1)}, u32[]{:S(2)}, u32[]{:S(2)}) collective-permute-start(bf16[128,128]{1,0:T(8,128)(2,1)S(1)} %get-tuple-element.52), channel_id=1, source_target_pairs={{0,1},{1,0},{2,3},{3,2},{4,5},{5,4},{6,7},{7,6},{8,9},{9,8},{10,11... | collective-permute-start | bytes 98312 | tf_op jit(solution)/shard_map/ppermute | solution.py:26

commit v17 on v14

--- a/solution.py
+++ b/solution.py
@@ -243,7 +243,7 @@
 
 
 def chip_order(chips):
-    return [0, chips - 1] + list(range(1, chips - 1))
+    return [0, chips // 2] + [m for m in range(1, chips) if m != chips // 2]
 
 
 def slot_orientation(device, slot, slots):
@@ -679,7 +679,7 @@
     low_from_half = exchange(low_send, 2)
     sums = backproject(weights, own_images, images_received, cos_table, sin_table, slots)
     folded = fold(low, low_from_half, mass, sums[1:])
-    chip_sums = [exchange(send, 4 * m) for m, send in zip(others, folded[2:])]
+    chip_sums = [exchange(send, 4 * m) for m, send in zip(others, folded[2:])][::-1]
     keep, send, mass = merge(sums[0], folded[0], folded[1], chip_sums)
     back, class_mass = finish(
         keep, exchange(send, 1), mass, 1.0 / math.sqrt(parts), CLASSES / (parts * dev_count)

time: 34.7 us -> 35 us (level)
  transfers between devices with their start and end apart: 10 -> 10, of which waited for: 8 -> 9; matrix products, arithmetic and copies ran while one was open for 0% -> 0% of each run, Pallas kernels for 13% -> 13%
where the time goes in v17:
time: 35 us; the launch traced here: 34.9 us
  starting transfers between devices  12.4 us (35%)
  waiting for transfers between devices  11.6 us (33%)
  Pallas kernels  10.1 us (29%)
  between operations  0.75 us (2%)
    ppermute x10, starting transfers between devices, exchange(): return lax.ppermute(value, 'particle', pairs)  12.4 us
    ppermute x10, waiting for transfers between devices, exchange(): return lax.ppermute(value, 'particle', pairs)  11.6 us
    pallas_call x1, Pallas kernels, project_other(): pl.pallas_call(project_other_kernel, in_specs=[pl.BlockSpec(memory_space=...  3.67 us
    pallas_call x1, Pallas kernels, project_own(): pl.pallas_call(project_own_kernel, in_specs=whole_vmem(3) + [pl.BlockSpec...  2.33 us
    pallas_call x2, Pallas kernels, correlate(): pl.pallas_call(functools.partial(kernel, chunk=4096), in_specs=whole_vmem...  1.56 us
    pallas_call x1, Pallas kernels, backproject(): pl.pallas_call(functools.partial(backproject_kernel, slots=slots, chunk=L...  1.34 us
  transfers between devices with their start and end apart: 10, of which 9 were waited for; matrix products, arithmetic and copies ran while one was open for 0% of the time, Pallas kernels for 13%

profile of v17, /device:TPU:0, one launch (start us, length us, event | category | flops | bytes accessed | tf_op | source)
XLA Modules:
  0.0 34.9 jit_solution(16235573077222449120)
XLA Ops:
  0.6 3.7 %project_other.1 = (bf16[32,16896]{1,0:T(8,128)(2,1)S(1)}, bf16[304,256]{1,0:T(8,128)(2,1)S(1)}, s32[1,16384]{1,0:T(1,128)S(1)}, f32[1,16384]{1,0:T(1,128)S(1)}) custom-call(bf16[2,8,2,32768]{3,2,1,0:T(2,128)(2,1)} %table_hbm.1, s32[1,16384]{1,0:T(1,128)} %index_hbm.1, f32[1,16384]{1,0:T(1,128)} %frac_hbm.1, bf16[32,32768]{1,0:T(8,128)(2,1)} %images_hbm.3), custom_call_target="tpu_custom_call" | custom-call | tf_op jit(solution)/shard_map/project_other/pallas_call | solution.py:169
  4.3 0.5 %collective-permute-start = (bf16[32,16896]{1,0:T(8,128)(2,1)S(1)}, bf16[32,16896]{1,0:T(8,128)(2,1)S(1)}, u32[]{:S(2)}, u32[]{:S(2)}) collective-permute-start(bf16[32,16896]{1,0:T(8,128)(2,1)S(1)} %get-tuple-element.33), channel_id=1, source_target_pairs={{0,1},{1,0},{2,3},{3,2},{4,5},{5,4},{6,7},{7,6},{8,9},{9,8},{10,11... | collective-permute-start | bytes 3244040 | tf_op jit(solution)/shard_map/ppermute | solution.py:26
  4.8 2.3 %project_own.1 = (bf16[128,128]{1,0:T(8,128)(2,1)S(1)}, bf16[32,16384]{1,0:T(8,128)(2,1)S(1)}) custom-call(bf16[304,256]{1,0:T(8,128)(2,1)S(1)} %get-tuple-element.29.table, s32[1,16384]{1,0:T(1,128)S(1)} %get-tuple-element.30.index_ref, f32[1,16384]{1,0:T(1,128)S(1)} %get-tuple-element.31.frac_ref, bf16[32,32768]{1,0:T(8,128)(2,1)} %images_hbm.3), custom_call_target="tpu_custom_call" | custom-call | flops 2000000000 | bytes 8000000 | tf_op jit(solution)/shard_map/project_own/pallas_call | solution.py:204
  7.2 4.0 %collective-permute-start.1 = (bf16[256,128]{1,0:T(8,128)(2,1)S(1)}, bf16[256,128]{1,0:T(8,128)(2,1)S(1)}, u32[]{:S(2)}, u32[]{:S(2)}) collective-permute-start(bf16[256,128]{1,0:T(8,128)(2,1)S(1)} %pair_rows.1.refs_0_), channel_id=1, source_target_pairs={{0,8},{1,9},{2,10},{3,11},{4,12},{5,13},{6,14},{7,15},{8,0},{9,1},... | collective-permute-start | bytes 196616 | tf_op jit(solution)/shard_map/ppermute | solution.py:26
  11.2 1.3 %collective-permute-start.3 = (bf16[256,128]{1,0:T(8,128)(2,1)S(1)}, bf16[256,128]{1,0:T(8,128)(2,1)S(1)}, u32[]{:S(2)}, u32[]{:S(2)}) collective-permute-start(bf16[256,128]{1,0:T(8,128)(2,1)S(1)} %pair_rows.1.refs_0_), channel_id=1, source_target_pairs={{0,12},{1,13},{2,14},{3,15},{4,8},{5,9},{6,10},{7,11},{8,4},{9,5},... | collective-permute-start | bytes 196616 | tf_op jit(solution)/shard_map/ppermute | solution.py:26
  12.5 0.2 collective-permute-start.2
  12.8 2.4 %collective-permute-done.1.refs_1_ = bf16[256,128]{1,0:T(8,128)(2,1)S(1)} collective-permute-done((bf16[256,128]{1,0:T(8,128)(2,1)S(1)}, bf16[256,128]{1,0:T(8,128)(2,1)S(1)}, u32[]{:S(2)}, u32[]{:S(2)}) %collective-permute-start.1) | collective-permute-done | bytes 65568 | tf_op jit(solution)/shard_map/ppermute | solution.py:26
  15.2 0.9 %correlate.2 = (f32[36,128]{1,0:T(8,128)S(1)}, f32[8,8192]{1,0:T(8,128)S(1)}, f32[8,8192]{1,0:T(8,128)S(1)}) custom-call(s32[2,8]{1,0:T(2,128)S(1)} %bitcast.6, bf16[32,16384]{1,0:T(8,128)(2,1)S(1)} %get-tuple-element.32.own_images, bf16[32,16896]{1,0:T(8,128)(2,1)S(1)} %collective-permute-done.other.other_images, bf16[256,128]{1,0:T(8,128)(2,1)S(1)} %pair_rows.1.refs_0_, ...), custom_call_target="tpu_custom_call" | custom-call | flops 1000000000 | bytes 4000000 | tf_op jit(solution)/shard_map/correlate/pallas_call | solution.py:361
  16.1 1.5 %collective-permute-done.3.refs_1_ = bf16[256,128]{1,0:T(8,128)(2,1)S(1)} collective-permute-done((bf16[256,128]{1,0:T(8,128)(2,1)S(1)}, bf16[256,128]{1,0:T(8,128)(2,1)S(1)}, u32[]{:S(2)}, u32[]{:S(2)}) %collective-permute-start.3) | collective-permute-done | bytes 65568 | tf_op jit(solution)/shard_map/ppermute | solution.py:26
  17.6 0.2 collective-permute-done.2.refs_0_
  17.8 0.7 %correlate.3.refs_1_ = f32[36,128]{1,0:T(8,128)S(1)} custom-call(f32[8,8192]{1,0:T(8,128)S(1)} %get-tuple-element.36.cos_ref, f32[8,8192]{1,0:T(8,128)S(1)} %get-tuple-element.37.sin_ref, bf16[32,16384]{1,0:T(8,128)(2,1)S(1)} %get-tuple-element.32.own_images, bf16[32,16896]{1,0:T(8,128)(2,1)S(1)} %collective-permute-done.other.other_images, ...), custom_call_target="tpu_custom_call" | custom-call | flops 1000000000 | bytes 4000000 | tf_op jit(solution)/shard_map/correlate/pallas_call | solution.py:361
  18.5 0.1 collective-permute-start.4
  18.6 1.2 %collective-permute-done.4.received = f32[80,128]{1,0:T(8,128)S(1)} collective-permute-done((f32[80,128]{1,0:T(8,128)S(1)}, f32[80,128]{1,0:T(8,128)S(1)}, u32[]{:S(2)}, u32[]{:S(2)}) %collective-permute-start.4) | collective-permute-done | bytes 40992 | tf_op jit(solution)/shard_map/ppermute | solution.py:26
  19.8 0.4 %posterior.1 = (bf16[64,64]{1,0:T(8,128)(2,1)S(1)}, f32[128,128]{1,0:T(8,128)S(1)}, bf16[144,128]{1,0:T(8,128)(2,1)S(1)}, f32[8,128]{1,0:T(8,128)S(1)}) custom-call(f32[80,128]{1,0:T(8,128)S(1)} %collect.1.mine, f32[80,128]{1,0:T(8,128)S(1)} %collective-permute-done.4.received, bf16[32,16384]{1,0:T(8,128)(2,1)S(1)} %get-tuple-element.32.own_images, ...), custom_call_target="tpu_custom_call" | custom-call | tf_op jit(solution)/shard_map/posterior/pallas_call | solution.py:478
  20.2 1.7 %collective-permute-start.5 = (bf16[144,128]{1,0:T(8,128)(2,1)S(1)}, bf16[144,128]{1,0:T(8,128)(2,1)S(1)}, u32[]{:S(2)}, u32[]{:S(2)}) collective-permute-start(bf16[144,128]{1,0:T(8,128)(2,1)S(1)} %get-tuple-element.41), channel_id=1, source_target_pairs={{0,2},{1,3},{2,0},{3,1},{4,6},{5,7},{6,4},{7,5},{8,10},{9,11},{10,... | collective-permute-start | bytes 110600 | tf_op jit(solution)/shard_map/ppermute | solution.py:26
  21.9 1.3 %backproject.1 = (f32[224,128]{1,0:T(8,128)S(1)}, bf16[224,128]{1,0:T(8,128)(2,1)S(1)}, bf16[224,128]{1,0:T(8,128)(2,1)S(1)}, bf16[224,128]{1,0:T(8,128)(2,1)S(1)}) custom-call(bf16[64,64]{1,0:T(8,128)(2,1)S(1)} %get-tuple-element.38.weight_ref, bf16[32,16384]{1,0:T(8,128)(2,1)S(1)} %get-tuple-element.32.own_images, ...), custom_call_target="tpu_custom_call" | custom-call | flops 2000000000 | bytes 8000000 | tf_op jit(solution)/shard_map/backproject/pallas_call | solution.py:528
  23.3 1.0 %collective-permute-done.5.low_received = bf16[144,128]{1,0:T(8,128)(2,1)S(1)} collective-permute-done((bf16[144,128]{1,0:T(8,128)(2,1)S(1)}, bf16[144,128]{1,0:T(8,128)(2,1)S(1)}, u32[]{:S(2)}, u32[]{:S(2)}) %collective-permute-start.5) | collective-permute-done | bytes 36896 | tf_op jit(solution)/shard_map/ppermute | solution.py:26
  24.2 3.4 %collective-permute-start.6 = (bf16[272,128]{1,0:T(8,128)(2,1)S(1)}, bf16[272,128]{1,0:T(8,128)(2,1)S(1)}, u32[]{:S(2)}, u32[]{:S(2)}) collective-permute-start(bf16[272,128]{1,0:T(8,128)(2,1)S(1)} %get-tuple-element.48), channel_id=1, source_target_pairs={{0,12},{1,13},{2,14},{3,15},{4,8},{5,9},{6,10},{7,11},{8,4},{9,5},... | collective-permute-start | bytes 208904 | tf_op jit(solution)/shard_map/ppermute | solution.py:26
  27.6 1.1 %collective-permute-start.8 = (bf16[272,128]{1,0:T(8,128)(2,1)S(1)}, bf16[272,128]{1,0:T(8,128)(2,1)S(1)}, u32[]{:S(2)}, u32[]{:S(2)}) collective-permute-start(bf16[272,128]{1,0:T(8,128)(2,1)S(1)} %get-tuple-element.50), channel_id=1, source_target_pairs={{0,8},{1,9},{2,10},{3,11},{4,12},{5,13},{6,14},{7,15},{8,0},{9,1},... | collective-permute-start | bytes 208904 | tf_op jit(solution)/shard_map/ppermute | solution.py:26
  28.7 1.8 %collective-permute-done.6.refs_0_ = bf16[272,128]{1,0:T(8,128)(2,1)S(1)} collective-permute-done((bf16[272,128]{1,0:T(8,128)(2,1)S(1)}, bf16[272,128]{1,0:T(8,128)(2,1)S(1)}, u32[]{:S(2)}, u32[]{:S(2)}) %collective-permute-start.6) | collective-permute-done | bytes 69664 | tf_op jit(solution)/shard_map/ppermute | solution.py:26
  30.5 1.5 %collective-permute-done.7.refs_1_ = bf16[272,128]{1,0:T(8,128)(2,1)S(1)} collective-permute-done((bf16[272,128]{1,0:T(8,128)(2,1)S(1)}, bf16[272,128]{1,0:T(8,128)(2,1)S(1)}, u32[]{:S(2)}, u32[]{:S(2)}) %collective-permute-start.7) | collective-permute-done | bytes 69664 | tf_op jit(solution)/shard_map/ppermute | solution.py:26
  32.0 0.9 %collective-permute-done.8.refs_2_ = bf16[272,128]{1,0:T(8,128)(2,1)S(1)} collective-permute-done((bf16[272,128]{1,0:T(8,128)(2,1)S(1)}, bf16[272,128]{1,0:T(8,128)(2,1)S(1)}, u32[]{:S(2)}, u32[]{:S(2)}) %collective-permute-start.8) | collective-permute-done | bytes 69664 | tf_op jit(solution)/shard_map/ppermute | solution.py:26
  33.0 1.2 %collective-permute-done.9.received = bf16[128,128]{1,0:T(8,128)(2,1)S(1)} collective-permute-done((bf16[128,128]{1,0:T(8,128)(2,1)S(1)}, bf16[128,128]{1,0:T(8,128)(2,1)S(1)}, u32[]{:S(2)}, u32[]{:S(2)}) %collective-permute-start.9) | collective-permute-done | bytes 32800 | tf_op jit(solution)/shard_map/ppermute | solution.py:26
  34.2 0.7 %finish.1 = (f32[256,128]{1,0:T(8,128)}, f32[8]{0:T(128)}) custom-call(f32[128,128]{1,0:T(8,128)S(1)} %get-tuple-element.51.own, bf16[128,128]{1,0:T(8,128)(2,1)S(1)} %collective-permute-done.9.received, f32[8,128]{1,0:T(8,128)S(1)} %get-tuple-element.53.mass), custom_call_target="tpu_custom_call" | custom-call | tf_op jit(solution)/shard_map/finish/pallas_call | solution.py:632
  (13 shorter events, 0.2 us)
Async XLA Ops:
  4.3 2.9 %collective-permute-start = (bf16[32,16896]{1,0:T(8,128)(2,1)S(1)}, bf16[32,16896]{1,0:T(8,128)(2,1)S(1)}, u32[]{:S(2)}, u32[]{:S(2)}) collective-permute-start(bf16[32,16896]{1,0:T(8,128)(2,1)S(1)} %get-tuple-element.33), channel_id=1, source_target_pairs={{0,1},{1,0},{2,3},{3,2},{4,5},{5,4},{6,7},{7,6},{8,9},{9,8},{10,11... | collective-permute-start | bytes 3244040 | tf_op jit(solution)/shard_map/ppermute | solution.py:26
  4.8 10.4 %copy-start.2 = (s32[8,2]{0,1:T(2,128)S(1)}, s32[8,2]{0,1:T(2,128)}, u32[]{:S(2)}) copy-start(s32[8,2]{0,1:T(2,128)} %param.13) | copy-start | bytes 196
  7.2 8.0 %collective-permute-start.1 = (bf16[256,128]{1,0:T(8,128)(2,1)S(1)}, bf16[256,128]{1,0:T(8,128)(2,1)S(1)}, u32[]{:S(2)}, u32[]{:S(2)}) collective-permute-start(bf16[256,128]{1,0:T(8,128)(2,1)S(1)} %pair_rows.1.refs_0_), channel_id=1, source_target_pairs={{0,8},{1,9},{2,10},{3,11},{4,12},{5,13},{6,14},{7,15},{8,0},{9,1},... | collective-permute-start | bytes 196616 | tf_op jit(solution)/shard_map/ppermute | solution.py:26
  11.2 6.4 %collective-permute-start.3 = (bf16[256,128]{1,0:T(8,128)(2,1)S(1)}, bf16[256,128]{1,0:T(8,128)(2,1)S(1)}, u32[]{:S(2)}, u32[]{:S(2)}) collective-permute-start(bf16[256,128]{1,0:T(8,128)(2,1)S(1)} %pair_rows.1.refs_0_), channel_id=1, source_target_pairs={{0,12},{1,13},{2,14},{3,15},{4,8},{5,9},{6,10},{7,11},{8,4},{9,5},... | collective-permute-start | bytes 196616 | tf_op jit(solution)/shard_map/ppermute | solution.py:26
  12.5 5.3 %collective-permute-start.2 = (bf16[256,128]{1,0:T(8,128)(2,1)S(1)}, bf16[256,128]{1,0:T(8,128)(2,1)S(1)}, u32[]{:S(2)}, u32[]{:S(2)}) collective-permute-start(bf16[256,128]{1,0:T(8,128)(2,1)S(1)} %pair_rows.1.refs_0_), channel_id=1, source_target_pairs={{0,4},{1,5},{2,6},{3,7},{4,0},{5,1},{6,2},{7,3},{8,12},{9,13},{10,... | collective-permute-start | bytes 196616 | tf_op jit(solution)/shard_map/ppermute | solution.py:26
  16.1 2.4 %copy-start = (f32[32]{0:T(128)S(1)}, f32[32]{0:T(128)}, u32[]{:S(2)}) copy-start(f32[32]{0:T(128)} %param.8) | copy-start | bytes 388
  16.1 2.4 %copy-start.1 = (s32[32]{0:T(128)S(1)}, s32[32]{0:T(128)}, u32[]{:S(2)}) copy-start(s32[32]{0:T(128)} %param.9) | copy-start | bytes 388
  18.5 1.3 %collective-permute-start.4 = (f32[80,128]{1,0:T(8,128)S(1)}, f32[80,128]{1,0:T(8,128)S(1)}, u32[]{:S(2)}, u32[]{:S(2)}) collective-permute-start(f32[80,128]{1,0:T(8,128)S(1)} %collect.1.mine), channel_id=1, source_target_pairs={{0,1},{1,0},{2,3},{3,2},{4,5},{5,4},{6,7},{7,6},{8,9},{9,8},{10,11... | collective-permute-start | bytes 122888 | tf_op jit(solution)/shard_map/ppermute | solution.py:26
  20.2 4.0 %collective-permute-start.5 = (bf16[144,128]{1,0:T(8,128)(2,1)S(1)}, bf16[144,128]{1,0:T(8,128)(2,1)S(1)}, u32[]{:S(2)}, u32[]{:S(2)}) collective-permute-start(bf16[144,128]{1,0:T(8,128)(2,1)S(1)} %get-tuple-element.41), channel_id=1, source_target_pairs={{0,2},{1,3},{2,0},{3,1},{4,6},{5,7},{6,4},{7,5},{8,10},{9,11},{10,... | collective-permute-start | bytes 110600 | tf_op jit(solution)/shard_map/ppermute | solution.py:26
  24.2 6.3 %collective-permute-start.6 = (bf16[272,128]{1,0:T(8,128)(2,1)S(1)}, bf16[272,128]{1,0:T(8,128)(2,1)S(1)}, u32[]{:S(2)}, u32[]{:S(2)}) collective-permute-start(bf16[272,128]{1,0:T(8,128)(2,1)S(1)} %get-tuple-element.48), channel_id=1, source_target_pairs={{0,12},{1,13},{2,14},{3,15},{4,8},{5,9},{6,10},{7,11},{8,4},{9,5},... | collective-permute-start | bytes 208904 | tf_op jit(solution)/shard_map/ppermute | solution.py:26
  27.6 4.3 %collective-permute-start.7 = (bf16[272,128]{1,0:T(8,128)(2,1)S(1)}, bf16[272,128]{1,0:T(8,128)(2,1)S(1)}, u32[]{:S(2)}, u32[]{:S(2)}) collective-permute-start(bf16[272,128]{1,0:T(8,128)(2,1)S(1)} %get-tuple-element.49), channel_id=1, source_target_pairs={{0,4},{1,5},{2,6},{3,7},{4,0},{5,1},{6,2},{7,3},{8,12},{9,13},{10,... | collective-permute-start | bytes 208904 | tf_op jit(solution)/shard_map/ppermute | solution.py:26
  27.6 5.2 %collective-permute-start.8 = (bf16[272,128]{1,0:T(8,128)(2,1)S(1)}, bf16[272,128]{1,0:T(8,128)(2,1)S(1)}, u32[]{:S(2)}, u32[]{:S(2)}) collective-permute-start(bf16[272,128]{1,0:T(8,128)(2,1)S(1)} %get-tuple-element.50), channel_id=1, source_target_pairs={{0,8},{1,9},{2,10},{3,11},{4,12},{5,13},{6,14},{7,15},{8,0},{9,1},... | collective-permute-start | bytes 208904 | tf_op jit(solution)/shard_map/ppermute | solution.py:26
  32.9 1.3 %collective-permute-start.9 = (bf16[128,128]{1,0:T(8,128)(2,1)S(1)}, bf16[128,128]{1,0:T(8,128)(2,1)S(1)}, u32[]{:S(2)}, u32[]{:S(2)}) collective-permute-start(bf16[128,128]{1,0:T(8,128)(2,1)S(1)} %get-tuple-element.52), channel_id=1, source_target_pairs={{0,1},{1,0},{2,3},{3,2},{4,5},{5,4},{6,7},{7,6},{8,9},{9,8},{10,11... | collective-permute-start | bytes 98312 | tf_op jit(solution)/shard_map/ppermute | solution.py:26

commit v18 on v17

--- a/solution.py
+++ b/solution.py
@@ -243,7 +243,7 @@
 
 
 def chip_order(chips):
-    return [0, chips // 2] + [m for m in range(1, chips) if m != chips // 2]
+    return [0, chips - 1] + list(range(1, chips - 1))
 
 
 def slot_orientation(device, slot, slots):

time: 35 us -> 35.9 us (1.026)
  waiting for transfers between devices: 11.6 us -> 12.6 us
    ppermute x10, waiting for transfers between devices: 11.6 us -> 12.6 us  [exchange(): return lax.ppermute(value, 'particle', pairs)]
  transfers between devices with their start and end apart: 10 -> 10, of which waited for: 9 -> 7; matrix products, arithmetic and copies ran while one was open for 0% -> 0% of each run, Pallas kernels for 13% -> 13%
where the time goes in v18:
time: 35.9 us; the launch traced here: 35.8 us
  waiting for transfers between devices  12.6 us (35%)
  starting transfers between devices  12.3 us (34%)
  Pallas kernels  10.1 us (28%)
  between operations  0.75 us (2%)
    ppermute x10, waiting for transfers between devices, exchange(): return lax.ppermute(value, 'particle', pairs)  12.6 us
    ppermute x10, starting transfers between devices, exchange(): return lax.ppermute(value, 'particle', pairs)  12.3 us
    pallas_call x1, Pallas kernels, project_other(): pl.pallas_call(project_other_kernel, in_specs=[pl.BlockSpec(memory_space=...  3.67 us
    pallas_call x1, Pallas kernels, project_own(): pl.pallas_call(project_own_kernel, in_specs=whole_vmem(3) + [pl.BlockSpec...  2.33 us
    pallas_call x2, Pallas kernels, correlate(): pl.pallas_call(functools.partial(kernel, chunk=4096), in_specs=whole_vmem...  1.56 us
    pallas_call x1, Pallas kernels, backproject(): pl.pallas_call(functools.partial(backproject_kernel, slots=slots, chunk=L...  1.34 us
  transfers between devices with their start and end apart: 10, of which 7 were waited for; matrix products, arithmetic and copies ran while one was open for 0% of the time, Pallas kernels for 13%

profile of v18, /device:TPU:0, one launch (start us, length us, event | category | flops | bytes accessed | tf_op | source)
XLA Modules:
  0.0 35.8 jit_solution(13285666000023236221)
XLA Ops:
  0.6 3.7 %project_other.1 = (bf16[32,16896]{1,0:T(8,128)(2,1)S(1)}, bf16[304,256]{1,0:T(8,128)(2,1)S(1)}, s32[1,16384]{1,0:T(1,128)S(1)}, f32[1,16384]{1,0:T(1,128)S(1)}) custom-call(bf16[2,8,2,32768]{3,2,1,0:T(2,128)(2,1)} %table_hbm.1, s32[1,16384]{1,0:T(1,128)} %index_hbm.1, f32[1,16384]{1,0:T(1,128)} %frac_hbm.1, bf16[32,32768]{1,0:T(8,128)(2,1)} %images_hbm.3), custom_call_target="tpu_custom_call" | custom-call | tf_op jit(solution)/shard_map/project_other/pallas_call | solution.py:169
  4.3 0.5 %collective-permute-start = (bf16[32,16896]{1,0:T(8,128)(2,1)S(1)}, bf16[32,16896]{1,0:T(8,128)(2,1)S(1)}, u32[]{:S(2)}, u32[]{:S(2)}) collective-permute-start(bf16[32,16896]{1,0:T(8,128)(2,1)S(1)} %get-tuple-element.33), channel_id=1, source_target_pairs={{0,1},{1,0},{2,3},{3,2},{4,5},{5,4},{6,7},{7,6},{8,9},{9,8},{10,11... | collective-permute-start | bytes 3244040 | tf_op jit(solution)/shard_map/ppermute | solution.py:26
  4.8 2.3 %project_own.1 = (bf16[128,128]{1,0:T(8,128)(2,1)S(1)}, bf16[32,16384]{1,0:T(8,128)(2,1)S(1)}) custom-call(bf16[304,256]{1,0:T(8,128)(2,1)S(1)} %get-tuple-element.29.table, s32[1,16384]{1,0:T(1,128)S(1)} %get-tuple-element.30.index_ref, f32[1,16384]{1,0:T(1,128)S(1)} %get-tuple-element.31.frac_ref, bf16[32,32768]{1,0:T(8,128)(2,1)} %images_hbm.3), custom_call_target="tpu_custom_call" | custom-call | flops 2000000000 | bytes 8000000 | tf_op jit(solution)/shard_map/project_own/pallas_call | solution.py:204
  7.2 5.0 %collective-permute-start.1 = (bf16[256,128]{1,0:T(8,128)(2,1)S(1)}, bf16[256,128]{1,0:T(8,128)(2,1)S(1)}, u32[]{:S(2)}, u32[]{:S(2)}) collective-permute-start(bf16[256,128]{1,0:T(8,128)(2,1)S(1)} %pair_rows.1.refs_0_), channel_id=1, source_target_pairs={{0,12},{1,13},{2,14},{3,15},{4,8},{5,9},{6,10},{7,11},{8,4},{9,5},... | collective-permute-start | bytes 196616 | tf_op jit(solution)/shard_map/ppermute | solution.py:26
  12.2 0.6 %collective-permute-start.2 = (bf16[256,128]{1,0:T(8,128)(2,1)S(1)}, bf16[256,128]{1,0:T(8,128)(2,1)S(1)}, u32[]{:S(2)}, u32[]{:S(2)}) collective-permute-start(bf16[256,128]{1,0:T(8,128)(2,1)S(1)} %pair_rows.1.refs_0_), channel_id=1, source_target_pairs={{0,4},{1,5},{2,6},{3,7},{4,0},{5,1},{6,2},{7,3},{8,12},{9,13},{10,... | collective-permute-start | bytes 196616 | tf_op jit(solution)/shard_map/ppermute | solution.py:26
  12.9 2.0 %collective-permute-done.1.refs_1_ = bf16[256,128]{1,0:T(8,128)(2,1)S(1)} collective-permute-done((bf16[256,128]{1,0:T(8,128)(2,1)S(1)}, bf16[256,128]{1,0:T(8,128)(2,1)S(1)}, u32[]{:S(2)}, u32[]{:S(2)}) %collective-permute-start.1) | collective-permute-done | bytes 65568 | tf_op jit(solution)/shard_map/ppermute | solution.py:26
  14.9 0.9 %correlate.2 = (f32[36,128]{1,0:T(8,128)S(1)}, f32[8,8192]{1,0:T(8,128)S(1)}, f32[8,8192]{1,0:T(8,128)S(1)}) custom-call(s32[2,8]{1,0:T(2,128)S(1)} %bitcast.6, bf16[32,16384]{1,0:T(8,128)(2,1)S(1)} %get-tuple-element.32.own_images, bf16[32,16896]{1,0:T(8,128)(2,1)S(1)} %collective-permute-done.other.other_images, bf16[256,128]{1,0:T(8,128)(2,1)S(1)} %pair_rows.1.refs_0_, ...), custom_call_target="tpu_custom_call" | custom-call | flops 1000000000 | bytes 4000000 | tf_op jit(solution)/shard_map/correlate/pallas_call | solution.py:361
  15.8 2.3 %collective-permute-done.3.refs_1_ = bf16[256,128]{1,0:T(8,128)(2,1)S(1)} collective-permute-done((bf16[256,128]{1,0:T(8,128)(2,1)S(1)}, bf16[256,128]{1,0:T(8,128)(2,1)S(1)}, u32[]{:S(2)}, u32[]{:S(2)}) %collective-permute-start.3) | collective-permute-done | bytes 65568 | tf_op jit(solution)/shard_map/ppermute | solution.py:26
  18.1 0.7 %correlate.3.refs_1_ = f32[36,128]{1,0:T(8,128)S(1)} custom-call(f32[8,8192]{1,0:T(8,128)S(1)} %get-tuple-element.36.cos_ref, f32[8,8192]{1,0:T(8,128)S(1)} %get-tuple-element.37.sin_ref, bf16[32,16384]{1,0:T(8,128)(2,1)S(1)} %get-tuple-element.32.own_images, bf16[32,16896]{1,0:T(8,128)(2,1)S(1)} %collective-permute-done.other.other_images, ...), custom_call_target="tpu_custom_call" | custom-call | flops 1000000000 | bytes 4000000 | tf_op jit(solution)/shard_map/correlate/pallas_call | solution.py:361
  18.8 0.0 copy-done
  18.8 0.1 collective-permute-start.4
  18.9 1.2 %collective-permute-done.4.received = f32[80,128]{1,0:T(8,128)S(1)} collective-permute-done((f32[80,128]{1,0:T(8,128)S(1)}, f32[80,128]{1,0:T(8,128)S(1)}, u32[]{:S(2)}, u32[]{:S(2)}) %collective-permute-start.4) | collective-permute-done | bytes 40992 | tf_op jit(solution)/shard_map/ppermute | solution.py:26
  20.1 0.4 %posterior.1 = (bf16[64,64]{1,0:T(8,128)(2,1)S(1)}, f32[128,128]{1,0:T(8,128)S(1)}, bf16[144,128]{1,0:T(8,128)(2,1)S(1)}, f32[8,128]{1,0:T(8,128)S(1)}) custom-call(f32[80,128]{1,0:T(8,128)S(1)} %collect.1.mine, f32[80,128]{1,0:T(8,128)S(1)} %collective-permute-done.4.received, bf16[32,16384]{1,0:T(8,128)(2,1)S(1)} %get-tuple-element.32.own_images, ...), custom_call_target="tpu_custom_call" | custom-call | tf_op jit(solution)/shard_map/posterior/pallas_call | solution.py:478
  20.5 1.6 %collective-permute-start.5 = (bf16[144,128]{1,0:T(8,128)(2,1)S(1)}, bf16[144,128]{1,0:T(8,128)(2,1)S(1)}, u32[]{:S(2)}, u32[]{:S(2)}) collective-permute-start(bf16[144,128]{1,0:T(8,128)(2,1)S(1)} %get-tuple-element.41), channel_id=1, source_target_pairs={{0,2},{1,3},{2,0},{3,1},{4,6},{5,7},{6,4},{7,5},{8,10},{9,11},{10,... | collective-permute-start | bytes 110600 | tf_op jit(solution)/shard_map/ppermute | solution.py:26
  22.1 1.3 %backproject.1 = (f32[224,128]{1,0:T(8,128)S(1)}, bf16[224,128]{1,0:T(8,128)(2,1)S(1)}, bf16[224,128]{1,0:T(8,128)(2,1)S(1)}, bf16[224,128]{1,0:T(8,128)(2,1)S(1)}) custom-call(bf16[64,64]{1,0:T(8,128)(2,1)S(1)} %get-tuple-element.38.weight_ref, bf16[32,16384]{1,0:T(8,128)(2,1)S(1)} %get-tuple-element.32.own_images, ...), custom_call_target="tpu_custom_call" | custom-call | flops 2000000000 | bytes 8000000 | tf_op jit(solution)/shard_map/backproject/pallas_call | solution.py:528
  23.4 1.1 %collective-permute-done.5.low_received = bf16[144,128]{1,0:T(8,128)(2,1)S(1)} collective-permute-done((bf16[144,128]{1,0:T(8,128)(2,1)S(1)}, bf16[144,128]{1,0:T(8,128)(2,1)S(1)}, u32[]{:S(2)}, u32[]{:S(2)}) %collective-permute-start.5) | collective-permute-done | bytes 36896 | tf_op jit(solution)/shard_map/ppermute | solution.py:26
  24.5 1.4 %collective-permute-start.6 = (bf16[272,128]{1,0:T(8,128)(2,1)S(1)}, bf16[272,128]{1,0:T(8,128)(2,1)S(1)}, u32[]{:S(2)}, u32[]{:S(2)}) collective-permute-start(bf16[272,128]{1,0:T(8,128)(2,1)S(1)} %get-tuple-element.48), channel_id=1, source_target_pairs={{0,8},{1,9},{2,10},{3,11},{4,12},{5,13},{6,14},{7,15},{8,0},{9,1},... | collective-permute-start | bytes 208904 | tf_op jit(solution)/shard_map/ppermute | solution.py:26
  25.9 1.7 %collective-permute-start.7 = (bf16[272,128]{1,0:T(8,128)(2,1)S(1)}, bf16[272,128]{1,0:T(8,128)(2,1)S(1)}, u32[]{:S(2)}, u32[]{:S(2)}) collective-permute-start(bf16[272,128]{1,0:T(8,128)(2,1)S(1)} %get-tuple-element.49), channel_id=1, source_target_pairs={{0,4},{1,5},{2,6},{3,7},{4,0},{5,1},{6,2},{7,3},{8,12},{9,13},{10,... | collective-permute-start | bytes 208904 | tf_op jit(solution)/shard_map/ppermute | solution.py:26
  27.7 1.3 %collective-permute-start.8 = (bf16[272,128]{1,0:T(8,128)(2,1)S(1)}, bf16[272,128]{1,0:T(8,128)(2,1)S(1)}, u32[]{:S(2)}, u32[]{:S(2)}) collective-permute-start(bf16[272,128]{1,0:T(8,128)(2,1)S(1)} %get-tuple-element.50), channel_id=1, source_target_pairs={{0,12},{1,13},{2,14},{3,15},{4,8},{5,9},{6,10},{7,11},{8,4},{9,5},... | collective-permute-start | bytes 208904 | tf_op jit(solution)/shard_map/ppermute | solution.py:26
  29.0 2.2 %collective-permute-done.6.refs_0_ = bf16[272,128]{1,0:T(8,128)(2,1)S(1)} collective-permute-done((bf16[272,128]{1,0:T(8,128)(2,1)S(1)}, bf16[272,128]{1,0:T(8,128)(2,1)S(1)}, u32[]{:S(2)}, u32[]{:S(2)}) %collective-permute-start.6) | collective-permute-done | bytes 69664 | tf_op jit(solution)/shard_map/ppermute | solution.py:26
  31.2 2.5 %collective-permute-done.8.refs_2_ = bf16[272,128]{1,0:T(8,128)(2,1)S(1)} collective-permute-done((bf16[272,128]{1,0:T(8,128)(2,1)S(1)}, bf16[272,128]{1,0:T(8,128)(2,1)S(1)}, u32[]{:S(2)}, u32[]{:S(2)}) %collective-permute-start.8) | collective-permute-done | bytes 69664 | tf_op jit(solution)/shard_map/ppermute | solution.py:26
  33.8 0.1 collective-permute-start.9
  33.9 1.2 %collective-permute-done.9.received = bf16[128,128]{1,0:T(8,128)(2,1)S(1)} collective-permute-done((bf16[128,128]{1,0:T(8,128)(2,1)S(1)}, bf16[128,128]{1,0:T(8,128)(2,1)S(1)}, u32[]{:S(2)}, u32[]{:S(2)}) %collective-permute-start.9) | collective-permute-done | bytes 32800 | tf_op jit(solution)/shard_map/ppermute | solution.py:26
  35.1 0.7 %finish.1 = (f32[256,128]{1,0:T(8,128)}, f32[8]{0:T(128)}) custom-call(f32[128,128]{1,0:T(8,128)S(1)} %get-tuple-element.51.own, bf16[128,128]{1,0:T(8,128)(2,1)S(1)} %collective-permute-done.9.received, f32[8,128]{1,0:T(8,128)S(1)} %get-tuple-element.53.mass), custom_call_target="tpu_custom_call" | custom-call | tf_op jit(solution)/shard_map/finish/pallas_call | solution.py:632
  (13 shorter events, 0.1 us)
Async XLA Ops:
  4.3 2.9 %collective-permute-start = (bf16[32,16896]{1,0:T(8,128)(2,1)S(1)}, bf16[32,16896]{1,0:T(8,128)(2,1)S(1)}, u32[]{:S(2)}, u32[]{:S(2)}) collective-permute-start(bf16[32,16896]{1,0:T(8,128)(2,1)S(1)} %get-tuple-element.33), channel_id=1, source_target_pairs={{0,1},{1,0},{2,3},{3,2},{4,5},{5,4},{6,7},{7,6},{8,9},{9,8},{10,11... | collective-permute-start | bytes 3244040 | tf_op jit(solution)/shard_map/ppermute | solution.py:26
  4.8 10.0 %copy-start.2 = (s32[8,2]{0,1:T(2,128)S(1)}, s32[8,2]{0,1:T(2,128)}, u32[]{:S(2)}) copy-start(s32[8,2]{0,1:T(2,128)} %param.13) | copy-start | bytes 196
  7.2 7.7 %collective-permute-start.1 = (bf16[256,128]{1,0:T(8,128)(2,1)S(1)}, bf16[256,128]{1,0:T(8,128)(2,1)S(1)}, u32[]{:S(2)}, u32[]{:S(2)}) collective-permute-start(bf16[256,128]{1,0:T(8,128)(2,1)S(1)} %pair_rows.1.refs_0_), channel_id=1, source_target_pairs={{0,12},{1,13},{2,14},{3,15},{4,8},{5,9},{6,10},{7,11},{8,4},{9,5},... | collective-permute-start | bytes 196616 | tf_op jit(solution)/shard_map/ppermute | solution.py:26
  12.2 5.9 %collective-permute-start.3 = (bf16[256,128]{1,0:T(8,128)(2,1)S(1)}, bf16[256,128]{1,0:T(8,128)(2,1)S(1)}, u32[]{:S(2)}, u32[]{:S(2)}) collective-permute-start(bf16[256,128]{1,0:T(8,128)(2,1)S(1)} %pair_rows.1.refs_0_), channel_id=1, source_target_pairs={{0,8},{1,9},{2,10},{3,11},{4,12},{5,13},{6,14},{7,15},{8,0},{9,1},... | collective-permute-start | bytes 196616 | tf_op jit(solution)/shard_map/ppermute | solution.py:26
  12.2 5.9 %collective-permute-start.2 = (bf16[256,128]{1,0:T(8,128)(2,1)S(1)}, bf16[256,128]{1,0:T(8,128)(2,1)S(1)}, u32[]{:S(2)}, u32[]{:S(2)}) collective-permute-start(bf16[256,128]{1,0:T(8,128)(2,1)S(1)} %pair_rows.1.refs_0_), channel_id=1, source_target_pairs={{0,4},{1,5},{2,6},{3,7},{4,0},{5,1},{6,2},{7,3},{8,12},{9,13},{10,... | collective-permute-start | bytes 196616 | tf_op jit(solution)/shard_map/ppermute | solution.py:26
  15.7 3.0 %copy-start = (f32[32]{0:T(128)S(1)}, f32[32]{0:T(128)}, u32[]{:S(2)}) copy-start(f32[32]{0:T(128)} %param.8) | copy-start | bytes 388
  15.8 3.0 %copy-start.1 = (s32[32]{0:T(128)S(1)}, s32[32]{0:T(128)}, u32[]{:S(2)}) copy-start(s32[32]{0:T(128)} %param.9) | copy-start | bytes 388
  18.8 1.3 %collective-permute-start.4 = (f32[80,128]{1,0:T(8,128)S(1)}, f32[80,128]{1,0:T(8,128)S(1)}, u32[]{:S(2)}, u32[]{:S(2)}) collective-permute-start(f32[80,128]{1,0:T(8,128)S(1)} %collect.1.mine), channel_id=1, source_target_pairs={{0,1},{1,0},{2,3},{3,2},{4,5},{5,4},{6,7},{7,6},{8,9},{9,8},{10,11... | collective-permute-start | bytes 122888 | tf_op jit(solution)/shard_map/ppermute | solution.py:26
  20.5 4.0 %collective-permute-start.5 = (bf16[144,128]{1,0:T(8,128)(2,1)S(1)}, bf16[144,128]{1,0:T(8,128)(2,1)S(1)}, u32[]{:S(2)}, u32[]{:S(2)}) collective-permute-start(bf16[144,128]{1,0:T(8,128)(2,1)S(1)} %get-tuple-element.41), channel_id=1, source_target_pairs={{0,2},{1,3},{2,0},{3,1},{4,6},{5,7},{6,4},{7,5},{8,10},{9,11},{10,... | collective-permute-start | bytes 110600 | tf_op jit(solution)/shard_map/ppermute | solution.py:26
  24.5 6.7 %collective-permute-start.6 = (bf16[272,128]{1,0:T(8,128)(2,1)S(1)}, bf16[272,128]{1,0:T(8,128)(2,1)S(1)}, u32[]{:S(2)}, u32[]{:S(2)}) collective-permute-start(bf16[272,128]{1,0:T(8,128)(2,1)S(1)} %get-tuple-element.48), channel_id=1, source_target_pairs={{0,8},{1,9},{2,10},{3,11},{4,12},{5,13},{6,14},{7,15},{8,0},{9,1},... | collective-permute-start | bytes 208904 | tf_op jit(solution)/shard_map/ppermute | solution.py:26
  25.9 5.3 %collective-permute-start.7 = (bf16[272,128]{1,0:T(8,128)(2,1)S(1)}, bf16[272,128]{1,0:T(8,128)(2,1)S(1)}, u32[]{:S(2)}, u32[]{:S(2)}) collective-permute-start(bf16[272,128]{1,0:T(8,128)(2,1)S(1)} %get-tuple-element.49), channel_id=1, source_target_pairs={{0,4},{1,5},{2,6},{3,7},{4,0},{5,1},{6,2},{7,3},{8,12},{9,13},{10,... | collective-permute-start | bytes 208904 | tf_op jit(solution)/shard_map/ppermute | solution.py:26
  27.7 6.1 %collective-permute-start.8 = (bf16[272,128]{1,0:T(8,128)(2,1)S(1)}, bf16[272,128]{1,0:T(8,128)(2,1)S(1)}, u32[]{:S(2)}, u32[]{:S(2)}) collective-permute-start(bf16[272,128]{1,0:T(8,128)(2,1)S(1)} %get-tuple-element.50), channel_id=1, source_target_pairs={{0,12},{1,13},{2,14},{3,15},{4,8},{5,9},{6,10},{7,11},{8,4},{9,5},... | collective-permute-start | bytes 208904 | tf_op jit(solution)/shard_map/ppermute | solution.py:26
  33.8 1.3 %collective-permute-start.9 = (bf16[128,128]{1,0:T(8,128)(2,1)S(1)}, bf16[128,128]{1,0:T(8,128)(2,1)S(1)}, u32[]{:S(2)}, u32[]{:S(2)}) collective-permute-start(bf16[128,128]{1,0:T(8,128)(2,1)S(1)} %get-tuple-element.52), channel_id=1, source_target_pairs={{0,1},{1,0},{2,3},{3,2},{4,5},{5,4},{6,7},{7,6},{8,9},{9,8},{10,11... | collective-permute-start | bytes 98312 | tf_op jit(solution)/shard_map/ppermute | solution.py:26
